TPU v7x, 32 devices: a whole 2x2x4 slice. The times are simulated.
32 devices in a mesh: chol: 8 (over z, y), walk: 4 (over x, core).
Axes of the slice: x: 2, y: 2, z: 4, core: 2. Of those that a mesh axis runs over, the one named last changes fastest.
Arguments:
- green_rows: bfloat16 [2048, 8, 256], P('chol', 'walk'), may hold values from -0.119628906 to 0.119628906
- cholesky_rot: bfloat16 [64, 256, 2048], P('chol'), may hold values from -0.125 to 0.125
- one_body: bfloat16 [2048, 256], P('chol'), may hold values from -0.25 to 0.25
- fields: float32 [64, 16], P('chol', 'walk'), may hold values from -5 to 5
- weights: float32 [8], P('walk'), may hold values from 0.3 to 3
- sources: int32 [16], P('walk'), may hold values from 0 to 7, as said below
- counts: int32 [4], replicated, may hold values from 0 to 4, as said below
- owners: int32 [4], replicated, may hold values from 0 to 3, each once
Outputs:
- energies: float32 [16], P('walk')
- new_weights: float32 [16], P('walk')
- density_panels: float32 [4, 131072], P('walk', 'chol')
Inputs may be any that keep to these rules, and one draw needn't show every extreme that they name: Slot j of group g is live exactly when j < counts[g]; the counts sum to 8, and some group has all 4 slots live. `sources`: entries of slots that are not live are read by no output.
All inputs are finite; a program needn't handle non-finite values.
Results may differ from a plain program's by a relative error of at most 0.0003.
Values may be sent and summed in bfloat16 or wider, within the bound.
No kernel may reach another device: no remote copies, remote signals or barrier semaphores. Data moves between devices by JAX's collectives and lax.ppermute only.
A program may use at most 192 MiB of HBM per device.

v0:
```python
import jax
import jax.numpy as jnp
from jax import lax
from jax.sharding import PartitionSpec as P

time_step = 0.02
root_step = 0.02**0.5


def measure(states, cholesky_rot, one_body):
    local_rows = states.shape[0]
    walker_count = states.shape[1]
    orbitals = states.shape[2]
    vectors_here = cholesky_rot.shape[0]
    basis_size = cholesky_rot.shape[2]
    flat_rot = cholesky_rot.reshape(vectors_here * orbitals, basis_size)
    folded = jnp.dot(
        flat_rot,
        lax.all_gather(
            states.reshape(local_rows, walker_count * orbitals), "chol", axis=0, tiled=True
        ),
        preferred_element_type=jnp.float32,
    )
    tensor = folded.reshape(vectors_here, orbitals, walker_count, orbitals)
    traces = jnp.sum(jnp.diagonal(tensor, axis1=1, axis2=3), axis=-1)
    exchange = jnp.einsum("cikj,cjki->k", tensor, tensor, precision=lax.Precision.HIGHEST)
    squares = jnp.sum(traces * traces, axis=0)
    onebody = jnp.einsum("mkn,mn->k", states, one_body, preferred_element_type=jnp.float32)
    return (traces, jnp.stack([exchange, squares, onebody]))


def per_device(green_rows, cholesky_rot, one_body, fields, weights, sources, counts, owners):
    walk_index = lax.axis_index("walk")
    walk_size = lax.axis_size("walk")
    slot_count = sources.shape[0]
    total_walkers = green_rows.shape[1] * walk_size
    slot_ids = jnp.arange(slot_count, dtype=jnp.int32)
    live_count = lax.dynamic_index_in_dim(counts, walk_index, 0, keepdims=False)
    live = (slot_ids < live_count).astype(jnp.float32)
    own_traces, own_stats = measure(green_rows, cholesky_rot, one_body)
    all_traces, all_stats = (
        lax.all_gather(own_traces, "walk", axis=1, tiled=True),
        lax.all_gather(own_stats, "walk", axis=1, tiled=True),
    )
    traces = jnp.take(all_traces, sources, axis=1)
    partial_stats = jnp.take(all_stats, sources, axis=1)
    drive_part = -root_step * jnp.sum(fields * traces, axis=0)
    stats, drive = lax.psum((partial_stats, drive_part), "chol")
    exchange = stats[0]
    squares = stats[1]
    onebody = stats[2]
    raw_energy = onebody + 0.5 * squares - 0.5 * exchange
    energies = live * raw_energy
    weight_sum = lax.psum(jnp.sum(weights), "walk")
    mean_weight = weight_sum / total_walkers
    new_weights = (
        live * mean_weight * jnp.exp(drive - 0.5 * time_step * squares - time_step * raw_energy)
    )
    weight_norm = lax.psum(jnp.sum(new_weights), "walk")
    pick = (sources[:, None] == jnp.arange(total_walkers, dtype=jnp.int32)[None, :]).astype(
        jnp.float32
    )
    spread = jnp.dot(new_weights, pick, precision=lax.Precision.HIGHEST)
    resident_weights = lax.psum_scatter(spread, "walk", scatter_dimension=0, tiled=True)
    partial_value = jnp.einsum(
        "b,mbj->mj",
        resident_weights,
        green_rows.astype(jnp.float32),
        precision=lax.Precision.HIGHEST,
    )
    local_rows = partial_value.shape[0]
    panel_width = partial_value.shape[1] // walk_size
    panels = partial_value.reshape(local_rows, walk_size, panel_width)
    onehot = (owners[None, :] == jnp.arange(walk_size, dtype=jnp.int32)[:, None]).astype(
        jnp.float32
    )
    arranged = jnp.einsum("kp,mpc->kmc", onehot, panels, precision=lax.Precision.HIGHEST)
    merged = lax.psum_scatter(
        arranged.reshape(walk_size, local_rows * panel_width),
        "walk",
        scatter_dimension=0,
        tiled=True,
    )
    return (energies, new_weights, merged / weight_norm)


def solution(mesh):
    return jax.shard_map(
        per_device,
        mesh=mesh,
        in_specs=(
            P("chol", "walk", None),
            P("chol", None, None),
            P("chol", None),
            P("chol", "walk"),
            P("walk"),
            P("walk"),
            P(),
            P(),
        ),
        out_specs=(P("walk"), P("walk"), P("walk", "chol")),
        check_vma=False,
    )
```

profile of v0, /device:TPU:0, one launch (start us, length us, event | category | flops | bytes accessed | tf_op | source)
XLA Modules:
  0.0 217.3 jit_solution(16039473352792890315)
XLA Ops:
  7.2 1.9 copy.30
  9.2 1.3 reduce_sum.47
  10.4 8.9 %psum.29 = f32[]{:T(128)} all-reduce(f32[]{:T(128)} %reduce_sum.47), channel_id=1, replica_groups=mesh['chol'=8,'walk'=4] {'walk'}, use_global_device_ids=true, to_apply=%region_4.5 | all-reduce | flops 1 | bytes 8 | tf_op jit(solution)/shard_map/psum | solution.py:54
  19.3 1.2 dynamic_slice.4
  21.2 1.3 dynamic-slice
  22.6 0.7 compare_select_fusion
  23.2 1.7 convolution_bitcast_fusion.1
  25.0 0.7 compare_and_fusion
  25.6 38.2 %all-gather.4.cloned.1.call-done = bf16[2048,512]{0,1:T(8,128)(2,1)} async-done(((bf16[256,512]{0,1:T(8,128)(2,1)}), bf16[2048,512]{0,1:T(8,128)(2,1)}) %all-gather.4.cloned.1.call-update) | async-done | bytes 2097168 | tf_op jit(solution)/shard_map/all_gather | solution.py:19
  63.9 10.5 %fusion = f32[8,256,2,256]{3,1,2,0:T(8,128)} fusion(bf16[2,256,2048,1]{2,1,0,3:T(8,128)(2,1)} %bitcast.74, bf16[8,256,2048]{2,1,0:T(8,128)(2,1)} %param.9), kind=kOutput, calls=%fused_computation.3 | convolution fusion | flops 4294967296 | bytes 14680064 | tf_op jit(solution)/shard_map/dot_general | solution.py:17
  74.4 5.3 %copy.27 = f32[2,8,256,256]{2,3,0,1:T(8,128)} copy(f32[2,8,256,256]{3,2,0,1:T(8,128)} %bitcast.63) | data formatting | bytes 8388608
  79.7 4.1 %multiply_reduce_fusion = f32[2]{0:T(128)S(1)} fusion(f32[2,8,256,256]{2,3,0,1:T(8,128)} %copy.27, f32[8,256,2,256]{3,1,2,0:T(8,128)} %fusion), kind=kLoop, calls=%fused_computation.5 | loop fusion | flops 2097150 | bytes 8388616 | tf_op jit(solution)/shard_map/cikj,cjki->k/dot_general | solution.py:26
  83.9 49.0 %copy.18 = f32[8,2,256,256]{0,1,3,2:T(2,128)} copy(f32[8,2,256,256]{3,2,1,0:T(8,128)} %bitcast.64) | data formatting | bytes 8388608 | tf_op jit(solution)/shard_map/jit(diagonal)/transpose | solution.py:25
  132.9 2.5 %gather_fusion = f32[256,8,2]{1,2,0:T(2,128)S(1)} fusion(f32[8,2,256,256]{0,1,3,2:T(2,128)} %copy.18, s32[256]{0:T(256)S(1)} %bitcast.65), kind=kCustom, calls=%fused_computation | custom fusion | bytes 34816 | tf_op jit(solution)/shard_map/jit(diagonal)/gather | solution.py:25
  135.9 5.1 %all-gather = f32[4,2,3]{2,1,0:T(2,128)S(1)} all-gather(f32[1,2,3]{2,1,0:T(2,128)S(1)} %bitcast.71), channel_id=1, replica_groups=mesh['chol'=8,'walk'=4] {'walk'}, dimensions={0}, use_global_device_ids=true | all-gather | bytes 120 | tf_op jit(solution)/shard_map/all_gather | solution.py:43
  140.9 5.1 %all-gather.1 = f32[4,2,8]{2,1,0:T(2,128)S(1)} all-gather(f32[1,2,8]{2,1,0:T(2,128)S(1)} %bitcast.70), channel_id=1, replica_groups=mesh['chol'=8,'walk'=4] {'walk'}, dimensions={0}, use_global_device_ids=true | all-gather | bytes 320 | tf_op jit(solution)/shard_map/all_gather | solution.py:42
  146.5 0.6 gather_fusion.2
  148.0 18.6 %all-reduce.2 = (f32[3,4]{0,1:T(4,128)S(1)}, f32[4]{0:T(128)S(1)}) all-reduce(f32[3,4]{0,1:T(4,128)S(1)} %select_bitcast_fusion, f32[4]{0:T(128)S(1)} %broadcast_multiply_fusion), channel_id=1, replica_groups=mesh['chol'=8,'walk'=4] {'chol'}, use_global_device_ids=true, to_apply=%region_2.3 | all-reduce | flops 16 | bytes 128 | tf_op jit(solution)/shard_map/psum | solution.py:48
  166.8 1.8 fusion.10
  168.8 6.4 %all-reduce.3 = (f32[8]{0:T(128)S(1)}, f32[]{:T(128)}) all-reduce(f32[8]{0:T(128)S(1)} %convolution_bitcast_fusion, f32[]{:T(128)} %get-tuple-element.9), channel_id=2, replica_groups=mesh['chol'=8,'walk'=4] {'walk'}, use_global_device_ids=true, to_apply=%region_7.8.clone | all-reduce | flops 9 | bytes 72
  175.2 1.0 fusion.9
  176.8 1.1 fusion.4
  177.9 29.6 %all-reduce.6.cloned.1.call-done = f32[4,16384]{1,0:T(4,128)} async-done(((f32[4,16384]{1,0:T(4,128)}), f32[4,16384]{1,0:T(4,128)}) %all-reduce.6.cloned.1.call-update) | async-done | bytes 262160
  207.5 3.0 %dynamic-slice_divide_fusion = f32[1,16384]{1,0:T(1,128)} fusion(f32[4,16384]{1,0:T(4,128)} %all-reduce.6.cloned.1.call-done, u32[]{:T(128)} %bitcast.39, f32[]{:T(128)} %get-tuple-element.8), kind=kLoop, calls=%fused_computation.9 | loop fusion | flops 16384 | bytes 131080 | tf_op jit(solution)/shard_map/div | solution.py:84
  (31 shorter events, 2.5 us)
Async XLA Ops:
  7.2 16.1 %copy-start = (bf16[256,256]{1,0:T(8,128)(2,1)S(1)}, bf16[256,256]{1,0:T(8,128)(2,1)}, u32[]{:S(2)}) copy-start(bf16[256,256]{1,0:T(8,128)(2,1)} %param.10) | copy-start | bytes 393220
  7.2 56.7 %all-gather.4.cloned.1.call-start = ((), (), s32[]{:S(2)}) async-start(), calls=%async_computation | async-start | bytes 2359296 | tf_op jit(solution)/shard_map/all_gather | solution.py:19
  9.1 198.4 %all-reduce.6.cloned.1.call-start = ((), (), s32[]{:S(2)}) async-start(), calls=%async_computation.1 | async-start | bytes 524288
  83.8 63.3 %copy-start.2 = (f32[8,4]{0,1:T(4,128)S(1)}, f32[8,4]{0,1:T(4,128)}, u32[]{:S(2)}) copy-start(f32[8,4]{0,1:T(4,128)} %param.11) | copy-start | bytes 388
  83.9 84.8 %copy-start.5 = (s32[4]{0:T(128)S(1)}, s32[4]{0:T(128)}, u32[]{:S(2)}) copy-start(s32[4]{0:T(128)} %param.13) | copy-start | bytes 52
  83.9 91.3 %copy-start.1 = (bf16[256,2,256]{2,1,0:T(2,128)(2,1)S(1)}, bf16[256,2,256]{2,1,0:T(2,128)(2,1)}, u32[]{:S(2)}) copy-start(bf16[256,2,256]{2,1,0:T(2,128)(2,1)} %param.8) | copy-start | bytes 786436
  83.9 93.0 %copy-start.3 = (s32[4]{0:T(128)S(1)}, s32[4]{0:T(128)}, u32[]{:S(2)}) copy-start(s32[4]{0:T(128)} %param.15) | copy-start | bytes 52
  168.6 41.9 %copy-start.4 = (f32[4]{0:T(128)}, f32[4]{0:T(128)S(1)}, u32[]{:S(2)}) copy-start(f32[4]{0:T(128)S(1)} %get-tuple-element.10) | copy-start | bytes 52
Sparse Core Ops, SparseCore 0:
  10.1 53.7 all-gather.3
  178.0 29.4 all-reduce.5
where the time goes:
time: 221 us; the launch traced here: 217 us
  waiting for transfers between devices  67.9 us (31%)
  local copies, waits for them, and re-layouts  63.1 us (29%)
  blocking collectives  44 us (20%)
  between operations  15.4 us (7%)
  matrix products  14.5 us (7%)
  other arithmetic  12.4 us (6%)
    transpose x1, local copies, waits for them, and re-layouts, measure(): traces = jnp.sum(jnp.diagonal(tensor, axis1=1, axis2=3), axis=-1)  49 us
    all_gather x1, waiting for transfers between devices, measure(): lax.all_gather(states.reshape(local_rows, walker_count * orbitals), 'chol...  38.2 us
    unnamed x3, waiting for transfers between devices  29.6 us
    psum x1, blocking collectives, per_device(): stats, drive = lax.psum((partial_stats, drive_part), 'chol')  18.6 us
    dot_general x1, matrix products, measure(): jnp.dot(flat_rot, lax.all_gather(states.reshape(local_rows, walker_count...  10.5 us
    psum x1, blocking collectives, per_device(): weight_sum = lax.psum(jnp.sum(weights), 'walk')  8.92 us
    unnamed x15, local copies, waits for them, and re-layouts  6.78 us
    unnamed x1, blocking collectives  6.36 us
  transfers between devices with their start and end apart: 2, of which 2 were waited for; matrix products, arithmetic and copies ran while one was open for 3% of the time, Pallas kernels for 0%

commit v1 on v0

v1 whole, which is shorter than its diff:
```python
import functools

import jax
import jax.numpy as jnp
from jax import lax
from jax.experimental import pallas as pl
from jax.experimental.pallas import tpu as pltpu
from jax.sharding import PartitionSpec as P

time_step = 0.02
root_step = 0.02**0.5
LANES = 128
VMEM_LIMIT = 48 * 1024 * 1024
RING_LIMIT = 16


def params(**more):
    return pltpu.CompilerParams(vmem_limit_bytes=VMEM_LIMIT, **more)


def vmem():
    return pl.BlockSpec(memory_space=pltpu.VMEM)


def smem():
    return pl.BlockSpec(memory_space=pltpu.SMEM)


def ring_order(size):
    return [2 * q if q < size // 2 else 2 * (size - 1 - q) + 1 for q in range(size)]


def ring_place(index, size):
    return jnp.where(index % 2 == 0, index // 2, size - 1 - index // 2)


def ring_owner(place, size):
    return jnp.where(place < size // 2, 2 * place, 2 * (size - 1 - place) + 1)


def split_walkers(green_rows):
    rows, walkers, orbitals = green_rows.shape

    def kernel(green_ref, *outs):
        for b in range(walkers):
            outs[b][...] = green_ref[:, b, :]

    return pl.pallas_call(
        kernel,
        name="split_walkers",
        out_shape=[jax.ShapeDtypeStruct((rows, orbitals), green_rows.dtype)] * walkers,
        in_specs=[vmem()],
        out_specs=[vmem()] * walkers,
        compiler_params=params(),
        cost_estimate=pl.CostEstimate(flops=0, bytes_accessed=4 * rows * walkers * orbitals, transcendentals=0),
    )(green_rows)


def gather_rows(blocks):
    size = lax.axis_size("chol")
    if size > RING_LIMIT or size % 2:
        return [(None, [lax.all_gather(x, "chol", axis=0, tiled=True) for x in blocks])]
    order = ring_order(size)
    ahead = [(order[q], order[(q + 1) % size]) for q in range(size)]
    back = [(order[q], order[(q - 1) % size]) for q in range(size)]
    parts = [(0, blocks)]
    right, left = blocks, blocks
    half = len(blocks) // 2
    for step in range(1, size // 2):
        right = [lax.ppermute(x, "chol", ahead) for x in right]
        left = [lax.ppermute(x, "chol", back) for x in left]
        parts.append((-step, right))
        parts.append((step, left))
    last = [lax.ppermute(x, "chol", ahead) for x in right[:half]]
    last += [lax.ppermute(x, "chol", back) for x in left[half:]]
    parts.append((size // 2, last))
    return parts


def pack(blocks, one_body, fields, weights, sources, owners):
    rows, orbitals = blocks[0].shape
    walk_size = lax.axis_size("walk")
    walkers = len(blocks)
    width = orbitals // walk_size
    pair = LANES // width
    vectors, slots = fields.shape
    table_rows = -(-(vectors + 2) // 8) * 8

    def kernel(*refs):
        green = refs[:walkers]
        body_ref, fields_ref, weights_ref, sources_ref, owners_ref = refs[walkers : walkers + 5]
        panels = refs[walkers + 5 : walkers + 5 + walk_size]
        onebody_ref, table_ref = refs[walkers + 5 + walk_size :]
        walk = lax.axis_index("walk")
        lane = lax.broadcasted_iota(jnp.int32, (1, LANES), 1)
        body = body_ref[...].astype(jnp.float32)
        onebody_ref[...] = jnp.zeros_like(onebody_ref)
        for b in range(walkers):
            total = jnp.sum(green[b][...].astype(jnp.float32) * body, axis=0, keepdims=True)
            folded = total[:, :LANES]
            for start in range(LANES, orbitals, LANES):
                folded = folded + total[:, start : start + LANES]
            onebody_ref[b : b + 1, :] = folded
        r = lax.broadcasted_iota(jnp.int32, (rows // pair, rows), 0)
        m = lax.broadcasted_iota(jnp.int32, (rows // pair, rows), 1)
        k = lax.broadcasted_iota(jnp.int32, (orbitals, LANES), 0)
        c = lax.broadcasted_iota(jnp.int32, (orbitals, LANES), 1)
        thinned = []
        for b in range(walkers):
            values = green[b][...]
            thinned.append(
                [
                    jnp.dot(
                        (m == r * pair + h).astype(jnp.bfloat16), values, preferred_element_type=jnp.float32
                    ).astype(jnp.bfloat16)
                    for h in range(pair)
                ]
            )
        for d in range(walk_size):
            target = lax.rem(walk + d, walk_size)
            panel = jnp.int32(0)
            for p in range(walk_size):
                panel = jnp.where(owners_ref[p] == target, p, panel)
            for b in range(walkers):
                total = jnp.zeros((rows // pair, LANES), jnp.float32)
                for h in range(pair):
                    take = (k == panel * width + c - h * width) & (c >= h * width) & (c < (h + 1) * width)
                    total += jnp.dot(
                        thinned[b][h], take.astype(jnp.bfloat16), preferred_element_type=jnp.float32
                    )
                panels[d][b] = total.astype(jnp.bfloat16)
        spread = jnp.zeros((vectors, LANES), jnp.float32)
        source = jnp.zeros((1, LANES), jnp.float32)
        for j in range(slots):
            mine = lane % slots == j
            spread += jnp.where(mine, fields_ref[:, j : j + 1], 0.0)
            source += jnp.where(mine, sources_ref[j].astype(jnp.float32), 0.0)
        weight = weights_ref[0]
        for j in range(1, weights.shape[0]):
            weight = weight + weights_ref[j]
        table_ref[...] = jnp.zeros_like(table_ref)
        table_ref[:vectors, :] = spread
        table_ref[vectors : vectors + 1, :] = source
        table_ref[vectors + 1 : vectors + 2, :] = jnp.zeros((1, LANES), jnp.float32) + weight

    out = pl.pallas_call(
        kernel,
        name="pack",
        out_shape=[jax.ShapeDtypeStruct((walkers, rows // pair, LANES), jnp.bfloat16)] * walk_size
        + [jax.ShapeDtypeStruct((8, LANES), jnp.float32), jax.ShapeDtypeStruct((table_rows, LANES), jnp.float32)],
        in_specs=[vmem()] * (walkers + 2) + [smem()] * 3,
        out_specs=[vmem()] * (walk_size + 2),
        compiler_params=params(),
        cost_estimate=pl.CostEstimate(flops=10**8, bytes_accessed=10**6, transcendentals=0),
    )(*blocks, one_body, fields, weights, sources, owners)
    return out[:walk_size], out[walk_size], out[walk_size + 1]


def shifted(x, d):
    size = lax.axis_size("walk")
    return lax.ppermute(x, "walk", [(q, (q + d) % size) for q in range(size)])


def merge_tables(tables, rows, walk, walk_size, slots, lane):
    total = jnp.zeros((rows, LANES), jnp.float32)
    for d, table in enumerate(tables):
        group = lax.rem(walk - d + walk_size, walk_size)
        total += jnp.where(lane // slots == group, table[:rows, :], 0.0)
    return total


def measure(cholesky_rot, parts, tables, onebody, slots):
    vectors, orbitals, basis = cholesky_rot.shape
    walkers = len(parts[0][1])
    walk_size = len(tables)
    chol_size = lax.axis_size("chol")
    shards = [x for _, arrays in parts for x in arrays]
    spots = [(shift, b) for shift, _ in parts for b in range(walkers)]
    eye_blocks = orbitals // LANES

    def kernel(*refs):
        chol_ref = refs[0]
        table_refs = refs[1 : 1 + walk_size]
        onebody_ref = refs[1 + walk_size]
        shard_refs = refs[2 + walk_size : 2 + walk_size + len(shards)]
        out_ref, rows_scr, exchange_scr, small_scr, sem = refs[2 + walk_size + len(shards) :]
        g = pl.program_id(0)
        walk = lax.axis_index("walk")
        chol = lax.axis_index("chol")
        lane = lax.broadcasted_iota(jnp.int32, (1, LANES), 1)
        tables_here = merge_tables([t[...] for t in table_refs], vectors + 1, walk, walk_size, slots, lane)
        picks = [
            jnp.where(
                (lane < slots * walk_size) & (tables_here[vectors : vectors + 1, :] == (walk * walkers + b).astype(jnp.float32)),
                1.0,
                0.0,
            )
            for b in range(walkers)
        ]

        @pl.when(g == 0)
        def _():
            place = ring_place(chol, chol_size)
            copies = []
            for n, (shard, (shift, b)) in enumerate(zip(shard_refs, spots)):
                rows = shard.shape[0]
                if shift is None:
                    start = 0
                else:
                    owner = ring_owner(lax.rem(place + shift + chol_size, chol_size), chol_size)
                    start = pl.multiple_of(owner * rows, rows)
                copies.append(
                    pltpu.make_async_copy(
                        shard,
                        rows_scr.at[pl.ds(start, rows), pl.ds(b * orbitals, orbitals)],
                        sem.at[n],
                    )
                )
            for copy in copies:
                copy.start()
            exchange_scr[...] = jnp.zeros_like(exchange_scr)
            small_scr[...] = jnp.zeros_like(small_scr)
            for copy in copies:
                copy.wait()

        tensor = jnp.dot(chol_ref[0], rows_scr[...], preferred_element_type=jnp.float32)
        row = lax.broadcasted_iota(jnp.int32, (LANES, LANES), 0)
        col = lax.broadcasted_iota(jnp.int32, (LANES, LANES), 1)
        eye = row == col
        field = jnp.sum(
            jnp.where(
                lax.broadcasted_iota(jnp.int32, (vectors, LANES), 0) == g, tables_here[:vectors, :], 0.0
            ),
            axis=0,
            keepdims=True,
        )
        drive = small_scr[walkers : walkers + 1, :]
        for b in range(walkers):
            block = tensor[:, b * orbitals : (b + 1) * orbitals]
            exchange_scr[b : b + 1, :] += jnp.sum(block * block.T, axis=0, keepdims=True)
            diagonal = jnp.zeros((1, LANES), jnp.float32)
            for q in range(eye_blocks):
                piece = block[q * LANES : (q + 1) * LANES, q * LANES : (q + 1) * LANES]
                diagonal += jnp.sum(jnp.where(eye, piece, 0.0), axis=0, keepdims=True)
            trace = jnp.sum(diagonal, axis=1, keepdims=True)
            small_scr[b : b + 1, :] += jnp.broadcast_to(trace * trace, (1, LANES))
            drive = drive - root_step * picks[b] * field * trace
        small_scr[walkers : walkers + 1, :] = drive

        @pl.when(g == vectors - 1)
        def _():
            raw = jnp.zeros((1, LANES), jnp.float32)
            squares = jnp.zeros((1, LANES), jnp.float32)
            for b in range(walkers):
                exchange = jnp.sum(exchange_scr[b : b + 1, :], axis=1, keepdims=True)
                single = jnp.sum(onebody_ref[b : b + 1, :], axis=1, keepdims=True)
                square = small_scr[b : b + 1, :]
                raw += picks[b] * (single + 0.5 * square - 0.5 * exchange)
                squares += picks[b] * square
            power = drive - 0.5 * time_step * squares - time_step * raw
            out_ref[...] = raw + pltpu.roll(power, slots * walk_size, 1)

    return pl.pallas_call(
        kernel,
        name="measure",
        grid=(vectors,),
        out_shape=jax.ShapeDtypeStruct((1, LANES), jnp.float32),
        in_specs=[pl.BlockSpec((1, orbitals, basis), lambda g: (g, 0, 0))]
        + [vmem()] * (walk_size + 1)
        + [pl.BlockSpec(memory_space=pl.ANY)] * len(shards),
        out_specs=vmem(),
        scratch_shapes=[
            pltpu.VMEM((basis, walkers * orbitals), jnp.bfloat16),
            pltpu.VMEM((8, orbitals), jnp.float32),
            pltpu.VMEM((8, LANES), jnp.float32),
            pltpu.SemaphoreType.DMA((len(shards),)),
        ],
        compiler_params=params(dimension_semantics=("arbitrary",)),
        cost_estimate=pl.CostEstimate(
            flops=2 * vectors * orbitals * basis * walkers * orbitals,
            bytes_accessed=2 * vectors * orbitals * basis,
            transcendentals=0,
        ),
    )(cholesky_rot, *tables, onebody, *shards)


def finish(stats, tables, panels, counts, vectors, slots):
    walk_size = len(tables)
    walkers, rows, _ = panels[0].shape

    def kernel(stats_ref, counts_ref, *refs):
        table_refs = refs[:walk_size]
        panel_refs = refs[walk_size : 2 * walk_size]
        energies_ref, weights_ref, density_ref = refs[2 * walk_size :]
        walk = lax.axis_index("walk")
        lane = lax.broadcasted_iota(jnp.int32, (1, LANES), 1)
        all_slots = slots * walk_size
        source = merge_tables(
            [t[vectors : vectors + 1, :] for t in table_refs], 1, walk, walk_size, slots, lane
        )
        total_weight = table_refs[0][vectors + 1 : vectors + 2, :]
        for t in table_refs[1:]:
            total_weight = total_weight + t[vectors + 1 : vectors + 2, :]
        mean_weight = total_weight / (walkers * walk_size)
        total = jnp.sum(stats_ref[...], axis=0, keepdims=True)
        power = pltpu.roll(total, LANES - all_slots, 1)
        live_count = jnp.zeros((1, LANES), jnp.int32)
        for q in range(walk_size):
            live_count = jnp.where(lane // slots == q, counts_ref[q], live_count)
        live = (lane < all_slots) & (lane % slots < live_count)
        energies = jnp.where(live, total, 0.0)
        new_weights = jnp.where(live, mean_weight * jnp.exp(jnp.where(live, power, 0.0)), 0.0)
        norm = jnp.sum(new_weights, axis=1, keepdims=True)
        density = jnp.zeros((rows, LANES), jnp.float32)
        for d in range(walk_size):
            group = lax.rem(walk - d + walk_size, walk_size)
            for b in range(walkers):
                walker = (group * walkers + b).astype(jnp.float32)
                share = jnp.sum(jnp.where(source == walker, new_weights, 0.0), axis=1, keepdims=True) / norm
                density += share * panel_refs[d][b].astype(jnp.float32)
        density_ref[...] = density
        first = lax.rem(LANES - walk * slots, LANES)
        energies_ref[...] = pltpu.roll(jnp.broadcast_to(energies, (8, LANES)), first, 1)[:1, :slots]
        weights_ref[...] = pltpu.roll(jnp.broadcast_to(new_weights, (8, LANES)), first, 1)[:1, :slots]

    return pl.pallas_call(
        kernel,
        name="finish",
        out_shape=[
            jax.ShapeDtypeStruct((1, slots), jnp.float32),
            jax.ShapeDtypeStruct((1, slots), jnp.float32),
            jax.ShapeDtypeStruct((rows, LANES), jnp.float32),
        ],
        in_specs=[vmem(), smem()] + [vmem()] * (2 * walk_size),
        out_specs=[vmem()] * 3,
        compiler_params=params(),
        cost_estimate=pl.CostEstimate(flops=10**6, bytes_accessed=6 * 10**5, transcendentals=128),
    )(stats, counts, *tables, *panels)


def per_device(green_rows, cholesky_rot, one_body, fields, weights, sources, counts, owners):
    walk_size = lax.axis_size("walk")
    vectors, slots = fields.shape
    blocks = split_walkers(green_rows)
    parts = gather_rows(blocks)
    panels, onebody, table = pack(blocks, one_body, fields, weights, sources, owners)
    panels = [panels[0]] + [shifted(panels[d], d) for d in range(1, walk_size)]
    tables = [table] + [shifted(table, d) for d in range(1, walk_size)]
    stats = measure(cholesky_rot, parts, tables, onebody, slots)
    stats = lax.all_gather(stats, ("chol", "walk"), axis=0, tiled=True)
    energies, new_weights, density = finish(stats, tables, panels, counts, vectors, slots)
    return energies.reshape(slots), new_weights.reshape(slots), density.reshape(1, density.size)


def solution(mesh):
    return jax.shard_map(
        per_device,
        mesh=mesh,
        in_specs=(
            P("chol", "walk", None),
            P("chol", None, None),
            P("chol", None),
            P("chol", "walk"),
            P("walk"),
            P("walk"),
            P(),
            P(),
        ),
        out_specs=(P("walk"), P("walk"), P("walk", "chol")),
        check_vma=False,
    )
```

time: 221 us -> 93.4 us (0.42); the launches traced: 217 us -> 93 us
  local copies, waits for them, and re-layouts: 63.1 us -> 4.57 us
  waiting for transfers between devices: 67.9 us -> 12.6 us
  starting transfers between devices: 0.08 us -> 21.1 us
  between operations: 15.4 us -> 0.7 us
  matrix products: 14.5 us -> 0 us
  Pallas kernels: 0 us -> 13.4 us
  other arithmetic: 12.4 us -> 0 us
  blocking collectives: 44 us -> 40.6 us
    transpose x1 -> x0, local copies, waits for them, and re-layouts: 49 us -> none  [measure(): traces = jnp.sum(jnp.diagonal(tensor, axis1=1, axis2=3), axis=-1)]
    all_gather x1 -> x0, waiting for transfers between devices: 38.2 us -> none  [measure(): lax.all_gather(states.reshape(local_rows, walker_count * orbitals), 'chol...]
    all_gather x2 -> x1, blocking collectives: 10.1 us -> 40.6 us  [per_device(): stats = lax.all_gather(stats, ('chol', 'walk'), axis=0, tiled=True)]
    unnamed x3 -> x0, waiting for transfers between devices: 29.6 us -> none
    psum x2 -> x0, blocking collectives: 27.5 us -> none  [the longest x1 18.6 us: per_device(): stats, drive = lax.psum((partial_stats, drive_part), 'chol')]
    ppermute x0 -> x20, starting transfers between devices: none -> 21.1 us  [the longest x6 11.2 us: gather_rows(): right = [lax.ppermute(x, 'chol', ahead) for x in right]]
    dot_general x5 -> x0, matrix products: 14.5 us -> none  [the longest x1 10.5 us: measure(): jnp.dot(flat_rot, lax.all_gather(states.reshape(local_rows, walker_count...]
    pallas_call x0 -> x4, Pallas kernels: none -> 13.4 us  [the longest x1 10.3 us: measure(): pl.pallas_call(kernel, name='measure', grid=(vectors,), out_shape=jax.Sha...]
  transfers between devices with their start and end apart: 2 -> 20, of which waited for: 2 -> 7; matrix products, arithmetic and copies ran while one was open for 3% -> 1% of each run, Pallas kernels for 0% -> 12%
where the time goes in v1:
time: 93.4 us; the launch traced here: 93 us
  blocking collectives  40.6 us (43%)
  starting transfers between devices  21.1 us (23%)
  Pallas kernels  13.4 us (14%)
  waiting for transfers between devices  12.6 us (13%)
  local copies, waits for them, and re-layouts  4.57 us (5%)
    all_gather x1, blocking collectives, per_device(): stats = lax.all_gather(stats, ('chol', 'walk'), axis=0, tiled=True)  40.6 us
    ppermute x6, starting transfers between devices, gather_rows(): right = [lax.ppermute(x, 'chol', ahead) for x in right]  11.2 us
    pallas_call x1, Pallas kernels, measure(): pl.pallas_call(kernel, name='measure', grid=(vectors,), out_shape=jax.Sha...  10.3 us
    ppermute x6, waiting for transfers between devices, shifted(): return lax.ppermute(x, 'walk', [(q, (q + d) % size) for q in range(size)])  5.9 us
    ppermute x6, starting transfers between devices, shifted(): return lax.ppermute(x, 'walk', [(q, (q + d) % size) for q in range(size)])  5.35 us
    ppermute x6, waiting for transfers between devices, gather_rows(): left = [lax.ppermute(x, 'chol', back) for x in left]  4.81 us
    unnamed x13, local copies, waits for them, and re-layouts  4.57 us
    ppermute x6, starting transfers between devices, gather_rows(): left = [lax.ppermute(x, 'chol', back) for x in left]  2.54 us
  transfers between devices with their start and end apart: 20, of which 7 were waited for; matrix products, arithmetic and copies ran while one was open for 1% of the time, Pallas kernels for 12%

profile of v1, /device:TPU:0, one launch (start us, length us, event | category | flops | bytes accessed | tf_op | source)
XLA Modules:
  0.0 93.0 jit_solution(1591900276436460895)
XLA Ops:
  0.6 0.9 %copy-done = bf16[256,2,256]{2,1,0:T(2,128)(2,1)S(1)} copy-done((bf16[256,2,256]{2,1,0:T(2,128)(2,1)S(1)}, bf16[256,2,256]{2,1,0:T(2,128)(2,1)}, u32[]{:S(2)}) %copy-start) | copy-done | bytes 262168
  2.1 3.1 %collective-permute-start.3 = (bf16[256,256]{1,0:T(8,128)(2,1)S(1)}, bf16[256,256]{1,0:T(8,128)(2,1)S(1)}, u32[]{:S(2)}, u32[]{:S(2)}) collective-permute-start(bf16[256,256]{1,0:T(8,128)(2,1)S(1)} %get-tuple-element.14.refs_0_.refs_6_), channel_id=1, source_target_pairs={{0,8},{8,16},{16,24},{24,28},{28,20},{20,12},{12,4},{4,0},{1,9},{9... | collective-permute-start | bytes 393224 | tf_op jit(solution)/shard_map/ppermute | solution.py:70
  5.2 2.0 %collective-permute-start.5 = (bf16[256,256]{1,0:T(8,128)(2,1)S(1)}, bf16[256,256]{1,0:T(8,128)(2,1)S(1)}, u32[]{:S(2)}, u32[]{:S(2)}) collective-permute-start(bf16[256,256]{1,0:T(8,128)(2,1)S(1)} %get-tuple-element.14.refs_0_.refs_6_), channel_id=1, source_target_pairs={{0,4},{8,0},{16,8},{24,16},{28,24},{20,28},{12,20},{4,12},{1,5},{9... | collective-permute-start | bytes 393224 | tf_op jit(solution)/shard_map/ppermute | solution.py:71
  7.3 1.8 %collective-permute-done.3.refs_8_ = bf16[256,256]{1,0:T(8,128)(2,1)S(1)} collective-permute-done((bf16[256,256]{1,0:T(8,128)(2,1)S(1)}, bf16[256,256]{1,0:T(8,128)(2,1)S(1)}, u32[]{:S(2)}, u32[]{:S(2)}) %collective-permute-start.3) | collective-permute-done | bytes 131104 | tf_op jit(solution)/shard_map/ppermute | solution.py:70
  9.1 2.5 %collective-permute-start.7 = (bf16[256,256]{1,0:T(8,128)(2,1)S(1)}, bf16[256,256]{1,0:T(8,128)(2,1)S(1)}, u32[]{:S(2)}, u32[]{:S(2)}) collective-permute-start(bf16[256,256]{1,0:T(8,128)(2,1)S(1)} %collective-permute-done.3.refs_8_), channel_id=1, source_target_pairs={{0,8},{8,16},{16,24},{24,28},{28,20},{20,12},{12,4},{4,0},{1,9},{9... | collective-permute-start | bytes 393224 | tf_op jit(solution)/shard_map/ppermute | solution.py:70
  11.6 2.6 %collective-permute-done.5.refs_10_ = bf16[256,256]{1,0:T(8,128)(2,1)S(1)} collective-permute-done((bf16[256,256]{1,0:T(8,128)(2,1)S(1)}, bf16[256,256]{1,0:T(8,128)(2,1)S(1)}, u32[]{:S(2)}, u32[]{:S(2)}) %collective-permute-start.5) | collective-permute-done | bytes 131104 | tf_op jit(solution)/shard_map/ppermute | solution.py:71
  14.2 2.0 %collective-permute-start.8 = (bf16[256,256]{1,0:T(8,128)(2,1)S(1)}, bf16[256,256]{1,0:T(8,128)(2,1)S(1)}, u32[]{:S(2)}, u32[]{:S(2)}) collective-permute-start(bf16[256,256]{1,0:T(8,128)(2,1)S(1)} %collective-permute-done.4.refs_9_), channel_id=1, source_target_pairs={{0,8},{8,16},{16,24},{24,28},{28,20},{20,12},{12,4},{4,0},{1,9},{9... | collective-permute-start | bytes 393224 | tf_op jit(solution)/shard_map/ppermute | solution.py:70
  16.2 1.6 %collective-permute-start.11 = (bf16[256,256]{1,0:T(8,128)(2,1)S(1)}, bf16[256,256]{1,0:T(8,128)(2,1)S(1)}, u32[]{:S(2)}, u32[]{:S(2)}) collective-permute-start(bf16[256,256]{1,0:T(8,128)(2,1)S(1)} %collective-permute-done.7.refs_12_), channel_id=1, source_target_pairs={{0,8},{8,16},{16,24},{24,28},{28,20},{20,12},{12,4},{4,0},{1,9},{9... | collective-permute-start | bytes 393224 | tf_op jit(solution)/shard_map/ppermute | solution.py:70
  18.2 2.2 %collective-permute-done.9.refs_14_ = bf16[256,256]{1,0:T(8,128)(2,1)S(1)} collective-permute-done((bf16[256,256]{1,0:T(8,128)(2,1)S(1)}, bf16[256,256]{1,0:T(8,128)(2,1)S(1)}, u32[]{:S(2)}, u32[]{:S(2)}) %collective-permute-start.9) | collective-permute-done | bytes 131104 | tf_op jit(solution)/shard_map/ppermute | solution.py:71
  20.6 1.9 %collective-permute-start.12 = (bf16[256,256]{1,0:T(8,128)(2,1)S(1)}, bf16[256,256]{1,0:T(8,128)(2,1)S(1)}, u32[]{:S(2)}, u32[]{:S(2)}) collective-permute-start(bf16[256,256]{1,0:T(8,128)(2,1)S(1)} %collective-permute-done.8.refs_13_), channel_id=1, source_target_pairs={{0,8},{8,16},{16,24},{24,28},{28,20},{20,12},{12,4},{4,0},{1,9},{9... | collective-permute-start | bytes 393224 | tf_op jit(solution)/shard_map/ppermute | solution.py:70
  22.6 1.7 %collective-permute-start.15 = (bf16[256,256]{1,0:T(8,128)(2,1)S(1)}, bf16[256,256]{1,0:T(8,128)(2,1)S(1)}, u32[]{:S(2)}, u32[]{:S(2)}) collective-permute-start(bf16[256,256]{1,0:T(8,128)(2,1)S(1)} %collective-permute-done.11.refs_16_), channel_id=1, source_target_pairs={{0,8},{8,16},{16,24},{24,28},{28,20},{20,12},{12,4},{4,0},{1,9},{9... | collective-permute-start | bytes 393224 | tf_op jit(solution)/shard_map/ppermute | solution.py:74
  24.6 0.8 copy.13.refs_3_
  25.3 0.9 copy-done.1
  26.3 0.7 copy-done.2
  28.2 1.2 %pack.1 = (bf16[2,128,128]{2,1,0:T(8,128)(2,1)S(1)}, bf16[2,128,128]{2,1,0:T(8,128)(2,1)S(1)}, bf16[2,128,128]{2,1,0:T(8,128)(2,1)S(1)}, bf16[2,128,128]{2,1,0:T...) custom-call(bf16[256,256]{1,0:T(8,128)(2,1)S(1)} %get-tuple-element.14.refs_0_.refs_6_, ...), custom_call_target="tpu_custom_call" | custom-call | flops 100000000 | bytes 1000000 | tf_op jit(solution)/shard_map/pack/pallas_call | solution.py:146
  29.5 1.4 %collective-permute-done.2.refs_4_.refs_3_ = f32[16,128]{1,0:T(8,128)S(1)} collective-permute-done((f32[16,128]{1,0:T(8,128)S(1)}, f32[16,128]{1,0:T(8,128)S(1)}, u32[]{:S(2)}, u32[]{:S(2)}) %collective-permute-start.2) | collective-permute-done | bytes 8224 | tf_op jit(solution)/shard_map/ppermute | solution.py:161
  30.8 1.6 %collective-permute-start.1 = (f32[16,128]{1,0:T(8,128)S(1)}, f32[16,128]{1,0:T(8,128)S(1)}, u32[]{:S(2)}, u32[]{:S(2)}) collective-permute-start(f32[16,128]{1,0:T(8,128)S(1)} %get-tuple-element.16.refs_1_.refs_0_), channel_id=1, source_target_pairs={{0,2},{1,3},{2,0},{3,1},{4,6},{5,7},{6,4},{7,5},{8,10},{9,11},{10,... | collective-permute-start | bytes 24584 | tf_op jit(solution)/shard_map/ppermute | solution.py:161
  32.5 2.0 %collective-permute-done.1.refs_3_.refs_2_ = f32[16,128]{1,0:T(8,128)S(1)} collective-permute-done((f32[16,128]{1,0:T(8,128)S(1)}, f32[16,128]{1,0:T(8,128)S(1)}, u32[]{:S(2)}, u32[]{:S(2)}) %collective-permute-start.1) | collective-permute-done | bytes 8224 | tf_op jit(solution)/shard_map/ppermute | solution.py:161
  35.0 2.5 %collective-permute-done.refs_2_.refs_1_ = f32[16,128]{1,0:T(8,128)S(1)} collective-permute-done((f32[16,128]{1,0:T(8,128)S(1)}, f32[16,128]{1,0:T(8,128)S(1)}, u32[]{:S(2)}, u32[]{:S(2)}) %collective-permute-start) | collective-permute-done | bytes 8224 | tf_op jit(solution)/shard_map/ppermute | solution.py:161
  37.6 1.7 %collective-permute-start.18 = (bf16[2,128,128]{2,1,0:T(8,128)(2,1)S(1)}, bf16[2,128,128]{2,1,0:T(8,128)(2,1)S(1)}, u32[]{:S(2)}, u32[]{:S(2)}) collective-permute-start(bf16[2,128,128]{2,1,0:T(8,128)(2,1)S(1)} %get-tuple-element.20), channel_id=1, source_target_pairs={{0,2},{1,3},{2,0},{3,1},{4,6},{5,7},{6,4},{7,5},{8,10},{9,11},{10,... | collective-permute-start | bytes 196616 | tf_op jit(solution)/shard_map/ppermute | solution.py:161
  39.2 1.4 %collective-permute-start.19 = (bf16[2,128,128]{2,1,0:T(8,128)(2,1)S(1)}, bf16[2,128,128]{2,1,0:T(8,128)(2,1)S(1)}, u32[]{:S(2)}, u32[]{:S(2)}) collective-permute-start(bf16[2,128,128]{2,1,0:T(8,128)(2,1)S(1)} %get-tuple-element.21), channel_id=1, source_target_pairs={{0,3},{1,0},{2,1},{3,2},{4,7},{5,4},{6,5},{7,6},{8,11},{9,8},{10,9... | collective-permute-start | bytes 196616 | tf_op jit(solution)/shard_map/ppermute | solution.py:161
  40.7 10.3 %measure.1 = f32[1,128]{1,0:T(1,128)S(1)} custom-call(bf16[8,256,2048]{2,1,0:T(8,128)(2,1)} %refs_0_.1, f32[16,128]{1,0:T(8,128)S(1)} %get-tuple-element.16.refs_1_.refs_0_, f32[16,128]{1,0:T(8,128)S(1)} %collective-permute-done.refs_2_.refs_1_, f32[16,128]{1,0:T(8,128)S(1)} %collective-permute-done.1.refs_3_.refs_2_, ...), custom_call_target="tpu_custom_call" | custom-call | flops 4294967296 | bytes 8388608 | tf_op jit(solution)/shard_map/measure/pallas_call | solution.py:263
  51.0 40.6 %all-gather = f32[32,1,128]{2,1,0:T(1,128)S(1)} all-gather(f32[1,1,128]{2,1,0:T(1,128)S(1)} %bitcast.6), channel_id=1, replica_groups=mesh['chol'=8,'walk'=4] {'chol','walk'}, dimensions={0}, use_global_device_ids=true | all-gather | bytes 16896 | tf_op jit(solution)/shard_map/all_gather | solution.py:350
  91.6 1.4 %finish.1 = (f32[1,4]{1,0:T(1,128)}, f32[1,4]{1,0:T(1,128)}, f32[128,128]{1,0:T(8,128)}) custom-call(f32[32,128]{1,0:T(8,128)S(1)} %bitcast.5, s32[4]{0:T(128)S(1)} %copy-done.5, f32[16,128]{1,0:T(8,128)S(1)} %get-tuple-element.16.refs_1_.refs_0_, f32[16,128]{1,0:T(8,128)S(1)} %collective-permute-done.refs_2_.refs_1_, ...), custom_call_target="tpu_custom_call" | custom-call | flops 1000000 | bytes 600000 | tf_op jit(solution)/shard_map/finish/pallas_call | solution.py:326
  (34 shorter events, 3.5 us)
Async XLA Ops:
  0.6 1.0 %copy-start = (bf16[256,2,256]{2,1,0:T(2,128)(2,1)S(1)}, bf16[256,2,256]{2,1,0:T(2,128)(2,1)}, u32[]{:S(2)}) copy-start(bf16[256,2,256]{2,1,0:T(2,128)(2,1)} %green_ref.1) | copy-start | bytes 786436
  1.6 90.1 %copy-start.5 = (s32[4]{0:T(128)S(1)}, s32[4]{0:T(128)}, u32[]{:S(2)}) copy-start(s32[4]{0:T(128)} %counts_ref.1) | copy-start | bytes 52
  2.1 7.0 %collective-permute-start.3 = (bf16[256,256]{1,0:T(8,128)(2,1)S(1)}, bf16[256,256]{1,0:T(8,128)(2,1)S(1)}, u32[]{:S(2)}, u32[]{:S(2)}) collective-permute-start(bf16[256,256]{1,0:T(8,128)(2,1)S(1)} %get-tuple-element.14.refs_0_.refs_6_), channel_id=1, source_target_pairs={{0,8},{8,16},{16,24},{24,28},{28,20},{20,12},{12,4},{4,0},{1,9},{9... | collective-permute-start | bytes 393224 | tf_op jit(solution)/shard_map/ppermute | solution.py:70
  5.2 6.4 %collective-permute-start.6 = (bf16[256,256]{1,0:T(8,128)(2,1)S(1)}, bf16[256,256]{1,0:T(8,128)(2,1)S(1)}, u32[]{:S(2)}, u32[]{:S(2)}) collective-permute-start(bf16[256,256]{1,0:T(8,128)(2,1)S(1)} %get-tuple-element.15.refs_1_.refs_7_), channel_id=1, source_target_pairs={{0,4},{8,0},{16,8},{24,16},{28,24},{20,28},{12,20},{4,12},{1,5},{9... | collective-permute-start | bytes 393224 | tf_op jit(solution)/shard_map/ppermute | solution.py:71
  5.2 8.9 %collective-permute-start.5 = (bf16[256,256]{1,0:T(8,128)(2,1)S(1)}, bf16[256,256]{1,0:T(8,128)(2,1)S(1)}, u32[]{:S(2)}, u32[]{:S(2)}) collective-permute-start(bf16[256,256]{1,0:T(8,128)(2,1)S(1)} %get-tuple-element.14.refs_0_.refs_6_), channel_id=1, source_target_pairs={{0,4},{8,0},{16,8},{24,16},{28,24},{20,28},{12,20},{4,12},{1,5},{9... | collective-permute-start | bytes 393224 | tf_op jit(solution)/shard_map/ppermute | solution.py:71
  7.2 7.0 %collective-permute-start.4 = (bf16[256,256]{1,0:T(8,128)(2,1)S(1)}, bf16[256,256]{1,0:T(8,128)(2,1)S(1)}, u32[]{:S(2)}, u32[]{:S(2)}) collective-permute-start(bf16[256,256]{1,0:T(8,128)(2,1)S(1)} %get-tuple-element.15.refs_1_.refs_7_), channel_id=1, source_target_pairs={{0,8},{8,16},{16,24},{24,28},{28,20},{20,12},{12,4},{4,0},{1,9},{9... | collective-permute-start | bytes 393224 | tf_op jit(solution)/shard_map/ppermute | solution.py:70
  9.1 7.1 %collective-permute-start.7 = (bf16[256,256]{1,0:T(8,128)(2,1)S(1)}, bf16[256,256]{1,0:T(8,128)(2,1)S(1)}, u32[]{:S(2)}, u32[]{:S(2)}) collective-permute-start(bf16[256,256]{1,0:T(8,128)(2,1)S(1)} %collective-permute-done.3.refs_8_), channel_id=1, source_target_pairs={{0,8},{8,16},{16,24},{24,28},{28,20},{20,12},{12,4},{4,0},{1,9},{9... | collective-permute-start | bytes 393224 | tf_op jit(solution)/shard_map/ppermute | solution.py:70
  11.6 6.2 %collective-permute-start.10 = (bf16[256,256]{1,0:T(8,128)(2,1)S(1)}, bf16[256,256]{1,0:T(8,128)(2,1)S(1)}, u32[]{:S(2)}, u32[]{:S(2)}) collective-permute-start(bf16[256,256]{1,0:T(8,128)(2,1)S(1)} %collective-permute-done.6.refs_11_), channel_id=1, source_target_pairs={{0,4},{8,0},{16,8},{24,16},{28,24},{20,28},{12,20},{4,12},{1,5},{9... | collective-permute-start | bytes 393224 | tf_op jit(solution)/shard_map/ppermute | solution.py:71
  14.2 6.3 %collective-permute-start.9 = (bf16[256,256]{1,0:T(8,128)(2,1)S(1)}, bf16[256,256]{1,0:T(8,128)(2,1)S(1)}, u32[]{:S(2)}, u32[]{:S(2)}) collective-permute-start(bf16[256,256]{1,0:T(8,128)(2,1)S(1)} %collective-permute-done.5.refs_10_), channel_id=1, source_target_pairs={{0,4},{8,0},{16,8},{24,16},{28,24},{20,28},{12,20},{4,12},{1,5},{9... | collective-permute-start | bytes 393224 | tf_op jit(solution)/shard_map/ppermute | solution.py:71
  14.2 6.4 %collective-permute-start.8 = (bf16[256,256]{1,0:T(8,128)(2,1)S(1)}, bf16[256,256]{1,0:T(8,128)(2,1)S(1)}, u32[]{:S(2)}, u32[]{:S(2)}) collective-permute-start(bf16[256,256]{1,0:T(8,128)(2,1)S(1)} %collective-permute-done.4.refs_9_), channel_id=1, source_target_pairs={{0,8},{8,16},{16,24},{24,28},{28,20},{20,12},{12,4},{4,0},{1,9},{9... | collective-permute-start | bytes 393224 | tf_op jit(solution)/shard_map/ppermute | solution.py:70
  16.2 6.4 %collective-permute-start.11 = (bf16[256,256]{1,0:T(8,128)(2,1)S(1)}, bf16[256,256]{1,0:T(8,128)(2,1)S(1)}, u32[]{:S(2)}, u32[]{:S(2)}) collective-permute-start(bf16[256,256]{1,0:T(8,128)(2,1)S(1)} %collective-permute-done.7.refs_12_), channel_id=1, source_target_pairs={{0,8},{8,16},{16,24},{24,28},{28,20},{20,12},{12,4},{4,0},{1,9},{9... | collective-permute-start | bytes 393224 | tf_op jit(solution)/shard_map/ppermute | solution.py:70
  17.8 6.5 %collective-permute-start.14 = (bf16[256,256]{1,0:T(8,128)(2,1)S(1)}, bf16[256,256]{1,0:T(8,128)(2,1)S(1)}, u32[]{:S(2)}, u32[]{:S(2)}) collective-permute-start(bf16[256,256]{1,0:T(8,128)(2,1)S(1)} %collective-permute-done.10.refs_15_), channel_id=1, source_target_pairs={{0,4},{8,0},{16,8},{24,16},{28,24},{20,28},{12,20},{4,12},{1,5},{9... | collective-permute-start | bytes 393224 | tf_op jit(solution)/shard_map/ppermute | solution.py:71
  20.5 17.1 %collective-permute-start.13 = (bf16[256,256]{1,0:T(8,128)(2,1)S(1)}, bf16[256,256]{1,0:T(8,128)(2,1)S(1)}, u32[]{:S(2)}, u32[]{:S(2)}) collective-permute-start(bf16[256,256]{1,0:T(8,128)(2,1)S(1)} %collective-permute-done.9.refs_14_), channel_id=1, source_target_pairs={{0,4},{8,0},{16,8},{24,16},{28,24},{20,28},{12,20},{4,12},{1,5},{9... | collective-permute-start | bytes 393224 | tf_op jit(solution)/shard_map/ppermute | solution.py:71
  20.6 18.7 %collective-permute-start.12 = (bf16[256,256]{1,0:T(8,128)(2,1)S(1)}, bf16[256,256]{1,0:T(8,128)(2,1)S(1)}, u32[]{:S(2)}, u32[]{:S(2)}) collective-permute-start(bf16[256,256]{1,0:T(8,128)(2,1)S(1)} %collective-permute-done.8.refs_13_), channel_id=1, source_target_pairs={{0,8},{8,16},{16,24},{24,28},{28,20},{20,12},{12,4},{4,0},{1,9},{9... | collective-permute-start | bytes 393224 | tf_op jit(solution)/shard_map/ppermute | solution.py:70
  22.6 18.1 %collective-permute-start.15 = (bf16[256,256]{1,0:T(8,128)(2,1)S(1)}, bf16[256,256]{1,0:T(8,128)(2,1)S(1)}, u32[]{:S(2)}, u32[]{:S(2)}) collective-permute-start(bf16[256,256]{1,0:T(8,128)(2,1)S(1)} %collective-permute-done.11.refs_16_), channel_id=1, source_target_pairs={{0,8},{8,16},{16,24},{24,28},{28,20},{20,12},{12,4},{4,0},{1,9},{9... | collective-permute-start | bytes 393224 | tf_op jit(solution)/shard_map/ppermute | solution.py:74
  24.3 16.4 %collective-permute-start.16 = (bf16[256,256]{1,0:T(8,128)(2,1)S(1)}, bf16[256,256]{1,0:T(8,128)(2,1)S(1)}, u32[]{:S(2)}, u32[]{:S(2)}) collective-permute-start(bf16[256,256]{1,0:T(8,128)(2,1)S(1)} %collective-permute-done.14.refs_19_), channel_id=1, source_target_pairs={{0,4},{8,0},{16,8},{24,16},{28,24},{20,28},{12,20},{4,12},{1,5},{9... | collective-permute-start | bytes 393224 | tf_op jit(solution)/shard_map/ppermute | solution.py:75
  25.3 0.9 copy-start.1
  26.9 0.7 copy-start.3
  29.4 1.4 %collective-permute-start.2 = (f32[16,128]{1,0:T(8,128)S(1)}, f32[16,128]{1,0:T(8,128)S(1)}, u32[]{:S(2)}, u32[]{:S(2)}) collective-permute-start(f32[16,128]{1,0:T(8,128)S(1)} %get-tuple-element.16.refs_1_.refs_0_), channel_id=1, source_target_pairs={{0,3},{1,0},{2,1},{3,2},{4,7},{5,4},{6,5},{7,6},{8,11},{9,8},{10,9... | collective-permute-start | bytes 24584 | tf_op jit(solution)/shard_map/ppermute | solution.py:161
  30.8 3.7 %collective-permute-start.1 = (f32[16,128]{1,0:T(8,128)S(1)}, f32[16,128]{1,0:T(8,128)S(1)}, u32[]{:S(2)}, u32[]{:S(2)}) collective-permute-start(f32[16,128]{1,0:T(8,128)S(1)} %get-tuple-element.16.refs_1_.refs_0_), channel_id=1, source_target_pairs={{0,2},{1,3},{2,0},{3,1},{4,6},{5,7},{6,4},{7,5},{8,10},{9,11},{10,... | collective-permute-start | bytes 24584 | tf_op jit(solution)/shard_map/ppermute | solution.py:161
  34.5 3.1 %collective-permute-start = (f32[16,128]{1,0:T(8,128)S(1)}, f32[16,128]{1,0:T(8,128)S(1)}, u32[]{:S(2)}, u32[]{:S(2)}) collective-permute-start(f32[16,128]{1,0:T(8,128)S(1)} %get-tuple-element.16.refs_1_.refs_0_), channel_id=1, source_target_pairs={{0,1},{1,2},{2,3},{3,0},{4,5},{5,6},{6,7},{7,4},{8,9},{9,10},{10,1... | collective-permute-start | bytes 24584 | tf_op jit(solution)/shard_map/ppermute | solution.py:161
  37.6 54.1 %collective-permute-start.17 = (bf16[2,128,128]{2,1,0:T(8,128)(2,1)S(1)}, bf16[2,128,128]{2,1,0:T(8,128)(2,1)S(1)}, u32[]{:S(2)}, u32[]{:S(2)}) collective-permute-start(bf16[2,128,128]{2,1,0:T(8,128)(2,1)S(1)} %get-tuple-element.19), channel_id=1, source_target_pairs={{0,1},{1,2},{2,3},{3,0},{4,5},{5,6},{6,7},{7,4},{8,9},{9,10},{10,1... | collective-permute-start | bytes 196616 | tf_op jit(solution)/shard_map/ppermute | solution.py:161
  37.6 54.1 %collective-permute-start.18 = (bf16[2,128,128]{2,1,0:T(8,128)(2,1)S(1)}, bf16[2,128,128]{2,1,0:T(8,128)(2,1)S(1)}, u32[]{:S(2)}, u32[]{:S(2)}) collective-permute-start(bf16[2,128,128]{2,1,0:T(8,128)(2,1)S(1)} %get-tuple-element.20), channel_id=1, source_target_pairs={{0,2},{1,3},{2,0},{3,1},{4,6},{5,7},{6,4},{7,5},{8,10},{9,11},{10,... | collective-permute-start | bytes 196616 | tf_op jit(solution)/shard_map/ppermute | solution.py:161
  39.2 52.4 %collective-permute-start.19 = (bf16[2,128,128]{2,1,0:T(8,128)(2,1)S(1)}, bf16[2,128,128]{2,1,0:T(8,128)(2,1)S(1)}, u32[]{:S(2)}, u32[]{:S(2)}) collective-permute-start(bf16[2,128,128]{2,1,0:T(8,128)(2,1)S(1)} %get-tuple-element.21), channel_id=1, source_target_pairs={{0,3},{1,0},{2,1},{3,2},{4,7},{5,4},{6,5},{7,6},{8,11},{9,8},{10,9... | collective-permute-start | bytes 196616 | tf_op jit(solution)/shard_map/ppermute | solution.py:161
  (2 other events, 1.3 us)

commit v2 on v1

v2 whole, which is shorter than its diff:
```python
import functools

import jax
import jax.numpy as jnp
from jax import lax
from jax.experimental import pallas as pl
from jax.experimental.pallas import tpu as pltpu
from jax.sharding import PartitionSpec as P

time_step = 0.02
root_step = 0.02**0.5
LANES = 128
VMEM_LIMIT = 16 * 1024 * 1024
RING_LIMIT = 16


def params(**more):
    return pltpu.CompilerParams(vmem_limit_bytes=VMEM_LIMIT, **more)


def vmem():
    return pl.BlockSpec(memory_space=pltpu.VMEM)


def smem():
    return pl.BlockSpec(memory_space=pltpu.SMEM)


def ring_order(size):
    return [2 * q if q < size // 2 else 2 * (size - 1 - q) + 1 for q in range(size)]


def ring_place(index, size):
    return jnp.where(index % 2 == 0, index // 2, size - 1 - index // 2)


def ring_owner(place, size):
    return jnp.where(place < size // 2, 2 * place, 2 * (size - 1 - place) + 1)


def split_walkers(green_rows):
    rows, walkers, orbitals = green_rows.shape
    steps = 4 if rows % 64 == 0 else 1

    def kernel(green_ref, out_ref):
        for b in range(walkers):
            out_ref[:, b * orbitals : (b + 1) * orbitals] = green_ref[:, b, :]

    return pl.pallas_call(
        kernel,
        name="split_walkers",
        grid=(steps,),
        out_shape=jax.ShapeDtypeStruct((rows, walkers * orbitals), green_rows.dtype),
        in_specs=[pl.BlockSpec((rows // steps, walkers, orbitals), lambda n: (n, 0, 0))],
        out_specs=pl.BlockSpec((rows // steps, walkers * orbitals), lambda n: (n, 0)),
        compiler_params=params(),
        cost_estimate=pl.CostEstimate(flops=0, bytes_accessed=4 * rows * walkers * orbitals, transcendentals=0),
    )(green_rows)


def column_start(shift, rows):
    size = lax.axis_size("chol")
    place = ring_place(lax.axis_index("chol"), size)
    owner = ring_owner(lax.rem(place + shift + size, size), size)
    return pl.multiple_of(owner * rows, rows)


def accumulate(cholesky_rot, parts, total, mark, fetch):
    vectors, orbitals, _ = cholesky_rot.shape
    rows, columns = parts[0][1].shape
    shifts = [shift for shift, _ in parts]
    count = len(parts)
    fresh = total is None

    def kernel(chol_ref, *refs):
        ins = refs[: len(arrays)]
        outs = refs[len(arrays) : len(arrays) + len(shapes)]
        blocks_scr, sems = refs[len(arrays) + len(shapes) :][:2]
        copies = []
        for n, shift in enumerate(shifts):
            start = column_start(shift, rows)
            copies.append(
                [
                    pltpu.make_async_copy(
                        chol_ref.at[g, :, pl.ds(start, rows)], blocks_scr.at[n, g], sems.at[n, g]
                    )
                    for g in range(vectors)
                ]
            )
        for g in range(vectors):
            for n in range(count):
                copies[n][g].start()
        if fetch is not None:
            ahead = pltpu.make_async_copy(
                chol_ref.at[:, :, pl.ds(column_start(fetch, rows), rows)], outs[2], refs[-1]
            )
            ahead.start()
        outs[1][...] = jnp.zeros_like(outs[1])
        for g in range(vectors):
            value = None if fresh else ins[count + 1][g]
            for n in range(count):
                copies[n][g].wait()
                term = jnp.dot(blocks_scr[n, g], ins[n][...], preferred_element_type=jnp.float32)
                value = term if value is None else value + term
            outs[0][g] = value
        if fetch is not None:
            ahead.wait()

    arrays = [x for _, x in parts] + [mark] + ([] if fresh else [total])
    shapes = [
        jax.ShapeDtypeStruct((vectors, orbitals, columns), jnp.float32),
        jax.ShapeDtypeStruct((8, LANES), jnp.float32),
    ]
    if fetch is not None:
        shapes.append(jax.ShapeDtypeStruct((vectors, orbitals, rows), cholesky_rot.dtype))
    return pl.pallas_call(
        kernel,
        name="accumulate",
        out_shape=shapes,
        in_specs=[pl.BlockSpec(memory_space=pl.ANY)] + [vmem()] * len(arrays),
        out_specs=[vmem()] * len(shapes),
        scratch_shapes=[
            pltpu.VMEM((count, vectors, orbitals, rows), cholesky_rot.dtype),
            pltpu.SemaphoreType.DMA((count, vectors)),
        ]
        + ([] if fetch is None else [pltpu.SemaphoreType.DMA]),
        compiler_params=params(),
        cost_estimate=pl.CostEstimate(
            flops=2 * count * vectors * orbitals * rows * columns,
            bytes_accessed=2 * count * vectors * orbitals * rows,
            transcendentals=0,
        ),
    )(cholesky_rot, *arrays)


def tie(*arrays):
    return lax.optimization_barrier(arrays)


def ring(cholesky_rot, own, packed):
    size = lax.axis_size("chol")
    rows, _ = own.shape
    order = ring_order(size)
    ahead = [(order[q], order[(q + 1) % size]) for q in range(size)]
    back = [(order[q], order[(q - 1) % size]) for q in range(size)]
    right = left = own
    parts = [(0, own)]
    total = None
    mark = packed[-1]
    steps = size // 2
    for step in range(1, steps):
        next_right = lax.ppermute(right, "chol", ahead)
        next_left = lax.ppermute(left, "chol", back)
        total, mark = accumulate(cholesky_rot, parts, total, mark, None)
        if step == 1:
            others = [shifted(packed[d], d) for d in range(1, len(packed) - 1)]
        if step == min(2, steps - 1):
            right, left, mark, *others = tie(next_right, next_left, mark, *others)
        else:
            right, left, mark = tie(next_right, next_left, mark)
        parts = [(-step, right), (step, left)]
    first = lax.ppermute(right[: rows // 2], "chol", ahead)
    second = lax.ppermute(left[rows // 2 :], "chol", back)
    total, _, block = accumulate(cholesky_rot, parts, total, mark, steps)
    return total, block, [first, second], [packed[0]] + others


def table_height(vectors):
    return -(-(vectors + 2) // 16) * 16


def pack(own, one_body, fields, weights, sources, owners):
    rows, orbitals = one_body.shape
    walk_size = lax.axis_size("walk")
    walkers = own.shape[1] // orbitals
    width = orbitals // walk_size
    pair = LANES // width
    vectors, slots = fields.shape
    table_rows = table_height(vectors)
    height = walkers * (rows // pair) + 3 * table_rows

    def kernel(*refs):
        own_ref, body_ref, fields_ref, weights_ref, sources_ref, owners_ref = refs[:6]
        packs = refs[6 : 6 + walk_size]
        onebody_ref, table_scr = refs[6 + walk_size :]
        green = [own_ref[:, b * orbitals : (b + 1) * orbitals] for b in range(walkers)]
        walk = lax.axis_index("walk")
        lane = lax.broadcasted_iota(jnp.int32, (1, LANES), 1)
        body = body_ref[...].astype(jnp.float32)
        onebody_ref[...] = jnp.zeros_like(onebody_ref)
        for b in range(walkers):
            total = jnp.sum(green[b].astype(jnp.float32) * body, axis=0, keepdims=True)
            folded = total[:, :LANES]
            for start in range(LANES, orbitals, LANES):
                folded = folded + total[:, start : start + LANES]
            onebody_ref[b : b + 1, :] = folded
        r = lax.broadcasted_iota(jnp.int32, (rows // pair, rows), 0)
        m = lax.broadcasted_iota(jnp.int32, (rows // pair, rows), 1)
        k = lax.broadcasted_iota(jnp.int32, (orbitals, LANES), 0)
        c = lax.broadcasted_iota(jnp.int32, (orbitals, LANES), 1)
        thinned = []
        for b in range(walkers):
            values = green[b]
            thinned.append(
                [
                    jnp.dot(
                        (m == r * pair + h).astype(jnp.bfloat16), values, preferred_element_type=jnp.float32
                    ).astype(jnp.bfloat16)
                    for h in range(pair)
                ]
            )
        for d in range(walk_size):
            target = lax.rem(walk + d, walk_size)
            panel = jnp.int32(0)
            for p in range(walk_size):
                panel = jnp.where(owners_ref[p] == target, p, panel)
            for b in range(walkers):
                total = jnp.zeros((rows // pair, LANES), jnp.float32)
                for h in range(pair):
                    take = (k == panel * width + c - h * width) & (c >= h * width) & (c < (h + 1) * width)
                    total += jnp.dot(
                        thinned[b][h], take.astype(jnp.bfloat16), preferred_element_type=jnp.float32
                    )
                packs[d][b * (rows // pair) : (b + 1) * (rows // pair), :] = total.astype(jnp.bfloat16)
        spread = jnp.zeros((vectors, LANES), jnp.float32)
        source = jnp.zeros((1, LANES), jnp.float32)
        for j in range(slots):
            mine = lane % slots == j
            spread += jnp.where(mine, fields_ref[:, j : j + 1], 0.0)
            source += jnp.where(mine, sources_ref[j].astype(jnp.float32), 0.0)
        weight = weights_ref[0]
        for j in range(1, weights.shape[0]):
            weight = weight + weights_ref[j]
        table_scr[...] = jnp.zeros_like(table_scr)
        table_scr[:vectors, :] = spread
        table_scr[vectors : vectors + 1, :] = source
        table_scr[vectors + 1 : vectors + 2, :] = jnp.zeros((1, LANES), jnp.float32) + weight
        rest = table_scr[...]
        for n in range(3):
            piece = rest.astype(jnp.bfloat16)
            rest = rest - piece.astype(jnp.float32)
            at = walkers * (rows // pair) + n * table_rows
            for d in range(walk_size):
                packs[d][at : at + table_rows, :] = piece

    out = pl.pallas_call(
        kernel,
        name="pack",
        out_shape=[jax.ShapeDtypeStruct((height, LANES), jnp.bfloat16)] * walk_size
        + [jax.ShapeDtypeStruct((8, LANES), jnp.float32)],
        in_specs=[vmem()] * 3 + [smem()] * 3,
        out_specs=[vmem()] * (walk_size + 1),
        scratch_shapes=[pltpu.VMEM((table_rows, LANES), jnp.float32)],
        compiler_params=params(),
        cost_estimate=pl.CostEstimate(flops=10**8, bytes_accessed=10**6, transcendentals=0),
    )(own, one_body, fields, weights, sources, owners)
    return out


def shifted(x, d):
    size = lax.axis_size("walk")
    return lax.ppermute(x, "walk", [(q, (q + d) % size) for q in range(size)])


def read_table(ref, vectors):
    height = table_height(vectors)
    start = ref.shape[0] - 3 * height
    parts = [ref[start + n * height : start + (n + 1) * height, :].astype(jnp.float32) for n in range(3)]
    return parts[0] + (parts[1] + parts[2])


def merge_tables(tables, walk, walk_size, slots, lane):
    total = jnp.zeros_like(tables[0])
    for d, table in enumerate(tables):
        group = lax.rem(walk - d + walk_size, walk_size)
        total += jnp.where(lane // slots == group, table, 0.0)
    return total


def measure(block, total, last, packs, onebody, slots):
    vectors, orbitals, depth = block.shape
    columns = last[0].shape[1]
    walkers = columns // orbitals
    walk_size = len(packs)
    devices = walk_size * lax.axis_size("chol")
    whole = total is None
    quads = orbitals // LANES

    def fold(x):
        return jnp.sum(x.reshape(-1, 8, LANES), axis=0)

    def kernel(*refs):
        block_ref, onebody_ref = refs[:2]
        pack_refs = refs[2 : 2 + walk_size]
        last_refs = refs[2 + walk_size : 2 + walk_size + len(last)]
        out_ref, depth_scr, tensor_scr = refs[-3:]
        walk = lax.axis_index("walk")
        lane = lax.broadcasted_iota(jnp.int32, (1, LANES), 1)
        table = merge_tables([read_table(x, vectors) for x in pack_refs], walk, walk_size, slots, lane)
        picks = [
            jnp.where(
                (lane < slots * walk_size) & (table[vectors : vectors + 1, :] == (walk * walkers + b).astype(jnp.float32)),
                1.0,
                0.0,
            )
            for b in range(walkers)
        ]
        at = 0
        for x in last_refs:
            depth_scr[at : at + x.shape[0], :] = x[...]
            at += x.shape[0]
        eye = lax.broadcasted_iota(jnp.int32, (LANES, LANES), 0) == lax.broadcasted_iota(
            jnp.int32, (LANES, LANES), 1
        )
        exchange = [jnp.zeros((8, LANES), jnp.float32) for _ in range(walkers)]
        squares = [jnp.zeros((1, 1), jnp.float32) for _ in range(walkers)]
        drive = jnp.zeros((1, LANES), jnp.float32)
        for g in range(vectors):
            value = jnp.dot(block_ref[g], depth_scr[...], preferred_element_type=jnp.float32)
            if not whole:
                value = value + refs[2 + walk_size + len(last)][g]
            tensor_scr[g % 2] = value
            for b in range(walkers):
                diagonal = jnp.zeros((LANES, LANES), jnp.float32)
                for q in range(quads):
                    for p in range(q + 1):
                        one = tensor_scr[
                            g % 2,
                            q * LANES : (q + 1) * LANES,
                            b * orbitals + p * LANES : b * orbitals + (p + 1) * LANES,
                        ]
                        if p == q:
                            exchange[b] = exchange[b] + fold(one * one.T)
                            diagonal = diagonal + one
                        else:
                            two = tensor_scr[
                                g % 2,
                                p * LANES : (p + 1) * LANES,
                                b * orbitals + q * LANES : b * orbitals + (q + 1) * LANES,
                            ]
                            exchange[b] = exchange[b] + 2.0 * fold(two * one.T)
                trace = jnp.sum(fold(jnp.where(eye, diagonal, 0.0)), axis=0, keepdims=True)
                trace = jnp.sum(trace, axis=1, keepdims=True)
                squares[b] = squares[b] + trace * trace
                drive = drive - root_step * picks[b] * table[g : g + 1, :] * trace
        raw = jnp.zeros((1, LANES), jnp.float32)
        square = jnp.zeros((1, LANES), jnp.float32)
        for b in range(walkers):
            swapped = jnp.sum(jnp.sum(exchange[b], axis=0, keepdims=True), axis=1, keepdims=True)
            single = jnp.sum(onebody_ref[b : b + 1, :], axis=1, keepdims=True)
            raw += picks[b] * (single + 0.5 * squares[b] - 0.5 * swapped)
            square += picks[b] * squares[b]
        power = drive - 0.5 * time_step * square - time_step * raw
        out_ref[...] = jnp.broadcast_to(raw + pltpu.roll(power, slots * walk_size, 1), (devices, LANES))

    arrays = list(last) + ([] if whole else [total])
    return pl.pallas_call(
        kernel,
        name="measure",
        out_shape=jax.ShapeDtypeStruct((devices, LANES), jnp.float32),
        in_specs=[vmem()] * (2 + walk_size + len(arrays)),
        out_specs=vmem(),
        scratch_shapes=[
            pltpu.VMEM((depth, columns), jnp.bfloat16),
            pltpu.VMEM((2, orbitals, columns), jnp.float32),
        ],
        compiler_params=params(),
        cost_estimate=pl.CostEstimate(
            flops=2 * vectors * orbitals * depth * columns,
            bytes_accessed=4 * vectors * orbitals * columns,
            transcendentals=0,
        ),
    )(block, onebody, *packs, *arrays)


def finish(stats, packs, counts, vectors, slots, walkers):
    walk_size = len(packs)
    rows = (packs[0].shape[0] - 3 * table_height(vectors)) // walkers

    def kernel(stats_ref, counts_ref, *refs):
        pack_refs = refs[:walk_size]
        energies_ref, weights_ref, density_ref = refs[walk_size:]
        walk = lax.axis_index("walk")
        lane = lax.broadcasted_iota(jnp.int32, (1, LANES), 1)
        all_slots = slots * walk_size
        tables = [read_table(x, vectors) for x in pack_refs]
        source = merge_tables([t[vectors : vectors + 1, :] for t in tables], walk, walk_size, slots, lane)
        total_weight = tables[0][vectors + 1 : vectors + 2, :]
        for t in tables[1:]:
            total_weight = total_weight + t[vectors + 1 : vectors + 2, :]
        mean_weight = total_weight / (walkers * walk_size)
        total = jnp.sum(stats_ref[...], axis=0, keepdims=True)
        power = pltpu.roll(total, LANES - all_slots, 1)
        live_count = jnp.zeros((1, LANES), jnp.int32)
        for q in range(walk_size):
            live_count = jnp.where(lane // slots == q, counts_ref[q], live_count)
        live = (lane < all_slots) & (lane % slots < live_count)
        energies = jnp.where(live, total, 0.0)
        new_weights = jnp.where(live, mean_weight * jnp.exp(jnp.where(live, power, 0.0)), 0.0)
        norm = jnp.sum(new_weights, axis=1, keepdims=True)
        density = jnp.zeros((rows, LANES), jnp.float32)
        for d in range(walk_size):
            group = lax.rem(walk - d + walk_size, walk_size)
            for b in range(walkers):
                walker = (group * walkers + b).astype(jnp.float32)
                share = jnp.sum(jnp.where(source == walker, new_weights, 0.0), axis=1, keepdims=True) / norm
                density += share * pack_refs[d][b * rows : (b + 1) * rows, :].astype(jnp.float32)
        density_ref[...] = density
        first = lax.rem(LANES - walk * slots, LANES)
        energies_ref[...] = pltpu.roll(jnp.broadcast_to(energies, (8, LANES)), first, 1)[:1, :slots]
        weights_ref[...] = pltpu.roll(jnp.broadcast_to(new_weights, (8, LANES)), first, 1)[:1, :slots]

    return pl.pallas_call(
        kernel,
        name="finish",
        out_shape=[
            jax.ShapeDtypeStruct((1, slots), jnp.float32),
            jax.ShapeDtypeStruct((1, slots), jnp.float32),
            jax.ShapeDtypeStruct((rows, LANES), jnp.float32),
        ],
        in_specs=[vmem(), smem()] + [vmem()] * walk_size,
        out_specs=[vmem()] * 3,
        compiler_params=params(),
        cost_estimate=pl.CostEstimate(flops=10**6, bytes_accessed=6 * 10**5, transcendentals=128),
    )(stats, counts, *packs)


def per_device(green_rows, cholesky_rot, one_body, fields, weights, sources, counts, owners):
    chol_size = lax.axis_size("chol")
    walk_size = lax.axis_size("walk")
    vectors, slots = fields.shape
    own = split_walkers(green_rows)
    packed = pack(own, one_body, fields, weights, sources, owners)
    if chol_size > RING_LIMIT or chol_size % 2:
        packs = [packed[0]] + [shifted(packed[d], d) for d in range(1, walk_size)]
        total, block, last = None, cholesky_rot, [lax.all_gather(own, "chol", axis=0, tiled=True)]
    else:
        total, block, last, packs = ring(cholesky_rot, own, packed)
    stats = measure(block, total, last, packs, packed[-1], slots)
    stats = lax.all_to_all(stats, ("chol", "walk"), split_axis=0, concat_axis=0, tiled=True)
    energies, new_weights, density = finish(stats, packs, counts, vectors, slots, green_rows.shape[1])
    return energies.reshape(slots), new_weights.reshape(slots), density.reshape(1, density.size)


def solution(mesh):
    return jax.shard_map(
        per_device,
        mesh=mesh,
        in_specs=(
            P("chol", "walk", None),
            P("chol", None, None),
            P("chol", None),
            P("chol", "walk"),
            P("walk"),
            P("walk"),
            P(),
            P(),
        ),
        out_specs=(P("walk"), P("walk"), P("walk", "chol")),
        check_vma=False,
    )
```

time: 93.4 us -> 55.2 us (0.59)
  blocking collectives: 40.6 us -> 11.7 us
  waiting for transfers between devices: 12.6 us -> 4.11 us
  starting transfers between devices: 21.1 us -> 12.7 us
  Pallas kernels: 13.4 us -> 17.7 us
  local copies, waits for them, and re-layouts: 4.57 us -> 7.97 us
    all_gather x1 -> x0, blocking collectives: 40.6 us -> none  [per_device(): stats = lax.all_gather(stats, ('chol', 'walk'), axis=0, tiled=True)]
    all_to_all x0 -> x1, blocking collectives: none -> 11.7 us  [per_device(): lax.all_to_all(stats, ('chol', 'walk'), split_axis=0, concat_axis=0, tile...]
    ppermute x14 -> x8, starting transfers between devices: 15.7 us -> 9.32 us  [the longest x3 6.72 us: ring(): next_right = lax.ppermute(right, 'chol', ahead)]
    ppermute x6 -> x3, waiting for transfers between devices: 5.9 us -> 0.01 us  [shifted(): return lax.ppermute(x, 'walk', [(q, (q + d) % size) for q in range(size)])]
    pallas_call x3 -> x7, Pallas kernels: 12.1 us -> 16.2 us  [the longest x4 13.1 us: accumulate(): pl.pallas_call(kernel, name='accumulate', out_shape=shapes, in_specs=[pl....]
    unnamed x13 -> x17, local copies, waits for them, and re-layouts: 4.57 us -> 7.95 us
    ppermute x14 -> x8, waiting for transfers between devices: 6.73 us -> 4.1 us  [the longest x3 2.09 us: ring(): next_left = lax.ppermute(left, 'chol', back)]
    ppermute x6 -> x3, starting transfers between devices: 5.35 us -> 3.38 us  [shifted(): return lax.ppermute(x, 'walk', [(q, (q + d) % size) for q in range(size)])]
  transfers between devices with their start and end apart: 20 -> 11, of which waited for: 7 -> 3; matrix products, arithmetic and copies ran while one was open for 1% -> 1% of each run, Pallas kernels for 12% -> 26%
where the time goes in v2:
time: 55.2 us; the launch traced here: 54.9 us
  Pallas kernels  17.7 us (32%)
  starting transfers between devices  12.7 us (23%)
  blocking collectives  11.7 us (21%)
  local copies, waits for them, and re-layouts  7.97 us (14%)
  waiting for transfers between devices  4.11 us (7%)
  between operations  0.79 us (1%)
    pallas_call x4, Pallas kernels, accumulate(): pl.pallas_call(kernel, name='accumulate', out_shape=shapes, in_specs=[pl....  13.1 us
    all_to_all x1, blocking collectives, per_device(): lax.all_to_all(stats, ('chol', 'walk'), split_axis=0, concat_axis=0, tile...  11.7 us
    unnamed x17, local copies, waits for them, and re-layouts  7.95 us
    ppermute x3, starting transfers between devices, ring(): next_right = lax.ppermute(right, 'chol', ahead)  6.72 us
    ppermute x3, starting transfers between devices, shifted(): return lax.ppermute(x, 'walk', [(q, (q + d) % size) for q in range(size)])  3.38 us
    ppermute x3, waiting for transfers between devices, ring(): next_left = lax.ppermute(left, 'chol', back)  2.09 us
    ppermute x3, waiting for transfers between devices, ring(): next_right = lax.ppermute(right, 'chol', ahead)  2.01 us
    ppermute x1, starting transfers between devices, ring(): first = lax.ppermute(right[:rows // 2], 'chol', ahead)  1.8 us
  transfers between devices with their start and end apart: 11, of which 3 were waited for; matrix products, arithmetic and copies ran while one was open for 1% of the time, Pallas kernels for 26%

profile of v2, /device:TPU:0, one launch (start us, length us, event | category | flops | bytes accessed | tf_op | source)
XLA Modules:
  0.0 54.9 jit_solution(10911242457486447970)
XLA Ops:
  0.6 0.9 %copy-done.2 = bf16[256,2,256]{2,1,0:T(2,128)(2,1)S(1)} copy-done((bf16[256,2,256]{2,1,0:T(2,128)(2,1)S(1)}, bf16[256,2,256]{2,1,0:T(2,128)(2,1)}, u32[]{:S(2)}) %copy-start.2) | copy-done | bytes 262168
  1.6 0.6 %split_walkers.1.refs_0_ = bf16[256,512]{1,0:T(8,128)(2,1)S(1)} custom-call(bf16[256,2,256]{2,1,0:T(2,128)(2,1)S(1)} %copy-done.2), custom_call_target="tpu_custom_call" | custom-call | bytes 524288 | tf_op jit(solution)/shard_map/split_walkers/pallas_call | solution.py:49
  2.2 3.1 %collective-permute-start = (bf16[256,512]{1,0:T(8,128)(2,1)S(1)}, bf16[256,512]{1,0:T(8,128)(2,1)S(1)}, u32[]{:S(2)}, u32[]{:S(2)}) collective-permute-start(bf16[256,512]{1,0:T(8,128)(2,1)S(1)} %split_walkers.1.refs_0_), channel_id=1, source_target_pairs={{0,8},{8,16},{16,24},{24,28},{28,20},{20,12},{12,4},{4,0},{1,9},{9... | collective-permute-start | bytes 786440 | tf_op jit(solution)/shard_map/ppermute | solution.py:152
  5.3 0.8 %copy.12.refs_2_ = f32[8,4]{1,0:T(8,128)S(1)} copy(f32[8,4]{0,1:T(4,128)} %param.11) | data formatting | bytes 256 | tf_op args[3]
  6.0 0.9 %copy-done.3 = bf16[256,256]{1,0:T(8,128)(2,1)S(1)} copy-done((bf16[256,256]{1,0:T(8,128)(2,1)S(1)}, bf16[256,256]{1,0:T(8,128)(2,1)}, u32[]{:S(2)}) %copy-start.3) | copy-done | bytes 131096
  7.0 0.7 %copy-done.4 = f32[2]{0:T(128)S(1)} copy-done((f32[2]{0:T(128)S(1)}, f32[2]{0:T(128)}, u32[]{:S(2)}) %copy-start.4) | copy-done | bytes 32
  7.6 0.7 %copy-done.5 = s32[4]{0:T(128)S(1)} copy-done((s32[4]{0:T(128)S(1)}, s32[4]{0:T(128)}, u32[]{:S(2)}) %copy-start.5) | copy-done | bytes 40
  8.3 0.7 %copy-done.6 = s32[4]{0:T(128)S(1)} copy-done((s32[4]{0:T(128)S(1)}, s32[4]{0:T(128)}, u32[]{:S(2)}) %copy-start.6) | copy-done | bytes 40
  8.9 1.2 %pack.1 = (bf16[304,128]{1,0:T(8,128)(2,1)S(1)}, bf16[304,128]{1,0:T(8,128)(2,1)S(1)}, bf16[304,128]{1,0:T(8,128)(2,1)S(1)}, bf16[304,128]{1,0:T(8,128)(2,1)S(1)}, f32[8,128]{1,0:T(8,128)S(1)}) custom-call(bf16[256,512]{1,0:T(8,128)(2,1)S(1)} %split_walkers.1.refs_0_, bf16[256,256]{1,0:T(8,128)(2,1)S(1)} %copy-done.3, f32[8,4]{1,0:T(8,128)S(1)} %copy.12.refs_2_, ...), custom_call_target="tpu_custom_call" | custom-call | flops 100000000 | bytes 1000000 | tf_op jit(solution)/shard_map/pack/pallas_call | solution.py:246
  10.1 3.4 %copy-done = bf16[8,256,2048]{2,1,0:T(8,128)(2,1)S(1)} copy-done((bf16[8,256,2048]{2,1,0:T(8,128)(2,1)S(1)}, bf16[8,256,2048]{2,1,0:T(8,128)(2,1)}, u32[]{:S(2)}) %copy-start) | copy-done | bytes 8388632
  13.5 2.1 %accumulate.4 = (f32[8,256,512]{2,1,0:T(8,128)S(1)}, f32[8,128]{1,0:T(8,128)S(1)}) custom-call(bf16[8,256,2048]{2,1,0:T(8,128)(2,1)S(1)} %copy-done, bf16[256,512]{1,0:T(8,128)(2,1)S(1)} %split_walkers.1.refs_0_, f32[8,128]{1,0:T(8,128)S(1)} %get-tuple-element.31.refs_1_), custom_call_target="tpu_custom_call" | custom-call | flops 536870912 | bytes 1048576 | tf_op jit(solution)/shard_map/accumulate/pallas_call | solution.py:116
  15.6 2.1 %collective-permute-start.2 = (bf16[256,512]{1,0:T(8,128)(2,1)S(1)}, bf16[256,512]{1,0:T(8,128)(2,1)S(1)}, u32[]{:S(2)}, u32[]{:S(2)}) collective-permute-start(bf16[256,512]{1,0:T(8,128)(2,1)S(1)} %collective-permute-done.refs_0_), channel_id=1, source_target_pairs={{0,8},{8,16},{16,24},{24,28},{28,20},{20,12},{12,4},{4,0},{1,9},{9... | collective-permute-start | bytes 786440 | tf_op jit(solution)/shard_map/ppermute | solution.py:152
  17.7 1.9 %collective-permute-start.5 = (bf16[304,128]{1,0:T(8,128)(2,1)S(1)}, bf16[304,128]{1,0:T(8,128)(2,1)S(1)}, u32[]{:S(2)}, u32[]{:S(2)}) collective-permute-start(bf16[304,128]{1,0:T(8,128)(2,1)S(1)} %get-tuple-element.39), channel_id=1, source_target_pairs={{0,2},{1,3},{2,0},{3,1},{4,6},{5,7},{6,4},{7,5},{8,10},{9,11},{10,... | collective-permute-start | bytes 233480 | tf_op jit(solution)/shard_map/ppermute | solution.py:262
  19.6 1.4 %collective-permute-start.6 = (bf16[304,128]{1,0:T(8,128)(2,1)S(1)}, bf16[304,128]{1,0:T(8,128)(2,1)S(1)}, u32[]{:S(2)}, u32[]{:S(2)}) collective-permute-start(bf16[304,128]{1,0:T(8,128)(2,1)S(1)} %get-tuple-element.40), channel_id=1, source_target_pairs={{0,3},{1,0},{2,1},{3,2},{4,7},{5,4},{6,5},{7,6},{8,11},{9,8},{10,9... | collective-permute-start | bytes 233480 | tf_op jit(solution)/shard_map/ppermute | solution.py:262
  21.0 3.4 %accumulate.5 = (f32[8,256,512]{2,1,0:T(8,128)S(1)}, f32[8,128]{1,0:T(8,128)S(1)}) custom-call(bf16[8,256,2048]{2,1,0:T(8,128)(2,1)S(1)} %copy-done.1, bf16[256,512]{1,0:T(8,128)(2,1)S(1)} %collective-permute-done.refs_0_, bf16[256,512]{1,0:T(8,128)(2,1)S(1)} %collective-permute-done.1.refs_1_, f32[8,128]{1,0:T(8,128)S(1)} %get-tuple-element.35.refs_2_, ...), custom_call_target="tpu_custom_call" | custom-call | flops 1073741824 | bytes 2097152 | tf_op jit(solution)/shard_map/accumulate/pallas_call | solution.py:116
  24.9 1.6 %collective-permute-start.7 = (bf16[256,512]{1,0:T(8,128)(2,1)S(1)}, bf16[256,512]{1,0:T(8,128)(2,1)S(1)}, u32[]{:S(2)}, u32[]{:S(2)}) collective-permute-start(bf16[256,512]{1,0:T(8,128)(2,1)S(1)} %collective-permute-done.2.refs_0_), channel_id=1, source_target_pairs={{0,8},{8,16},{16,24},{24,28},{28,20},{20,12},{12,4},{4,0},{1,9},{9... | collective-permute-start | bytes 786440 | tf_op jit(solution)/shard_map/ppermute | solution.py:152
  26.9 3.4 %accumulate.6 = (f32[8,256,512]{2,1,0:T(8,128)S(1)}, f32[8,128]{1,0:T(8,128)S(1)}) custom-call(bf16[8,256,2048]{2,1,0:T(8,128)(2,1)S(1)} %copy-done.1, bf16[256,512]{1,0:T(8,128)(2,1)S(1)} %collective-permute-done.2.refs_0_, bf16[256,512]{1,0:T(8,128)(2,1)S(1)} %collective-permute-done.3.refs_1_, f32[8,128]{1,0:T(8,128)S(1)} %get-tuple-element.43.refs_2_, ...), custom_call_target="tpu_custom_call" | custom-call | flops 1073741824 | bytes 2097152 | tf_op jit(solution)/shard_map/accumulate/pallas_call | solution.py:116
  30.3 2.0 %collective-permute-done.7.refs_0_ = bf16[256,512]{1,0:T(8,128)(2,1)S(1)} collective-permute-done((bf16[256,512]{1,0:T(8,128)(2,1)S(1)}, bf16[256,512]{1,0:T(8,128)(2,1)S(1)}, u32[]{:S(2)}, u32[]{:S(2)}) %collective-permute-start.7) | collective-permute-done | bytes 262176 | tf_op jit(solution)/shard_map/ppermute | solution.py:152
  32.3 1.7 %collective-permute-done.8.refs_1_ = bf16[256,512]{1,0:T(8,128)(2,1)S(1)} collective-permute-done((bf16[256,512]{1,0:T(8,128)(2,1)S(1)}, bf16[256,512]{1,0:T(8,128)(2,1)S(1)}, u32[]{:S(2)}, u32[]{:S(2)}) %collective-permute-start.8) | collective-permute-done | bytes 262176 | tf_op jit(solution)/shard_map/ppermute | solution.py:153
  34.4 1.8 %collective-permute-start.9 = (bf16[128,512]{1,0:T(8,128)(2,1)S(1)}, bf16[128,512]{1,0:T(8,128)(2,1)S(1)}, u32[]{:S(2)}, u32[]{:S(2)}) collective-permute-start(bf16[128,512]{1,0:T(8,128)(2,1)S(1)} %slice.6), channel_id=1, source_target_pairs={{0,8},{8,16},{16,24},{24,28},{28,20},{20,12},{12,4},{4,0},{1,9},{9... | collective-permute-start | bytes 393224 | tf_op jit(solution)/shard_map/ppermute | solution.py:162
  36.2 4.2 %accumulate.7 = (f32[8,256,512]{2,1,0:T(8,128)S(1)}, f32[8,128]{1,0:T(8,128)}, bf16[8,256,256]{2,1,0:T(8,128)(2,1)S(1)}) custom-call(bf16[8,256,2048]{2,1,0:T(8,128)(2,1)S(1)} %copy-done.1, bf16[256,512]{1,0:T(8,128)(2,1)S(1)} %collective-permute-done.7.refs_0_, bf16[256,512]{1,0:T(8,128)(2,1)S(1)} %collective-permute-done.8.refs_1_, ...), custom_call_target="tpu_custom_call" | custom-call | flops 1073741824 | bytes 2097152 | tf_op jit(solution)/shard_map/accumulate/pallas_call | solution.py:116
  40.4 1.4 %measure.1 = f32[32,128]{1,0:T(8,128)S(1)} custom-call(bf16[8,256,256]{2,1,0:T(8,128)(2,1)S(1)} %get-tuple-element.50.refs_0_, f32[8,128]{1,0:T(8,128)S(1)} %get-tuple-element.31.refs_1_, bf16[304,128]{1,0:T(8,128)(2,1)S(1)} %get-tuple-element.51.refs_2_.refs_0_, bf16[304,128]{1,0:T(8,128)(2,1)S(1)} %collective-permute-done.4.refs_3_.refs_1_, ...), custom_call_target="tpu_custom_call" | custom-call | flops 536870912 | bytes 4194304 | tf_op jit(solution)/shard_map/measure/pallas_call | solution.py:357
  41.8 11.7 %all_to_all.11 = f32[32,1,128]{2,1,0:T(1,128)S(1)} all-to-all(f32[32,1,128]{2,1,0:T(1,128)S(1)} %bitcast.7), channel_id=1, replica_groups=mesh['chol'=8,'walk'=4] {'chol','walk'}, dimensions={0} | all-to-all | bytes 32768 | tf_op jit(solution)/shard_map/all_to_all | solution.py:440
  53.5 1.4 %finish.1 = (f32[1,4]{1,0:T(1,128)}, f32[1,4]{1,0:T(1,128)}, f32[128,128]{1,0:T(8,128)}) custom-call(f32[32,128]{1,0:T(8,128)S(1)} %bitcast.8, s32[4]{0:T(128)S(1)} %copy-done.7, bf16[304,128]{1,0:T(8,128)(2,1)S(1)} %get-tuple-element.51.refs_2_.refs_0_, bf16[304,128]{1,0:T(8,128)(2,1)S(1)} %collective-permute-done.4.refs_3_.refs_1_, ...), custom_call_target="tpu_custom_call" | custom-call | flops 1000000 | bytes 600000 | tf_op jit(solution)/shard_map/finish/pallas_call | solution.py:413
  (26 shorter events, 1.2 us)
Async XLA Ops:
  0.6 1.0 %copy-start.2 = (bf16[256,2,256]{2,1,0:T(2,128)(2,1)S(1)}, bf16[256,2,256]{2,1,0:T(2,128)(2,1)}, u32[]{:S(2)}) copy-start(bf16[256,2,256]{2,1,0:T(2,128)(2,1)} %green_ref.1) | copy-start | bytes 786436
  2.2 13.4 %collective-permute-start = (bf16[256,512]{1,0:T(8,128)(2,1)S(1)}, bf16[256,512]{1,0:T(8,128)(2,1)S(1)}, u32[]{:S(2)}, u32[]{:S(2)}) collective-permute-start(bf16[256,512]{1,0:T(8,128)(2,1)S(1)} %split_walkers.1.refs_0_), channel_id=1, source_target_pairs={{0,8},{8,16},{16,24},{24,28},{28,20},{20,12},{12,4},{4,0},{1,9},{9... | collective-permute-start | bytes 786440 | tf_op jit(solution)/shard_map/ppermute | solution.py:152
  5.3 10.3 %collective-permute-start.1 = (bf16[256,512]{1,0:T(8,128)(2,1)S(1)}, bf16[256,512]{1,0:T(8,128)(2,1)S(1)}, u32[]{:S(2)}, u32[]{:S(2)}) collective-permute-start(bf16[256,512]{1,0:T(8,128)(2,1)S(1)} %split_walkers.1.refs_0_), channel_id=1, source_target_pairs={{0,4},{8,0},{16,8},{24,16},{28,24},{20,28},{12,20},{4,12},{1,5},{9... | collective-permute-start | bytes 786440 | tf_op jit(solution)/shard_map/ppermute | solution.py:153
  6.0 0.9 %copy-start.3 = (bf16[256,256]{1,0:T(8,128)(2,1)S(1)}, bf16[256,256]{1,0:T(8,128)(2,1)}, u32[]{:S(2)}) copy-start(bf16[256,256]{1,0:T(8,128)(2,1)} %refs_1_.1) | copy-start | bytes 393220
  7.0 0.7 %copy-start.4 = (f32[2]{0:T(128)S(1)}, f32[2]{0:T(128)}, u32[]{:S(2)}) copy-start(f32[2]{0:T(128)} %refs_3_.1) | copy-start | bytes 28
  7.6 0.7 %copy-start.5 = (s32[4]{0:T(128)S(1)}, s32[4]{0:T(128)}, u32[]{:S(2)}) copy-start(s32[4]{0:T(128)} %refs_4_.1) | copy-start | bytes 52
  8.3 0.7 %copy-start.6 = (s32[4]{0:T(128)S(1)}, s32[4]{0:T(128)}, u32[]{:S(2)}) copy-start(s32[4]{0:T(128)} %refs_5_.1) | copy-start | bytes 52
  10.1 3.4 %copy-start = (bf16[8,256,2048]{2,1,0:T(8,128)(2,1)S(1)}, bf16[8,256,2048]{2,1,0:T(8,128)(2,1)}, u32[]{:S(2)}) copy-start(bf16[8,256,2048]{2,1,0:T(8,128)(2,1)} %chol_ref.7) | copy-start | bytes 25165828
  13.5 7.6 %copy-start.1 = (bf16[8,256,2048]{2,1,0:T(8,128)(2,1)S(1)}, bf16[8,256,2048]{2,1,0:T(8,128)(2,1)}, u32[]{:S(2)}) copy-start(bf16[8,256,2048]{2,1,0:T(8,128)(2,1)} %chol_ref.7) | copy-start | bytes 25165828
  15.6 8.9 %collective-permute-start.2 = (bf16[256,512]{1,0:T(8,128)(2,1)S(1)}, bf16[256,512]{1,0:T(8,128)(2,1)S(1)}, u32[]{:S(2)}, u32[]{:S(2)}) collective-permute-start(bf16[256,512]{1,0:T(8,128)(2,1)S(1)} %collective-permute-done.refs_0_), channel_id=1, source_target_pairs={{0,8},{8,16},{16,24},{24,28},{28,20},{20,12},{12,4},{4,0},{1,9},{9... | collective-permute-start | bytes 786440 | tf_op jit(solution)/shard_map/ppermute | solution.py:152
  17.7 7.2 %collective-permute-start.3 = (bf16[256,512]{1,0:T(8,128)(2,1)S(1)}, bf16[256,512]{1,0:T(8,128)(2,1)S(1)}, u32[]{:S(2)}, u32[]{:S(2)}) collective-permute-start(bf16[256,512]{1,0:T(8,128)(2,1)S(1)} %collective-permute-done.1.refs_1_), channel_id=1, source_target_pairs={{0,4},{8,0},{16,8},{24,16},{28,24},{20,28},{12,20},{4,12},{1,5},{9... | collective-permute-start | bytes 786440 | tf_op jit(solution)/shard_map/ppermute | solution.py:153
  17.7 6.8 %collective-permute-start.4 = (bf16[304,128]{1,0:T(8,128)(2,1)S(1)}, bf16[304,128]{1,0:T(8,128)(2,1)S(1)}, u32[]{:S(2)}, u32[]{:S(2)}) collective-permute-start(bf16[304,128]{1,0:T(8,128)(2,1)S(1)} %get-tuple-element.38), channel_id=1, source_target_pairs={{0,1},{1,2},{2,3},{3,0},{4,5},{5,6},{6,7},{7,4},{8,9},{9,10},{10,1... | collective-permute-start | bytes 233480 | tf_op jit(solution)/shard_map/ppermute | solution.py:262
  17.7 6.8 %collective-permute-start.5 = (bf16[304,128]{1,0:T(8,128)(2,1)S(1)}, bf16[304,128]{1,0:T(8,128)(2,1)S(1)}, u32[]{:S(2)}, u32[]{:S(2)}) collective-permute-start(bf16[304,128]{1,0:T(8,128)(2,1)S(1)} %get-tuple-element.39), channel_id=1, source_target_pairs={{0,2},{1,3},{2,0},{3,1},{4,6},{5,7},{6,4},{7,5},{8,10},{9,11},{10,... | collective-permute-start | bytes 233480 | tf_op jit(solution)/shard_map/ppermute | solution.py:262
  19.6 4.9 %collective-permute-start.6 = (bf16[304,128]{1,0:T(8,128)(2,1)S(1)}, bf16[304,128]{1,0:T(8,128)(2,1)S(1)}, u32[]{:S(2)}, u32[]{:S(2)}) collective-permute-start(bf16[304,128]{1,0:T(8,128)(2,1)S(1)} %get-tuple-element.40), channel_id=1, source_target_pairs={{0,3},{1,0},{2,1},{3,2},{4,7},{5,4},{6,5},{7,6},{8,11},{9,8},{10,9... | collective-permute-start | bytes 233480 | tf_op jit(solution)/shard_map/ppermute | solution.py:262
  24.9 7.5 %collective-permute-start.7 = (bf16[256,512]{1,0:T(8,128)(2,1)S(1)}, bf16[256,512]{1,0:T(8,128)(2,1)S(1)}, u32[]{:S(2)}, u32[]{:S(2)}) collective-permute-start(bf16[256,512]{1,0:T(8,128)(2,1)S(1)} %collective-permute-done.2.refs_0_), channel_id=1, source_target_pairs={{0,8},{8,16},{16,24},{24,28},{28,20},{20,12},{12,4},{4,0},{1,9},{9... | collective-permute-start | bytes 786440 | tf_op jit(solution)/shard_map/ppermute | solution.py:152
  26.4 7.6 %collective-permute-start.8 = (bf16[256,512]{1,0:T(8,128)(2,1)S(1)}, bf16[256,512]{1,0:T(8,128)(2,1)S(1)}, u32[]{:S(2)}, u32[]{:S(2)}) collective-permute-start(bf16[256,512]{1,0:T(8,128)(2,1)S(1)} %collective-permute-done.3.refs_1_), channel_id=1, source_target_pairs={{0,4},{8,0},{16,8},{24,16},{28,24},{20,28},{12,20},{4,12},{1,5},{9... | collective-permute-start | bytes 786440 | tf_op jit(solution)/shard_map/ppermute | solution.py:153
  34.1 6.4 %collective-permute-start.10 = (bf16[128,512]{1,0:T(8,128)(2,1)S(1)}, bf16[128,512]{1,0:T(8,128)(2,1)S(1)}, u32[]{:S(2)}, u32[]{:S(2)}) collective-permute-start(bf16[128,512]{1,0:T(8,128)(2,1)S(1)} %slice.7), channel_id=1, source_target_pairs={{0,4},{8,0},{16,8},{24,16},{28,24},{20,28},{12,20},{4,12},{1,5},{9... | collective-permute-start | bytes 393224 | tf_op jit(solution)/shard_map/ppermute | solution.py:163
  34.4 6.0 %collective-permute-start.9 = (bf16[128,512]{1,0:T(8,128)(2,1)S(1)}, bf16[128,512]{1,0:T(8,128)(2,1)S(1)}, u32[]{:S(2)}, u32[]{:S(2)}) collective-permute-start(bf16[128,512]{1,0:T(8,128)(2,1)S(1)} %slice.6), channel_id=1, source_target_pairs={{0,8},{8,16},{16,24},{24,28},{28,20},{20,12},{12,4},{4,0},{1,9},{9... | collective-permute-start | bytes 393224 | tf_op jit(solution)/shard_map/ppermute | solution.py:162
  40.4 13.0 %copy-start.7 = (s32[4]{0:T(128)S(1)}, s32[4]{0:T(128)}, u32[]{:S(2)}) copy-start(s32[4]{0:T(128)} %counts_ref.1) | copy-start | bytes 52

commit v3 on v2

v3 whole, which is shorter than its diff:
```python
import functools

import jax
import jax.numpy as jnp
from jax import lax
from jax.experimental import pallas as pl
from jax.experimental.pallas import tpu as pltpu
from jax.sharding import PartitionSpec as P

time_step = 0.02
root_step = 0.02**0.5
LANES = 128
VMEM_LIMIT = 16 * 1024 * 1024
PACK_LIMIT = 54 * 1024 * 1024
FETCH_LIMIT = 42 * 1024 * 1024
RING_LIMIT = 16


def params(limit=VMEM_LIMIT):
    return pltpu.CompilerParams(vmem_limit_bytes=limit)


def vmem():
    return pl.BlockSpec(memory_space=pltpu.VMEM)


def smem():
    return pl.BlockSpec(memory_space=pltpu.SMEM)


def ring_order(size):
    return [2 * q if q < size // 2 else 2 * (size - 1 - q) + 1 for q in range(size)]


def ring_place(index, size):
    return jnp.where(index % 2 == 0, index // 2, size - 1 - index // 2)


def ring_owner(place, size):
    return jnp.where(place < size // 2, 2 * place, 2 * (size - 1 - place) + 1)


def column_start(shift, rows):
    size = lax.axis_size("chol")
    place = ring_place(lax.axis_index("chol"), size)
    owner = ring_owner(lax.rem(place + shift + size, size), size)
    return pl.multiple_of(owner * rows, rows)


def accumulate(blocks, first, parts, total, mark):
    size, width = blocks.shape
    rows, walkers, orbitals = parts[0].shape
    count = len(parts)
    fresh = total is None
    arrays = list(parts) + [mark] + ([] if fresh else [total])

    def kernel(blocks_ref, *refs):
        shards = refs[:count]
        total_ref, mark_ref = refs[len(arrays) :]
        mark_ref[...] = jnp.zeros_like(mark_ref)
        lhs = blocks_ref[:, first * rows : (first + count) * rows]
        for b in range(walkers):
            rhs = jnp.concatenate([x[:, b, :] for x in shards], axis=0)
            value = jnp.dot(lhs, rhs, preferred_element_type=jnp.float32)
            total_ref[b] = value if fresh else refs[count + 1][b] + value

    return pl.pallas_call(
        kernel,
        name="accumulate",
        out_shape=[
            jax.ShapeDtypeStruct((walkers, size, orbitals), jnp.float32),
            jax.ShapeDtypeStruct((8, LANES), jnp.float32),
        ],
        in_specs=[vmem()] * (1 + len(arrays)),
        out_specs=[vmem()] * 2,
        compiler_params=params(),
        cost_estimate=pl.CostEstimate(
            flops=2 * count * size * rows * walkers * orbitals,
            bytes_accessed=2 * count * size * rows,
            transcendentals=0,
        ),
    )(blocks, *arrays)


def tie(*arrays):
    return lax.optimization_barrier(arrays)


def arrival_shifts(size):
    shifts = [0]
    for step in range(1, size // 2):
        shifts += [-step, step]
    return shifts + [size // 2]


def ring(own, cholesky_rot, onebody, packed):
    size = lax.axis_size("chol")
    rows = own.shape[0]
    order = ring_order(size)
    ahead = [(order[q], order[(q + 1) % size]) for q in range(size)]
    back = [(order[q], order[(q - 1) % size]) for q in range(size)]
    right = left = own
    parts = [own]
    first = 0
    total = None
    steps = size // 2
    blocks, mark = fetch(cholesky_rot, arrival_shifts(size))
    for step in range(1, steps):
        next_right = lax.ppermute(right, "chol", ahead)
        next_left = lax.ppermute(left, "chol", back)
        if step > 1:
            total, mark = accumulate(blocks, first, parts, total, mark)
            first += len(parts)
            parts = []
        if step == 1:
            others = [shifted(packed[d], d) for d in range(1, len(packed))]
        if step == 1:
            right, left, mark, onebody = tie(next_right, next_left, mark, onebody)
        elif step == 2:
            right, left, mark, *others = tie(next_right, next_left, mark, *others)
        else:
            right, left, mark = tie(next_right, next_left, mark)
        parts = parts + [right, left]
    last = [lax.ppermute(right[: rows // 2], "chol", ahead), lax.ppermute(left[rows // 2 :], "chol", back)]
    total, _ = accumulate(blocks, first, parts, total, mark)
    return blocks, onebody, total, last, [packed[0]] + others


def table_height(vectors):
    return -(-(vectors + 2) // 16) * 16


def fetch(cholesky_rot, shifts):
    vectors, orbitals, basis = cholesky_rot.shape
    rows = basis // len(shifts)

    def kernel(chol_any, blocks_ref, mark_ref, sems):
        mark_ref[...] = jnp.zeros_like(mark_ref)
        copies = []
        for n, shift in enumerate(shifts):
            start = 0 if shift is None else column_start(shift, rows)
            for g in range(vectors):
                copies.append(
                    pltpu.make_async_copy(
                        chol_any.at[g, :, pl.ds(start, rows)],
                        blocks_ref.at[pl.ds(g * orbitals, orbitals), pl.ds(n * rows, rows)],
                        sems.at[n, g],
                    )
                )
        for copy in copies:
            copy.start()
        for copy in copies:
            copy.wait()

    return pl.pallas_call(
        kernel,
        name="fetch",
        out_shape=[
            jax.ShapeDtypeStruct((vectors * orbitals, basis), cholesky_rot.dtype),
            jax.ShapeDtypeStruct((8, LANES), jnp.float32),
        ],
        in_specs=[pl.BlockSpec(memory_space=pl.ANY)],
        out_specs=[vmem()] * 2,
        scratch_shapes=[pltpu.SemaphoreType.DMA((len(shifts), vectors))],
        compiler_params=params(FETCH_LIMIT),
        cost_estimate=pl.CostEstimate(flops=0, bytes_accessed=2 * cholesky_rot.size, transcendentals=0),
    )(cholesky_rot)


def pack(own, one_body, fields, weights, sources, owners):
    rows, walkers, orbitals = own.shape
    walk_size = lax.axis_size("walk")
    width = orbitals // walk_size
    pair = LANES // width
    vectors, slots = fields.shape
    table_rows = table_height(vectors)
    height = walkers * (rows // pair) + 3 * table_rows

    def kernel(own_any, body_any, fields_any, weights_any, sources_any, owners_any, *refs):
        onebody_ref = refs[0]
        packs = refs[1 : 1 + walk_size]
        own_ref, body_ref, fields_ref, weights_ref, sources_ref, owners_ref, table_scr, sems = refs[1 + walk_size :]
        places = [
            (own_any, own_ref),
            (body_any, body_ref),
            (fields_any, fields_ref),
            (weights_any, weights_ref),
            (sources_any, sources_ref),
            (owners_any, owners_ref),
        ]
        small = [pltpu.make_async_copy(a, b, sems.at[n]) for n, (a, b) in enumerate(places)]
        for copy in small:
            copy.start()
        for copy in small:
            copy.wait()
        green = [own_ref[:, b, :] for b in range(walkers)]
        walk = lax.axis_index("walk")
        lane = lax.broadcasted_iota(jnp.int32, (1, LANES), 1)
        body = body_ref[...].astype(jnp.float32)
        onebody_ref[...] = jnp.zeros_like(onebody_ref)
        for b in range(walkers):
            total = jnp.sum(green[b].astype(jnp.float32) * body, axis=0, keepdims=True)
            folded = total[:, :LANES]
            for start in range(LANES, orbitals, LANES):
                folded = folded + total[:, start : start + LANES]
            onebody_ref[b : b + 1, :] = folded
        r = lax.broadcasted_iota(jnp.int32, (rows // pair, rows), 0)
        m = lax.broadcasted_iota(jnp.int32, (rows // pair, rows), 1)
        k = lax.broadcasted_iota(jnp.int32, (orbitals, LANES), 0)
        c = lax.broadcasted_iota(jnp.int32, (orbitals, LANES), 1)
        thinned = []
        for b in range(walkers):
            values = green[b]
            thinned.append(
                [
                    jnp.dot(
                        (m == r * pair + h).astype(jnp.bfloat16), values, preferred_element_type=jnp.float32
                    ).astype(jnp.bfloat16)
                    for h in range(pair)
                ]
            )
        for d in range(walk_size):
            target = lax.rem(walk + d, walk_size)
            panel = jnp.int32(0)
            for p in range(walk_size):
                panel = jnp.where(owners_ref[p] == target, p, panel)
            for b in range(walkers):
                total = jnp.zeros((rows // pair, LANES), jnp.float32)
                for h in range(pair):
                    take = (k == panel * width + c - h * width) & (c >= h * width) & (c < (h + 1) * width)
                    total += jnp.dot(
                        thinned[b][h], take.astype(jnp.bfloat16), preferred_element_type=jnp.float32
                    )
                packs[d][b * (rows // pair) : (b + 1) * (rows // pair), :] = total.astype(jnp.bfloat16)
        spread = jnp.zeros((vectors, LANES), jnp.float32)
        source = jnp.zeros((1, LANES), jnp.float32)
        corner = lax.broadcasted_iota(jnp.int32, (vectors, vectors), 0) == lax.broadcasted_iota(
            jnp.int32, (vectors, vectors), 1
        )
        for j in range(slots):
            mine = lane % slots == j
            upright = jnp.sum(jnp.where(corner, fields_ref[j : j + 1, :], 0.0), axis=1, keepdims=True)
            spread += jnp.where(mine, upright, 0.0)
            source += jnp.where(mine, sources_ref[j].astype(jnp.float32), 0.0)
        weight = weights_ref[0]
        for j in range(1, weights.shape[0]):
            weight = weight + weights_ref[j]
        table_scr[...] = jnp.zeros_like(table_scr)
        table_scr[:vectors, :] = spread
        table_scr[vectors : vectors + 1, :] = source
        table_scr[vectors + 1 : vectors + 2, :] = jnp.zeros((1, LANES), jnp.float32) + weight
        rest = table_scr[...]
        for n in range(3):
            piece = rest.astype(jnp.bfloat16)
            rest = rest - piece.astype(jnp.float32)
            at = walkers * (rows // pair) + n * table_rows
            for d in range(walk_size):
                packs[d][at : at + table_rows, :] = piece

    return pl.pallas_call(
        kernel,
        name="pack",
        out_shape=[
            jax.ShapeDtypeStruct((8, LANES), jnp.float32),
        ]
        + [jax.ShapeDtypeStruct((height, LANES), jnp.bfloat16)] * walk_size,
        in_specs=[pl.BlockSpec(memory_space=pl.ANY)] * 6,
        out_specs=[vmem()] * (walk_size + 1),
        scratch_shapes=[
            pltpu.VMEM(own.shape, own.dtype),
            pltpu.VMEM(one_body.shape, one_body.dtype),
            pltpu.VMEM((slots, vectors), jnp.float32),
            pltpu.SMEM(weights.shape, weights.dtype),
            pltpu.SMEM(sources.shape, sources.dtype),
            pltpu.SMEM(owners.shape, owners.dtype),
            pltpu.VMEM((table_rows, LANES), jnp.float32),
            pltpu.SemaphoreType.DMA((6,)),
        ],
        compiler_params=params(PACK_LIMIT),
        cost_estimate=pl.CostEstimate(flops=10**8, bytes_accessed=10**6, transcendentals=0),
    )(own, one_body, fields.T, weights, sources, owners)


def shifted(x, d):
    size = lax.axis_size("walk")
    return lax.ppermute(x, "walk", [(q, (q + d) % size) for q in range(size)])


def read_table(ref, vectors):
    height = table_height(vectors)
    start = ref.shape[0] - 3 * height
    parts = [ref[start + n * height : start + (n + 1) * height, :].astype(jnp.float32) for n in range(3)]
    return parts[0] + (parts[1] + parts[2])


def merge_tables(tables, walk, walk_size, slots, lane):
    total = jnp.zeros_like(tables[0])
    for d, table in enumerate(tables):
        group = lax.rem(walk - d + walk_size, walk_size)
        total += jnp.where(lane // slots == group, table, 0.0)
    return total


def measure(blocks, first, total, last, packs, onebody, vectors, slots):
    _, walkers, orbitals = last[0].shape
    depth = sum(x.shape[0] for x in last)
    walk_size = len(packs)
    targets = lax.axis_size("chol")
    whole = total is None
    quads = orbitals // LANES

    def fold(x):
        return jnp.sum(x.reshape(-1, 8, LANES), axis=0)

    def kernel(*refs):
        blocks_ref, onebody_ref = refs[:2]
        pack_refs = refs[2 : 2 + walk_size]
        last_refs = refs[2 + walk_size : 2 + walk_size + len(last)]
        out_ref, tensor_scr = refs[-2:]
        walk = lax.axis_index("walk")
        lane = lax.broadcasted_iota(jnp.int32, (1, LANES), 1)
        table = merge_tables([read_table(x, vectors) for x in pack_refs], walk, walk_size, slots, lane)
        picks = [
            jnp.where(
                (lane < slots * walk_size) & (table[vectors : vectors + 1, :] == (walk * walkers + b).astype(jnp.float32)),
                1.0,
                0.0,
            )
            for b in range(walkers)
        ]
        rhs = [jnp.concatenate([x[:, b, :] for x in last_refs], axis=0) for b in range(walkers)]
        eye = lax.broadcasted_iota(jnp.int32, (LANES, LANES), 0) == lax.broadcasted_iota(
            jnp.int32, (LANES, LANES), 1
        )
        exchange = [jnp.zeros((8, LANES), jnp.float32) for _ in range(walkers)]
        squares = [jnp.zeros((1, 1), jnp.float32) for _ in range(walkers)]
        drive = jnp.zeros((1, LANES), jnp.float32)
        for b in range(walkers):
            value = jnp.dot(
                blocks_ref[:, first * depth : (first + 1) * depth], rhs[b], preferred_element_type=jnp.float32
            )
            tensor_scr[b] = value if whole else refs[2 + walk_size + len(last)][b] + value
        for g in range(vectors):
            top = g * orbitals
            for b in range(walkers):
                diagonal = jnp.zeros((LANES, LANES), jnp.float32)
                for q in range(quads):
                    for p in range(q + 1):
                        one = tensor_scr[
                            b, top + q * LANES : top + (q + 1) * LANES, p * LANES : (p + 1) * LANES
                        ]
                        if p == q:
                            exchange[b] = exchange[b] + fold(one * one.T)
                            diagonal = diagonal + one
                        else:
                            two = tensor_scr[
                                b, top + p * LANES : top + (p + 1) * LANES, q * LANES : (q + 1) * LANES
                            ]
                            exchange[b] = exchange[b] + 2.0 * fold(two * one.T)
                trace = jnp.sum(fold(jnp.where(eye, diagonal, 0.0)), axis=0, keepdims=True)
                trace = jnp.sum(trace, axis=1, keepdims=True)
                squares[b] = squares[b] + trace * trace
                drive = drive - root_step * picks[b] * table[g : g + 1, :] * trace
        raw = jnp.zeros((1, LANES), jnp.float32)
        square = jnp.zeros((1, LANES), jnp.float32)
        for b in range(walkers):
            swapped = jnp.sum(jnp.sum(exchange[b], axis=0, keepdims=True), axis=1, keepdims=True)
            single = jnp.sum(onebody_ref[b : b + 1, :], axis=1, keepdims=True)
            raw += picks[b] * (single + 0.5 * squares[b] - 0.5 * swapped)
            square += picks[b] * squares[b]
        power = drive - 0.5 * time_step * square - time_step * raw
        out_ref[...] = jnp.broadcast_to(raw + pltpu.roll(power, slots * walk_size, 1), (targets, LANES))

    arrays = list(last) + ([] if whole else [total])
    return pl.pallas_call(
        kernel,
        name="measure",
        out_shape=jax.ShapeDtypeStruct((targets, LANES), jnp.float32),
        in_specs=[vmem()] * (2 + walk_size + len(arrays)),
        out_specs=vmem(),
        scratch_shapes=[
            pltpu.VMEM((walkers, vectors * orbitals, orbitals), jnp.float32),
        ],
        compiler_params=params(),
        cost_estimate=pl.CostEstimate(
            flops=2 * vectors * orbitals * depth * walkers * orbitals,
            bytes_accessed=2 * vectors * orbitals * depth,
            transcendentals=0,
        ),
    )(blocks, onebody, *packs, *arrays)


def add_up(stats, targets):
    def kernel(stats_ref, out_ref):
        out_ref[...] = jnp.broadcast_to(jnp.sum(stats_ref[...], axis=0, keepdims=True), out_ref.shape)

    return pl.pallas_call(
        kernel,
        name="add_up",
        out_shape=jax.ShapeDtypeStruct((targets, LANES), jnp.float32),
        in_specs=[vmem()],
        out_specs=vmem(),
        compiler_params=params(),
    )(stats)


def finish(stats, packs, counts, vectors, slots, walkers):
    walk_size = len(packs)
    rows = (packs[0].shape[0] - 3 * table_height(vectors)) // walkers

    def kernel(stats_ref, counts_ref, *refs):
        pack_refs = refs[:walk_size]
        energies_ref, weights_ref, density_ref = refs[walk_size:]
        walk = lax.axis_index("walk")
        lane = lax.broadcasted_iota(jnp.int32, (1, LANES), 1)
        all_slots = slots * walk_size
        tables = [read_table(x, vectors) for x in pack_refs]
        source = merge_tables([t[vectors : vectors + 1, :] for t in tables], walk, walk_size, slots, lane)
        total_weight = tables[0][vectors + 1 : vectors + 2, :]
        for t in tables[1:]:
            total_weight = total_weight + t[vectors + 1 : vectors + 2, :]
        mean_weight = total_weight / (walkers * walk_size)
        total = jnp.sum(stats_ref[...], axis=0, keepdims=True)
        power = pltpu.roll(total, LANES - all_slots, 1)
        live_count = jnp.zeros((1, LANES), jnp.int32)
        for q in range(walk_size):
            live_count = jnp.where(lane // slots == q, counts_ref[q], live_count)
        live = (lane < all_slots) & (lane % slots < live_count)
        energies = jnp.where(live, total, 0.0)
        new_weights = jnp.where(live, mean_weight * jnp.exp(jnp.where(live, power, 0.0)), 0.0)
        norm = jnp.sum(new_weights, axis=1, keepdims=True)
        density = jnp.zeros((rows, LANES), jnp.float32)
        for d in range(walk_size):
            group = lax.rem(walk - d + walk_size, walk_size)
            for b in range(walkers):
                walker = (group * walkers + b).astype(jnp.float32)
                share = jnp.sum(jnp.where(source == walker, new_weights, 0.0), axis=1, keepdims=True) / norm
                density += share * pack_refs[d][b * rows : (b + 1) * rows, :].astype(jnp.float32)
        density_ref[...] = density
        first = lax.rem(LANES - walk * slots, LANES)
        energies_ref[...] = pltpu.roll(jnp.broadcast_to(energies, (8, LANES)), first, 1)[:1, :slots]
        weights_ref[...] = pltpu.roll(jnp.broadcast_to(new_weights, (8, LANES)), first, 1)[:1, :slots]

    return pl.pallas_call(
        kernel,
        name="finish",
        out_shape=[
            jax.ShapeDtypeStruct((1, slots), jnp.float32),
            jax.ShapeDtypeStruct((1, slots), jnp.float32),
            jax.ShapeDtypeStruct((rows, LANES), jnp.float32),
        ],
        in_specs=[vmem(), smem()] + [vmem()] * walk_size,
        out_specs=[vmem()] * 3,
        compiler_params=params(),
        cost_estimate=pl.CostEstimate(flops=10**6, bytes_accessed=6 * 10**5, transcendentals=128),
    )(stats, counts, *packs)


def per_device(green_rows, cholesky_rot, one_body, fields, weights, sources, counts, owners):
    chol_size = lax.axis_size("chol")
    walk_size = lax.axis_size("walk")
    vectors, slots = fields.shape
    walkers = green_rows.shape[1]
    onebody, *packed = pack(green_rows, one_body, fields, weights, sources, owners)
    if chol_size > RING_LIMIT or chol_size % 2 or chol_size < 6:
        blocks, first = fetch(cholesky_rot, [None])[0], 0
        packs = [packed[0]] + [shifted(packed[d], d) for d in range(1, walk_size)]
        total, last = None, [lax.all_gather(green_rows, "chol", axis=0, tiled=True)]
    else:
        blocks, onebody, total, last, packs = ring(green_rows, cholesky_rot, onebody, packed)
        first = chol_size - 1
    stats = measure(blocks, first, total, last, packs, onebody, vectors, slots)
    stats = lax.all_to_all(stats, "chol", split_axis=0, concat_axis=0, tiled=True)
    stats = add_up(stats, walk_size)
    stats = lax.all_to_all(stats, "walk", split_axis=0, concat_axis=0, tiled=True)
    energies, new_weights, density = finish(stats, packs, counts, vectors, slots, walkers)
    return energies.reshape(slots), new_weights.reshape(slots), density.reshape(1, density.size)


def solution(mesh):
    return jax.shard_map(
        per_device,
        mesh=mesh,
        in_specs=(
            P("chol", "walk", None),
            P("chol", None, None),
            P("chol", None),
            P("chol", "walk"),
            P("walk"),
            P("walk"),
            P(),
            P(),
        ),
        out_specs=(P("walk"), P("walk"), P("walk", "chol")),
        check_vma=False,
    )
```

time: 55.2 us -> 56 us (1.014)
  local copies, waits for them, and re-layouts: 7.97 us -> 0.2 us
  waiting for transfers between devices: 4.11 us -> 9.6 us
  blocking collectives: 11.7 us -> 16.1 us
  Pallas kernels: 17.7 us -> 17 us
    unnamed x17 -> x8, local copies, waits for them, and re-layouts: 7.95 us -> 0.02 us
    all_to_all x1 -> x2, blocking collectives: 11.7 us -> 16.1 us  [the longest x1 9.79 us: per_device(): lax.all_to_all(stats, 'chol', split_axis=0, concat_axis=0, tiled=True)]
    ppermute x3, starting transfers between devices: 0.48 us -> 3.98 us  [ring(): next_left = lax.ppermute(left, 'chol', back)]
    ppermute x3, starting transfers between devices: 6.72 us -> 3.22 us  [ring(): next_right = lax.ppermute(right, 'chol', ahead)]
    ppermute x3, waiting for transfers between devices: 2.01 us -> 4.88 us  [ring(): next_right = lax.ppermute(right, 'chol', ahead)]
    ppermute x2, waiting for transfers between devices: 0.01 us -> 2.23 us  [the longest x1 1.58 us: ring(): lax.ppermute(left[rows // 2:], 'chol', back)]
    pallas_call x7, Pallas kernels: 16.2 us -> 15.6 us  [the longest x3 6.5 us: accumulate(): pl.pallas_call(kernel, name='accumulate', out_shape=[jax.ShapeDtypeStruct...]
  transfers between devices with their start and end apart: 11 -> 11, of which waited for: 3 -> 7; matrix products, arithmetic and copies ran while one was open for 1% -> 0% of each run, Pallas kernels for 26% -> 25%
where the time goes in v3:
time: 56 us; the launch traced here: 55.8 us
  Pallas kernels  17 us (30%)
  blocking collectives  16.1 us (29%)
  starting transfers between devices  12.2 us (22%)
  waiting for transfers between devices  9.6 us (17%)
  between operations  0.72 us (1%)
    all_to_all x1, blocking collectives, per_device(): lax.all_to_all(stats, 'chol', split_axis=0, concat_axis=0, tiled=True)  9.79 us
    pallas_call x3, Pallas kernels, accumulate(): pl.pallas_call(kernel, name='accumulate', out_shape=[jax.ShapeDtypeStruct...  6.5 us
    all_to_all x1, blocking collectives, per_device(): lax.all_to_all(stats, 'walk', split_axis=0, concat_axis=0, tiled=True)  6.29 us
    ppermute x3, waiting for transfers between devices, ring(): next_right = lax.ppermute(right, 'chol', ahead)  4.88 us
    pallas_call x1, Pallas kernels, fetch(): pl.pallas_call(kernel, name='fetch', out_shape=[jax.ShapeDtypeStruct((vec...  4.15 us
    ppermute x3, starting transfers between devices, ring(): next_left = lax.ppermute(left, 'chol', back)  3.98 us
    ppermute x3, starting transfers between devices, ring(): next_right = lax.ppermute(right, 'chol', ahead)  3.22 us
    pallas_call x1, Pallas kernels, pack(): pl.pallas_call(kernel, name='pack', out_shape=[jax.ShapeDtypeStruct((8, L...  3.17 us
  transfers between devices with their start and end apart: 11, of which 7 were waited for; matrix products, arithmetic and copies ran while one was open for 0% of the time, Pallas kernels for 25%

profile of v3, /device:TPU:0, one launch (start us, length us, event | category | flops | bytes accessed | tf_op | source)
XLA Modules:
  0.0 55.8 jit_solution(12437201296940934600)
XLA Ops:
  0.6 3.0 %collective-permute-start.1 = (bf16[256,2,256]{2,1,0:T(2,128)(2,1)}, bf16[256,2,256]{2,1,0:T(2,128)(2,1)S(1)}, u32[]{:S(2)}, u32[]{:S(2)}) collective-permute-start(bf16[256,2,256]{2,1,0:T(2,128)(2,1)} %refs_0_.1), channel_id=1, source_target_pairs={{0,4},{8,0},{16,8},{24,16},{28,24},{20,28},{12,20},{4,12},{1,5},{9... | collective-permute-start | bytes 786440 | tf_op jit(solution)/shard_map/ppermute | solution.py:110
  3.8 4.1 %fetch.1 = (bf16[2048,2048]{1,0:T(8,128)(2,1)S(1)}, f32[8,128]{1,0:T(8,128)S(1)}) custom-call(bf16[8,256,2048]{2,1,0:T(8,128)(2,1)} %chol_any.1), custom_call_target="tpu_custom_call" | custom-call | bytes 8388608 | tf_op jit(solution)/shard_map/fetch/pallas_call | solution.py:155
  7.9 3.2 %pack.1 = (f32[8,128]{1,0:T(8,128)}, bf16[304,128]{1,0:T(8,128)(2,1)}, bf16[304,128]{1,0:T(8,128)(2,1)}, bf16[304,128]{1,0:T(8,128)(2,1)}, bf16[304,128]{1,0:T(8,128)(2,1)}) custom-call(bf16[256,2,256]{2,1,0:T(2,128)(2,1)} %refs_0_.1, bf16[256,256]{1,0:T(8,128)(2,1)} %body_any.1, f32[4,8]{1,0:T(4,128)} %bitcast.16, f32[2]{0:T(128)} %weights_any.1, ...), custom_call_target="tpu_custom_call" | custom-call | flops 100000000 | bytes 1000000 | tf_op jit(solution)/shard_map/pack/pallas_call | solution.py:260
  11.1 0.5 collective-permute-done.refs_1_
  11.6 1.5 %collective-permute-start.2 = (bf16[256,2,256]{2,1,0:T(2,128)(2,1)S(1)}, bf16[256,2,256]{2,1,0:T(2,128)(2,1)S(1)}, u32[]{:S(2)}, u32[]{:S(2)}) collective-permute-start(bf16[256,2,256]{2,1,0:T(2,128)(2,1)S(1)} %collective-permute-done.refs_1_), channel_id=1, source_target_pairs={{0,8},{8,16},{16,24},{24,28},{28,20},{20,12},{12,4},{4,0},{1,9},{9... | collective-permute-start | bytes 786440 | tf_op jit(solution)/shard_map/ppermute | solution.py:109
  13.2 0.5 collective-permute-start.3
  13.7 1.5 %collective-permute-start.5 = (bf16[304,128]{1,0:T(8,128)(2,1)}, bf16[304,128]{1,0:T(8,128)(2,1)S(1)}, u32[]{:S(2)}, u32[]{:S(2)}) collective-permute-start(bf16[304,128]{1,0:T(8,128)(2,1)} %get-tuple-element.41), channel_id=1, source_target_pairs={{0,2},{1,3},{2,0},{3,1},{4,6},{5,7},{6,4},{7,5},{8,10},{9,11},{10,... | collective-permute-start | bytes 233480 | tf_op jit(solution)/shard_map/ppermute | solution.py:286
  15.2 1.4 %collective-permute-start.6 = (bf16[304,128]{1,0:T(8,128)(2,1)}, bf16[304,128]{1,0:T(8,128)(2,1)S(1)}, u32[]{:S(2)}, u32[]{:S(2)}) collective-permute-start(bf16[304,128]{1,0:T(8,128)(2,1)} %get-tuple-element.42), channel_id=1, source_target_pairs={{0,3},{1,0},{2,1},{3,2},{4,7},{5,4},{6,5},{7,6},{8,11},{9,8},{10,9... | collective-permute-start | bytes 233480 | tf_op jit(solution)/shard_map/ppermute | solution.py:286
  16.6 2.4 %accumulate.3 = (f32[2,2048,256]{2,1,0:T(8,128)S(1)}, f32[8,128]{1,0:T(8,128)S(1)}) custom-call(bf16[2048,2048]{1,0:T(8,128)(2,1)S(1)} %get-tuple-element.31.blocks_ref.refs_0_, bf16[256,2,256]{2,1,0:T(2,128)(2,1)S(1)} %copy-done, bf16[256,2,256]{2,1,0:T(2,128)(2,1)S(1)} %collective-permute-done.refs_1_, ...), custom_call_target="tpu_custom_call" | custom-call | flops 1610612736 | bytes 3145728 | tf_op jit(solution)/shard_map/accumulate/pallas_call | solution.py:67
  19.3 1.0 %collective-permute-done.3.refs_1_ = bf16[256,2,256]{2,1,0:T(2,128)(2,1)S(1)} collective-permute-done((bf16[256,2,256]{2,1,0:T(2,128)(2,1)S(1)}, bf16[256,2,256]{2,1,0:T(2,128)(2,1)S(1)}, u32[]{:S(2)}, u32[]{:S(2)}) %collective-permute-start.3) | collective-permute-done | bytes 262176 | tf_op jit(solution)/shard_map/ppermute | solution.py:110
  20.4 1.6 %collective-permute-start.7 = (bf16[256,2,256]{2,1,0:T(2,128)(2,1)S(1)}, bf16[256,2,256]{2,1,0:T(2,128)(2,1)S(1)}, u32[]{:S(2)}, u32[]{:S(2)}) collective-permute-start(bf16[256,2,256]{2,1,0:T(2,128)(2,1)S(1)} %collective-permute-done.2.refs_0_), channel_id=1, source_target_pairs={{0,8},{8,16},{16,24},{24,28},{28,20},{20,12},{12,4},{4,0},{1,9},{9... | collective-permute-start | bytes 786440 | tf_op jit(solution)/shard_map/ppermute | solution.py:109
  21.9 0.4 collective-permute-start.8
  22.4 1.8 %accumulate.4 = (f32[2,2048,256]{2,1,0:T(8,128)S(1)}, f32[8,128]{1,0:T(8,128)S(1)}) custom-call(bf16[2048,2048]{1,0:T(8,128)(2,1)S(1)} %get-tuple-element.31.blocks_ref.refs_0_, bf16[256,2,256]{2,1,0:T(2,128)(2,1)S(1)} %collective-permute-done.2.refs_0_, bf16[256,2,256]{2,1,0:T(2,128)(2,1)S(1)} %collective-permute-done.3.refs_1_, ...), custom_call_target="tpu_custom_call" | custom-call | flops 1073741824 | bytes 2097152 | tf_op jit(solution)/shard_map/accumulate/pallas_call | solution.py:67
  24.2 4.4 %collective-permute-done.7.refs_0_ = bf16[256,2,256]{2,1,0:T(2,128)(2,1)S(1)} collective-permute-done((bf16[256,2,256]{2,1,0:T(2,128)(2,1)S(1)}, bf16[256,2,256]{2,1,0:T(2,128)(2,1)S(1)}, u32[]{:S(2)}, u32[]{:S(2)}) %collective-permute-start.7) | collective-permute-done | bytes 262176 | tf_op jit(solution)/shard_map/ppermute | solution.py:109
  28.5 1.2 %collective-permute-done.8.refs_1_ = bf16[256,2,256]{2,1,0:T(2,128)(2,1)S(1)} collective-permute-done((bf16[256,2,256]{2,1,0:T(2,128)(2,1)S(1)}, bf16[256,2,256]{2,1,0:T(2,128)(2,1)S(1)}, u32[]{:S(2)}, u32[]{:S(2)}) %collective-permute-start.8) | collective-permute-done | bytes 262176 | tf_op jit(solution)/shard_map/ppermute | solution.py:110
  30.0 1.6 %collective-permute-start.9 = (bf16[128,2,256]{2,1,0:T(2,128)(2,1)S(1)}, bf16[128,2,256]{2,1,0:T(2,128)(2,1)S(1)}, u32[]{:S(2)}, u32[]{:S(2)}) collective-permute-start(bf16[128,2,256]{2,1,0:T(2,128)(2,1)S(1)} %slice.6), channel_id=1, source_target_pairs={{0,8},{8,16},{16,24},{24,28},{28,20},{20,12},{12,4},{4,0},{1,9},{9... | collective-permute-start | bytes 393224 | tf_op jit(solution)/shard_map/ppermute | solution.py:124
  31.6 0.4 collective-permute-start.10
  32.0 2.3 %accumulate.5 = (f32[2,2048,256]{2,1,0:T(8,128)S(1)}, f32[8,128]{1,0:T(8,128)}) custom-call(bf16[2048,2048]{1,0:T(8,128)(2,1)S(1)} %get-tuple-element.31.blocks_ref.refs_0_, bf16[256,2,256]{2,1,0:T(2,128)(2,1)S(1)} %collective-permute-done.7.refs_0_, bf16[256,2,256]{2,1,0:T(2,128)(2,1)S(1)} %collective-permute-done.8.refs_1_, ...), custom_call_target="tpu_custom_call" | custom-call | flops 1073741824 | bytes 2097152 | tf_op jit(solution)/shard_map/accumulate/pallas_call | solution.py:67
  34.3 0.6 %collective-permute-done.9.refs_6_ = bf16[128,2,256]{2,1,0:T(2,128)(2,1)S(1)} collective-permute-done((bf16[128,2,256]{2,1,0:T(2,128)(2,1)S(1)}, bf16[128,2,256]{2,1,0:T(2,128)(2,1)S(1)}, u32[]{:S(2)}, u32[]{:S(2)}) %collective-permute-start.9) | collective-permute-done | bytes 131104 | tf_op jit(solution)/shard_map/ppermute | solution.py:124
  35.0 1.6 %collective-permute-done.10.refs_7_ = bf16[128,2,256]{2,1,0:T(2,128)(2,1)S(1)} collective-permute-done((bf16[128,2,256]{2,1,0:T(2,128)(2,1)S(1)}, bf16[128,2,256]{2,1,0:T(2,128)(2,1)S(1)}, u32[]{:S(2)}, u32[]{:S(2)}) %collective-permute-start.10) | collective-permute-done | bytes 131104 | tf_op jit(solution)/shard_map/ppermute | solution.py:124
  36.6 1.8 %measure.1 = f32[8,128]{1,0:T(8,128)S(1)} custom-call(bf16[2048,2048]{1,0:T(8,128)(2,1)S(1)} %get-tuple-element.31.blocks_ref.refs_0_, f32[8,128]{1,0:T(8,128)S(1)} %copy-done.2, bf16[304,128]{1,0:T(8,128)(2,1)S(1)} %copy-done.1, bf16[304,128]{1,0:T(8,128)(2,1)S(1)} %collective-permute-done.4.refs_3_.refs_1_, ...), custom_call_target="tpu_custom_call" | custom-call | flops 536870912 | bytes 1048576 | tf_op jit(solution)/shard_map/measure/pallas_call | solution.py:375
  38.3 9.8 %all_to_all.22 = f32[8,1,128]{2,1,0:T(1,128)S(1)} all-to-all(f32[8,1,128]{2,1,0:T(1,128)S(1)} %bitcast.12), channel_id=1, replica_groups=mesh['chol'=8,'walk'=4] {'chol'}, dimensions={0} | all-to-all | bytes 8192 | tf_op jit(solution)/shard_map/all_to_all | solution.py:473
  48.1 6.3 %all_to_all.23 = f32[4,1,128]{2,1,0:T(1,128)S(1)} all-to-all(f32[4,1,128]{2,1,0:T(1,128)S(1)} %bitcast.15), channel_id=1, replica_groups=mesh['chol'=8,'walk'=4] {'walk'}, dimensions={0} | all-to-all | bytes 4096 | tf_op jit(solution)/shard_map/all_to_all | solution.py:475
  54.4 1.4 %finish.1 = (f32[1,4]{1,0:T(1,128)}, f32[1,4]{1,0:T(1,128)}, f32[128,128]{1,0:T(8,128)}) custom-call(f32[4,128]{1,0:T(4,128)S(1)} %bitcast.14, s32[4]{0:T(128)S(1)} %copy-done.3, bf16[304,128]{1,0:T(8,128)(2,1)S(1)} %copy-done.1, bf16[304,128]{1,0:T(8,128)(2,1)S(1)} %collective-permute-done.4.refs_3_.refs_1_, ...), custom_call_target="tpu_custom_call" | custom-call | flops 1000000 | bytes 600000 | tf_op jit(solution)/shard_map/finish/pallas_call | solution.py:444
  (18 shorter events, 0.6 us)
Async XLA Ops:
  0.6 16.0 %copy-start = (bf16[256,2,256]{2,1,0:T(2,128)(2,1)S(1)}, bf16[256,2,256]{2,1,0:T(2,128)(2,1)}, u32[]{:S(2)}) copy-start(bf16[256,2,256]{2,1,0:T(2,128)(2,1)} %refs_0_.1) | copy-start | bytes 786436
  0.6 10.5 %collective-permute-start.1 = (bf16[256,2,256]{2,1,0:T(2,128)(2,1)}, bf16[256,2,256]{2,1,0:T(2,128)(2,1)S(1)}, u32[]{:S(2)}, u32[]{:S(2)}) collective-permute-start(bf16[256,2,256]{2,1,0:T(2,128)(2,1)} %refs_0_.1), channel_id=1, source_target_pairs={{0,4},{8,0},{16,8},{24,16},{28,24},{20,28},{12,20},{4,12},{1,5},{9... | collective-permute-start | bytes 786440 | tf_op jit(solution)/shard_map/ppermute | solution.py:110
  3.7 8.0 %collective-permute-start = (bf16[256,2,256]{2,1,0:T(2,128)(2,1)}, bf16[256,2,256]{2,1,0:T(2,128)(2,1)S(1)}, u32[]{:S(2)}, u32[]{:S(2)}) collective-permute-start(bf16[256,2,256]{2,1,0:T(2,128)(2,1)} %refs_0_.1), channel_id=1, source_target_pairs={{0,8},{8,16},{16,24},{24,28},{28,20},{20,12},{12,4},{4,0},{1,9},{9... | collective-permute-start | bytes 786440 | tf_op jit(solution)/shard_map/ppermute | solution.py:109
  11.6 7.7 %collective-permute-start.2 = (bf16[256,2,256]{2,1,0:T(2,128)(2,1)S(1)}, bf16[256,2,256]{2,1,0:T(2,128)(2,1)S(1)}, u32[]{:S(2)}, u32[]{:S(2)}) collective-permute-start(bf16[256,2,256]{2,1,0:T(2,128)(2,1)S(1)} %collective-permute-done.refs_1_), channel_id=1, source_target_pairs={{0,8},{8,16},{16,24},{24,28},{28,20},{20,12},{12,4},{4,0},{1,9},{9... | collective-permute-start | bytes 786440 | tf_op jit(solution)/shard_map/ppermute | solution.py:109
  13.2 7.2 %collective-permute-start.3 = (bf16[256,2,256]{2,1,0:T(2,128)(2,1)S(1)}, bf16[256,2,256]{2,1,0:T(2,128)(2,1)S(1)}, u32[]{:S(2)}, u32[]{:S(2)}) collective-permute-start(bf16[256,2,256]{2,1,0:T(2,128)(2,1)S(1)} %collective-permute-done.1.refs_2_), channel_id=1, source_target_pairs={{0,4},{8,0},{16,8},{24,16},{28,24},{20,28},{12,20},{4,12},{1,5},{9... | collective-permute-start | bytes 786440 | tf_op jit(solution)/shard_map/ppermute | solution.py:110
  13.7 5.4 %collective-permute-start.4 = (bf16[304,128]{1,0:T(8,128)(2,1)}, bf16[304,128]{1,0:T(8,128)(2,1)S(1)}, u32[]{:S(2)}, u32[]{:S(2)}) collective-permute-start(bf16[304,128]{1,0:T(8,128)(2,1)} %get-tuple-element.40), channel_id=1, source_target_pairs={{0,1},{1,2},{2,3},{3,0},{4,5},{5,6},{6,7},{7,4},{8,9},{9,10},{10,1... | collective-permute-start | bytes 233480 | tf_op jit(solution)/shard_map/ppermute | solution.py:286
  13.7 5.4 %collective-permute-start.5 = (bf16[304,128]{1,0:T(8,128)(2,1)}, bf16[304,128]{1,0:T(8,128)(2,1)S(1)}, u32[]{:S(2)}, u32[]{:S(2)}) collective-permute-start(bf16[304,128]{1,0:T(8,128)(2,1)} %get-tuple-element.41), channel_id=1, source_target_pairs={{0,2},{1,3},{2,0},{3,1},{4,6},{5,7},{6,4},{7,5},{8,10},{9,11},{10,... | collective-permute-start | bytes 233480 | tf_op jit(solution)/shard_map/ppermute | solution.py:286
  15.2 4.1 %collective-permute-start.6 = (bf16[304,128]{1,0:T(8,128)(2,1)}, bf16[304,128]{1,0:T(8,128)(2,1)S(1)}, u32[]{:S(2)}, u32[]{:S(2)}) collective-permute-start(bf16[304,128]{1,0:T(8,128)(2,1)} %get-tuple-element.42), channel_id=1, source_target_pairs={{0,3},{1,0},{2,1},{3,2},{4,7},{5,4},{6,5},{7,6},{8,11},{9,8},{10,9... | collective-permute-start | bytes 233480 | tf_op jit(solution)/shard_map/ppermute | solution.py:286
  20.4 8.2 %collective-permute-start.7 = (bf16[256,2,256]{2,1,0:T(2,128)(2,1)S(1)}, bf16[256,2,256]{2,1,0:T(2,128)(2,1)S(1)}, u32[]{:S(2)}, u32[]{:S(2)}) collective-permute-start(bf16[256,2,256]{2,1,0:T(2,128)(2,1)S(1)} %collective-permute-done.2.refs_0_), channel_id=1, source_target_pairs={{0,8},{8,16},{16,24},{24,28},{28,20},{20,12},{12,4},{4,0},{1,9},{9... | collective-permute-start | bytes 786440 | tf_op jit(solution)/shard_map/ppermute | solution.py:109
  21.9 7.8 %collective-permute-start.8 = (bf16[256,2,256]{2,1,0:T(2,128)(2,1)S(1)}, bf16[256,2,256]{2,1,0:T(2,128)(2,1)S(1)}, u32[]{:S(2)}, u32[]{:S(2)}) collective-permute-start(bf16[256,2,256]{2,1,0:T(2,128)(2,1)S(1)} %collective-permute-done.3.refs_1_), channel_id=1, source_target_pairs={{0,4},{8,0},{16,8},{24,16},{28,24},{20,28},{12,20},{4,12},{1,5},{9... | collective-permute-start | bytes 786440 | tf_op jit(solution)/shard_map/ppermute | solution.py:110
  30.0 5.0 %collective-permute-start.9 = (bf16[128,2,256]{2,1,0:T(2,128)(2,1)S(1)}, bf16[128,2,256]{2,1,0:T(2,128)(2,1)S(1)}, u32[]{:S(2)}, u32[]{:S(2)}) collective-permute-start(bf16[128,2,256]{2,1,0:T(2,128)(2,1)S(1)} %slice.6), channel_id=1, source_target_pairs={{0,8},{8,16},{16,24},{24,28},{28,20},{20,12},{12,4},{4,0},{1,9},{9... | collective-permute-start | bytes 393224 | tf_op jit(solution)/shard_map/ppermute | solution.py:124
  31.6 5.0 %collective-permute-start.10 = (bf16[128,2,256]{2,1,0:T(2,128)(2,1)S(1)}, bf16[128,2,256]{2,1,0:T(2,128)(2,1)S(1)}, u32[]{:S(2)}, u32[]{:S(2)}) collective-permute-start(bf16[128,2,256]{2,1,0:T(2,128)(2,1)S(1)} %slice.7), channel_id=1, source_target_pairs={{0,4},{8,0},{16,8},{24,16},{28,24},{20,28},{12,20},{4,12},{1,5},{9... | collective-permute-start | bytes 393224 | tf_op jit(solution)/shard_map/ppermute | solution.py:124
  32.0 4.5 %copy-start.1 = (bf16[304,128]{1,0:T(8,128)(2,1)S(1)}, bf16[304,128]{1,0:T(8,128)(2,1)}, u32[]{:S(2)}) copy-start(bf16[304,128]{1,0:T(8,128)(2,1)} %get-tuple-element.35.refs_2_.refs_0_) | copy-start | bytes 233476
  32.0 4.5 %copy-start.2 = (f32[8,128]{1,0:T(8,128)S(1)}, f32[8,128]{1,0:T(8,128)}, u32[]{:S(2)}) copy-start(f32[8,128]{1,0:T(8,128)} %get-tuple-element.34.refs_1_) | copy-start | bytes 12292
  36.6 17.8 %copy-start.3 = (s32[4]{0:T(128)S(1)}, s32[4]{0:T(128)}, u32[]{:S(2)}) copy-start(s32[4]{0:T(128)} %counts_ref.1) | copy-start | bytes 52

commit v4 on v3

--- a/solution.py
+++ b/solution.py
@@ -12,7 +12,7 @@
 LANES = 128
 VMEM_LIMIT = 16 * 1024 * 1024
 PACK_LIMIT = 54 * 1024 * 1024
-FETCH_LIMIT = 42 * 1024 * 1024
+ACCUMULATE_LIMIT = 43 * 1024 * 1024
 RING_LIMIT = 16
 
 
@@ -47,50 +47,86 @@
     return pl.multiple_of(owner * rows, rows)
 
 
-def accumulate(blocks, first, parts, total, mark):
-    size, width = blocks.shape
-    rows, walkers, orbitals = parts[0].shape
+def accumulate(cholesky_rot, shifts, parts, total, mark, ahead):
+    vectors, orbitals, _ = cholesky_rot.shape
+    rows, walkers, _ = parts[0].shape
     count = len(parts)
-    fresh = total is None
-    arrays = list(parts) + [mark] + ([] if fresh else [total])
-
-    def kernel(blocks_ref, *refs):
-        shards = refs[:count]
-        total_ref, mark_ref = refs[len(arrays) :]
-        mark_ref[...] = jnp.zeros_like(mark_ref)
-        lhs = blocks_ref[:, first * rows : (first + count) * rows]
-        for b in range(walkers):
-            rhs = jnp.concatenate([x[:, b, :] for x in shards], axis=0)
-            value = jnp.dot(lhs, rhs, preferred_element_type=jnp.float32)
-            total_ref[b] = value if fresh else refs[count + 1][b] + value
+    size = vectors * orbitals
+    chunks = vectors // 2 if vectors % 2 == 0 else vectors
+    each = vectors // chunks
+    arrays = list(parts) + ([] if mark is None else [mark]) + ([] if total is None else [total])
+    shapes = [
+        jax.ShapeDtypeStruct((walkers, size, orbitals), jnp.float32),
+        jax.ShapeDtypeStruct((8, LANES), jnp.float32),
+    ]
+    if ahead is not None:
+        shapes.append(jax.ShapeDtypeStruct((size, rows), cholesky_rot.dtype))
+
+    def kernel(chol_any, *refs):
+        ins = refs[: len(arrays)]
+        outs = refs[len(arrays) : len(arrays) + len(shapes)]
+        blocks_scr, sems = refs[len(arrays) + len(shapes) :]
+
+        def columns(shift, g, target):
+            return chol_any.at[g, :, pl.ds(column_start(shift, rows), rows)], target
+
+        copies = []
+        for g in range(vectors):
+            for n, shift in enumerate(shifts):
+                copies.append(
+                    pltpu.make_async_copy(
+                        *columns(
+                            shift, g, blocks_scr.at[pl.ds(g * orbitals, orbitals), pl.ds(n * rows, rows)]
+                        ),
+                        sems.at[g * (count + 1) + n],
+                    )
+                )
+        for copy in copies:
+            copy.start()
+        later = []
+        if ahead is not None:
+            for g in range(vectors):
+                later.append(
+                    pltpu.make_async_copy(
+                        *columns(ahead, g, outs[2].at[pl.ds(g * orbitals, orbitals), :]),
+                        sems.at[g * (count + 1) + count],
+                    )
+                )
+            for copy in later:
+                copy.start()
+        outs[1][...] = jnp.zeros_like(outs[1])
+        rhs = [jnp.concatenate([x[:, b, :] for x in ins[:count]], axis=0) for b in range(walkers)]
+        for q in range(chunks):
+            for copy in copies[q * each * count : (q + 1) * each * count]:
+                copy.wait()
+            at = slice(q * each * orbitals, (q + 1) * each * orbitals)
+            for b in range(walkers):
+                value = jnp.dot(blocks_scr[at, :], rhs[b], preferred_element_type=jnp.float32)
+                outs[0][b, at, :] = value if total is None else ins[-1][b, at, :] + value
+        for copy in later:
+            copy.wait()
 
     return pl.pallas_call(
         kernel,
         name="accumulate",
-        out_shape=[
-            jax.ShapeDtypeStruct((walkers, size, orbitals), jnp.float32),
-            jax.ShapeDtypeStruct((8, LANES), jnp.float32),
+        out_shape=shapes,
+        in_specs=[pl.BlockSpec(memory_space=pl.ANY)] + [vmem()] * len(arrays),
+        out_specs=[vmem()] * len(shapes),
+        scratch_shapes=[
+            pltpu.VMEM((size, count * rows), cholesky_rot.dtype),
+            pltpu.SemaphoreType.DMA((vectors * (count + 1),)),
         ],
-        in_specs=[vmem()] * (1 + len(arrays)),
-        out_specs=[vmem()] * 2,
-        compiler_params=params(),
+        compiler_params=params(ACCUMULATE_LIMIT),
         cost_estimate=pl.CostEstimate(
             flops=2 * count * size * rows * walkers * orbitals,
             bytes_accessed=2 * count * size * rows,
             transcendentals=0,
         ),
-    )(blocks, *arrays)
+    )(cholesky_rot, *arrays)
 
 
 def tie(*arrays):
     return lax.optimization_barrier(arrays)
-
-
-def arrival_shifts(size):
-    shifts = [0]
-    for step in range(1, size // 2):
-        shifts += [-step, step]
-    return shifts + [size // 2]
 
 
 def ring(own, cholesky_rot, onebody, packed):
@@ -99,72 +135,30 @@
     order = ring_order(size)
     ahead = [(order[q], order[(q + 1) % size]) for q in range(size)]
     back = [(order[q], order[(q - 1) % size]) for q in range(size)]
-    right = left = own
-    parts = [own]
-    first = 0
-    total = None
     steps = size // 2
-    blocks, mark = fetch(cholesky_rot, arrival_shifts(size))
-    for step in range(1, steps):
-        next_right = lax.ppermute(right, "chol", ahead)
-        next_left = lax.ppermute(left, "chol", back)
-        if step > 1:
-            total, mark = accumulate(blocks, first, parts, total, mark)
-            first += len(parts)
-            parts = []
-        if step == 1:
-            others = [shifted(packed[d], d) for d in range(1, len(packed))]
-        if step == 1:
-            right, left, mark, onebody = tie(next_right, next_left, mark, onebody)
-        elif step == 2:
-            right, left, mark, *others = tie(next_right, next_left, mark, *others)
-        else:
-            right, left, mark = tie(next_right, next_left, mark)
-        parts = parts + [right, left]
+    right, left = lax.ppermute(own, "chol", ahead), lax.ppermute(own, "chol", back)
+    right, onebody = tie(right, onebody)
+    left, onebody = tie(left, onebody)
+    next_right, next_left = lax.ppermute(right, "chol", ahead), lax.ppermute(left, "chol", back)
+    total, mark = accumulate(cholesky_rot, [0, -1, 1], [own, right, left], None, None, None)
+    right, mark = tie(next_right, mark)
+    left, mark = tie(next_left, mark)
+    others = packed[1:]
+    for step in range(3, steps):
+        next_right, next_left = lax.ppermute(right, "chol", ahead), lax.ppermute(left, "chol", back)
+        if step == 3:
+            *others, mark = tie(*others, mark)
+            others = [shifted(x, d + 1) for d, x in enumerate(others)]
+        total, mark = accumulate(cholesky_rot, [1 - step, step - 1], [right, left], total, mark, None)
+        right, mark = tie(next_right, mark)
+        left, mark, *others = tie(next_left, mark, *others)
     last = [lax.ppermute(right[: rows // 2], "chol", ahead), lax.ppermute(left[rows // 2 :], "chol", back)]
-    total, _ = accumulate(blocks, first, parts, total, mark)
-    return blocks, onebody, total, last, [packed[0]] + others
+    total, _, block = accumulate(cholesky_rot, [1 - steps, steps - 1], [right, left], total, mark, steps)
+    return block, onebody, total, last, [packed[0]] + others
 
 
 def table_height(vectors):
     return -(-(vectors + 2) // 16) * 16
-
-
-def fetch(cholesky_rot, shifts):
-    vectors, orbitals, basis = cholesky_rot.shape
-    rows = basis // len(shifts)
-
-    def kernel(chol_any, blocks_ref, mark_ref, sems):
-        mark_ref[...] = jnp.zeros_like(mark_ref)
-        copies = []
-        for n, shift in enumerate(shifts):
-            start = 0 if shift is None else column_start(shift, rows)
-            for g in range(vectors):
-                copies.append(
-                    pltpu.make_async_copy(
-                        chol_any.at[g, :, pl.ds(start, rows)],
-                        blocks_ref.at[pl.ds(g * orbitals, orbitals), pl.ds(n * rows, rows)],
-                        sems.at[n, g],
-                    )
-                )
-        for copy in copies:
-            copy.start()
-        for copy in copies:
-            copy.wait()
-
-    return pl.pallas_call(
-        kernel,
-        name="fetch",
-        out_shape=[
-            jax.ShapeDtypeStruct((vectors * orbitals, basis), cholesky_rot.dtype),
-            jax.ShapeDtypeStruct((8, LANES), jnp.float32),
-        ],
-        in_specs=[pl.BlockSpec(memory_space=pl.ANY)],
-        out_specs=[vmem()] * 2,
-        scratch_shapes=[pltpu.SemaphoreType.DMA((len(shifts), vectors))],
-        compiler_params=params(FETCH_LIMIT),
-        cost_estimate=pl.CostEstimate(flops=0, bytes_accessed=2 * cholesky_rot.size, transcendentals=0),
-    )(cholesky_rot)
 
 
 def pack(own, one_body, fields, weights, sources, owners):
@@ -301,11 +295,11 @@
     return total
 
 
-def measure(blocks, first, total, last, packs, onebody, vectors, slots):
+def measure(block, total, last, packs, onebody, vectors, slots):
     _, walkers, orbitals = last[0].shape
     depth = sum(x.shape[0] for x in last)
     walk_size = len(packs)
-    targets = lax.axis_size("chol")
+    targets = walk_size * lax.axis_size("chol")
     whole = total is None
     quads = orbitals // LANES
 
@@ -313,7 +307,7 @@
         return jnp.sum(x.reshape(-1, 8, LANES), axis=0)
 
     def kernel(*refs):
-        blocks_ref, onebody_ref = refs[:2]
+        block_ref, onebody_ref = refs[:2]
         pack_refs = refs[2 : 2 + walk_size]
         last_refs = refs[2 + walk_size : 2 + walk_size + len(last)]
         out_ref, tensor_scr = refs[-2:]
@@ -336,9 +330,7 @@
         squares = [jnp.zeros((1, 1), jnp.float32) for _ in range(walkers)]
         drive = jnp.zeros((1, LANES), jnp.float32)
         for b in range(walkers):
-            value = jnp.dot(
-                blocks_ref[:, first * depth : (first + 1) * depth], rhs[b], preferred_element_type=jnp.float32
-            )
+            value = jnp.dot(block_ref[...], rhs[b], preferred_element_type=jnp.float32)
             tensor_scr[b] = value if whole else refs[2 + walk_size + len(last)][b] + value
         for g in range(vectors):
             top = g * orbitals
@@ -387,21 +379,7 @@
             bytes_accessed=2 * vectors * orbitals * depth,
             transcendentals=0,
         ),
-    )(blocks, onebody, *packs, *arrays)
-
-
-def add_up(stats, targets):
-    def kernel(stats_ref, out_ref):
-        out_ref[...] = jnp.broadcast_to(jnp.sum(stats_ref[...], axis=0, keepdims=True), out_ref.shape)
-
-    return pl.pallas_call(
-        kernel,
-        name="add_up",
-        out_shape=jax.ShapeDtypeStruct((targets, LANES), jnp.float32),
-        in_specs=[vmem()],
-        out_specs=vmem(),
-        compiler_params=params(),
-    )(stats)
+    )(block, onebody, *packs, *arrays)
 
 
 def finish(stats, packs, counts, vectors, slots, walkers):
@@ -462,17 +440,14 @@
     vectors, slots = fields.shape
     walkers = green_rows.shape[1]
     onebody, *packed = pack(green_rows, one_body, fields, weights, sources, owners)
-    if chol_size > RING_LIMIT or chol_size % 2 or chol_size < 6:
-        blocks, first = fetch(cholesky_rot, [None])[0], 0
+    if chol_size > RING_LIMIT or chol_size % 2 or chol_size < 8:
+        block = cholesky_rot.reshape(-1, cholesky_rot.shape[2])
         packs = [packed[0]] + [shifted(packed[d], d) for d in range(1, walk_size)]
         total, last = None, [lax.all_gather(green_rows, "chol", axis=0, tiled=True)]
     else:
-        blocks, onebody, total, last, packs = ring(green_rows, cholesky_rot, onebody, packed)
-        first = chol_size - 1
-    stats = measure(blocks, first, total, last, packs, onebody, vectors, slots)
-    stats = lax.all_to_all(stats, "chol", split_axis=0, concat_axis=0, tiled=True)
-    stats = add_up(stats, walk_size)
-    stats = lax.all_to_all(stats, "walk", split_axis=0, concat_axis=0, tiled=True)
+        block, onebody, total, last, packs = ring(green_rows, cholesky_rot, onebody, packed)
+    stats = measure(block, total, last, packs, onebody, vectors, slots)
+    stats = lax.all_to_all(stats, ("chol", "walk"), split_axis=0, concat_axis=0, tiled=True)
     energies, new_weights, density = finish(stats, packs, counts, vectors, slots, walkers)
     return energies.reshape(slots), new_weights.reshape(slots), density.reshape(1, density.size)
 

time: 56 us -> 48.6 us (0.87)
  waiting for transfers between devices: 9.6 us -> 3.85 us
  blocking collectives: 16.1 us -> 11.8 us
  Pallas kernels: 17 us -> 18.1 us
  local copies, waits for them, and re-layouts: 0.2 us -> 1.16 us
    all_to_all x2 -> x1, blocking collectives: 16.1 us -> 11.8 us  [per_device(): lax.all_to_all(stats, ('chol', 'walk'), split_axis=0, concat_axis=0, tile...]
    ppermute x6, waiting for transfers between devices: 7.15 us -> 3.26 us  [the longest x1 3.25 us: ring(): lax.ppermute(own, 'chol', ahead)]
    ppermute x1, waiting for transfers between devices: 1.58 us -> 0.01 us  [ring(): lax.ppermute(left[rows // 2:], 'chol', back)]
    ppermute x1, starting transfers between devices: 0.45 us -> 1.57 us  [ring(): lax.ppermute(left[rows // 2:], 'chol', back)]
    pallas_call x5 -> x3, Pallas kernels: 10.7 us -> 11.6 us  [accumulate(): pl.pallas_call(kernel, name='accumulate', out_shape=shapes, in_specs=[pl....]
    unnamed x8 -> x14, local copies, waits for them, and re-layouts: 0.02 us -> 0.97 us
    ppermute x1, starting transfers between devices: 1.63 us -> 0.74 us  [ring(): lax.ppermute(right[:rows // 2], 'chol', ahead)]
  transfers between devices with their start and end apart: 11 -> 11, of which waited for: 7 -> 2; matrix products, arithmetic and copies ran while one was open for 0% -> 0% of each run, Pallas kernels for 25% -> 31%
where the time goes in v4:
time: 48.6 us; the launch traced here: 48.4 us
  Pallas kernels  18.1 us (37%)
  starting transfers between devices  12.7 us (26%)
  blocking collectives  11.8 us (24%)
  waiting for transfers between devices  3.85 us (8%)
  local copies, waits for them, and re-layouts  1.16 us (2%)
  between operations  0.76 us (2%)
    all_to_all x1, blocking collectives, per_device(): lax.all_to_all(stats, ('chol', 'walk'), split_axis=0, concat_axis=0, tile...  11.8 us
    pallas_call x3, Pallas kernels, accumulate(): pl.pallas_call(kernel, name='accumulate', out_shape=shapes, in_specs=[pl....  11.6 us
    ppermute x2, starting transfers between devices, ring(): lax.ppermute(right, 'chol', ahead)  3.64 us
    ppermute x1, waiting for transfers between devices, ring(): lax.ppermute(own, 'chol', ahead)  3.25 us
    pallas_call x1, Pallas kernels, pack(): pl.pallas_call(kernel, name='pack', out_shape=[jax.ShapeDtypeStruct((8, L...  3.19 us
    ppermute x3, starting transfers between devices, shifted(): return lax.ppermute(x, 'walk', [(q, (q + d) % size) for q in range(size)])  3.17 us
    ppermute x1, starting transfers between devices, ring(): lax.ppermute(own, 'chol', ahead)  3.08 us
    pallas_call x1, Pallas kernels, measure(): pl.pallas_call(kernel, name='measure', out_shape=jax.ShapeDtypeStruct((ta...  1.9 us
  transfers between devices with their start and end apart: 11, of which 2 were waited for; matrix products, arithmetic and copies ran while one was open for 0% of the time, Pallas kernels for 31%

profile of v4, /device:TPU:0, one launch (start us, length us, event | category | flops | bytes accessed | tf_op | source)
XLA Modules:
  0.0 48.4 jit_solution(9879902099086603474)
XLA Ops:
  0.6 3.1 %collective-permute-start = (bf16[256,2,256]{2,1,0:T(2,128)(2,1)}, bf16[256,2,256]{2,1,0:T(2,128)(2,1)S(1)}, u32[]{:S(2)}, u32[]{:S(2)}) collective-permute-start(bf16[256,2,256]{2,1,0:T(2,128)(2,1)} %refs_0_.1), channel_id=1, source_target_pairs={{0,8},{8,16},{16,24},{24,28},{28,20},{20,12},{12,4},{4,0},{1,9},{9... | collective-permute-start | bytes 786440 | tf_op jit(solution)/shard_map/ppermute | solution.py:139
  3.7 0.0 collective-permute-start.2
  3.7 3.2 %pack.1 = (f32[8,128]{1,0:T(8,128)}, bf16[304,128]{1,0:T(8,128)(2,1)}, bf16[304,128]{1,0:T(8,128)(2,1)}, bf16[304,128]{1,0:T(8,128)(2,1)}, bf16[304,128]{1,0:T(8,128)(2,1)}) custom-call(bf16[256,2,256]{2,1,0:T(2,128)(2,1)} %refs_0_.1, bf16[256,256]{1,0:T(8,128)(2,1)} %body_any.1, f32[4,8]{1,0:T(4,128)} %bitcast.10, f32[2]{0:T(128)} %weights_any.1, ...), custom_call_target="tpu_custom_call" | custom-call | flops 100000000 | bytes 1000000 | tf_op jit(solution)/shard_map/pack/pallas_call | solution.py:254
  6.9 3.2 %collective-permute-done.refs_1_ = bf16[256,2,256]{2,1,0:T(2,128)(2,1)S(1)} collective-permute-done((bf16[256,2,256]{2,1,0:T(2,128)(2,1)}, bf16[256,2,256]{2,1,0:T(2,128)(2,1)S(1)}, u32[]{:S(2)}, u32[]{:S(2)}) %collective-permute-start) | collective-permute-done | bytes 262176 | tf_op jit(solution)/shard_map/ppermute | solution.py:139
  10.2 1.8 %collective-permute-start.1 = (bf16[256,2,256]{2,1,0:T(2,128)(2,1)S(1)}, bf16[256,2,256]{2,1,0:T(2,128)(2,1)S(1)}, u32[]{:S(2)}, u32[]{:S(2)}) collective-permute-start(bf16[256,2,256]{2,1,0:T(2,128)(2,1)S(1)} %collective-permute-done.refs_1_), channel_id=1, source_target_pairs={{0,8},{8,16},{16,24},{24,28},{28,20},{20,12},{12,4},{4,0},{1,9},{9... | collective-permute-start | bytes 786440 | tf_op jit(solution)/shard_map/ppermute | solution.py:142
  12.0 0.0 collective-permute-done.2.refs_2_
  12.0 0.2 collective-permute-start.4
  12.2 0.9 %copy-done = bf16[256,2,256]{2,1,0:T(2,128)(2,1)S(1)} copy-done((bf16[256,2,256]{2,1,0:T(2,128)(2,1)S(1)}, bf16[256,2,256]{2,1,0:T(2,128)(2,1)}, u32[]{:S(2)}) %copy-start) | copy-done | bytes 262168
  13.2 4.5 %accumulate.3 = (f32[2,2048,256]{2,1,0:T(8,128)S(1)}, f32[8,128]{1,0:T(8,128)S(1)}) custom-call(bf16[8,256,2048]{2,1,0:T(8,128)(2,1)} %chol_any.5, bf16[256,2,256]{2,1,0:T(2,128)(2,1)S(1)} %copy-done, bf16[256,2,256]{2,1,0:T(2,128)(2,1)S(1)} %collective-permute-done.refs_1_, bf16[256,2,256]{2,1,0:T(2,128)(2,1)S(1)} %collective-permute-done.2.refs_2_), custom_call_target="tpu_custom_call" | custom-call | flops 1610612736 | bytes 3145728 | tf_op jit(solution)/shard_map/accumulate/pallas_call | solution.py:109
  17.7 1.8 %collective-permute-start.3 = (bf16[256,2,256]{2,1,0:T(2,128)(2,1)S(1)}, bf16[256,2,256]{2,1,0:T(2,128)(2,1)S(1)}, u32[]{:S(2)}, u32[]{:S(2)}) collective-permute-start(bf16[256,2,256]{2,1,0:T(2,128)(2,1)S(1)} %collective-permute-done.1.refs_0_), channel_id=1, source_target_pairs={{0,8},{8,16},{16,24},{24,28},{28,20},{20,12},{12,4},{4,0},{1,9},{9... | collective-permute-start | bytes 786440 | tf_op jit(solution)/shard_map/ppermute | solution.py:148
  19.5 0.2 collective-permute-start.5
  19.8 1.8 %collective-permute-start.7 = (bf16[304,128]{1,0:T(8,128)(2,1)S(1)}, bf16[304,128]{1,0:T(8,128)(2,1)S(1)}, u32[]{:S(2)}, u32[]{:S(2)}) collective-permute-start(bf16[304,128]{1,0:T(8,128)(2,1)S(1)} %copy-done.5), channel_id=1, source_target_pairs={{0,2},{1,3},{2,0},{3,1},{4,6},{5,7},{6,4},{7,5},{8,10},{9,11},{10,... | collective-permute-start | bytes 233480 | tf_op jit(solution)/shard_map/ppermute | solution.py:280
  21.6 1.4 %collective-permute-start.8 = (bf16[304,128]{1,0:T(8,128)(2,1)S(1)}, bf16[304,128]{1,0:T(8,128)(2,1)S(1)}, u32[]{:S(2)}, u32[]{:S(2)}) collective-permute-start(bf16[304,128]{1,0:T(8,128)(2,1)S(1)} %copy-done.4), channel_id=1, source_target_pairs={{0,3},{1,0},{2,1},{3,2},{4,7},{5,4},{6,5},{7,6},{8,11},{9,8},{10,9... | collective-permute-start | bytes 233480 | tf_op jit(solution)/shard_map/ppermute | solution.py:280
  22.9 3.3 %accumulate.4 = (f32[2,2048,256]{2,1,0:T(8,128)S(1)}, f32[8,128]{1,0:T(8,128)S(1)}) custom-call(bf16[8,256,2048]{2,1,0:T(8,128)(2,1)} %chol_any.5, bf16[256,2,256]{2,1,0:T(2,128)(2,1)S(1)} %collective-permute-done.1.refs_0_, bf16[256,2,256]{2,1,0:T(2,128)(2,1)S(1)} %collective-permute-done.4.refs_1_, f32[8,128]{1,0:T(8,128)S(1)} %get-tuple-element.48.refs_2_, ...), custom_call_target="tpu_custom_call" | custom-call | flops 1073741824 | bytes 2097152 | tf_op jit(solution)/shard_map/accumulate/pallas_call | solution.py:109
  26.3 0.1 slice.7
  26.4 1.6 %collective-permute-start.10 = (bf16[128,2,256]{2,1,0:T(2,128)(2,1)S(1)}, bf16[128,2,256]{2,1,0:T(2,128)(2,1)S(1)}, u32[]{:S(2)}, u32[]{:S(2)}) collective-permute-start(bf16[128,2,256]{2,1,0:T(2,128)(2,1)S(1)} %slice.7), channel_id=1, source_target_pairs={{0,4},{8,0},{16,8},{24,16},{28,24},{20,28},{12,20},{4,12},{1,5},{9... | collective-permute-start | bytes 393224 | tf_op jit(solution)/shard_map/ppermute | solution.py:155
  27.9 0.1 slice.6
  28.0 0.7 %collective-permute-start.9 = (bf16[128,2,256]{2,1,0:T(2,128)(2,1)S(1)}, bf16[128,2,256]{2,1,0:T(2,128)(2,1)S(1)}, u32[]{:S(2)}, u32[]{:S(2)}) collective-permute-start(bf16[128,2,256]{2,1,0:T(2,128)(2,1)S(1)} %slice.6), channel_id=1, source_target_pairs={{0,8},{8,16},{16,24},{24,28},{28,20},{20,12},{12,4},{4,0},{1,9},{9... | collective-permute-start | bytes 393224 | tf_op jit(solution)/shard_map/ppermute | solution.py:155
  28.8 3.9 %accumulate.5 = (f32[2,2048,256]{2,1,0:T(8,128)S(1)}, f32[8,128]{1,0:T(8,128)}, bf16[2048,256]{1,0:T(8,128)(2,1)S(1)}) custom-call(bf16[8,256,2048]{2,1,0:T(8,128)(2,1)} %chol_any.5, bf16[256,2,256]{2,1,0:T(2,128)(2,1)S(1)} %collective-permute-done.3.refs_0_, bf16[256,2,256]{2,1,0:T(2,128)(2,1)S(1)} %collective-permute-done.5.refs_1_, ...), custom_call_target="tpu_custom_call" | custom-call | flops 1073741824 | bytes 2097152 | tf_op jit(solution)/shard_map/accumulate/pallas_call | solution.py:109
  32.6 0.0 copy-start.3
  32.7 0.6 %collective-permute-done.9.refs_6_ = bf16[128,2,256]{2,1,0:T(2,128)(2,1)S(1)} collective-permute-done((bf16[128,2,256]{2,1,0:T(2,128)(2,1)S(1)}, bf16[128,2,256]{2,1,0:T(2,128)(2,1)S(1)}, u32[]{:S(2)}, u32[]{:S(2)}) %collective-permute-start.9) | collective-permute-done | bytes 131104 | tf_op jit(solution)/shard_map/ppermute | solution.py:155
  33.3 1.9 %measure.1 = f32[32,128]{1,0:T(8,128)S(1)} custom-call(bf16[2048,256]{1,0:T(8,128)(2,1)S(1)} %get-tuple-element.59.refs_0_, f32[8,128]{1,0:T(8,128)S(1)} %copy-done.2, bf16[304,128]{1,0:T(8,128)(2,1)S(1)} %copy-done.1, bf16[304,128]{1,0:T(8,128)(2,1)S(1)} %collective-permute-done.6.refs_3_.refs_1_, ...), custom_call_target="tpu_custom_call" | custom-call | flops 536870912 | bytes 1048576 | tf_op jit(solution)/shard_map/measure/pallas_call | solution.py:367
  35.1 11.8 %all_to_all.11 = f32[32,1,128]{2,1,0:T(1,128)S(1)} all-to-all(f32[32,1,128]{2,1,0:T(1,128)S(1)} %bitcast.8), channel_id=1, replica_groups=mesh['chol'=8,'walk'=4] {'chol','walk'}, dimensions={0} | all-to-all | bytes 32768 | tf_op jit(solution)/shard_map/all_to_all | solution.py:450
  47.0 1.4 %finish.1 = (f32[1,4]{1,0:T(1,128)}, f32[1,4]{1,0:T(1,128)}, f32[128,128]{1,0:T(8,128)}) custom-call(f32[32,128]{1,0:T(8,128)S(1)} %bitcast.9, s32[4]{0:T(128)S(1)} %copy-done.3, bf16[304,128]{1,0:T(8,128)(2,1)S(1)} %copy-done.1, bf16[304,128]{1,0:T(8,128)(2,1)S(1)} %collective-permute-done.6.refs_3_.refs_1_, ...), custom_call_target="tpu_custom_call" | custom-call | flops 1000000 | bytes 600000 | tf_op jit(solution)/shard_map/finish/pallas_call | solution.py:422
  (21 shorter events, 0.0 us)
Async XLA Ops:
  0.6 9.5 %collective-permute-start = (bf16[256,2,256]{2,1,0:T(2,128)(2,1)}, bf16[256,2,256]{2,1,0:T(2,128)(2,1)S(1)}, u32[]{:S(2)}, u32[]{:S(2)}) collective-permute-start(bf16[256,2,256]{2,1,0:T(2,128)(2,1)} %refs_0_.1), channel_id=1, source_target_pairs={{0,8},{8,16},{16,24},{24,28},{28,20},{20,12},{12,4},{4,0},{1,9},{9... | collective-permute-start | bytes 786440 | tf_op jit(solution)/shard_map/ppermute | solution.py:139
  3.7 8.3 %collective-permute-start.2 = (bf16[256,2,256]{2,1,0:T(2,128)(2,1)}, bf16[256,2,256]{2,1,0:T(2,128)(2,1)S(1)}, u32[]{:S(2)}, u32[]{:S(2)}) collective-permute-start(bf16[256,2,256]{2,1,0:T(2,128)(2,1)} %refs_0_.1), channel_id=1, source_target_pairs={{0,4},{8,0},{16,8},{24,16},{28,24},{20,28},{12,20},{4,12},{1,5},{9... | collective-permute-start | bytes 786440 | tf_op jit(solution)/shard_map/ppermute | solution.py:139
  10.2 7.5 %collective-permute-start.1 = (bf16[256,2,256]{2,1,0:T(2,128)(2,1)S(1)}, bf16[256,2,256]{2,1,0:T(2,128)(2,1)S(1)}, u32[]{:S(2)}, u32[]{:S(2)}) collective-permute-start(bf16[256,2,256]{2,1,0:T(2,128)(2,1)S(1)} %collective-permute-done.refs_1_), channel_id=1, source_target_pairs={{0,8},{8,16},{16,24},{24,28},{28,20},{20,12},{12,4},{4,0},{1,9},{9... | collective-permute-start | bytes 786440 | tf_op jit(solution)/shard_map/ppermute | solution.py:142
  12.0 7.6 %collective-permute-start.4 = (bf16[256,2,256]{2,1,0:T(2,128)(2,1)S(1)}, bf16[256,2,256]{2,1,0:T(2,128)(2,1)S(1)}, u32[]{:S(2)}, u32[]{:S(2)}) collective-permute-start(bf16[256,2,256]{2,1,0:T(2,128)(2,1)S(1)} %collective-permute-done.2.refs_2_), channel_id=1, source_target_pairs={{0,4},{8,0},{16,8},{24,16},{28,24},{20,28},{12,20},{4,12},{1,5},{9... | collective-permute-start | bytes 786440 | tf_op jit(solution)/shard_map/ppermute | solution.py:142
  12.2 0.9 %copy-start = (bf16[256,2,256]{2,1,0:T(2,128)(2,1)S(1)}, bf16[256,2,256]{2,1,0:T(2,128)(2,1)}, u32[]{:S(2)}) copy-start(bf16[256,2,256]{2,1,0:T(2,128)(2,1)} %refs_0_.1) | copy-start | bytes 786436
  13.2 6.6 %copy-start.6 = (bf16[304,128]{1,0:T(8,128)(2,1)S(1)}, bf16[304,128]{1,0:T(8,128)(2,1)}, u32[]{:S(2)}) copy-start(bf16[304,128]{1,0:T(8,128)(2,1)} %get-tuple-element.53) | copy-start | bytes 233476
  13.2 6.6 %copy-start.5 = (bf16[304,128]{1,0:T(8,128)(2,1)S(1)}, bf16[304,128]{1,0:T(8,128)(2,1)}, u32[]{:S(2)}) copy-start(bf16[304,128]{1,0:T(8,128)(2,1)} %get-tuple-element.54) | copy-start | bytes 233476
  13.2 8.4 %copy-start.4 = (bf16[304,128]{1,0:T(8,128)(2,1)S(1)}, bf16[304,128]{1,0:T(8,128)(2,1)}, u32[]{:S(2)}) copy-start(bf16[304,128]{1,0:T(8,128)(2,1)} %get-tuple-element.55) | copy-start | bytes 233476
  17.7 8.5 %collective-permute-start.3 = (bf16[256,2,256]{2,1,0:T(2,128)(2,1)S(1)}, bf16[256,2,256]{2,1,0:T(2,128)(2,1)S(1)}, u32[]{:S(2)}, u32[]{:S(2)}) collective-permute-start(bf16[256,2,256]{2,1,0:T(2,128)(2,1)S(1)} %collective-permute-done.1.refs_0_), channel_id=1, source_target_pairs={{0,8},{8,16},{16,24},{24,28},{28,20},{20,12},{12,4},{4,0},{1,9},{9... | collective-permute-start | bytes 786440 | tf_op jit(solution)/shard_map/ppermute | solution.py:148
  19.5 6.7 %collective-permute-start.5 = (bf16[256,2,256]{2,1,0:T(2,128)(2,1)S(1)}, bf16[256,2,256]{2,1,0:T(2,128)(2,1)S(1)}, u32[]{:S(2)}, u32[]{:S(2)}) collective-permute-start(bf16[256,2,256]{2,1,0:T(2,128)(2,1)S(1)} %collective-permute-done.4.refs_1_), channel_id=1, source_target_pairs={{0,4},{8,0},{16,8},{24,16},{28,24},{20,28},{12,20},{4,12},{1,5},{9... | collective-permute-start | bytes 786440 | tf_op jit(solution)/shard_map/ppermute | solution.py:148
  19.8 6.5 %collective-permute-start.6 = (bf16[304,128]{1,0:T(8,128)(2,1)S(1)}, bf16[304,128]{1,0:T(8,128)(2,1)S(1)}, u32[]{:S(2)}, u32[]{:S(2)}) collective-permute-start(bf16[304,128]{1,0:T(8,128)(2,1)S(1)} %copy-done.6), channel_id=1, source_target_pairs={{0,1},{1,2},{2,3},{3,0},{4,5},{5,6},{6,7},{7,4},{8,9},{9,10},{10,1... | collective-permute-start | bytes 233480 | tf_op jit(solution)/shard_map/ppermute | solution.py:280
  19.8 6.5 %collective-permute-start.7 = (bf16[304,128]{1,0:T(8,128)(2,1)S(1)}, bf16[304,128]{1,0:T(8,128)(2,1)S(1)}, u32[]{:S(2)}, u32[]{:S(2)}) collective-permute-start(bf16[304,128]{1,0:T(8,128)(2,1)S(1)} %copy-done.5), channel_id=1, source_target_pairs={{0,2},{1,3},{2,0},{3,1},{4,6},{5,7},{6,4},{7,5},{8,10},{9,11},{10,... | collective-permute-start | bytes 233480 | tf_op jit(solution)/shard_map/ppermute | solution.py:280
  21.6 4.7 %collective-permute-start.8 = (bf16[304,128]{1,0:T(8,128)(2,1)S(1)}, bf16[304,128]{1,0:T(8,128)(2,1)S(1)}, u32[]{:S(2)}, u32[]{:S(2)}) collective-permute-start(bf16[304,128]{1,0:T(8,128)(2,1)S(1)} %copy-done.4), channel_id=1, source_target_pairs={{0,3},{1,0},{2,1},{3,2},{4,7},{5,4},{6,5},{7,6},{8,11},{9,8},{10,9... | collective-permute-start | bytes 233480 | tf_op jit(solution)/shard_map/ppermute | solution.py:280
  26.4 6.3 %collective-permute-start.10 = (bf16[128,2,256]{2,1,0:T(2,128)(2,1)S(1)}, bf16[128,2,256]{2,1,0:T(2,128)(2,1)S(1)}, u32[]{:S(2)}, u32[]{:S(2)}) collective-permute-start(bf16[128,2,256]{2,1,0:T(2,128)(2,1)S(1)} %slice.7), channel_id=1, source_target_pairs={{0,4},{8,0},{16,8},{24,16},{28,24},{20,28},{12,20},{4,12},{1,5},{9... | collective-permute-start | bytes 393224 | tf_op jit(solution)/shard_map/ppermute | solution.py:155
  28.0 5.2 %collective-permute-start.9 = (bf16[128,2,256]{2,1,0:T(2,128)(2,1)S(1)}, bf16[128,2,256]{2,1,0:T(2,128)(2,1)S(1)}, u32[]{:S(2)}, u32[]{:S(2)}) collective-permute-start(bf16[128,2,256]{2,1,0:T(2,128)(2,1)S(1)} %slice.6), channel_id=1, source_target_pairs={{0,8},{8,16},{16,24},{24,28},{28,20},{20,12},{12,4},{4,0},{1,9},{9... | collective-permute-start | bytes 393224 | tf_op jit(solution)/shard_map/ppermute | solution.py:155
  28.8 4.5 %copy-start.1 = (bf16[304,128]{1,0:T(8,128)(2,1)S(1)}, bf16[304,128]{1,0:T(8,128)(2,1)}, u32[]{:S(2)}) copy-start(bf16[304,128]{1,0:T(8,128)(2,1)} %get-tuple-element.61.refs_2_.refs_0_) | copy-start | bytes 233476
  28.8 4.5 %copy-start.2 = (f32[8,128]{1,0:T(8,128)S(1)}, f32[8,128]{1,0:T(8,128)}, u32[]{:S(2)}) copy-start(f32[8,128]{1,0:T(8,128)} %get-tuple-element.60.refs_1_) | copy-start | bytes 12292
  32.6 14.4 %copy-start.3 = (s32[4]{0:T(128)S(1)}, s32[4]{0:T(128)}, u32[]{:S(2)}) copy-start(s32[4]{0:T(128)} %counts_ref.1) | copy-start | bytes 52

commit v5 on v4

--- a/solution.py
+++ b/solution.py
@@ -1,5 +1,3 @@
-import functools
-
 import jax
 import jax.numpy as jnp
 from jax import lax
@@ -12,7 +10,8 @@
 LANES = 128
 VMEM_LIMIT = 16 * 1024 * 1024
 PACK_LIMIT = 54 * 1024 * 1024
-ACCUMULATE_LIMIT = 43 * 1024 * 1024
+ACCUMULATE_LIMIT = 40 * 1024 * 1024
+FETCH_LIMIT = 48 * 1024 * 1024
 RING_LIMIT = 16
 
 
@@ -47,79 +46,83 @@
     return pl.multiple_of(owner * rows, rows)
 
 
-def accumulate(cholesky_rot, shifts, parts, total, mark, ahead):
+def start_columns(chol_any, shifts, rows, target, sems):
+    vectors, orbitals, _ = chol_any.shape
+    copies = []
+    for g in range(vectors):
+        for n, shift in enumerate(shifts):
+            copies.append(
+                pltpu.make_async_copy(
+                    chol_any.at[g, :, pl.ds(column_start(shift, rows), rows)],
+                    target.at[pl.ds(g * orbitals, orbitals), pl.ds(n * rows, rows)],
+                    sems.at[g * len(shifts) + n],
+                )
+            )
+    for copy in copies:
+        copy.start()
+    return copies
+
+
+def fetch(cholesky_rot, shifts, rows):
+    vectors, orbitals, _ = cholesky_rot.shape
+
+    def kernel(chol_any, blocks_ref, mark_ref, sems):
+        copies = start_columns(chol_any, shifts, rows, blocks_ref, sems)
+        mark_ref[...] = jnp.zeros_like(mark_ref)
+        for copy in copies:
+            copy.wait()
+
+    return pl.pallas_call(
+        kernel,
+        name="fetch",
+        out_shape=[
+            jax.ShapeDtypeStruct((vectors * orbitals, len(shifts) * rows), cholesky_rot.dtype),
+            jax.ShapeDtypeStruct((8, LANES), jnp.float32),
+        ],
+        in_specs=[pl.BlockSpec(memory_space=pl.ANY)],
+        out_specs=[vmem()] * 2,
+        scratch_shapes=[pltpu.SemaphoreType.DMA((vectors * len(shifts),))],
+        compiler_params=params(FETCH_LIMIT),
+        cost_estimate=pl.CostEstimate(
+            flops=0, bytes_accessed=4 * vectors * orbitals * len(shifts) * rows, transcendentals=0
+        ),
+    )(cholesky_rot)
+
+
+def accumulate(cholesky_rot, blocks, parts, total, mark, ahead):
     vectors, orbitals, _ = cholesky_rot.shape
     rows, walkers, _ = parts[0].shape
-    count = len(parts)
     size = vectors * orbitals
-    chunks = vectors // 2 if vectors % 2 == 0 else vectors
-    each = vectors // chunks
-    arrays = list(parts) + ([] if mark is None else [mark]) + ([] if total is None else [total])
-    shapes = [
-        jax.ShapeDtypeStruct((walkers, size, orbitals), jnp.float32),
-        jax.ShapeDtypeStruct((8, LANES), jnp.float32),
-    ]
-    if ahead is not None:
-        shapes.append(jax.ShapeDtypeStruct((size, rows), cholesky_rot.dtype))
+    arrays = [blocks] + list(parts) + [mark] + ([] if total is None else [total])
 
     def kernel(chol_any, *refs):
-        ins = refs[: len(arrays)]
-        outs = refs[len(arrays) : len(arrays) + len(shapes)]
-        blocks_scr, sems = refs[len(arrays) + len(shapes) :]
-
-        def columns(shift, g, target):
-            return chol_any.at[g, :, pl.ds(column_start(shift, rows), rows)], target
-
-        copies = []
-        for g in range(vectors):
-            for n, shift in enumerate(shifts):
-                copies.append(
-                    pltpu.make_async_copy(
-                        *columns(
-                            shift, g, blocks_scr.at[pl.ds(g * orbitals, orbitals), pl.ds(n * rows, rows)]
-                        ),
-                        sems.at[g * (count + 1) + n],
-                    )
-                )
+        blocks_ref = refs[0]
+        shards = refs[1 : 1 + len(parts)]
+        total_ref, mark_ref, ahead_ref, sems = refs[len(arrays) :]
+        copies = start_columns(chol_any, ahead, rows, ahead_ref, sems)
+        mark_ref[...] = jnp.zeros_like(mark_ref)
+        for b in range(walkers):
+            rhs = jnp.concatenate([x[:, b, :] for x in shards], axis=0)
+            value = jnp.dot(blocks_ref[...], rhs, preferred_element_type=jnp.float32)
+            total_ref[b] = value if total is None else refs[len(arrays) - 1][b] + value
         for copy in copies:
-            copy.start()
-        later = []
-        if ahead is not None:
-            for g in range(vectors):
-                later.append(
-                    pltpu.make_async_copy(
-                        *columns(ahead, g, outs[2].at[pl.ds(g * orbitals, orbitals), :]),
-                        sems.at[g * (count + 1) + count],
-                    )
-                )
-            for copy in later:
-                copy.start()
-        outs[1][...] = jnp.zeros_like(outs[1])
-        rhs = [jnp.concatenate([x[:, b, :] for x in ins[:count]], axis=0) for b in range(walkers)]
-        for q in range(chunks):
-            for copy in copies[q * each * count : (q + 1) * each * count]:
-                copy.wait()
-            at = slice(q * each * orbitals, (q + 1) * each * orbitals)
-            for b in range(walkers):
-                value = jnp.dot(blocks_scr[at, :], rhs[b], preferred_element_type=jnp.float32)
-                outs[0][b, at, :] = value if total is None else ins[-1][b, at, :] + value
-        for copy in later:
             copy.wait()
 
     return pl.pallas_call(
         kernel,
         name="accumulate",
-        out_shape=shapes,
+        out_shape=[
+            jax.ShapeDtypeStruct((walkers, size, orbitals), jnp.float32),
+            jax.ShapeDtypeStruct((8, LANES), jnp.float32),
+            jax.ShapeDtypeStruct((size, len(ahead) * rows), cholesky_rot.dtype),
+        ],
         in_specs=[pl.BlockSpec(memory_space=pl.ANY)] + [vmem()] * len(arrays),
-        out_specs=[vmem()] * len(shapes),
-        scratch_shapes=[
-            pltpu.VMEM((size, count * rows), cholesky_rot.dtype),
-            pltpu.SemaphoreType.DMA((vectors * (count + 1),)),
-        ],
+        out_specs=[vmem()] * 3,
+        scratch_shapes=[pltpu.SemaphoreType.DMA((vectors * len(ahead),))],
         compiler_params=params(ACCUMULATE_LIMIT),
         cost_estimate=pl.CostEstimate(
-            flops=2 * count * size * rows * walkers * orbitals,
-            bytes_accessed=2 * count * size * rows,
+            flops=2 * len(parts) * size * rows * walkers * orbitals,
+            bytes_accessed=4 * len(ahead) * size * rows,
             transcendentals=0,
         ),
     )(cholesky_rot, *arrays)
@@ -136,25 +139,33 @@
     ahead = [(order[q], order[(q + 1) % size]) for q in range(size)]
     back = [(order[q], order[(q - 1) % size]) for q in range(size)]
     steps = size // 2
-    right, left = lax.ppermute(own, "chol", ahead), lax.ppermute(own, "chol", back)
-    right, onebody = tie(right, onebody)
-    left, onebody = tie(left, onebody)
-    next_right, next_left = lax.ppermute(right, "chol", ahead), lax.ppermute(left, "chol", back)
-    total, mark = accumulate(cholesky_rot, [0, -1, 1], [own, right, left], None, None, None)
-    right, mark = tie(next_right, mark)
-    left, mark = tie(next_left, mark)
-    others = packed[1:]
-    for step in range(3, steps):
+    right = left = own
+    parts = [own]
+    total = None
+    for step in range(1, steps):
         next_right, next_left = lax.ppermute(right, "chol", ahead), lax.ppermute(left, "chol", back)
-        if step == 3:
-            *others, mark = tie(*others, mark)
-            others = [shifted(x, d + 1) for d, x in enumerate(others)]
-        total, mark = accumulate(cholesky_rot, [1 - step, step - 1], [right, left], total, mark, None)
-        right, mark = tie(next_right, mark)
-        left, mark, *others = tie(next_left, mark, *others)
+        if step == 1:
+            blocks, mark = fetch(cholesky_rot, [0, -1, 1], rows)
+            right, onebody = tie(next_right, onebody)
+            left, mark, *packed = tie(next_left, mark, *packed)
+        else:
+            total, mark, blocks = accumulate(cholesky_rot, blocks, parts, total, mark, [-step, step])
+            parts = []
+            if step == 2:
+                far = exchange_far(packed)
+                right, mark = tie(next_right, mark)
+                left, far = tie(next_left, far)
+            elif step == 3:
+                near = exchange_near(packed, far)
+                right, mark = tie(next_right, mark)
+                left, *near = tie(next_left, *near)
+            else:
+                right, mark = tie(next_right, mark)
+                left = next_left
+        parts = parts + [right, left]
     last = [lax.ppermute(right[: rows // 2], "chol", ahead), lax.ppermute(left[rows // 2 :], "chol", back)]
-    total, _, block = accumulate(cholesky_rot, [1 - steps, steps - 1], [right, left], total, mark, steps)
-    return block, onebody, total, last, [packed[0]] + others
+    total, _, blocks = accumulate(cholesky_rot, blocks, parts, total, mark, [steps])
+    return blocks, onebody, total, last, [packed[0], far] + near
 
 
 def table_height(vectors):
@@ -168,12 +179,19 @@
     pair = LANES // width
     vectors, slots = fields.shape
     table_rows = table_height(vectors)
-    height = walkers * (rows // pair) + 3 * table_rows
+    panel_rows = walkers * (rows // pair)
+    both = panel_rows + 3 * table_rows
+    if walk_size == 4:
+        heights = [both, both + panel_rows, both]
+        spots = [(0, 0), (2, 0), (1, 0), (1, both)]
+    else:
+        heights = [both] * walk_size
+        spots = [(d, 0) for d in range(walk_size)]
 
     def kernel(own_any, body_any, fields_any, weights_any, sources_any, owners_any, *refs):
         onebody_ref = refs[0]
-        packs = refs[1 : 1 + walk_size]
-        own_ref, body_ref, fields_ref, weights_ref, sources_ref, owners_ref, table_scr, sems = refs[1 + walk_size :]
+        packs = refs[1 : 1 + len(heights)]
+        own_ref, body_ref, fields_ref, weights_ref, sources_ref, owners_ref, table_scr, sems = refs[1 + len(heights) :]
         places = [
             (own_any, own_ref),
             (body_any, body_ref),
@@ -214,7 +232,8 @@
                 ]
             )
         for d in range(walk_size):
-            target = lax.rem(walk + d, walk_size)
+            target = walk_partner(walk, d, walk_size, False)
+            out, top = spots[d]
             panel = jnp.int32(0)
             for p in range(walk_size):
                 panel = jnp.where(owners_ref[p] == target, p, panel)
@@ -225,7 +244,7 @@
                     total += jnp.dot(
                         thinned[b][h], take.astype(jnp.bfloat16), preferred_element_type=jnp.float32
                     )
-                packs[d][b * (rows // pair) : (b + 1) * (rows // pair), :] = total.astype(jnp.bfloat16)
+                packs[out][top + b * (rows // pair) : top + (b + 1) * (rows // pair), :] = total.astype(jnp.bfloat16)
         spread = jnp.zeros((vectors, LANES), jnp.float32)
         source = jnp.zeros((1, LANES), jnp.float32)
         corner = lax.broadcasted_iota(jnp.int32, (vectors, vectors), 0) == lax.broadcasted_iota(
@@ -247,8 +266,8 @@
         for n in range(3):
             piece = rest.astype(jnp.bfloat16)
             rest = rest - piece.astype(jnp.float32)
-            at = walkers * (rows // pair) + n * table_rows
-            for d in range(walk_size):
+            at = panel_rows + n * table_rows
+            for d in range(len(heights)):
                 packs[d][at : at + table_rows, :] = piece
 
     return pl.pallas_call(
@@ -257,9 +276,9 @@
         out_shape=[
             jax.ShapeDtypeStruct((8, LANES), jnp.float32),
         ]
-        + [jax.ShapeDtypeStruct((height, LANES), jnp.bfloat16)] * walk_size,
+        + [jax.ShapeDtypeStruct((height, LANES), jnp.bfloat16) for height in heights],
         in_specs=[pl.BlockSpec(memory_space=pl.ANY)] * 6,
-        out_specs=[vmem()] * (walk_size + 1),
+        out_specs=[vmem()] * (len(heights) + 1),
         scratch_shapes=[
             pltpu.VMEM(own.shape, own.dtype),
             pltpu.VMEM(one_body.shape, one_body.dtype),
@@ -275,30 +294,54 @@
     )(own, one_body, fields.T, weights, sources, owners)
 
 
-def shifted(x, d):
+def walk_partner(walk, d, size, back):
+    if size == 4:
+        return lax.bitwise_xor(walk, d)
+    return lax.rem(walk + (size - d if back else d), size)
+
+
+def exchange_far(packed):
     size = lax.axis_size("walk")
-    return lax.ppermute(x, "walk", [(q, (q + d) % size) for q in range(size)])
-
-
-def read_table(ref, vectors):
+    if size != 4:
+        return lax.ppermute(packed[1], "walk", [(q, (q + 1) % size) for q in range(size)])
+    return lax.ppermute(packed[1], "walk", [(q, q ^ 2) for q in range(size)])
+
+
+def exchange_near(packed, far):
+    size = lax.axis_size("walk")
+    if size != 4:
+        return [
+            lax.ppermute(packed[d], "walk", [(q, (q + d) % size) for q in range(size)]) for d in range(2, size)
+        ]
+    keep, _, near = packed
+    panel = far.shape[0] - keep.shape[0]
+    return [lax.ppermute(jnp.concatenate([near, far[panel:]], axis=0), "walk", [(q, q ^ 1) for q in range(size)])]
+
+
+def walk_places(panel, table, size):
+    if size != 4:
+        return [(d, 0, panel) for d in range(size)]
+    return [(0, 0, panel), (2, 0, panel), (1, 0, panel), (2, panel + 2 * table, panel + table)]
+
+
+def read_table(ref, at, vectors):
     height = table_height(vectors)
-    start = ref.shape[0] - 3 * height
-    parts = [ref[start + n * height : start + (n + 1) * height, :].astype(jnp.float32) for n in range(3)]
+    parts = [ref[at + n * height : at + (n + 1) * height, :].astype(jnp.float32) for n in range(3)]
     return parts[0] + (parts[1] + parts[2])
 
 
 def merge_tables(tables, walk, walk_size, slots, lane):
     total = jnp.zeros_like(tables[0])
     for d, table in enumerate(tables):
-        group = lax.rem(walk - d + walk_size, walk_size)
+        group = walk_partner(walk, d, walk_size, True)
         total += jnp.where(lane // slots == group, table, 0.0)
     return total
 
 
-def measure(block, total, last, packs, onebody, vectors, slots):
+def measure(block, total, last, packs, places, onebody, vectors, slots):
     _, walkers, orbitals = last[0].shape
     depth = sum(x.shape[0] for x in last)
-    walk_size = len(packs)
+    walk_size = len(places)
     targets = walk_size * lax.axis_size("chol")
     whole = total is None
     quads = orbitals // LANES
@@ -308,12 +351,14 @@
 
     def kernel(*refs):
         block_ref, onebody_ref = refs[:2]
-        pack_refs = refs[2 : 2 + walk_size]
-        last_refs = refs[2 + walk_size : 2 + walk_size + len(last)]
+        pack_refs = refs[2 : 2 + len(packs)]
+        last_refs = refs[2 + len(packs) : 2 + len(packs) + len(last)]
         out_ref, tensor_scr = refs[-2:]
         walk = lax.axis_index("walk")
         lane = lax.broadcasted_iota(jnp.int32, (1, LANES), 1)
-        table = merge_tables([read_table(x, vectors) for x in pack_refs], walk, walk_size, slots, lane)
+        table = merge_tables(
+            [read_table(pack_refs[n], at, vectors) for n, _, at in places], walk, walk_size, slots, lane
+        )
         picks = [
             jnp.where(
                 (lane < slots * walk_size) & (table[vectors : vectors + 1, :] == (walk * walkers + b).astype(jnp.float32)),
@@ -331,7 +376,7 @@
         drive = jnp.zeros((1, LANES), jnp.float32)
         for b in range(walkers):
             value = jnp.dot(block_ref[...], rhs[b], preferred_element_type=jnp.float32)
-            tensor_scr[b] = value if whole else refs[2 + walk_size + len(last)][b] + value
+            tensor_scr[b] = value if whole else refs[2 + len(packs) + len(last)][b] + value
         for g in range(vectors):
             top = g * orbitals
             for b in range(walkers):
@@ -368,7 +413,7 @@
         kernel,
         name="measure",
         out_shape=jax.ShapeDtypeStruct((targets, LANES), jnp.float32),
-        in_specs=[vmem()] * (2 + walk_size + len(arrays)),
+        in_specs=[vmem()] * (2 + len(packs) + len(arrays)),
         out_specs=vmem(),
         scratch_shapes=[
             pltpu.VMEM((walkers, vectors * orbitals, orbitals), jnp.float32),
@@ -382,17 +427,17 @@
     )(block, onebody, *packs, *arrays)
 
 
-def finish(stats, packs, counts, vectors, slots, walkers):
-    walk_size = len(packs)
+def finish(stats, packs, places, counts, vectors, slots, walkers):
+    walk_size = len(places)
     rows = (packs[0].shape[0] - 3 * table_height(vectors)) // walkers
 
     def kernel(stats_ref, counts_ref, *refs):
-        pack_refs = refs[:walk_size]
-        energies_ref, weights_ref, density_ref = refs[walk_size:]
+        pack_refs = refs[: len(packs)]
+        energies_ref, weights_ref, density_ref = refs[len(packs) :]
         walk = lax.axis_index("walk")
         lane = lax.broadcasted_iota(jnp.int32, (1, LANES), 1)
         all_slots = slots * walk_size
-        tables = [read_table(x, vectors) for x in pack_refs]
+        tables = [read_table(pack_refs[n], at, vectors) for n, _, at in places]
         source = merge_tables([t[vectors : vectors + 1, :] for t in tables], walk, walk_size, slots, lane)
         total_weight = tables[0][vectors + 1 : vectors + 2, :]
         for t in tables[1:]:
@@ -408,12 +453,12 @@
         new_weights = jnp.where(live, mean_weight * jnp.exp(jnp.where(live, power, 0.0)), 0.0)
         norm = jnp.sum(new_weights, axis=1, keepdims=True)
         density = jnp.zeros((rows, LANES), jnp.float32)
-        for d in range(walk_size):
-            group = lax.rem(walk - d + walk_size, walk_size)
+        for d, (n, top, _) in enumerate(places):
+            group = walk_partner(walk, d, walk_size, True)
             for b in range(walkers):
                 walker = (group * walkers + b).astype(jnp.float32)
                 share = jnp.sum(jnp.where(source == walker, new_weights, 0.0), axis=1, keepdims=True) / norm
-                density += share * pack_refs[d][b * rows : (b + 1) * rows, :].astype(jnp.float32)
+                density += share * pack_refs[n][top + b * rows : top + (b + 1) * rows, :].astype(jnp.float32)
         density_ref[...] = density
         first = lax.rem(LANES - walk * slots, LANES)
         energies_ref[...] = pltpu.roll(jnp.broadcast_to(energies, (8, LANES)), first, 1)[:1, :slots]
@@ -427,7 +472,7 @@
             jax.ShapeDtypeStruct((1, slots), jnp.float32),
             jax.ShapeDtypeStruct((rows, LANES), jnp.float32),
         ],
-        in_specs=[vmem(), smem()] + [vmem()] * walk_size,
+        in_specs=[vmem(), smem()] + [vmem()] * len(packs),
         out_specs=[vmem()] * 3,
         compiler_params=params(),
         cost_estimate=pl.CostEstimate(flops=10**6, bytes_accessed=6 * 10**5, transcendentals=128),
@@ -442,13 +487,16 @@
     onebody, *packed = pack(green_rows, one_body, fields, weights, sources, owners)
     if chol_size > RING_LIMIT or chol_size % 2 or chol_size < 8:
         block = cholesky_rot.reshape(-1, cholesky_rot.shape[2])
-        packs = [packed[0]] + [shifted(packed[d], d) for d in range(1, walk_size)]
+        far = exchange_far(packed)
+        packs = [packed[0], far] + exchange_near(packed, far)
         total, last = None, [lax.all_gather(green_rows, "chol", axis=0, tiled=True)]
     else:
         block, onebody, total, last, packs = ring(green_rows, cholesky_rot, onebody, packed)
-    stats = measure(block, total, last, packs, onebody, vectors, slots)
+    table = 3 * table_height(vectors)
+    places = walk_places(packs[0].shape[0] - table, table, walk_size)
+    stats = measure(block, total, last, packs, places, onebody, vectors, slots)
     stats = lax.all_to_all(stats, ("chol", "walk"), split_axis=0, concat_axis=0, tiled=True)
-    energies, new_weights, density = finish(stats, packs, counts, vectors, slots, walkers)
+    energies, new_weights, density = finish(stats, packs, places, counts, vectors, slots, walkers)
     return energies.reshape(slots), new_weights.reshape(slots), density.reshape(1, density.size)
 
 

time: 48.6 us -> 47.2 us (0.971)
  blocking collectives: 11.8 us -> 9.93 us
  Pallas kernels: 18.1 us -> 19.9 us
  starting transfers between devices: 12.7 us -> 11 us
  waiting for transfers between devices: 3.85 us -> 5.1 us
  local copies, waits for them, and re-layouts: 1.16 us -> 0.21 us
    ppermute x5 -> x2, starting transfers between devices: 6.26 us -> 1.77 us  [the longest x1 1.7 us: exchange_far(): return lax.ppermute(packed[1], 'walk', [(q, q ^ 2) for q in range(size)])]
    ppermute x5 -> x2, waiting for transfers between devices: 3.26 us -> 0.01 us  [the longest x1 0.01 us: exchange_far(): return lax.ppermute(packed[1], 'walk', [(q, q ^ 2) for q in range(size)])]
    ppermute x2 -> x3, starting transfers between devices: 3.64 us -> 6.44 us  [ring(): lax.ppermute(right, 'chol', ahead)]
    ppermute x2 -> x3, waiting for transfers between devices: 0.01 us -> 2.39 us  [ring(): lax.ppermute(left, 'chol', back)]
    all_to_all x1, blocking collectives: 11.8 us -> 9.93 us  [per_device(): lax.all_to_all(stats, ('chol', 'walk'), split_axis=0, concat_axis=0, tile...]
    ppermute x2 -> x3, waiting for transfers between devices: 0.01 us -> 1.83 us  [ring(): lax.ppermute(right, 'chol', ahead)]
    pallas_call x3 -> x4, Pallas kernels: 11.6 us -> 13.4 us  [the longest x3 11.3 us: accumulate(): pl.pallas_call(kernel, name='accumulate', out_shape=[jax.ShapeDtypeStruct...]
    ppermute x1, starting transfers between devices: 1.57 us -> 0.5 us  [ring(): lax.ppermute(left[rows // 2:], 'chol', back)]
  transfers between devices with their start and end apart: 11 -> 10, of which waited for: 2 -> 5; matrix products, arithmetic and copies ran while one was open for 0% -> 0% of each run, Pallas kernels for 31% -> 35%
where the time goes in v5:
time: 47.2 us; the launch traced here: 46.9 us
  Pallas kernels  19.9 us (42%)
  starting transfers between devices  11 us (23%)
  blocking collectives  9.93 us (21%)
  waiting for transfers between devices  5.1 us (11%)
  between operations  0.74 us (2%)
    pallas_call x3, Pallas kernels, accumulate(): pl.pallas_call(kernel, name='accumulate', out_shape=[jax.ShapeDtypeStruct...  11.3 us
    all_to_all x1, blocking collectives, per_device(): lax.all_to_all(stats, ('chol', 'walk'), split_axis=0, concat_axis=0, tile...  9.93 us
    ppermute x3, starting transfers between devices, ring(): lax.ppermute(right, 'chol', ahead)  6.44 us
    pallas_call x1, Pallas kernels, pack(): pl.pallas_call(kernel, name='pack', out_shape=[jax.ShapeDtypeStruct((8, L...  3.16 us
    ppermute x3, waiting for transfers between devices, ring(): lax.ppermute(left, 'chol', back)  2.39 us
    pallas_call x1, Pallas kernels, fetch(): pl.pallas_call(kernel, name='fetch', out_shape=[jax.ShapeDtypeStruct((vec...  2.17 us
    pallas_call x1, Pallas kernels, measure(): pl.pallas_call(kernel, name='measure', out_shape=jax.ShapeDtypeStruct((ta...  1.88 us
    ppermute x3, waiting for transfers between devices, ring(): lax.ppermute(right, 'chol', ahead)  1.83 us
  transfers between devices with their start and end apart: 10, of which 5 were waited for; matrix products, arithmetic and copies ran while one was open for 0% of the time, Pallas kernels for 35%

profile of v5, /device:TPU:0, one launch (start us, length us, event | category | flops | bytes accessed | tf_op | source)
XLA Modules:
  0.0 46.9 jit_solution(2746580977296190972)
XLA Ops:
  0.6 3.1 %collective-permute-start = (bf16[256,2,256]{2,1,0:T(2,128)(2,1)}, bf16[256,2,256]{2,1,0:T(2,128)(2,1)S(1)}, u32[]{:S(2)}, u32[]{:S(2)}) collective-permute-start(bf16[256,2,256]{2,1,0:T(2,128)(2,1)} %refs_1_.1), channel_id=1, source_target_pairs={{0,8},{8,16},{16,24},{24,28},{28,20},{20,12},{12,4},{4,0},{1,9},{9... | collective-permute-start | bytes 786440 | tf_op jit(solution)/shard_map/ppermute | solution.py:146
  3.7 2.2 %fetch.1 = (bf16[2048,768]{1,0:T(8,128)(2,1)S(1)}, f32[8,128]{1,0:T(8,128)S(1)}) custom-call(bf16[8,256,2048]{2,1,0:T(8,128)(2,1)} %chol_any.7), custom_call_target="tpu_custom_call" | custom-call | bytes 6291456 | tf_op jit(solution)/shard_map/fetch/pallas_call | solution.py:75
  5.9 3.2 %pack.1 = (f32[8,128]{1,0:T(8,128)}, bf16[304,128]{1,0:T(8,128)(2,1)}, bf16[560,128]{1,0:T(8,128)(2,1)}, bf16[304,128]{1,0:T(8,128)(2,1)}) custom-call(bf16[256,2,256]{2,1,0:T(2,128)(2,1)} %refs_1_.1, bf16[256,256]{1,0:T(8,128)(2,1)} %body_any.1, f32[4,8]{1,0:T(4,128)} %bitcast.10, f32[2]{0:T(128)} %weights_any.1, s32[4]{0:T(128)} %sources_any.1, s32[4]{0:T(128)} %owners_any.1), custom_call_target="tpu_custom_call" | custom-call | flops 100000000 | bytes 1000000 | tf_op jit(solution)/shard_map/pack/pallas_call | solution.py:273
  9.1 1.1 %collective-permute-done.refs_2_ = bf16[256,2,256]{2,1,0:T(2,128)(2,1)S(1)} collective-permute-done((bf16[256,2,256]{2,1,0:T(2,128)(2,1)}, bf16[256,2,256]{2,1,0:T(2,128)(2,1)S(1)}, u32[]{:S(2)}, u32[]{:S(2)}) %collective-permute-start) | collective-permute-done | bytes 262176 | tf_op jit(solution)/shard_map/ppermute | solution.py:146
  10.2 1.8 %collective-permute-start.2 = (bf16[256,2,256]{2,1,0:T(2,128)(2,1)S(1)}, bf16[256,2,256]{2,1,0:T(2,128)(2,1)S(1)}, u32[]{:S(2)}, u32[]{:S(2)}) collective-permute-start(bf16[256,2,256]{2,1,0:T(2,128)(2,1)S(1)} %collective-permute-done.refs_2_), channel_id=1, source_target_pairs={{0,8},{8,16},{16,24},{24,28},{28,20},{20,12},{12,4},{4,0},{1,9},{9... | collective-permute-start | bytes 786440 | tf_op jit(solution)/shard_map/ppermute | solution.py:146
  12.0 0.2 collective-permute-start.3
  12.2 1.7 %collective-permute-start.4 = (bf16[560,128]{1,0:T(8,128)(2,1)}, bf16[560,128]{1,0:T(8,128)(2,1)S(1)}, u32[]{:S(2)}, u32[]{:S(2)}) collective-permute-start(bf16[560,128]{1,0:T(8,128)(2,1)} %get-tuple-element.47), channel_id=1, source_target_pairs={{0,2},{1,3},{2,0},{3,1},{4,6},{5,7},{6,4},{7,5},{8,10},{9,11},{10,... | collective-permute-start | bytes 430088 | tf_op jit(solution)/shard_map/ppermute | solution.py:307
  13.9 4.1 %accumulate.3 = (f32[2,2048,256]{2,1,0:T(8,128)S(1)}, f32[8,128]{1,0:T(8,128)S(1)}, bf16[2048,512]{1,0:T(8,128)(2,1)S(1)}) custom-call(bf16[8,256,2048]{2,1,0:T(8,128)(2,1)} %chol_any.7, bf16[2048,768]{1,0:T(8,128)(2,1)S(1)} %get-tuple-element.35.refs_0_, bf16[256,2,256]{2,1,0:T(2,128)(2,1)S(1)} %copy-done, ...), custom_call_target="tpu_custom_call" | custom-call | flops 1610612736 | bytes 4194304 | tf_op jit(solution)/shard_map/accumulate/pallas_call | solution.py:111
  18.1 0.8 %collective-permute-done.3.refs_2_ = bf16[256,2,256]{2,1,0:T(2,128)(2,1)S(1)} collective-permute-done((bf16[256,2,256]{2,1,0:T(2,128)(2,1)S(1)}, bf16[256,2,256]{2,1,0:T(2,128)(2,1)S(1)}, u32[]{:S(2)}, u32[]{:S(2)}) %collective-permute-start.3) | collective-permute-done | bytes 262176 | tf_op jit(solution)/shard_map/ppermute | solution.py:146
  18.9 1.6 %collective-permute-start.5 = (bf16[256,2,256]{2,1,0:T(2,128)(2,1)S(1)}, bf16[256,2,256]{2,1,0:T(2,128)(2,1)S(1)}, u32[]{:S(2)}, u32[]{:S(2)}) collective-permute-start(bf16[256,2,256]{2,1,0:T(2,128)(2,1)S(1)} %collective-permute-done.2.refs_1_), channel_id=1, source_target_pairs={{0,8},{8,16},{16,24},{24,28},{28,20},{20,12},{12,4},{4,0},{1,9},{9... | collective-permute-start | bytes 786440 | tf_op jit(solution)/shard_map/ppermute | solution.py:146
  20.5 0.4 collective-permute-start.6
  20.9 0.1 collective-permute-start.7
  21.0 3.5 %accumulate.4 = (f32[2,2048,256]{2,1,0:T(8,128)S(1)}, f32[8,128]{1,0:T(8,128)S(1)}, bf16[2048,512]{1,0:T(8,128)(2,1)S(1)}) custom-call(bf16[8,256,2048]{2,1,0:T(8,128)(2,1)} %chol_any.7, bf16[2048,512]{1,0:T(8,128)(2,1)S(1)} %get-tuple-element.44.refs_0_, bf16[256,2,256]{2,1,0:T(2,128)(2,1)S(1)} %collective-permute-done.2.refs_1_, ...), custom_call_target="tpu_custom_call" | custom-call | flops 1073741824 | bytes 4194304 | tf_op jit(solution)/shard_map/accumulate/pallas_call | solution.py:111
  24.5 0.7 %collective-permute-done.5.refs_1_ = bf16[256,2,256]{2,1,0:T(2,128)(2,1)S(1)} collective-permute-done((bf16[256,2,256]{2,1,0:T(2,128)(2,1)S(1)}, bf16[256,2,256]{2,1,0:T(2,128)(2,1)S(1)}, u32[]{:S(2)}, u32[]{:S(2)}) %collective-permute-start.5) | collective-permute-done | bytes 262176 | tf_op jit(solution)/shard_map/ppermute | solution.py:146
  25.2 1.6 %collective-permute-done.6.refs_2_ = bf16[256,2,256]{2,1,0:T(2,128)(2,1)S(1)} collective-permute-done((bf16[256,2,256]{2,1,0:T(2,128)(2,1)S(1)}, bf16[256,2,256]{2,1,0:T(2,128)(2,1)S(1)}, u32[]{:S(2)}, u32[]{:S(2)}) %collective-permute-start.6) | collective-permute-done | bytes 262176 | tf_op jit(solution)/shard_map/ppermute | solution.py:146
  26.8 0.1 slice.10
  26.9 1.6 %collective-permute-start.8 = (bf16[128,2,256]{2,1,0:T(2,128)(2,1)S(1)}, bf16[128,2,256]{2,1,0:T(2,128)(2,1)S(1)}, u32[]{:S(2)}, u32[]{:S(2)}) collective-permute-start(bf16[128,2,256]{2,1,0:T(2,128)(2,1)S(1)} %slice.10), channel_id=1, source_target_pairs={{0,8},{8,16},{16,24},{24,28},{28,20},{20,12},{12,4},{4,0},{1,9},{9... | collective-permute-start | bytes 393224 | tf_op jit(solution)/shard_map/ppermute | solution.py:166
  28.6 0.1 slice.11
  28.6 0.5 %collective-permute-start.9 = (bf16[128,2,256]{2,1,0:T(2,128)(2,1)S(1)}, bf16[128,2,256]{2,1,0:T(2,128)(2,1)S(1)}, u32[]{:S(2)}, u32[]{:S(2)}) collective-permute-start(bf16[128,2,256]{2,1,0:T(2,128)(2,1)S(1)} %slice.11), channel_id=1, source_target_pairs={{0,4},{8,0},{16,8},{24,16},{28,24},{20,28},{12,20},{4,12},{1,5},{9... | collective-permute-start | bytes 393224 | tf_op jit(solution)/shard_map/ppermute | solution.py:166
  29.2 3.6 %accumulate.5 = (f32[2,2048,256]{2,1,0:T(8,128)S(1)}, f32[8,128]{1,0:T(8,128)}, bf16[2048,256]{1,0:T(8,128)(2,1)S(1)}) custom-call(bf16[8,256,2048]{2,1,0:T(8,128)(2,1)} %chol_any.7, bf16[2048,512]{1,0:T(8,128)(2,1)S(1)} %get-tuple-element.51.refs_0_, bf16[256,2,256]{2,1,0:T(2,128)(2,1)S(1)} %collective-permute-done.5.refs_1_, ...), custom_call_target="tpu_custom_call" | custom-call | flops 1073741824 | bytes 2097152 | tf_op jit(solution)/shard_map/accumulate/pallas_call | solution.py:111
  32.8 0.9 %collective-permute-done.9.refs_6_ = bf16[128,2,256]{2,1,0:T(2,128)(2,1)S(1)} collective-permute-done((bf16[128,2,256]{2,1,0:T(2,128)(2,1)S(1)}, bf16[128,2,256]{2,1,0:T(2,128)(2,1)S(1)}, u32[]{:S(2)}, u32[]{:S(2)}) %collective-permute-start.9) | collective-permute-done | bytes 131104 | tf_op jit(solution)/shard_map/ppermute | solution.py:166
  33.7 1.9 %measure.1 = f32[32,128]{1,0:T(8,128)S(1)} custom-call(bf16[2048,256]{1,0:T(8,128)(2,1)S(1)} %get-tuple-element.59.refs_0_, f32[8,128]{1,0:T(8,128)S(1)} %copy-done.2, bf16[304,128]{1,0:T(8,128)(2,1)S(1)} %copy-done.1, bf16[560,128]{1,0:T(8,128)(2,1)S(1)} %collective-permute-done.4.refs_3_.refs_1_, ...), custom_call_target="tpu_custom_call" | custom-call | flops 536870912 | bytes 1048576 | tf_op jit(solution)/shard_map/measure/pallas_call | solution.py:412
  35.6 9.9 %all_to_all.11 = f32[32,1,128]{2,1,0:T(1,128)S(1)} all-to-all(f32[32,1,128]{2,1,0:T(1,128)S(1)} %bitcast.8), channel_id=1, replica_groups=mesh['chol'=8,'walk'=4] {'chol','walk'}, dimensions={0} | all-to-all | bytes 32768 | tf_op jit(solution)/shard_map/all_to_all | solution.py:498
  45.5 1.4 %finish.1 = (f32[1,4]{1,0:T(1,128)}, f32[1,4]{1,0:T(1,128)}, f32[128,128]{1,0:T(8,128)}) custom-call(f32[32,128]{1,0:T(8,128)S(1)} %bitcast.9, s32[4]{0:T(128)S(1)} %copy-done.3, bf16[304,128]{1,0:T(8,128)(2,1)S(1)} %copy-done.1, bf16[560,128]{1,0:T(8,128)(2,1)S(1)} %collective-permute-done.4.refs_3_.refs_1_, ...), custom_call_target="tpu_custom_call" | custom-call | flops 1000000 | bytes 600000 | tf_op jit(solution)/shard_map/finish/pallas_call | solution.py:467
  (18 shorter events, 0.1 us)
Async XLA Ops:
  0.6 13.3 %copy-start = (bf16[256,2,256]{2,1,0:T(2,128)(2,1)S(1)}, bf16[256,2,256]{2,1,0:T(2,128)(2,1)}, u32[]{:S(2)}) copy-start(bf16[256,2,256]{2,1,0:T(2,128)(2,1)} %refs_1_.1) | copy-start | bytes 786436
  0.6 9.5 %collective-permute-start = (bf16[256,2,256]{2,1,0:T(2,128)(2,1)}, bf16[256,2,256]{2,1,0:T(2,128)(2,1)S(1)}, u32[]{:S(2)}, u32[]{:S(2)}) collective-permute-start(bf16[256,2,256]{2,1,0:T(2,128)(2,1)} %refs_1_.1), channel_id=1, source_target_pairs={{0,8},{8,16},{16,24},{24,28},{28,20},{20,12},{12,4},{4,0},{1,9},{9... | collective-permute-start | bytes 786440 | tf_op jit(solution)/shard_map/ppermute | solution.py:146
  3.7 8.3 %collective-permute-start.1 = (bf16[256,2,256]{2,1,0:T(2,128)(2,1)}, bf16[256,2,256]{2,1,0:T(2,128)(2,1)S(1)}, u32[]{:S(2)}, u32[]{:S(2)}) collective-permute-start(bf16[256,2,256]{2,1,0:T(2,128)(2,1)} %refs_1_.1), channel_id=1, source_target_pairs={{0,4},{8,0},{16,8},{24,16},{28,24},{20,28},{12,20},{4,12},{1,5},{9... | collective-permute-start | bytes 786440 | tf_op jit(solution)/shard_map/ppermute | solution.py:146
  10.2 7.9 %collective-permute-start.2 = (bf16[256,2,256]{2,1,0:T(2,128)(2,1)S(1)}, bf16[256,2,256]{2,1,0:T(2,128)(2,1)S(1)}, u32[]{:S(2)}, u32[]{:S(2)}) collective-permute-start(bf16[256,2,256]{2,1,0:T(2,128)(2,1)S(1)} %collective-permute-done.refs_2_), channel_id=1, source_target_pairs={{0,8},{8,16},{16,24},{24,28},{28,20},{20,12},{12,4},{4,0},{1,9},{9... | collective-permute-start | bytes 786440 | tf_op jit(solution)/shard_map/ppermute | solution.py:146
  12.0 6.9 %collective-permute-start.3 = (bf16[256,2,256]{2,1,0:T(2,128)(2,1)S(1)}, bf16[256,2,256]{2,1,0:T(2,128)(2,1)S(1)}, u32[]{:S(2)}, u32[]{:S(2)}) collective-permute-start(bf16[256,2,256]{2,1,0:T(2,128)(2,1)S(1)} %collective-permute-done.1.refs_3_), channel_id=1, source_target_pairs={{0,4},{8,0},{16,8},{24,16},{28,24},{20,28},{12,20},{4,12},{1,5},{9... | collective-permute-start | bytes 786440 | tf_op jit(solution)/shard_map/ppermute | solution.py:146
  12.2 5.8 %collective-permute-start.4 = (bf16[560,128]{1,0:T(8,128)(2,1)}, bf16[560,128]{1,0:T(8,128)(2,1)S(1)}, u32[]{:S(2)}, u32[]{:S(2)}) collective-permute-start(bf16[560,128]{1,0:T(8,128)(2,1)} %get-tuple-element.47), channel_id=1, source_target_pairs={{0,2},{1,3},{2,0},{3,1},{4,6},{5,7},{6,4},{7,5},{8,10},{9,11},{10,... | collective-permute-start | bytes 430088 | tf_op jit(solution)/shard_map/ppermute | solution.py:307
  13.9 7.0 %copy-start.4 = (bf16[304,128]{1,0:T(8,128)(2,1)S(1)}, bf16[304,128]{1,0:T(8,128)(2,1)}, u32[]{:S(2)}) copy-start(bf16[304,128]{1,0:T(8,128)(2,1)} %get-tuple-element.54) | copy-start | bytes 233476
  18.9 6.4 %collective-permute-start.5 = (bf16[256,2,256]{2,1,0:T(2,128)(2,1)S(1)}, bf16[256,2,256]{2,1,0:T(2,128)(2,1)S(1)}, u32[]{:S(2)}, u32[]{:S(2)}) collective-permute-start(bf16[256,2,256]{2,1,0:T(2,128)(2,1)S(1)} %collective-permute-done.2.refs_1_), channel_id=1, source_target_pairs={{0,8},{8,16},{16,24},{24,28},{28,20},{20,12},{12,4},{4,0},{1,9},{9... | collective-permute-start | bytes 786440 | tf_op jit(solution)/shard_map/ppermute | solution.py:146
  20.5 6.4 %collective-permute-start.6 = (bf16[256,2,256]{2,1,0:T(2,128)(2,1)S(1)}, bf16[256,2,256]{2,1,0:T(2,128)(2,1)S(1)}, u32[]{:S(2)}, u32[]{:S(2)}) collective-permute-start(bf16[256,2,256]{2,1,0:T(2,128)(2,1)S(1)} %collective-permute-done.3.refs_2_), channel_id=1, source_target_pairs={{0,4},{8,0},{16,8},{24,16},{28,24},{20,28},{12,20},{4,12},{1,5},{9... | collective-permute-start | bytes 786440 | tf_op jit(solution)/shard_map/ppermute | solution.py:146
  20.9 4.3 %collective-permute-start.7 = (bf16[608,128]{1,0:T(8,128)(2,1)S(1)}, bf16[608,128]{1,0:T(8,128)(2,1)S(1)}, u32[]{:S(2)}, u32[]{:S(2)}) collective-permute-start(bf16[608,128]{1,0:T(8,128)(2,1)S(1)} %pad_maximum_fusion), channel_id=1, source_target_pairs={{0,1},{1,0},{2,3},{3,2},{4,5},{5,4},{6,7},{7,6},{8,9},{9,8},{10,11... | collective-permute-start | bytes 466952 | tf_op jit(solution)/shard_map/ppermute | solution.py:318
  26.9 5.9 %collective-permute-start.8 = (bf16[128,2,256]{2,1,0:T(2,128)(2,1)S(1)}, bf16[128,2,256]{2,1,0:T(2,128)(2,1)S(1)}, u32[]{:S(2)}, u32[]{:S(2)}) collective-permute-start(bf16[128,2,256]{2,1,0:T(2,128)(2,1)S(1)} %slice.10), channel_id=1, source_target_pairs={{0,8},{8,16},{16,24},{24,28},{28,20},{20,12},{12,4},{4,0},{1,9},{9... | collective-permute-start | bytes 393224 | tf_op jit(solution)/shard_map/ppermute | solution.py:166
  28.6 5.0 %collective-permute-start.9 = (bf16[128,2,256]{2,1,0:T(2,128)(2,1)S(1)}, bf16[128,2,256]{2,1,0:T(2,128)(2,1)S(1)}, u32[]{:S(2)}, u32[]{:S(2)}) collective-permute-start(bf16[128,2,256]{2,1,0:T(2,128)(2,1)S(1)} %slice.11), channel_id=1, source_target_pairs={{0,4},{8,0},{16,8},{24,16},{28,24},{20,28},{12,20},{4,12},{1,5},{9... | collective-permute-start | bytes 393224 | tf_op jit(solution)/shard_map/ppermute | solution.py:166
  29.2 4.5 %copy-start.1 = (bf16[304,128]{1,0:T(8,128)(2,1)S(1)}, bf16[304,128]{1,0:T(8,128)(2,1)}, u32[]{:S(2)}) copy-start(bf16[304,128]{1,0:T(8,128)(2,1)} %get-tuple-element.61.refs_2_.refs_0_) | copy-start | bytes 233476
  29.2 4.5 %copy-start.2 = (f32[8,128]{1,0:T(8,128)S(1)}, f32[8,128]{1,0:T(8,128)}, u32[]{:S(2)}) copy-start(f32[8,128]{1,0:T(8,128)} %get-tuple-element.60.refs_1_) | copy-start | bytes 12292
  32.8 12.7 %copy-start.3 = (s32[4]{0:T(128)S(1)}, s32[4]{0:T(128)}, u32[]{:S(2)}) copy-start(s32[4]{0:T(128)} %counts_ref.1) | copy-start | bytes 52

commit v6 on v5

--- a/solution.py
+++ b/solution.py
@@ -42,31 +42,29 @@
 def column_start(shift, rows):
     size = lax.axis_size("chol")
     place = ring_place(lax.axis_index("chol"), size)
+    shift = jnp.where(lax.axis_index("walk") % 2 == 0, shift, -shift)
     owner = ring_owner(lax.rem(place + shift + size, size), size)
     return pl.multiple_of(owner * rows, rows)
 
 
 def start_columns(chol_any, shifts, rows, target, sems):
-    vectors, orbitals, _ = chol_any.shape
-    copies = []
-    for g in range(vectors):
-        for n, shift in enumerate(shifts):
-            copies.append(
-                pltpu.make_async_copy(
-                    chol_any.at[g, :, pl.ds(column_start(shift, rows), rows)],
-                    target.at[pl.ds(g * orbitals, orbitals), pl.ds(n * rows, rows)],
-                    sems.at[g * len(shifts) + n],
-                )
-            )
+    copies = [
+        pltpu.make_async_copy(
+            chol_any.at[:, :, pl.ds(column_start(shift, rows), rows)],
+            target.at[:, :, pl.ds(n * rows, rows)],
+            sems.at[n],
+        )
+        for n, shift in enumerate(shifts)
+    ]
     for copy in copies:
         copy.start()
     return copies
 
 
-def fetch(cholesky_rot, shifts, rows):
+def fetch(cholesky_rot, shifts, rows, mark):
     vectors, orbitals, _ = cholesky_rot.shape
 
-    def kernel(chol_any, blocks_ref, mark_ref, sems):
+    def kernel(chol_any, mark_any, blocks_ref, mark_ref, sems):
         copies = start_columns(chol_any, shifts, rows, blocks_ref, sems)
         mark_ref[...] = jnp.zeros_like(mark_ref)
         for copy in copies:
@@ -76,17 +74,17 @@
         kernel,
         name="fetch",
         out_shape=[
-            jax.ShapeDtypeStruct((vectors * orbitals, len(shifts) * rows), cholesky_rot.dtype),
+            jax.ShapeDtypeStruct((vectors, orbitals, len(shifts) * rows), cholesky_rot.dtype),
             jax.ShapeDtypeStruct((8, LANES), jnp.float32),
         ],
-        in_specs=[pl.BlockSpec(memory_space=pl.ANY)],
+        in_specs=[pl.BlockSpec(memory_space=pl.ANY)] * 2,
         out_specs=[vmem()] * 2,
-        scratch_shapes=[pltpu.SemaphoreType.DMA((vectors * len(shifts),))],
+        scratch_shapes=[pltpu.SemaphoreType.DMA((len(shifts),))],
         compiler_params=params(FETCH_LIMIT),
         cost_estimate=pl.CostEstimate(
             flops=0, bytes_accessed=4 * vectors * orbitals * len(shifts) * rows, transcendentals=0
         ),
-    )(cholesky_rot)
+    )(cholesky_rot, mark)
 
 
 def accumulate(cholesky_rot, blocks, parts, total, mark, ahead):
@@ -103,7 +101,9 @@
         mark_ref[...] = jnp.zeros_like(mark_ref)
         for b in range(walkers):
             rhs = jnp.concatenate([x[:, b, :] for x in shards], axis=0)
-            value = jnp.dot(blocks_ref[...], rhs, preferred_element_type=jnp.float32)
+            value = jnp.dot(
+                blocks_ref[...].reshape(size, -1), rhs, preferred_element_type=jnp.float32
+            )
             total_ref[b] = value if total is None else refs[len(arrays) - 1][b] + value
         for copy in copies:
             copy.wait()
@@ -114,11 +114,11 @@
         out_shape=[
             jax.ShapeDtypeStruct((walkers, size, orbitals), jnp.float32),
             jax.ShapeDtypeStruct((8, LANES), jnp.float32),
-            jax.ShapeDtypeStruct((size, len(ahead) * rows), cholesky_rot.dtype),
+            jax.ShapeDtypeStruct((vectors, orbitals, len(ahead) * rows), cholesky_rot.dtype),
         ],
         in_specs=[pl.BlockSpec(memory_space=pl.ANY)] + [vmem()] * len(arrays),
         out_specs=[vmem()] * 3,
-        scratch_shapes=[pltpu.SemaphoreType.DMA((vectors * len(ahead),))],
+        scratch_shapes=[pltpu.SemaphoreType.DMA((len(ahead),))],
         compiler_params=params(ACCUMULATE_LIMIT),
         cost_estimate=pl.CostEstimate(
             flops=2 * len(parts) * size * rows * walkers * orbitals,
@@ -134,38 +134,47 @@
 
 def ring(own, cholesky_rot, onebody, packed):
     size = lax.axis_size("chol")
+    walk_size = lax.axis_size("walk")
     rows = own.shape[0]
     order = ring_order(size)
-    ahead = [(order[q], order[(q + 1) % size]) for q in range(size)]
-    back = [(order[q], order[(q - 1) % size]) for q in range(size)]
+    pairs = [[], []]
+    for q in range(size):
+        for w in range(walk_size):
+            for n, turn in enumerate((1 - 2 * (w % 2), 2 * (w % 2) - 1)):
+                pairs[n].append((order[q] * walk_size + w, order[(q + turn) % size] * walk_size + w))
+
+    def send(x, n):
+        return lax.ppermute(x, ("chol", "walk"), pairs[n])
+
     steps = size // 2
-    right = left = own
-    parts = [own]
+    one = send(own, 0)
+    other, onebody = tie(own, onebody)
+    other = send(other, 1)
+    blocks, mark = fetch(cholesky_rot, [0, -1, 1], rows, onebody)
+    held = [own]
     total = None
     for step in range(1, steps):
-        next_right, next_left = lax.ppermute(right, "chol", ahead), lax.ppermute(left, "chol", back)
+        final = step == steps - 1
+        one, mark = tie(one, mark)
+        next_one = send(one[: rows // 2] if final else one, 0)
         if step == 1:
-            blocks, mark = fetch(cholesky_rot, [0, -1, 1], rows)
-            right, onebody = tie(next_right, onebody)
-            left, mark, *packed = tie(next_left, mark, *packed)
+            *packed, mark = tie(*packed, mark)
+            far = exchange_far(packed)
         else:
-            total, mark, blocks = accumulate(cholesky_rot, blocks, parts, total, mark, [-step, step])
-            parts = []
-            if step == 2:
-                far = exchange_far(packed)
-                right, mark = tie(next_right, mark)
-                left, far = tie(next_left, far)
-            elif step == 3:
-                near = exchange_near(packed, far)
-                right, mark = tie(next_right, mark)
-                left, *near = tie(next_left, *near)
-            else:
-                right, mark = tie(next_right, mark)
-                left = next_left
-        parts = parts + [right, left]
-    last = [lax.ppermute(right[: rows // 2], "chol", ahead), lax.ppermute(left[rows // 2 :], "chol", back)]
-    total, _, blocks = accumulate(cholesky_rot, blocks, parts, total, mark, [steps])
-    return blocks, onebody, total, last, [packed[0], far] + near
+            total, mark, blocks = accumulate(cholesky_rot, blocks, held, total, mark, [-step, step])
+            held = []
+        if step == 2:
+            other, mark, far = tie(other, mark, far)
+            near = exchange_near(packed, far)
+        elif step == 3:
+            other, mark, *near = tie(other, mark, *near)
+        else:
+            other, mark = tie(other, mark)
+        next_other = send(other[rows // 2 :] if final else other, 1)
+        held = held + [one, other]
+        one, other = next_one, next_other
+    total, _, blocks = accumulate(cholesky_rot, blocks, held, total, mark, [steps])
+    return blocks, onebody, total, [one, other], [packed[0], far] + near
 
 
 def table_height(vectors):
@@ -375,7 +384,9 @@
         squares = [jnp.zeros((1, 1), jnp.float32) for _ in range(walkers)]
         drive = jnp.zeros((1, LANES), jnp.float32)
         for b in range(walkers):
-            value = jnp.dot(block_ref[...], rhs[b], preferred_element_type=jnp.float32)
+            value = jnp.dot(
+                block_ref[...].reshape(vectors * orbitals, depth), rhs[b], preferred_element_type=jnp.float32
+            )
             tensor_scr[b] = value if whole else refs[2 + len(packs) + len(last)][b] + value
         for g in range(vectors):
             top = g * orbitals
@@ -486,7 +497,7 @@
     walkers = green_rows.shape[1]
     onebody, *packed = pack(green_rows, one_body, fields, weights, sources, owners)
     if chol_size > RING_LIMIT or chol_size % 2 or chol_size < 8:
-        block = cholesky_rot.reshape(-1, cholesky_rot.shape[2])
+        block = cholesky_rot
         far = exchange_far(packed)
         packs = [packed[0], far] + exchange_near(packed, far)
         total, last = None, [lax.all_gather(green_rows, "chol", axis=0, tiled=True)]

time: 47.2 us -> 52.8 us (1.12)
  waiting for transfers between devices: 5.1 us -> 7.98 us
  blocking collectives: 9.93 us -> 11.8 us
  Pallas kernels: 19.9 us -> 19.2 us
  starting transfers between devices: 11 us -> 11.7 us
  local copies, waits for them, and re-layouts: 0.21 us -> 0.9 us
    ppermute x8, waiting for transfers between devices: 5.09 us -> 7.98 us  [send(): return lax.ppermute(x, ('chol', 'walk'), pairs[n])]
    all_to_all x1, blocking collectives: 9.93 us -> 11.8 us  [per_device(): lax.all_to_all(stats, ('chol', 'walk'), split_axis=0, concat_axis=0, tile...]
    ppermute x8, starting transfers between devices: 9.27 us -> 10.3 us  [send(): return lax.ppermute(x, ('chol', 'walk'), pairs[n])]
    unnamed x10 -> x14, local copies, waits for them, and re-layouts: 0.02 us -> 0.71 us
  transfers between devices with their start and end apart: 10 -> 10, of which waited for: 5 -> 5; matrix products, arithmetic and copies ran while one was open for 0% -> 0% of each run, Pallas kernels for 35% -> 30%
where the time goes in v6:
time: 52.8 us; the launch traced here: 52.5 us
  Pallas kernels  19.2 us (36%)
  blocking collectives  11.8 us (22%)
  starting transfers between devices  11.7 us (22%)
  waiting for transfers between devices  7.98 us (15%)
  local copies, waits for them, and re-layouts  0.9 us (2%)
  between operations  0.82 us (2%)
    all_to_all x1, blocking collectives, per_device(): lax.all_to_all(stats, ('chol', 'walk'), split_axis=0, concat_axis=0, tile...  11.8 us
    pallas_call x3, Pallas kernels, accumulate(): pl.pallas_call(kernel, name='accumulate', out_shape=[jax.ShapeDtypeStruct...  10.8 us
    ppermute x8, starting transfers between devices, send(): return lax.ppermute(x, ('chol', 'walk'), pairs[n])  10.3 us
    ppermute x8, waiting for transfers between devices, send(): return lax.ppermute(x, ('chol', 'walk'), pairs[n])  7.98 us
    pallas_call x1, Pallas kernels, pack(): pl.pallas_call(kernel, name='pack', out_shape=[jax.ShapeDtypeStruct((8, L...  3.17 us
    pallas_call x1, Pallas kernels, fetch(): pl.pallas_call(kernel, name='fetch', out_shape=[jax.ShapeDtypeStruct((vec...  1.95 us
    pallas_call x1, Pallas kernels, measure(): pl.pallas_call(kernel, name='measure', out_shape=jax.ShapeDtypeStruct((ta...  1.88 us
    pallas_call x1, Pallas kernels, finish(): pl.pallas_call(kernel, name='finish', out_shape=[jax.ShapeDtypeStruct((1,...  1.43 us
  transfers between devices with their start and end apart: 10, of which 5 were waited for; matrix products, arithmetic and copies ran while one was open for 0% of the time, Pallas kernels for 30%

profile of v6, /device:TPU:0, one launch (start us, length us, event | category | flops | bytes accessed | tf_op | source)
XLA Modules:
  0.0 52.5 jit_solution(5218231804237258806)
XLA Ops:
  0.6 3.1 %collective-permute-start = (bf16[256,2,256]{2,1,0:T(2,128)(2,1)}, bf16[256,2,256]{2,1,0:T(2,128)(2,1)S(1)}, u32[]{:S(2)}, u32[]{:S(2)}) collective-permute-start(bf16[256,2,256]{2,1,0:T(2,128)(2,1)} %refs_1_.1), channel_id=1, source_target_pairs={{0,8},{1,5},{2,10},{3,7},{8,16},{9,1},{10,18},{11,3},{16,24},{17,9... | collective-permute-start | bytes 786440 | tf_op jit(solution)/shard_map/ppermute | solution.py:147
  3.7 3.2 %pack.1 = (f32[8,128]{1,0:T(8,128)}, bf16[304,128]{1,0:T(8,128)(2,1)}, bf16[560,128]{1,0:T(8,128)(2,1)}, bf16[304,128]{1,0:T(8,128)(2,1)}) custom-call(bf16[256,2,256]{2,1,0:T(2,128)(2,1)} %refs_1_.1, bf16[256,256]{1,0:T(8,128)(2,1)} %body_any.1, f32[4,8]{1,0:T(4,128)} %bitcast.10, f32[2]{0:T(128)} %weights_any.1, s32[4]{0:T(128)} %sources_any.1, s32[4]{0:T(128)} %owners_any.1), custom_call_target="tpu_custom_call" | custom-call | flops 100000000 | bytes 1000000 | tf_op jit(solution)/shard_map/pack/pallas_call | solution.py:282
  6.9 0.1 collective-permute-start.1
  7.0 0.7 %copy-done.2 = f32[8,128]{1,0:T(8,128)S(1)} copy-done((f32[8,128]{1,0:T(8,128)S(1)}, f32[8,128]{1,0:T(8,128)}, u32[]{:S(2)}) %copy-start.2) | copy-done | bytes 4120
  7.7 2.0 %fetch.1 = (bf16[8,256,768]{2,1,0:T(8,128)(2,1)S(1)}, f32[8,128]{1,0:T(8,128)S(1)}) custom-call(bf16[8,256,2048]{2,1,0:T(8,128)(2,1)} %chol_any.7, f32[8,128]{1,0:T(8,128)S(1)} %copy-done.2), custom_call_target="tpu_custom_call" | custom-call | bytes 6291456 | tf_op jit(solution)/shard_map/fetch/pallas_call | solution.py:73
  9.6 2.1 %collective-permute-start.2 = (bf16[256,2,256]{2,1,0:T(2,128)(2,1)S(1)}, bf16[256,2,256]{2,1,0:T(2,128)(2,1)S(1)}, u32[]{:S(2)}, u32[]{:S(2)}) collective-permute-start(bf16[256,2,256]{2,1,0:T(2,128)(2,1)S(1)} %collective-permute-done.refs_2_), channel_id=1, source_target_pairs={{0,8},{1,5},{2,10},{3,7},{8,16},{9,1},{10,18},{11,3},{16,24},{17,9... | collective-permute-start | bytes 786440 | tf_op jit(solution)/shard_map/ppermute | solution.py:147
  11.7 3.5 %collective-permute-done.1.refs_3_ = bf16[256,2,256]{2,1,0:T(2,128)(2,1)S(1)} collective-permute-done((bf16[256,2,256]{2,1,0:T(2,128)(2,1)}, bf16[256,2,256]{2,1,0:T(2,128)(2,1)S(1)}, u32[]{:S(2)}, u32[]{:S(2)}) %collective-permute-start.1) | collective-permute-done | bytes 262176 | tf_op jit(solution)/shard_map/ppermute | solution.py:147
  15.2 1.3 %collective-permute-start.4 = (bf16[560,128]{1,0:T(8,128)(2,1)S(1)}, bf16[560,128]{1,0:T(8,128)(2,1)S(1)}, u32[]{:S(2)}, u32[]{:S(2)}) collective-permute-start(bf16[560,128]{1,0:T(8,128)(2,1)S(1)} %copy-done.6), channel_id=1, source_target_pairs={{0,2},{1,3},{2,0},{3,1},{4,6},{5,7},{6,4},{7,5},{8,10},{9,11},{10,... | collective-permute-start | bytes 430088 | tf_op jit(solution)/shard_map/ppermute | solution.py:316
  16.5 1.4 %collective-permute-done.2.refs_1_ = bf16[256,2,256]{2,1,0:T(2,128)(2,1)S(1)} collective-permute-done((bf16[256,2,256]{2,1,0:T(2,128)(2,1)S(1)}, bf16[256,2,256]{2,1,0:T(2,128)(2,1)S(1)}, u32[]{:S(2)}, u32[]{:S(2)}) %collective-permute-start.2) | collective-permute-done | bytes 262176 | tf_op jit(solution)/shard_map/ppermute | solution.py:147
  17.9 2.5 %collective-permute-start.5 = (bf16[256,2,256]{2,1,0:T(2,128)(2,1)S(1)}, bf16[256,2,256]{2,1,0:T(2,128)(2,1)S(1)}, u32[]{:S(2)}, u32[]{:S(2)}) collective-permute-start(bf16[256,2,256]{2,1,0:T(2,128)(2,1)S(1)} %collective-permute-done.2.refs_1_), channel_id=1, source_target_pairs={{0,8},{1,5},{2,10},{3,7},{8,16},{9,1},{10,18},{11,3},{16,24},{17,9... | collective-permute-start | bytes 786440 | tf_op jit(solution)/shard_map/ppermute | solution.py:147
  20.4 4.0 %accumulate.3 = (f32[2,2048,256]{2,1,0:T(8,128)S(1)}, f32[8,128]{1,0:T(8,128)S(1)}, bf16[8,256,512]{2,1,0:T(8,128)(2,1)S(1)}) custom-call(bf16[8,256,2048]{2,1,0:T(8,128)(2,1)} %chol_any.7, bf16[8,256,768]{2,1,0:T(8,128)(2,1)S(1)} %get-tuple-element.42.refs_0_, bf16[256,2,256]{2,1,0:T(2,128)(2,1)S(1)} %copy-done, ...), custom_call_target="tpu_custom_call" | custom-call | flops 1610612736 | bytes 4194304 | tf_op jit(solution)/shard_map/accumulate/pallas_call | solution.py:111
  24.4 0.1 collective-permute-start.6
  24.5 0.1 collective-permute-start.7
  24.6 1.6 %collective-permute-done.5.refs_1_ = bf16[256,2,256]{2,1,0:T(2,128)(2,1)S(1)} collective-permute-done((bf16[256,2,256]{2,1,0:T(2,128)(2,1)S(1)}, bf16[256,2,256]{2,1,0:T(2,128)(2,1)S(1)}, u32[]{:S(2)}, u32[]{:S(2)}) %collective-permute-start.5) | collective-permute-done | bytes 262176 | tf_op jit(solution)/shard_map/ppermute | solution.py:147
  26.2 0.1 slice.10
  26.3 2.5 %collective-permute-start.8 = (bf16[128,2,256]{2,1,0:T(2,128)(2,1)S(1)}, bf16[128,2,256]{2,1,0:T(2,128)(2,1)S(1)}, u32[]{:S(2)}, u32[]{:S(2)}) collective-permute-start(bf16[128,2,256]{2,1,0:T(2,128)(2,1)S(1)} %slice.10), channel_id=1, source_target_pairs={{0,8},{1,5},{2,10},{3,7},{8,16},{9,1},{10,18},{11,3},{16,24},{17,9... | collective-permute-start | bytes 393224 | tf_op jit(solution)/shard_map/ppermute | solution.py:147
  28.8 3.3 %accumulate.4 = (f32[2,2048,256]{2,1,0:T(8,128)S(1)}, f32[8,128]{1,0:T(8,128)S(1)}, bf16[8,256,512]{2,1,0:T(8,128)(2,1)S(1)}) custom-call(bf16[8,256,2048]{2,1,0:T(8,128)(2,1)} %chol_any.7, bf16[8,256,512]{2,1,0:T(8,128)(2,1)S(1)} %get-tuple-element.54.refs_0_, bf16[256,2,256]{2,1,0:T(2,128)(2,1)S(1)} %collective-permute-done.2.refs_1_, ...), custom_call_target="tpu_custom_call" | custom-call | flops 1073741824 | bytes 4194304 | tf_op jit(solution)/shard_map/accumulate/pallas_call | solution.py:111
  32.2 0.1 collective-permute-done.6.refs_2_
  32.2 0.1 slice.11
  32.4 3.5 %accumulate.5 = (f32[2,2048,256]{2,1,0:T(8,128)S(1)}, f32[8,128]{1,0:T(8,128)}, bf16[8,256,256]{2,1,0:T(8,128)(2,1)S(1)}) custom-call(bf16[8,256,2048]{2,1,0:T(8,128)(2,1)} %chol_any.7, bf16[8,256,512]{2,1,0:T(8,128)(2,1)S(1)} %get-tuple-element.62.refs_0_, bf16[256,2,256]{2,1,0:T(2,128)(2,1)S(1)} %collective-permute-done.5.refs_1_, ...), custom_call_target="tpu_custom_call" | custom-call | flops 1073741824 | bytes 2097152 | tf_op jit(solution)/shard_map/accumulate/pallas_call | solution.py:111
  35.9 1.4 %collective-permute-done.9.refs_6_ = bf16[128,2,256]{2,1,0:T(2,128)(2,1)S(1)} collective-permute-done((bf16[128,2,256]{2,1,0:T(2,128)(2,1)S(1)}, bf16[128,2,256]{2,1,0:T(2,128)(2,1)S(1)}, u32[]{:S(2)}, u32[]{:S(2)}) %collective-permute-start.9) | collective-permute-done | bytes 131104 | tf_op jit(solution)/shard_map/ppermute | solution.py:147
  37.3 1.9 %measure.1 = f32[32,128]{1,0:T(8,128)S(1)} custom-call(bf16[8,256,256]{2,1,0:T(8,128)(2,1)S(1)} %get-tuple-element.70.refs_0_, f32[8,128]{1,0:T(8,128)S(1)} %copy-done.3, bf16[304,128]{1,0:T(8,128)(2,1)S(1)} %copy-done.1, bf16[560,128]{1,0:T(8,128)(2,1)S(1)} %collective-permute-done.4.refs_3_.refs_1_, ...), custom_call_target="tpu_custom_call" | custom-call | flops 536870912 | bytes 1048576 | tf_op jit(solution)/shard_map/measure/pallas_call | solution.py:423
  39.2 11.8 %all_to_all.11 = f32[32,1,128]{2,1,0:T(1,128)S(1)} all-to-all(f32[32,1,128]{2,1,0:T(1,128)S(1)} %bitcast.8), channel_id=1, replica_groups=mesh['chol'=8,'walk'=4] {'chol','walk'}, dimensions={0} | all-to-all | bytes 32768 | tf_op jit(solution)/shard_map/all_to_all | solution.py:509
  51.0 1.4 %finish.1 = (f32[1,4]{1,0:T(1,128)}, f32[1,4]{1,0:T(1,128)}, f32[128,128]{1,0:T(8,128)}) custom-call(f32[32,128]{1,0:T(8,128)S(1)} %bitcast.9, s32[4]{0:T(128)S(1)} %copy-done.4, bf16[304,128]{1,0:T(8,128)(2,1)S(1)} %copy-done.1, bf16[560,128]{1,0:T(8,128)(2,1)S(1)} %collective-permute-done.4.refs_3_.refs_1_, ...), custom_call_target="tpu_custom_call" | custom-call | flops 1000000 | bytes 600000 | tf_op jit(solution)/shard_map/finish/pallas_call | solution.py:478
  (22 shorter events, 0.1 us)
Async XLA Ops:
  0.6 9.0 %collective-permute-start = (bf16[256,2,256]{2,1,0:T(2,128)(2,1)}, bf16[256,2,256]{2,1,0:T(2,128)(2,1)S(1)}, u32[]{:S(2)}, u32[]{:S(2)}) collective-permute-start(bf16[256,2,256]{2,1,0:T(2,128)(2,1)} %refs_1_.1), channel_id=1, source_target_pairs={{0,8},{1,5},{2,10},{3,7},{8,16},{9,1},{10,18},{11,3},{16,24},{17,9... | collective-permute-start | bytes 786440 | tf_op jit(solution)/shard_map/ppermute | solution.py:147
  6.9 13.5 %copy-start = (bf16[256,2,256]{2,1,0:T(2,128)(2,1)S(1)}, bf16[256,2,256]{2,1,0:T(2,128)(2,1)}, u32[]{:S(2)}) copy-start(bf16[256,2,256]{2,1,0:T(2,128)(2,1)} %refs_1_.1) | copy-start | bytes 786436
  6.9 8.3 %collective-permute-start.1 = (bf16[256,2,256]{2,1,0:T(2,128)(2,1)}, bf16[256,2,256]{2,1,0:T(2,128)(2,1)S(1)}, u32[]{:S(2)}, u32[]{:S(2)}) collective-permute-start(bf16[256,2,256]{2,1,0:T(2,128)(2,1)} %refs_1_.1), channel_id=1, source_target_pairs={{0,4},{1,9},{2,6},{3,11},{8,0},{9,17},{10,2},{11,19},{16,8},{17,25... | collective-permute-start | bytes 786440 | tf_op jit(solution)/shard_map/ppermute | solution.py:147
  7.0 0.7 %copy-start.2 = (f32[8,128]{1,0:T(8,128)S(1)}, f32[8,128]{1,0:T(8,128)}, u32[]{:S(2)}) copy-start(f32[8,128]{1,0:T(8,128)} %get-tuple-element.41.mark_any.refs_1_) | copy-start | bytes 12292
  7.7 7.6 %copy-start.6 = (bf16[560,128]{1,0:T(8,128)(2,1)S(1)}, bf16[560,128]{1,0:T(8,128)(2,1)}, u32[]{:S(2)}) copy-start(bf16[560,128]{1,0:T(8,128)(2,1)} %get-tuple-element.57) | copy-start | bytes 430084
  9.6 8.3 %collective-permute-start.2 = (bf16[256,2,256]{2,1,0:T(2,128)(2,1)S(1)}, bf16[256,2,256]{2,1,0:T(2,128)(2,1)S(1)}, u32[]{:S(2)}, u32[]{:S(2)}) collective-permute-start(bf16[256,2,256]{2,1,0:T(2,128)(2,1)S(1)} %collective-permute-done.refs_2_), channel_id=1, source_target_pairs={{0,8},{1,5},{2,10},{3,7},{8,16},{9,1},{10,18},{11,3},{16,24},{17,9... | collective-permute-start | bytes 786440 | tf_op jit(solution)/shard_map/ppermute | solution.py:147
  15.2 9.1 %collective-permute-start.3 = (bf16[256,2,256]{2,1,0:T(2,128)(2,1)S(1)}, bf16[256,2,256]{2,1,0:T(2,128)(2,1)S(1)}, u32[]{:S(2)}, u32[]{:S(2)}) collective-permute-start(bf16[256,2,256]{2,1,0:T(2,128)(2,1)S(1)} %collective-permute-done.1.refs_3_), channel_id=1, source_target_pairs={{0,4},{1,9},{2,6},{3,11},{8,0},{9,17},{10,2},{11,19},{16,8},{17,25... | collective-permute-start | bytes 786440 | tf_op jit(solution)/shard_map/ppermute | solution.py:147
  15.2 9.1 %collective-permute-start.4 = (bf16[560,128]{1,0:T(8,128)(2,1)S(1)}, bf16[560,128]{1,0:T(8,128)(2,1)S(1)}, u32[]{:S(2)}, u32[]{:S(2)}) collective-permute-start(bf16[560,128]{1,0:T(8,128)(2,1)S(1)} %copy-done.6), channel_id=1, source_target_pairs={{0,2},{1,3},{2,0},{3,1},{4,6},{5,7},{6,4},{7,5},{8,10},{9,11},{10,... | collective-permute-start | bytes 430088 | tf_op jit(solution)/shard_map/ppermute | solution.py:316
  17.9 8.3 %collective-permute-start.5 = (bf16[256,2,256]{2,1,0:T(2,128)(2,1)S(1)}, bf16[256,2,256]{2,1,0:T(2,128)(2,1)S(1)}, u32[]{:S(2)}, u32[]{:S(2)}) collective-permute-start(bf16[256,2,256]{2,1,0:T(2,128)(2,1)S(1)} %collective-permute-done.2.refs_1_), channel_id=1, source_target_pairs={{0,8},{1,5},{2,10},{3,7},{8,16},{9,1},{10,18},{11,3},{16,24},{17,9... | collective-permute-start | bytes 786440 | tf_op jit(solution)/shard_map/ppermute | solution.py:147
  20.4 4.1 %copy-start.5 = (bf16[304,128]{1,0:T(8,128)(2,1)S(1)}, bf16[304,128]{1,0:T(8,128)(2,1)}, u32[]{:S(2)}) copy-start(bf16[304,128]{1,0:T(8,128)(2,1)} %get-tuple-element.65) | copy-start | bytes 233476
  24.4 7.8 %collective-permute-start.6 = (bf16[256,2,256]{2,1,0:T(2,128)(2,1)S(1)}, bf16[256,2,256]{2,1,0:T(2,128)(2,1)S(1)}, u32[]{:S(2)}, u32[]{:S(2)}) collective-permute-start(bf16[256,2,256]{2,1,0:T(2,128)(2,1)S(1)} %collective-permute-done.3.refs_2_), channel_id=1, source_target_pairs={{0,4},{1,9},{2,6},{3,11},{8,0},{9,17},{10,2},{11,19},{16,8},{17,25... | collective-permute-start | bytes 786440 | tf_op jit(solution)/shard_map/ppermute | solution.py:147
  24.5 7.7 %collective-permute-start.7 = (bf16[608,128]{1,0:T(8,128)(2,1)S(1)}, bf16[608,128]{1,0:T(8,128)(2,1)S(1)}, u32[]{:S(2)}, u32[]{:S(2)}) collective-permute-start(bf16[608,128]{1,0:T(8,128)(2,1)S(1)} %pad_maximum_fusion), channel_id=1, source_target_pairs={{0,1},{1,0},{2,3},{3,2},{4,5},{5,4},{6,7},{7,6},{8,9},{9,8},{10,11... | collective-permute-start | bytes 466952 | tf_op jit(solution)/shard_map/ppermute | solution.py:327
  26.3 9.6 %collective-permute-start.8 = (bf16[128,2,256]{2,1,0:T(2,128)(2,1)S(1)}, bf16[128,2,256]{2,1,0:T(2,128)(2,1)S(1)}, u32[]{:S(2)}, u32[]{:S(2)}) collective-permute-start(bf16[128,2,256]{2,1,0:T(2,128)(2,1)S(1)} %slice.10), channel_id=1, source_target_pairs={{0,8},{1,5},{2,10},{3,7},{8,16},{9,1},{10,18},{11,3},{16,24},{17,9... | collective-permute-start | bytes 393224 | tf_op jit(solution)/shard_map/ppermute | solution.py:147
  32.3 5.0 %collective-permute-start.9 = (bf16[128,2,256]{2,1,0:T(2,128)(2,1)S(1)}, bf16[128,2,256]{2,1,0:T(2,128)(2,1)S(1)}, u32[]{:S(2)}, u32[]{:S(2)}) collective-permute-start(bf16[128,2,256]{2,1,0:T(2,128)(2,1)S(1)} %slice.11), channel_id=1, source_target_pairs={{0,4},{1,9},{2,6},{3,11},{8,0},{9,17},{10,2},{11,19},{16,8},{17,25... | collective-permute-start | bytes 393224 | tf_op jit(solution)/shard_map/ppermute | solution.py:147
  32.4 5.0 %copy-start.1 = (bf16[304,128]{1,0:T(8,128)(2,1)S(1)}, bf16[304,128]{1,0:T(8,128)(2,1)}, u32[]{:S(2)}) copy-start(bf16[304,128]{1,0:T(8,128)(2,1)} %get-tuple-element.71.refs_2_.refs_0_) | copy-start | bytes 233476
  32.4 4.9 %copy-start.3 = (f32[8,128]{1,0:T(8,128)S(1)}, f32[8,128]{1,0:T(8,128)}, u32[]{:S(2)}) copy-start(f32[8,128]{1,0:T(8,128)} %get-tuple-element.41.mark_any.refs_1_) | copy-start | bytes 12292
  35.9 15.2 %copy-start.4 = (s32[4]{0:T(128)S(1)}, s32[4]{0:T(128)}, u32[]{:S(2)}) copy-start(s32[4]{0:T(128)} %counts_ref.1) | copy-start | bytes 52

commit v7 on v5

--- a/solution.py
+++ b/solution.py
@@ -10,8 +10,7 @@
 LANES = 128
 VMEM_LIMIT = 16 * 1024 * 1024
 PACK_LIMIT = 54 * 1024 * 1024
-ACCUMULATE_LIMIT = 40 * 1024 * 1024
-FETCH_LIMIT = 48 * 1024 * 1024
+ACCUMULATE_LIMIT = 24 * 1024 * 1024
 RING_LIMIT = 16
 
 
@@ -46,67 +45,23 @@
     return pl.multiple_of(owner * rows, rows)
 
 
-def start_columns(chol_any, shifts, rows, target, sems):
-    vectors, orbitals, _ = chol_any.shape
-    copies = []
-    for g in range(vectors):
-        for n, shift in enumerate(shifts):
-            copies.append(
-                pltpu.make_async_copy(
-                    chol_any.at[g, :, pl.ds(column_start(shift, rows), rows)],
-                    target.at[pl.ds(g * orbitals, orbitals), pl.ds(n * rows, rows)],
-                    sems.at[g * len(shifts) + n],
-                )
-            )
-    for copy in copies:
-        copy.start()
-    return copies
-
-
-def fetch(cholesky_rot, shifts, rows):
-    vectors, orbitals, _ = cholesky_rot.shape
-
-    def kernel(chol_any, blocks_ref, mark_ref, sems):
-        copies = start_columns(chol_any, shifts, rows, blocks_ref, sems)
-        mark_ref[...] = jnp.zeros_like(mark_ref)
-        for copy in copies:
-            copy.wait()
-
-    return pl.pallas_call(
-        kernel,
-        name="fetch",
-        out_shape=[
-            jax.ShapeDtypeStruct((vectors * orbitals, len(shifts) * rows), cholesky_rot.dtype),
-            jax.ShapeDtypeStruct((8, LANES), jnp.float32),
-        ],
-        in_specs=[pl.BlockSpec(memory_space=pl.ANY)],
-        out_specs=[vmem()] * 2,
-        scratch_shapes=[pltpu.SemaphoreType.DMA((vectors * len(shifts),))],
-        compiler_params=params(FETCH_LIMIT),
-        cost_estimate=pl.CostEstimate(
-            flops=0, bytes_accessed=4 * vectors * orbitals * len(shifts) * rows, transcendentals=0
-        ),
-    )(cholesky_rot)
-
-
-def accumulate(cholesky_rot, blocks, parts, total, mark, ahead):
+def accumulate(cholesky_rot, shifts, parts, total, mark):
     vectors, orbitals, _ = cholesky_rot.shape
     rows, walkers, _ = parts[0].shape
     size = vectors * orbitals
-    arrays = [blocks] + list(parts) + [mark] + ([] if total is None else [total])
-
-    def kernel(chol_any, *refs):
-        blocks_ref = refs[0]
-        shards = refs[1 : 1 + len(parts)]
-        total_ref, mark_ref, ahead_ref, sems = refs[len(arrays) :]
-        copies = start_columns(chol_any, ahead, rows, ahead_ref, sems)
+    arrays = list(parts) + ([] if mark is None else [mark]) + ([] if total is None else [total])
+
+    def kernel(chol_ref, *refs):
+        shards = refs[: len(parts)]
+        total_ref, mark_ref = refs[len(arrays) :]
         mark_ref[...] = jnp.zeros_like(mark_ref)
+        lhs = jnp.concatenate(
+            [chol_ref[:, :, pl.ds(column_start(shift, rows), rows)].reshape(size, rows) for shift in shifts], axis=1
+        )
         for b in range(walkers):
             rhs = jnp.concatenate([x[:, b, :] for x in shards], axis=0)
-            value = jnp.dot(blocks_ref[...], rhs, preferred_element_type=jnp.float32)
+            value = jnp.dot(lhs, rhs, preferred_element_type=jnp.float32)
             total_ref[b] = value if total is None else refs[len(arrays) - 1][b] + value
-        for copy in copies:
-            copy.wait()
 
     return pl.pallas_call(
         kernel,
@@ -114,15 +69,13 @@
         out_shape=[
             jax.ShapeDtypeStruct((walkers, size, orbitals), jnp.float32),
             jax.ShapeDtypeStruct((8, LANES), jnp.float32),
-            jax.ShapeDtypeStruct((size, len(ahead) * rows), cholesky_rot.dtype),
         ],
-        in_specs=[pl.BlockSpec(memory_space=pl.ANY)] + [vmem()] * len(arrays),
-        out_specs=[vmem()] * 3,
-        scratch_shapes=[pltpu.SemaphoreType.DMA((vectors * len(ahead),))],
+        in_specs=[vmem()] * (1 + len(arrays)),
+        out_specs=[vmem()] * 2,
         compiler_params=params(ACCUMULATE_LIMIT),
         cost_estimate=pl.CostEstimate(
             flops=2 * len(parts) * size * rows * walkers * orbitals,
-            bytes_accessed=4 * len(ahead) * size * rows,
+            bytes_accessed=2 * len(parts) * size * rows,
             transcendentals=0,
         ),
     )(cholesky_rot, *arrays)
@@ -140,39 +93,39 @@
     back = [(order[q], order[(q - 1) % size]) for q in range(size)]
     steps = size // 2
     right = left = own
-    parts = [own]
-    total = None
+    shifts, parts = [0], [own]
+    total = mark = None
     for step in range(1, steps):
         next_right, next_left = lax.ppermute(right, "chol", ahead), lax.ppermute(left, "chol", back)
         if step == 1:
-            blocks, mark = fetch(cholesky_rot, [0, -1, 1], rows)
             right, onebody = tie(next_right, onebody)
-            left, mark, *packed = tie(next_left, mark, *packed)
+            left, *packed = tie(next_left, *packed)
+        elif step == 2:
+            far = exchange_far(packed)
+            right = next_right
+            left, far = tie(next_left, far)
         else:
-            total, mark, blocks = accumulate(cholesky_rot, blocks, parts, total, mark, [-step, step])
-            parts = []
-            if step == 2:
-                far = exchange_far(packed)
-                right, mark = tie(next_right, mark)
-                left, far = tie(next_left, far)
-            elif step == 3:
+            if step == 3:
                 near = exchange_near(packed, far)
-                right, mark = tie(next_right, mark)
-                left, *near = tie(next_left, *near)
+            total, mark = accumulate(cholesky_rot, shifts[:-2], parts[:-2], total, mark)
+            shifts, parts = shifts[-2:], parts[-2:]
+            right, mark = tie(next_right, mark)
+            if step == 3:
+                left, mark, *near = tie(next_left, mark, *near)
             else:
-                right, mark = tie(next_right, mark)
-                left = next_left
+                left, mark = tie(next_left, mark)
+        shifts += [-step, step]
         parts = parts + [right, left]
     last = [lax.ppermute(right[: rows // 2], "chol", ahead), lax.ppermute(left[rows // 2 :], "chol", back)]
-    total, _, blocks = accumulate(cholesky_rot, blocks, parts, total, mark, [steps])
-    return blocks, onebody, total, last, [packed[0], far] + near
+    total, _ = accumulate(cholesky_rot, shifts, parts, total, mark)
+    return onebody, total, last, [packed[0], far] + near
 
 
 def table_height(vectors):
     return -(-(vectors + 2) // 16) * 16
 
 
-def pack(own, one_body, fields, weights, sources, owners):
+def pack(own, one_body, fields, weights, sources, owners, cholesky_rot):
     rows, walkers, orbitals = own.shape
     walk_size = lax.axis_size("walk")
     width = orbitals // walk_size
@@ -188,7 +141,7 @@
         heights = [both] * walk_size
         spots = [(d, 0) for d in range(walk_size)]
 
-    def kernel(own_any, body_any, fields_any, weights_any, sources_any, owners_any, *refs):
+    def kernel(own_any, body_any, fields_any, weights_any, sources_any, owners_any, chol_any, *refs):
         onebody_ref = refs[0]
         packs = refs[1 : 1 + len(heights)]
         own_ref, body_ref, fields_ref, weights_ref, sources_ref, owners_ref, table_scr, sems = refs[1 + len(heights) :]
@@ -277,7 +230,7 @@
             jax.ShapeDtypeStruct((8, LANES), jnp.float32),
         ]
         + [jax.ShapeDtypeStruct((height, LANES), jnp.bfloat16) for height in heights],
-        in_specs=[pl.BlockSpec(memory_space=pl.ANY)] * 6,
+        in_specs=[pl.BlockSpec(memory_space=pl.ANY)] * 7,
         out_specs=[vmem()] * (len(heights) + 1),
         scratch_shapes=[
             pltpu.VMEM(own.shape, own.dtype),
@@ -291,7 +244,7 @@
         ],
         compiler_params=params(PACK_LIMIT),
         cost_estimate=pl.CostEstimate(flops=10**8, bytes_accessed=10**6, transcendentals=0),
-    )(own, one_body, fields.T, weights, sources, owners)
+    )(own, one_body, fields.T, weights, sources, owners, cholesky_rot)
 
 
 def walk_partner(walk, d, size, back):
@@ -338,7 +291,7 @@
     return total
 
 
-def measure(block, total, last, packs, places, onebody, vectors, slots):
+def measure(cholesky_rot, total, last, packs, places, onebody, vectors, slots):
     _, walkers, orbitals = last[0].shape
     depth = sum(x.shape[0] for x in last)
     walk_size = len(places)
@@ -350,7 +303,7 @@
         return jnp.sum(x.reshape(-1, 8, LANES), axis=0)
 
     def kernel(*refs):
-        block_ref, onebody_ref = refs[:2]
+        chol_ref, onebody_ref = refs[:2]
         pack_refs = refs[2 : 2 + len(packs)]
         last_refs = refs[2 + len(packs) : 2 + len(packs) + len(last)]
         out_ref, tensor_scr = refs[-2:]
@@ -374,8 +327,10 @@
         exchange = [jnp.zeros((8, LANES), jnp.float32) for _ in range(walkers)]
         squares = [jnp.zeros((1, 1), jnp.float32) for _ in range(walkers)]
         drive = jnp.zeros((1, LANES), jnp.float32)
+        start = 0 if whole else column_start(lax.axis_size("chol") // 2, depth)
+        lhs = chol_ref[:, :, pl.ds(start, depth)].reshape(vectors * orbitals, depth)
         for b in range(walkers):
-            value = jnp.dot(block_ref[...], rhs[b], preferred_element_type=jnp.float32)
+            value = jnp.dot(lhs, rhs[b], preferred_element_type=jnp.float32)
             tensor_scr[b] = value if whole else refs[2 + len(packs) + len(last)][b] + value
         for g in range(vectors):
             top = g * orbitals
@@ -424,7 +379,7 @@
             bytes_accessed=2 * vectors * orbitals * depth,
             transcendentals=0,
         ),
-    )(block, onebody, *packs, *arrays)
+    )(cholesky_rot, onebody, *packs, *arrays)
 
 
 def finish(stats, packs, places, counts, vectors, slots, walkers):
@@ -484,17 +439,16 @@
     walk_size = lax.axis_size("walk")
     vectors, slots = fields.shape
     walkers = green_rows.shape[1]
-    onebody, *packed = pack(green_rows, one_body, fields, weights, sources, owners)
+    onebody, *packed = pack(green_rows, one_body, fields, weights, sources, owners, cholesky_rot)
     if chol_size > RING_LIMIT or chol_size % 2 or chol_size < 8:
-        block = cholesky_rot.reshape(-1, cholesky_rot.shape[2])
         far = exchange_far(packed)
         packs = [packed[0], far] + exchange_near(packed, far)
         total, last = None, [lax.all_gather(green_rows, "chol", axis=0, tiled=True)]
     else:
-        block, onebody, total, last, packs = ring(green_rows, cholesky_rot, onebody, packed)
+        onebody, total, last, packs = ring(green_rows, cholesky_rot, onebody, packed)
     table = 3 * table_height(vectors)
     places = walk_places(packs[0].shape[0] - table, table, walk_size)
-    stats = measure(block, total, last, packs, places, onebody, vectors, slots)
+    stats = measure(cholesky_rot, total, last, packs, places, onebody, vectors, slots)
     stats = lax.all_to_all(stats, ("chol", "walk"), split_axis=0, concat_axis=0, tiled=True)
     energies, new_weights, density = finish(stats, packs, places, counts, vectors, slots, walkers)
     return energies.reshape(slots), new_weights.reshape(slots), density.reshape(1, density.size)

time: 47.2 us -> 47.8 us (1.013)
  Pallas kernels: 19.9 us -> 13 us
  waiting for transfers between devices: 5.1 us -> 9.39 us
  blocking collectives: 9.93 us -> 12.3 us
  other arithmetic: 0.01 us -> 0.9 us
    ppermute x3, starting transfers between devices: 0.7 us -> 6.29 us  [ring(): lax.ppermute(left, 'chol', back)]
    ppermute x3, starting transfers between devices: 6.44 us -> 0.91 us  [ring(): lax.ppermute(right, 'chol', ahead)]
    pallas_call x3 -> x2, Pallas kernels: 11.3 us -> 6.35 us  [accumulate(): pl.pallas_call(kernel, name='accumulate', out_shape=[jax.ShapeDtypeStruct...]
    ppermute x1, waiting for transfers between devices: 0.01 us -> 3.65 us  [exchange_far(): return lax.ppermute(packed[1], 'walk', [(q, q ^ 2) for q in range(size)])]
    all_to_all x1, blocking collectives: 9.93 us -> 12.3 us  [per_device(): lax.all_to_all(stats, ('chol', 'walk'), split_axis=0, concat_axis=0, tile...]
    pallas_call x1 -> x0, Pallas kernels: 2.17 us -> none  [fetch(): pl.pallas_call(kernel, name='fetch', out_shape=[jax.ShapeDtypeStruct((vec...]
    ppermute x1, starting transfers between devices: 1.63 us -> 0.5 us  [ring(): lax.ppermute(right[:rows // 2], 'chol', ahead)]
    ppermute x1, starting transfers between devices: 0.5 us -> 1.58 us  [ring(): lax.ppermute(left[rows // 2:], 'chol', back)]
  transfers between devices with their start and end apart: 10 -> 10, of which waited for: 5 -> 4; matrix products, arithmetic and copies ran while one was open for 0% -> 2% of each run, Pallas kernels for 35% -> 20%
where the time goes in v7:
time: 47.8 us; the launch traced here: 47.6 us
  Pallas kernels  13 us (27%)
  blocking collectives  12.3 us (26%)
  starting transfers between devices  11 us (23%)
  waiting for transfers between devices  9.39 us (20%)
  other arithmetic  0.9 us (2%)
  between operations  0.72 us (2%)
    all_to_all x1, blocking collectives, per_device(): lax.all_to_all(stats, ('chol', 'walk'), split_axis=0, concat_axis=0, tile...  12.3 us
    pallas_call x2, Pallas kernels, accumulate(): pl.pallas_call(kernel, name='accumulate', out_shape=[jax.ShapeDtypeStruct...  6.35 us
    ppermute x3, starting transfers between devices, ring(): lax.ppermute(left, 'chol', back)  6.29 us
    ppermute x1, waiting for transfers between devices, exchange_far(): return lax.ppermute(packed[1], 'walk', [(q, q ^ 2) for q in range(size)])  3.65 us
    pallas_call x1, Pallas kernels, pack(): pl.pallas_call(kernel, name='pack', out_shape=[jax.ShapeDtypeStruct((8, L...  3.32 us
    ppermute x3, waiting for transfers between devices, ring(): lax.ppermute(left, 'chol', back)  3.27 us
    ppermute x3, waiting for transfers between devices, ring(): lax.ppermute(right, 'chol', ahead)  2.45 us
    pallas_call x1, Pallas kernels, measure(): pl.pallas_call(kernel, name='measure', out_shape=jax.ShapeDtypeStruct((ta...  1.93 us
  transfers between devices with their start and end apart: 10, of which 4 were waited for; matrix products, arithmetic and copies ran while one was open for 2% of the time, Pallas kernels for 20%

profile of v7, /device:TPU:0, one launch (start us, length us, event | category | flops | bytes accessed | tf_op | source)
XLA Modules:
  0.0 47.6 jit_solution(3954880964813941291)
XLA Ops:
  0.6 3.0 %collective-permute-start.1 = (bf16[256,2,256]{2,1,0:T(2,128)(2,1)}, bf16[256,2,256]{2,1,0:T(2,128)(2,1)S(1)}, u32[]{:S(2)}, u32[]{:S(2)}) collective-permute-start(bf16[256,2,256]{2,1,0:T(2,128)(2,1)} %refs_0_.2), channel_id=1, source_target_pairs={{0,4},{8,0},{16,8},{24,16},{28,24},{20,28},{12,20},{4,12},{1,5},{9... | collective-permute-start | bytes 786440 | tf_op jit(solution)/shard_map/ppermute | solution.py:99
  3.7 0.1 collective-permute-start
  3.8 3.3 %pack.1 = (f32[8,128]{1,0:T(8,128)}, bf16[304,128]{1,0:T(8,128)(2,1)}, bf16[560,128]{1,0:T(8,128)(2,1)}, bf16[304,128]{1,0:T(8,128)(2,1)}) custom-call(bf16[256,2,256]{2,1,0:T(2,128)(2,1)} %refs_0_.2, bf16[256,256]{1,0:T(8,128)(2,1)} %body_any.1, f32[4,8]{1,0:T(4,128)} %bitcast.10, f32[2]{0:T(128)} %weights_any.1, s32[4]{0:T(128)} %sources_any.1, ...), custom_call_target="tpu_custom_call" | custom-call | flops 100000000 | bytes 1000000 | tf_op jit(solution)/shard_map/pack/pallas_call | solution.py:226
  7.1 3.1 %collective-permute-done.1.refs_2_ = bf16[256,2,256]{2,1,0:T(2,128)(2,1)S(1)} collective-permute-done((bf16[256,2,256]{2,1,0:T(2,128)(2,1)}, bf16[256,2,256]{2,1,0:T(2,128)(2,1)S(1)}, u32[]{:S(2)}, u32[]{:S(2)}) %collective-permute-start.1) | collective-permute-done | bytes 262176 | tf_op jit(solution)/shard_map/ppermute | solution.py:99
  10.2 1.7 %collective-permute-start.2 = (bf16[256,2,256]{2,1,0:T(2,128)(2,1)S(1)}, bf16[256,2,256]{2,1,0:T(2,128)(2,1)S(1)}, u32[]{:S(2)}, u32[]{:S(2)}) collective-permute-start(bf16[256,2,256]{2,1,0:T(2,128)(2,1)S(1)} %collective-permute-done.1.refs_2_), channel_id=1, source_target_pairs={{0,4},{8,0},{16,8},{24,16},{28,24},{20,28},{12,20},{4,12},{1,5},{9... | collective-permute-start | bytes 786440 | tf_op jit(solution)/shard_map/ppermute | solution.py:99
  11.9 0.3 collective-permute-start.5
  12.3 1.7 %collective-permute-start.3 = (bf16[560,128]{1,0:T(8,128)(2,1)}, bf16[560,128]{1,0:T(8,128)(2,1)S(1)}, u32[]{:S(2)}, u32[]{:S(2)}) collective-permute-start(bf16[560,128]{1,0:T(8,128)(2,1)} %get-tuple-element.33), channel_id=1, source_target_pairs={{0,2},{1,3},{2,0},{3,1},{4,6},{5,7},{6,4},{7,5},{8,10},{9,11},{10,... | collective-permute-start | bytes 430088 | tf_op jit(solution)/shard_map/ppermute | solution.py:260
  13.9 3.7 %collective-permute-done.3.refs_3_.refs_1_ = bf16[560,128]{1,0:T(8,128)(2,1)S(1)} collective-permute-done((bf16[560,128]{1,0:T(8,128)(2,1)}, bf16[560,128]{1,0:T(8,128)(2,1)S(1)}, u32[]{:S(2)}, u32[]{:S(2)}) %collective-permute-start.3) | collective-permute-done | bytes 143392 | tf_op jit(solution)/shard_map/ppermute | solution.py:260
  17.6 0.2 collective-permute-done.2.refs_1_
  17.7 1.6 %collective-permute-start.4 = (bf16[256,2,256]{2,1,0:T(2,128)(2,1)S(1)}, bf16[256,2,256]{2,1,0:T(2,128)(2,1)S(1)}, u32[]{:S(2)}, u32[]{:S(2)}) collective-permute-start(bf16[256,2,256]{2,1,0:T(2,128)(2,1)S(1)} %collective-permute-done.2.refs_1_), channel_id=1, source_target_pairs={{0,4},{8,0},{16,8},{24,16},{28,24},{20,28},{12,20},{4,12},{1,5},{9... | collective-permute-start | bytes 786440 | tf_op jit(solution)/shard_map/ppermute | solution.py:99
  19.3 0.4 collective-permute-start.6
  19.8 0.9 %pad_maximum_fusion = bf16[608,128]{1,0:T(8,128)(2,1)S(1)} fusion(bf16[304,128]{1,0:T(8,128)(2,1)S(1)} %slice.9, bf16[304,128]{1,0:T(8,128)(2,1)} %get-tuple-element.39), kind=kLoop, calls=%fused_computation | loop fusion | flops 311296 | bytes 311296 | tf_op jit(solution)/shard_map/concatenate | solution.py:271
  20.7 0.1 collective-permute-start.7
  20.8 2.5 %accumulate.2 = (f32[2,2048,256]{2,1,0:T(8,128)S(1)}, f32[8,128]{1,0:T(8,128)S(1)}) custom-call(bf16[8,256,2048]{2,1,0:T(8,128)(2,1)S(1)} %copy-done, bf16[256,2,256]{2,1,0:T(2,128)(2,1)S(1)} %copy-done.1, bf16[256,2,256]{2,1,0:T(2,128)(2,1)S(1)} %collective-permute-done.refs_1_, bf16[256,2,256]{2,1,0:T(2,128)(2,1)S(1)} %collective-permute-done.1.refs_2_), custom_call_target="tpu_custom_call" | custom-call | flops 1610612736 | bytes 3145728 | tf_op jit(solution)/shard_map/accumulate/pallas_call | solution.py:66
  23.2 2.4 %collective-permute-done.6.refs_2_ = bf16[256,2,256]{2,1,0:T(2,128)(2,1)S(1)} collective-permute-done((bf16[256,2,256]{2,1,0:T(2,128)(2,1)S(1)}, bf16[256,2,256]{2,1,0:T(2,128)(2,1)S(1)}, u32[]{:S(2)}, u32[]{:S(2)}) %collective-permute-start.6) | collective-permute-done | bytes 262176 | tf_op jit(solution)/shard_map/ppermute | solution.py:99
  25.7 0.1 slice.11
  25.8 0.1 slice.10
  25.9 0.5 %collective-permute-start.8 = (bf16[128,2,256]{2,1,0:T(2,128)(2,1)S(1)}, bf16[128,2,256]{2,1,0:T(2,128)(2,1)S(1)}, u32[]{:S(2)}, u32[]{:S(2)}) collective-permute-start(bf16[128,2,256]{2,1,0:T(2,128)(2,1)S(1)} %slice.10), channel_id=1, source_target_pairs={{0,8},{8,16},{16,24},{24,28},{28,20},{20,12},{12,4},{4,0},{1,9},{9... | collective-permute-start | bytes 393224 | tf_op jit(solution)/shard_map/ppermute | solution.py:119
  26.4 1.6 %collective-permute-start.9 = (bf16[128,2,256]{2,1,0:T(2,128)(2,1)S(1)}, bf16[128,2,256]{2,1,0:T(2,128)(2,1)S(1)}, u32[]{:S(2)}, u32[]{:S(2)}) collective-permute-start(bf16[128,2,256]{2,1,0:T(2,128)(2,1)S(1)} %slice.11), channel_id=1, source_target_pairs={{0,4},{8,0},{16,8},{24,16},{28,24},{20,28},{12,20},{4,12},{1,5},{9... | collective-permute-start | bytes 393224 | tf_op jit(solution)/shard_map/ppermute | solution.py:119
  28.0 3.9 %accumulate.3 = (f32[2,2048,256]{2,1,0:T(8,128)S(1)}, f32[8,128]{1,0:T(8,128)}) custom-call(bf16[8,256,2048]{2,1,0:T(8,128)(2,1)S(1)} %copy-done, bf16[256,2,256]{2,1,0:T(2,128)(2,1)S(1)} %collective-permute-done.5.refs_0_, bf16[256,2,256]{2,1,0:T(2,128)(2,1)S(1)} %collective-permute-done.2.refs_1_, bf16[256,2,256]{2,1,0:T(2,128)(2,1)S(1)} %collective-permute-done.6.refs_2_, ...), custom_call_target="tpu_custom_call" | custom-call | flops 2147483648 | bytes 4194304 | tf_op jit(solution)/shard_map/accumulate/pallas_call | solution.py:66
  31.9 0.0 copy-start.4
  31.9 1.9 %measure.1 = f32[32,128]{1,0:T(8,128)S(1)} custom-call(bf16[8,256,2048]{2,1,0:T(8,128)(2,1)S(1)} %copy-done, f32[8,128]{1,0:T(8,128)S(1)} %copy-done.3, bf16[304,128]{1,0:T(8,128)(2,1)S(1)} %copy-done.2, bf16[560,128]{1,0:T(8,128)(2,1)S(1)} %collective-permute-done.3.refs_3_.refs_1_, bf16[608,128]{1,0:T(8,128)(2,1)S(1)} %collective-permute-done.7.refs_4_.refs_2_, ...), custom_call_target="tpu_custom_call" | custom-call | flops 536870912 | bytes 1048576 | tf_op jit(solution)/shard_map/measure/pallas_call | solution.py:367
  33.8 12.3 %all_to_all.11 = f32[32,1,128]{2,1,0:T(1,128)S(1)} all-to-all(f32[32,1,128]{2,1,0:T(1,128)S(1)} %bitcast.8), channel_id=1, replica_groups=mesh['chol'=8,'walk'=4] {'chol','walk'}, dimensions={0} | all-to-all | bytes 32768 | tf_op jit(solution)/shard_map/all_to_all | solution.py:452
  46.1 1.4 %finish.1 = (f32[1,4]{1,0:T(1,128)}, f32[1,4]{1,0:T(1,128)}, f32[128,128]{1,0:T(8,128)}) custom-call(f32[32,128]{1,0:T(8,128)S(1)} %bitcast.9, s32[4]{0:T(128)S(1)} %copy-done.4, bf16[304,128]{1,0:T(8,128)(2,1)S(1)} %copy-done.2, bf16[560,128]{1,0:T(8,128)(2,1)S(1)} %collective-permute-done.3.refs_3_.refs_1_, ...), custom_call_target="tpu_custom_call" | custom-call | flops 1000000 | bytes 600000 | tf_op jit(solution)/shard_map/finish/pallas_call | solution.py:422
  (16 shorter events, 0.0 us)
Async XLA Ops:
  0.6 9.6 %collective-permute-start.1 = (bf16[256,2,256]{2,1,0:T(2,128)(2,1)}, bf16[256,2,256]{2,1,0:T(2,128)(2,1)S(1)}, u32[]{:S(2)}, u32[]{:S(2)}) collective-permute-start(bf16[256,2,256]{2,1,0:T(2,128)(2,1)} %refs_0_.2), channel_id=1, source_target_pairs={{0,4},{8,0},{16,8},{24,16},{28,24},{20,28},{12,20},{4,12},{1,5},{9... | collective-permute-start | bytes 786440 | tf_op jit(solution)/shard_map/ppermute | solution.py:99
  3.7 8.3 %collective-permute-start = (bf16[256,2,256]{2,1,0:T(2,128)(2,1)}, bf16[256,2,256]{2,1,0:T(2,128)(2,1)S(1)}, u32[]{:S(2)}, u32[]{:S(2)}) collective-permute-start(bf16[256,2,256]{2,1,0:T(2,128)(2,1)} %refs_0_.2), channel_id=1, source_target_pairs={{0,8},{8,16},{16,24},{24,28},{28,20},{20,12},{12,4},{4,0},{1,9},{9... | collective-permute-start | bytes 786440 | tf_op jit(solution)/shard_map/ppermute | solution.py:99
  3.8 17.0 %copy-start = (bf16[8,256,2048]{2,1,0:T(8,128)(2,1)S(1)}, bf16[8,256,2048]{2,1,0:T(8,128)(2,1)}, u32[]{:S(2)}) copy-start(bf16[8,256,2048]{2,1,0:T(8,128)(2,1)} %refs_0_.3) | copy-start | bytes 25165828
  3.8 17.0 %copy-start.1 = (bf16[256,2,256]{2,1,0:T(2,128)(2,1)S(1)}, bf16[256,2,256]{2,1,0:T(2,128)(2,1)}, u32[]{:S(2)}) copy-start(bf16[256,2,256]{2,1,0:T(2,128)(2,1)} %refs_0_.2) | copy-start | bytes 786436
  10.2 7.5 %collective-permute-start.2 = (bf16[256,2,256]{2,1,0:T(2,128)(2,1)S(1)}, bf16[256,2,256]{2,1,0:T(2,128)(2,1)S(1)}, u32[]{:S(2)}, u32[]{:S(2)}) collective-permute-start(bf16[256,2,256]{2,1,0:T(2,128)(2,1)S(1)} %collective-permute-done.1.refs_2_), channel_id=1, source_target_pairs={{0,4},{8,0},{16,8},{24,16},{28,24},{20,28},{12,20},{4,12},{1,5},{9... | collective-permute-start | bytes 786440 | tf_op jit(solution)/shard_map/ppermute | solution.py:99
  11.9 7.4 %collective-permute-start.5 = (bf16[256,2,256]{2,1,0:T(2,128)(2,1)S(1)}, bf16[256,2,256]{2,1,0:T(2,128)(2,1)S(1)}, u32[]{:S(2)}, u32[]{:S(2)}) collective-permute-start(bf16[256,2,256]{2,1,0:T(2,128)(2,1)S(1)} %collective-permute-done.refs_1_), channel_id=1, source_target_pairs={{0,8},{8,16},{16,24},{24,28},{28,20},{20,12},{12,4},{4,0},{1,9},{9... | collective-permute-start | bytes 786440 | tf_op jit(solution)/shard_map/ppermute | solution.py:99
  12.3 5.3 %collective-permute-start.3 = (bf16[560,128]{1,0:T(8,128)(2,1)}, bf16[560,128]{1,0:T(8,128)(2,1)S(1)}, u32[]{:S(2)}, u32[]{:S(2)}) collective-permute-start(bf16[560,128]{1,0:T(8,128)(2,1)} %get-tuple-element.33), channel_id=1, source_target_pairs={{0,2},{1,3},{2,0},{3,1},{4,6},{5,7},{6,4},{7,5},{8,10},{9,11},{10,... | collective-permute-start | bytes 430088 | tf_op jit(solution)/shard_map/ppermute | solution.py:260
  17.7 8.0 %collective-permute-start.4 = (bf16[256,2,256]{2,1,0:T(2,128)(2,1)S(1)}, bf16[256,2,256]{2,1,0:T(2,128)(2,1)S(1)}, u32[]{:S(2)}, u32[]{:S(2)}) collective-permute-start(bf16[256,2,256]{2,1,0:T(2,128)(2,1)S(1)} %collective-permute-done.2.refs_1_), channel_id=1, source_target_pairs={{0,4},{8,0},{16,8},{24,16},{28,24},{20,28},{12,20},{4,12},{1,5},{9... | collective-permute-start | bytes 786440 | tf_op jit(solution)/shard_map/ppermute | solution.py:99
  19.3 6.4 %collective-permute-start.6 = (bf16[256,2,256]{2,1,0:T(2,128)(2,1)S(1)}, bf16[256,2,256]{2,1,0:T(2,128)(2,1)S(1)}, u32[]{:S(2)}, u32[]{:S(2)}) collective-permute-start(bf16[256,2,256]{2,1,0:T(2,128)(2,1)S(1)} %collective-permute-done.5.refs_0_), channel_id=1, source_target_pairs={{0,8},{8,16},{16,24},{24,28},{28,20},{20,12},{12,4},{4,0},{1,9},{9... | collective-permute-start | bytes 786440 | tf_op jit(solution)/shard_map/ppermute | solution.py:99
  20.7 5.0 %collective-permute-start.7 = (bf16[608,128]{1,0:T(8,128)(2,1)S(1)}, bf16[608,128]{1,0:T(8,128)(2,1)S(1)}, u32[]{:S(2)}, u32[]{:S(2)}) collective-permute-start(bf16[608,128]{1,0:T(8,128)(2,1)S(1)} %pad_maximum_fusion), channel_id=1, source_target_pairs={{0,1},{1,0},{2,3},{3,2},{4,5},{5,4},{6,7},{7,6},{8,9},{9,8},{10,11... | collective-permute-start | bytes 466952 | tf_op jit(solution)/shard_map/ppermute | solution.py:271
  25.9 6.0 %collective-permute-start.8 = (bf16[128,2,256]{2,1,0:T(2,128)(2,1)S(1)}, bf16[128,2,256]{2,1,0:T(2,128)(2,1)S(1)}, u32[]{:S(2)}, u32[]{:S(2)}) collective-permute-start(bf16[128,2,256]{2,1,0:T(2,128)(2,1)S(1)} %slice.10), channel_id=1, source_target_pairs={{0,8},{8,16},{16,24},{24,28},{28,20},{20,12},{12,4},{4,0},{1,9},{9... | collective-permute-start | bytes 393224 | tf_op jit(solution)/shard_map/ppermute | solution.py:119
  26.4 5.5 %collective-permute-start.9 = (bf16[128,2,256]{2,1,0:T(2,128)(2,1)S(1)}, bf16[128,2,256]{2,1,0:T(2,128)(2,1)S(1)}, u32[]{:S(2)}, u32[]{:S(2)}) collective-permute-start(bf16[128,2,256]{2,1,0:T(2,128)(2,1)S(1)} %slice.11), channel_id=1, source_target_pairs={{0,4},{8,0},{16,8},{24,16},{28,24},{20,28},{12,20},{4,12},{1,5},{9... | collective-permute-start | bytes 393224 | tf_op jit(solution)/shard_map/ppermute | solution.py:119
  28.0 3.9 %copy-start.2 = (bf16[304,128]{1,0:T(8,128)(2,1)S(1)}, bf16[304,128]{1,0:T(8,128)(2,1)}, u32[]{:S(2)}) copy-start(bf16[304,128]{1,0:T(8,128)(2,1)} %get-tuple-element.31.refs_2_.refs_0_) | copy-start | bytes 233476
  28.0 3.9 %copy-start.3 = (f32[8,128]{1,0:T(8,128)S(1)}, f32[8,128]{1,0:T(8,128)}, u32[]{:S(2)}) copy-start(f32[8,128]{1,0:T(8,128)} %get-tuple-element.27.refs_1_) | copy-start | bytes 12292
  31.9 14.3 %copy-start.4 = (s32[4]{0:T(128)S(1)}, s32[4]{0:T(128)}, u32[]{:S(2)}) copy-start(s32[4]{0:T(128)} %counts_ref.1) | copy-start | bytes 52

commit v8 on v7

--- a/solution.py
+++ b/solution.py
@@ -87,38 +87,35 @@
 
 def ring(own, cholesky_rot, onebody, packed):
     size = lax.axis_size("chol")
-    rows = own.shape[0]
     order = ring_order(size)
-    ahead = [(order[q], order[(q + 1) % size]) for q in range(size)]
-    back = [(order[q], order[(q - 1) % size]) for q in range(size)]
-    steps = size // 2
-    right = left = own
-    shifts, parts = [0], [own]
+
+    def send(x, places):
+        return lax.ppermute(x, "chol", [(order[q], order[(q + places) % size]) for q in range(size)])
+
+    steps = size // 2 - 1
+    right, left = send(own, 1), send(own, -1)
+    opposite = send(own, size // 2)
+    right, onebody = tie(right, onebody)
+    left, *packed = tie(left, *packed)
+    shifts, parts = [0, -1, 1], [own, right, left]
     total = mark = None
-    for step in range(1, steps):
-        next_right, next_left = lax.ppermute(right, "chol", ahead), lax.ppermute(left, "chol", back)
-        if step == 1:
-            right, onebody = tie(next_right, onebody)
-            left, *packed = tie(next_left, *packed)
-        elif step == 2:
+    for step in range(2, steps + 1):
+        next_right, next_left = send(right, 1), send(left, -1)
+        if step == 2:
             far = exchange_far(packed)
-            right = next_right
-            left, far = tie(next_left, far)
+        elif step == 3:
+            near = exchange_near(packed, far)
+        if step == steps:
+            opposite, mark = tie(opposite, mark)
+            shifts, parts = shifts + [size // 2], parts + [opposite]
+        total, mark = accumulate(cholesky_rot, shifts, parts, total, mark)
+        right, mark = tie(next_right, mark)
+        if step == 2:
+            left, mark, far = tie(next_left, mark, far)
         else:
-            if step == 3:
-                near = exchange_near(packed, far)
-            total, mark = accumulate(cholesky_rot, shifts[:-2], parts[:-2], total, mark)
-            shifts, parts = shifts[-2:], parts[-2:]
-            right, mark = tie(next_right, mark)
-            if step == 3:
-                left, mark, *near = tie(next_left, mark, *near)
-            else:
-                left, mark = tie(next_left, mark)
-        shifts += [-step, step]
-        parts = parts + [right, left]
-    last = [lax.ppermute(right[: rows // 2], "chol", ahead), lax.ppermute(left[rows // 2 :], "chol", back)]
-    total, _ = accumulate(cholesky_rot, shifts, parts, total, mark)
-    return onebody, total, last, [packed[0], far] + near
+            left, mark = tie(next_left, mark)
+        shifts, parts = [-step, step], [right, left]
+    return onebody, total, shifts, parts, [packed[0], far] + near
 
 
 def table_height(vectors):
@@ -291,9 +288,10 @@
     return total
 
 
-def measure(cholesky_rot, total, last, packs, places, onebody, vectors, slots):
+def measure(cholesky_rot, total, shifts, last, packs, places, onebody, vectors, slots):
     _, walkers, orbitals = last[0].shape
-    depth = sum(x.shape[0] for x in last)
+    rows = last[0].shape[0]
+    depth = rows * len(last)
     walk_size = len(places)
     targets = walk_size * lax.axis_size("chol")
     whole = total is None
@@ -327,8 +325,9 @@
         exchange = [jnp.zeros((8, LANES), jnp.float32) for _ in range(walkers)]
         squares = [jnp.zeros((1, 1), jnp.float32) for _ in range(walkers)]
         drive = jnp.zeros((1, LANES), jnp.float32)
-        start = 0 if whole else column_start(lax.axis_size("chol") // 2, depth)
-        lhs = chol_ref[:, :, pl.ds(start, depth)].reshape(vectors * orbitals, depth)
+        starts = [0 if shift is None else column_start(shift, rows) for shift in shifts]
+        blocks = [chol_ref[:, :, pl.ds(start, rows)].reshape(vectors * orbitals, rows) for start in starts]
+        lhs = jnp.concatenate(blocks, axis=1)
         for b in range(walkers):
             value = jnp.dot(lhs, rhs[b], preferred_element_type=jnp.float32)
             tensor_scr[b] = value if whole else refs[2 + len(packs) + len(last)][b] + value
@@ -443,12 +442,12 @@
     if chol_size > RING_LIMIT or chol_size % 2 or chol_size < 8:
         far = exchange_far(packed)
         packs = [packed[0], far] + exchange_near(packed, far)
-        total, last = None, [lax.all_gather(green_rows, "chol", axis=0, tiled=True)]
+        total, shifts, last = None, [None], [lax.all_gather(green_rows, "chol", axis=0, tiled=True)]
     else:
-        onebody, total, last, packs = ring(green_rows, cholesky_rot, onebody, packed)
+        onebody, total, shifts, last, packs = ring(green_rows, cholesky_rot, onebody, packed)
     table = 3 * table_height(vectors)
     places = walk_places(packs[0].shape[0] - table, table, walk_size)
-    stats = measure(cholesky_rot, total, last, packs, places, onebody, vectors, slots)
+    stats = measure(cholesky_rot, total, shifts, last, packs, places, onebody, vectors, slots)
     stats = lax.all_to_all(stats, ("chol", "walk"), split_axis=0, concat_axis=0, tiled=True)
     energies, new_weights, density = finish(stats, packs, places, counts, vectors, slots, walkers)
     return energies.reshape(slots), new_weights.reshape(slots), density.reshape(1, density.size)

time: 47.8 us -> 50.5 us (1.056)
  starting transfers between devices: 11 us -> 16.6 us
  waiting for transfers between devices: 9.39 us -> 5.75 us
  blocking collectives: 12.3 us -> 14.5 us
  other arithmetic: 0.9 us -> 0.01 us
    ppermute x8 -> x7, starting transfers between devices: 9.28 us -> 15 us  [send(): lax.ppermute(x, 'chol', [(order[q], order[(q + places) % size]) for q in...]
    ppermute x1, waiting for transfers between devices: 3.65 us -> 1.33 us  [exchange_far(): return lax.ppermute(packed[1], 'walk', [(q, q ^ 2) for q in range(size)])]
    all_to_all x1, blocking collectives: 12.3 us -> 14.5 us  [per_device(): lax.all_to_all(stats, ('chol', 'walk'), split_axis=0, concat_axis=0, tile...]
    ppermute x8 -> x7, waiting for transfers between devices: 5.73 us -> 4.41 us  [send(): lax.ppermute(x, 'chol', [(order[q], order[(q + places) % size]) for q in...]
    concatenate x1, other arithmetic: 0.9 us -> 0.01 us  [exchange_near(): jnp.concatenate([near, far[panel:]], axis=0)]
    pallas_call x2, Pallas kernels: 6.35 us -> 5.48 us  [accumulate(): pl.pallas_call(kernel, name='accumulate', out_shape=[jax.ShapeDtypeStruct...]
    pallas_call x1, Pallas kernels: 1.93 us -> 2.54 us  [measure(): pl.pallas_call(kernel, name='measure', out_shape=jax.ShapeDtypeStruct((ta...]
  transfers between devices with their start and end apart: 10 -> 9, of which waited for: 4 -> 5; matrix products, arithmetic and copies ran while one was open for 2% -> 0% of each run, Pallas kernels for 20% -> 17%
where the time goes in v8:
time: 50.5 us; the launch traced here: 50.4 us
  starting transfers between devices  16.6 us (33%)
  blocking collectives  14.5 us (29%)
  Pallas kernels  12.8 us (25%)
  waiting for transfers between devices  5.75 us (11%)
  between operations  0.7 us (1%)
    ppermute x7, starting transfers between devices, send(): lax.ppermute(x, 'chol', [(order[q], order[(q + places) % size]) for q in...  15 us
    all_to_all x1, blocking collectives, per_device(): lax.all_to_all(stats, ('chol', 'walk'), split_axis=0, concat_axis=0, tile...  14.5 us
    pallas_call x2, Pallas kernels, accumulate(): pl.pallas_call(kernel, name='accumulate', out_shape=[jax.ShapeDtypeStruct...  5.48 us
    ppermute x7, waiting for transfers between devices, send(): lax.ppermute(x, 'chol', [(order[q], order[(q + places) % size]) for q in...  4.41 us
    pallas_call x1, Pallas kernels, pack(): pl.pallas_call(kernel, name='pack', out_shape=[jax.ShapeDtypeStruct((8, L...  3.32 us
    pallas_call x1, Pallas kernels, measure(): pl.pallas_call(kernel, name='measure', out_shape=jax.ShapeDtypeStruct((ta...  2.54 us
    ppermute x1, starting transfers between devices, exchange_far(): return lax.ppermute(packed[1], 'walk', [(q, q ^ 2) for q in range(size)])  1.49 us
    pallas_call x1, Pallas kernels, finish(): pl.pallas_call(kernel, name='finish', out_shape=[jax.ShapeDtypeStruct((1,...  1.43 us
  transfers between devices with their start and end apart: 9, of which 5 were waited for; matrix products, arithmetic and copies ran while one was open for 0% of the time, Pallas kernels for 17%

profile of v8, /device:TPU:0, one launch (start us, length us, event | category | flops | bytes accessed | tf_op | source)
XLA Modules:
  0.0 50.4 jit_solution(1895283912988991548)
XLA Ops:
  0.6 3.1 %collective-permute-start = (bf16[256,2,256]{2,1,0:T(2,128)(2,1)}, bf16[256,2,256]{2,1,0:T(2,128)(2,1)S(1)}, u32[]{:S(2)}, u32[]{:S(2)}) collective-permute-start(bf16[256,2,256]{2,1,0:T(2,128)(2,1)} %refs_0_.2), channel_id=1, source_target_pairs={{0,8},{8,16},{16,24},{24,28},{28,20},{20,12},{12,4},{4,0},{1,9},{9... | collective-permute-start | bytes 786440 | tf_op jit(solution)/shard_map/ppermute | solution.py:93
  3.7 0.0 collective-permute-start.1
  3.7 3.3 %pack.1 = (f32[8,128]{1,0:T(8,128)}, bf16[304,128]{1,0:T(8,128)(2,1)}, bf16[560,128]{1,0:T(8,128)(2,1)}, bf16[304,128]{1,0:T(8,128)(2,1)}) custom-call(bf16[256,2,256]{2,1,0:T(2,128)(2,1)} %refs_0_.2, bf16[256,256]{1,0:T(8,128)(2,1)} %body_any.1, f32[4,8]{1,0:T(4,128)} %bitcast.10, f32[2]{0:T(128)} %weights_any.1, s32[4]{0:T(128)} %sources_any.1, ...), custom_call_target="tpu_custom_call" | custom-call | flops 100000000 | bytes 1000000 | tf_op jit(solution)/shard_map/pack/pallas_call | solution.py:223
  7.0 3.1 %collective-permute-done.refs_1_ = bf16[256,2,256]{2,1,0:T(2,128)(2,1)S(1)} collective-permute-done((bf16[256,2,256]{2,1,0:T(2,128)(2,1)}, bf16[256,2,256]{2,1,0:T(2,128)(2,1)S(1)}, u32[]{:S(2)}, u32[]{:S(2)}) %collective-permute-start) | collective-permute-done | bytes 262176 | tf_op jit(solution)/shard_map/ppermute | solution.py:93
  10.2 1.8 %collective-permute-start.3 = (bf16[256,2,256]{2,1,0:T(2,128)(2,1)S(1)}, bf16[256,2,256]{2,1,0:T(2,128)(2,1)S(1)}, u32[]{:S(2)}, u32[]{:S(2)}) collective-permute-start(bf16[256,2,256]{2,1,0:T(2,128)(2,1)S(1)} %collective-permute-done.refs_1_), channel_id=1, source_target_pairs={{0,8},{8,16},{16,24},{24,28},{28,20},{20,12},{12,4},{4,0},{1,9},{9... | collective-permute-start | bytes 786440 | tf_op jit(solution)/shard_map/ppermute | solution.py:93
  12.0 0.0 collective-permute-done.1.refs_2_
  12.0 0.2 collective-permute-start.2
  12.2 4.8 %collective-permute-start.8 = (bf16[256,2,256]{2,1,0:T(2,128)(2,1)S(1)}, bf16[256,2,256]{2,1,0:T(2,128)(2,1)S(1)}, u32[]{:S(2)}, u32[]{:S(2)}) collective-permute-start(bf16[256,2,256]{2,1,0:T(2,128)(2,1)S(1)} %copy-done.1), channel_id=1, source_target_pairs={{0,28},{8,20},{16,12},{24,4},{28,0},{20,8},{12,16},{4,24},{1,29},{... | collective-permute-start | bytes 786440 | tf_op jit(solution)/shard_map/ppermute | solution.py:93
  17.0 1.5 %collective-permute-start.4 = (bf16[560,128]{1,0:T(8,128)(2,1)}, bf16[560,128]{1,0:T(8,128)(2,1)S(1)}, u32[]{:S(2)}, u32[]{:S(2)}) collective-permute-start(bf16[560,128]{1,0:T(8,128)(2,1)} %get-tuple-element.36), channel_id=1, source_target_pairs={{0,2},{1,3},{2,0},{3,1},{4,6},{5,7},{6,4},{7,5},{8,10},{9,11},{10,... | collective-permute-start | bytes 430088 | tf_op jit(solution)/shard_map/ppermute | solution.py:257
  18.5 2.5 %accumulate.2 = (f32[2,2048,256]{2,1,0:T(8,128)S(1)}, f32[8,128]{1,0:T(8,128)S(1)}) custom-call(bf16[8,256,2048]{2,1,0:T(8,128)(2,1)S(1)} %copy-done, bf16[256,2,256]{2,1,0:T(2,128)(2,1)S(1)} %copy-done.1, bf16[256,2,256]{2,1,0:T(2,128)(2,1)S(1)} %collective-permute-done.refs_1_, bf16[256,2,256]{2,1,0:T(2,128)(2,1)S(1)} %collective-permute-done.1.refs_2_), custom_call_target="tpu_custom_call" | custom-call | flops 1610612736 | bytes 3145728 | tf_op jit(solution)/shard_map/accumulate/pallas_call | solution.py:66
  20.9 0.0 collective-permute-done.3.refs_0_
  21.0 1.3 %collective-permute-done.4.refs_3_.refs_1_ = bf16[560,128]{1,0:T(8,128)(2,1)S(1)} collective-permute-done((bf16[560,128]{1,0:T(8,128)(2,1)}, bf16[560,128]{1,0:T(8,128)(2,1)S(1)}, u32[]{:S(2)}, u32[]{:S(2)}) %collective-permute-start.4) | collective-permute-done | bytes 143392 | tf_op jit(solution)/shard_map/ppermute | solution.py:257
  22.3 0.6 %collective-permute-start.7 = (bf16[256,2,256]{2,1,0:T(2,128)(2,1)S(1)}, bf16[256,2,256]{2,1,0:T(2,128)(2,1)S(1)}, u32[]{:S(2)}, u32[]{:S(2)}) collective-permute-start(bf16[256,2,256]{2,1,0:T(2,128)(2,1)S(1)} %collective-permute-done.2.refs_1_), channel_id=1, source_target_pairs={{0,4},{8,0},{16,8},{24,16},{28,24},{20,28},{12,20},{4,12},{1,5},{9... | collective-permute-start | bytes 786440 | tf_op jit(solution)/shard_map/ppermute | solution.py:93
  22.9 4.6 %collective-permute-start.6 = (bf16[256,2,256]{2,1,0:T(2,128)(2,1)S(1)}, bf16[256,2,256]{2,1,0:T(2,128)(2,1)S(1)}, u32[]{:S(2)}, u32[]{:S(2)}) collective-permute-start(bf16[256,2,256]{2,1,0:T(2,128)(2,1)S(1)} %collective-permute-done.3.refs_0_), channel_id=1, source_target_pairs={{0,8},{8,16},{16,24},{24,28},{28,20},{20,12},{12,4},{4,0},{1,9},{9... | collective-permute-start | bytes 786440 | tf_op jit(solution)/shard_map/ppermute | solution.py:93
  27.5 0.1 collective-permute-start.5
  27.6 0.7 %collective-permute-done.8.refs_2_ = bf16[256,2,256]{2,1,0:T(2,128)(2,1)S(1)} collective-permute-done((bf16[256,2,256]{2,1,0:T(2,128)(2,1)S(1)}, bf16[256,2,256]{2,1,0:T(2,128)(2,1)S(1)}, u32[]{:S(2)}, u32[]{:S(2)}) %collective-permute-start.8) | collective-permute-done | bytes 262176 | tf_op jit(solution)/shard_map/ppermute | solution.py:93
  28.3 3.0 %accumulate.3 = (f32[2,2048,256]{2,1,0:T(8,128)S(1)}, f32[8,128]{1,0:T(8,128)}) custom-call(bf16[8,256,2048]{2,1,0:T(8,128)(2,1)S(1)} %copy-done, bf16[256,2,256]{2,1,0:T(2,128)(2,1)S(1)} %collective-permute-done.3.refs_0_, bf16[256,2,256]{2,1,0:T(2,128)(2,1)S(1)} %collective-permute-done.2.refs_1_, bf16[256,2,256]{2,1,0:T(2,128)(2,1)S(1)} %collective-permute-done.8.refs_2_, ...), custom_call_target="tpu_custom_call" | custom-call | flops 1610612736 | bytes 3145728 | tf_op jit(solution)/shard_map/accumulate/pallas_call | solution.py:66
  31.3 0.4 collective-permute-done.7.refs_6_
  31.7 0.1 collective-permute-done.6.refs_5_
  31.9 0.0 collective-permute-done.5.refs_4_.refs_2_
  31.9 0.0 copy-start.4
  31.9 2.5 %measure.1 = f32[32,128]{1,0:T(8,128)S(1)} custom-call(bf16[8,256,2048]{2,1,0:T(8,128)(2,1)S(1)} %copy-done, f32[8,128]{1,0:T(8,128)S(1)} %copy-done.3, bf16[304,128]{1,0:T(8,128)(2,1)S(1)} %copy-done.2, bf16[560,128]{1,0:T(8,128)(2,1)S(1)} %collective-permute-done.4.refs_3_.refs_1_, bf16[608,128]{1,0:T(8,128)(2,1)S(1)} %collective-permute-done.5.refs_4_.refs_2_, ...), custom_call_target="tpu_custom_call" | custom-call | flops 1073741824 | bytes 2097152 | tf_op jit(solution)/shard_map/measure/pallas_call | solution.py:366
  34.4 14.5 %all_to_all.11 = f32[32,1,128]{2,1,0:T(1,128)S(1)} all-to-all(f32[32,1,128]{2,1,0:T(1,128)S(1)} %bitcast.8), channel_id=1, replica_groups=mesh['chol'=8,'walk'=4] {'chol','walk'}, dimensions={0} | all-to-all | bytes 32768 | tf_op jit(solution)/shard_map/all_to_all | solution.py:451
  48.9 1.4 %finish.1 = (f32[1,4]{1,0:T(1,128)}, f32[1,4]{1,0:T(1,128)}, f32[128,128]{1,0:T(8,128)}) custom-call(f32[32,128]{1,0:T(8,128)S(1)} %bitcast.9, s32[4]{0:T(128)S(1)} %copy-done.4, bf16[304,128]{1,0:T(8,128)(2,1)S(1)} %copy-done.2, bf16[560,128]{1,0:T(8,128)(2,1)S(1)} %collective-permute-done.4.refs_3_.refs_1_, ...), custom_call_target="tpu_custom_call" | custom-call | flops 1000000 | bytes 600000 | tf_op jit(solution)/shard_map/finish/pallas_call | solution.py:421
  (14 shorter events, 0.0 us)
Async XLA Ops:
  0.6 9.5 %collective-permute-start = (bf16[256,2,256]{2,1,0:T(2,128)(2,1)}, bf16[256,2,256]{2,1,0:T(2,128)(2,1)S(1)}, u32[]{:S(2)}, u32[]{:S(2)}) collective-permute-start(bf16[256,2,256]{2,1,0:T(2,128)(2,1)} %refs_0_.2), channel_id=1, source_target_pairs={{0,8},{8,16},{16,24},{24,28},{28,20},{20,12},{12,4},{4,0},{1,9},{9... | collective-permute-start | bytes 786440 | tf_op jit(solution)/shard_map/ppermute | solution.py:93
  3.7 8.3 %collective-permute-start.1 = (bf16[256,2,256]{2,1,0:T(2,128)(2,1)}, bf16[256,2,256]{2,1,0:T(2,128)(2,1)S(1)}, u32[]{:S(2)}, u32[]{:S(2)}) collective-permute-start(bf16[256,2,256]{2,1,0:T(2,128)(2,1)} %refs_0_.2), channel_id=1, source_target_pairs={{0,4},{8,0},{16,8},{24,16},{28,24},{20,28},{12,20},{4,12},{1,5},{9... | collective-permute-start | bytes 786440 | tf_op jit(solution)/shard_map/ppermute | solution.py:93
  3.7 8.5 %copy-start.1 = (bf16[256,2,256]{2,1,0:T(2,128)(2,1)S(1)}, bf16[256,2,256]{2,1,0:T(2,128)(2,1)}, u32[]{:S(2)}) copy-start(bf16[256,2,256]{2,1,0:T(2,128)(2,1)} %refs_0_.2) | copy-start | bytes 786436
  3.7 14.8 %copy-start = (bf16[8,256,2048]{2,1,0:T(8,128)(2,1)S(1)}, bf16[8,256,2048]{2,1,0:T(8,128)(2,1)}, u32[]{:S(2)}) copy-start(bf16[8,256,2048]{2,1,0:T(8,128)(2,1)} %refs_0_.3) | copy-start | bytes 25165828
  10.2 10.8 %collective-permute-start.3 = (bf16[256,2,256]{2,1,0:T(2,128)(2,1)S(1)}, bf16[256,2,256]{2,1,0:T(2,128)(2,1)S(1)}, u32[]{:S(2)}, u32[]{:S(2)}) collective-permute-start(bf16[256,2,256]{2,1,0:T(2,128)(2,1)S(1)} %collective-permute-done.refs_1_), channel_id=1, source_target_pairs={{0,8},{8,16},{16,24},{24,28},{28,20},{20,12},{12,4},{4,0},{1,9},{9... | collective-permute-start | bytes 786440 | tf_op jit(solution)/shard_map/ppermute | solution.py:93
  12.0 15.5 %copy-start.5 = (bf16[304,128]{1,0:T(8,128)(2,1)S(1)}, bf16[304,128]{1,0:T(8,128)(2,1)}, u32[]{:S(2)}) copy-start(bf16[304,128]{1,0:T(8,128)(2,1)} %get-tuple-element.38) | copy-start | bytes 233476
  12.0 10.3 %collective-permute-start.2 = (bf16[256,2,256]{2,1,0:T(2,128)(2,1)S(1)}, bf16[256,2,256]{2,1,0:T(2,128)(2,1)S(1)}, u32[]{:S(2)}, u32[]{:S(2)}) collective-permute-start(bf16[256,2,256]{2,1,0:T(2,128)(2,1)S(1)} %collective-permute-done.1.refs_2_), channel_id=1, source_target_pairs={{0,4},{8,0},{16,8},{24,16},{28,24},{20,28},{12,20},{4,12},{1,5},{9... | collective-permute-start | bytes 786440 | tf_op jit(solution)/shard_map/ppermute | solution.py:93
  12.2 16.1 %collective-permute-start.8 = (bf16[256,2,256]{2,1,0:T(2,128)(2,1)S(1)}, bf16[256,2,256]{2,1,0:T(2,128)(2,1)S(1)}, u32[]{:S(2)}, u32[]{:S(2)}) collective-permute-start(bf16[256,2,256]{2,1,0:T(2,128)(2,1)S(1)} %copy-done.1), channel_id=1, source_target_pairs={{0,28},{8,20},{16,12},{24,4},{28,0},{20,8},{12,16},{4,24},{1,29},{... | collective-permute-start | bytes 786440 | tf_op jit(solution)/shard_map/ppermute | solution.py:93
  17.0 5.3 %collective-permute-start.4 = (bf16[560,128]{1,0:T(8,128)(2,1)}, bf16[560,128]{1,0:T(8,128)(2,1)S(1)}, u32[]{:S(2)}, u32[]{:S(2)}) collective-permute-start(bf16[560,128]{1,0:T(8,128)(2,1)} %get-tuple-element.36), channel_id=1, source_target_pairs={{0,2},{1,3},{2,0},{3,1},{4,6},{5,7},{6,4},{7,5},{8,10},{9,11},{10,... | collective-permute-start | bytes 430088 | tf_op jit(solution)/shard_map/ppermute | solution.py:257
  22.3 9.4 %collective-permute-start.7 = (bf16[256,2,256]{2,1,0:T(2,128)(2,1)S(1)}, bf16[256,2,256]{2,1,0:T(2,128)(2,1)S(1)}, u32[]{:S(2)}, u32[]{:S(2)}) collective-permute-start(bf16[256,2,256]{2,1,0:T(2,128)(2,1)S(1)} %collective-permute-done.2.refs_1_), channel_id=1, source_target_pairs={{0,4},{8,0},{16,8},{24,16},{28,24},{20,28},{12,20},{4,12},{1,5},{9... | collective-permute-start | bytes 786440 | tf_op jit(solution)/shard_map/ppermute | solution.py:93
  22.9 9.0 %collective-permute-start.6 = (bf16[256,2,256]{2,1,0:T(2,128)(2,1)S(1)}, bf16[256,2,256]{2,1,0:T(2,128)(2,1)S(1)}, u32[]{:S(2)}, u32[]{:S(2)}) collective-permute-start(bf16[256,2,256]{2,1,0:T(2,128)(2,1)S(1)} %collective-permute-done.3.refs_0_), channel_id=1, source_target_pairs={{0,8},{8,16},{16,24},{24,28},{28,20},{20,12},{12,4},{4,0},{1,9},{9... | collective-permute-start | bytes 786440 | tf_op jit(solution)/shard_map/ppermute | solution.py:93
  27.5 4.4 %collective-permute-start.5 = (bf16[608,128]{1,0:T(8,128)(2,1)S(1)}, bf16[608,128]{1,0:T(8,128)(2,1)S(1)}, u32[]{:S(2)}, u32[]{:S(2)}) collective-permute-start(bf16[608,128]{1,0:T(8,128)(2,1)S(1)} %pad_maximum_fusion), channel_id=1, source_target_pairs={{0,1},{1,0},{2,3},{3,2},{4,5},{5,4},{6,7},{7,6},{8,9},{9,8},{10,11... | collective-permute-start | bytes 466952 | tf_op jit(solution)/shard_map/ppermute | solution.py:268
  28.3 3.6 %copy-start.2 = (bf16[304,128]{1,0:T(8,128)(2,1)S(1)}, bf16[304,128]{1,0:T(8,128)(2,1)}, u32[]{:S(2)}) copy-start(bf16[304,128]{1,0:T(8,128)(2,1)} %get-tuple-element.31.refs_2_.refs_0_) | copy-start | bytes 233476
  28.3 3.6 %copy-start.3 = (f32[8,128]{1,0:T(8,128)S(1)}, f32[8,128]{1,0:T(8,128)}, u32[]{:S(2)}) copy-start(f32[8,128]{1,0:T(8,128)} %get-tuple-element.27.refs_1_) | copy-start | bytes 12292
  31.9 17.1 %copy-start.4 = (s32[4]{0:T(128)S(1)}, s32[4]{0:T(128)}, u32[]{:S(2)}) copy-start(s32[4]{0:T(128)} %counts_ref.1) | copy-start | bytes 52

commit v9 on v7

--- a/solution.py
+++ b/solution.py
@@ -100,23 +100,19 @@
         if step == 1:
             right, onebody = tie(next_right, onebody)
             left, *packed = tie(next_left, *packed)
-        elif step == 2:
-            far = exchange_far(packed)
-            right = next_right
-            left, far = tie(next_left, far)
         else:
-            if step == 3:
+            if step == 2:
+                far = exchange_far(packed)
+            elif step == 3:
                 near = exchange_near(packed, far)
-            total, mark = accumulate(cholesky_rot, shifts[:-2], parts[:-2], total, mark)
-            shifts, parts = shifts[-2:], parts[-2:]
+            total, mark = accumulate(cholesky_rot, shifts, parts, total, mark)
+            shifts, parts = [], []
             right, mark = tie(next_right, mark)
-            if step == 3:
-                left, mark, *near = tie(next_left, mark, *near)
-            else:
-                left, mark = tie(next_left, mark)
+            left, mark = tie(next_left, mark)
         shifts += [-step, step]
         parts = parts + [right, left]
     last = [lax.ppermute(right[: rows // 2], "chol", ahead), lax.ppermute(left[rows // 2 :], "chol", back)]
+    mark, *near = tie(mark, *near)
     total, _ = accumulate(cholesky_rot, shifts, parts, total, mark)
     return onebody, total, last, [packed[0], far] + near
 
@@ -449,7 +445,10 @@
     table = 3 * table_height(vectors)
     places = walk_places(packs[0].shape[0] - table, table, walk_size)
     stats = measure(cholesky_rot, total, last, packs, places, onebody, vectors, slots)
-    stats = lax.all_to_all(stats, ("chol", "walk"), split_axis=0, concat_axis=0, tiled=True)
+    turned = [list(range(stats.shape[0]))[::-1]]
+    stats = lax.all_to_all(
+        stats, ("chol", "walk"), split_axis=0, concat_axis=0, axis_index_groups=turned, tiled=True
+    )
     energies, new_weights, density = finish(stats, packs, places, counts, vectors, slots, walkers)
     return energies.reshape(slots), new_weights.reshape(slots), density.reshape(1, density.size)
 

time: 47.8 us -> 46.5 us (0.973)
  blocking collectives: 12.3 us -> 10.8 us
  waiting for transfers between devices: 9.39 us -> 10.5 us
  other arithmetic: 0.9 us -> 0.01 us
    ppermute x3, starting transfers between devices: 6.29 us -> 0.78 us  [ring(): lax.ppermute(left, 'chol', back)]
    ppermute x3, starting transfers between devices: 0.91 us -> 6.35 us  [ring(): lax.ppermute(right, 'chol', ahead)]
    ppermute x3, waiting for transfers between devices: 2.45 us -> 7 us  [ring(): lax.ppermute(right, 'chol', ahead)]
    ppermute x1, waiting for transfers between devices: 3.65 us -> 0.01 us  [exchange_far(): return lax.ppermute(packed[1], 'walk', [(q, q ^ 2) for q in range(size)])]
    ppermute x3, waiting for transfers between devices: 3.27 us -> 1.29 us  [ring(): lax.ppermute(left, 'chol', back)]
    ppermute x1, waiting for transfers between devices: 0.01 us -> 1.58 us  [ring(): lax.ppermute(left[rows // 2:], 'chol', back)]
    all_to_all x1, blocking collectives: 12.3 us -> 10.8 us  [per_device(): lax.all_to_all(stats, ('chol', 'walk'), split_axis=0, concat_axis=0, axis...]
    ppermute x1, starting transfers between devices: 0.5 us -> 1.63 us  [ring(): lax.ppermute(right[:rows // 2], 'chol', ahead)]
  transfers between devices with their start and end apart: 10 -> 10, of which waited for: 4 -> 6; matrix products, arithmetic and copies ran while one was open for 2% -> 0% of each run, Pallas kernels for 20% -> 21%
where the time goes in v9:
time: 46.5 us; the launch traced here: 46.3 us
  Pallas kernels  13.1 us (28%)
  starting transfers between devices  11 us (24%)
  blocking collectives  10.8 us (23%)
  waiting for transfers between devices  10.5 us (23%)
  between operations  0.71 us (2%)
    all_to_all x1, blocking collectives, per_device(): lax.all_to_all(stats, ('chol', 'walk'), split_axis=0, concat_axis=0, axis...  10.8 us
    ppermute x3, waiting for transfers between devices, ring(): lax.ppermute(right, 'chol', ahead)  7 us
    pallas_call x3, Pallas kernels, accumulate(): pl.pallas_call(kernel, name='accumulate', out_shape=[jax.ShapeDtypeStruct...  6.58 us
    ppermute x3, starting transfers between devices, ring(): lax.ppermute(right, 'chol', ahead)  6.35 us
    pallas_call x1, Pallas kernels, pack(): pl.pallas_call(kernel, name='pack', out_shape=[jax.ShapeDtypeStruct((8, L...  3.32 us
    pallas_call x1, Pallas kernels, measure(): pl.pallas_call(kernel, name='measure', out_shape=jax.ShapeDtypeStruct((ta...  1.81 us
    ppermute x1, starting transfers between devices, exchange_far(): return lax.ppermute(packed[1], 'walk', [(q, q ^ 2) for q in range(size)])  1.71 us
    ppermute x1, starting transfers between devices, ring(): lax.ppermute(right[:rows // 2], 'chol', ahead)  1.63 us
  transfers between devices with their start and end apart: 10, of which 6 were waited for; matrix products, arithmetic and copies ran while one was open for 0% of the time, Pallas kernels for 21%

profile of v9, /device:TPU:0, one launch (start us, length us, event | category | flops | bytes accessed | tf_op | source)
XLA Modules:
  0.0 46.3 jit_solution(18278603376457966514)
XLA Ops:
  0.6 3.1 %collective-permute-start = (bf16[256,2,256]{2,1,0:T(2,128)(2,1)}, bf16[256,2,256]{2,1,0:T(2,128)(2,1)S(1)}, u32[]{:S(2)}, u32[]{:S(2)}) collective-permute-start(bf16[256,2,256]{2,1,0:T(2,128)(2,1)} %refs_0_.2), channel_id=1, source_target_pairs={{0,8},{8,16},{16,24},{24,28},{28,20},{20,12},{12,4},{4,0},{1,9},{9... | collective-permute-start | bytes 786440 | tf_op jit(solution)/shard_map/ppermute | solution.py:99
  3.7 3.3 %pack.1 = (f32[8,128]{1,0:T(8,128)}, bf16[304,128]{1,0:T(8,128)(2,1)}, bf16[560,128]{1,0:T(8,128)(2,1)}, bf16[304,128]{1,0:T(8,128)(2,1)}) custom-call(bf16[256,2,256]{2,1,0:T(2,128)(2,1)} %refs_0_.2, bf16[256,256]{1,0:T(8,128)(2,1)} %body_any.1, f32[4,8]{1,0:T(4,128)} %bitcast.10, f32[2]{0:T(128)} %weights_any.1, s32[4]{0:T(128)} %sources_any.1, ...), custom_call_target="tpu_custom_call" | custom-call | flops 100000000 | bytes 1000000 | tf_op jit(solution)/shard_map/pack/pallas_call | solution.py:222
  7.0 3.1 %collective-permute-done.refs_1_ = bf16[256,2,256]{2,1,0:T(2,128)(2,1)S(1)} collective-permute-done((bf16[256,2,256]{2,1,0:T(2,128)(2,1)}, bf16[256,2,256]{2,1,0:T(2,128)(2,1)S(1)}, u32[]{:S(2)}, u32[]{:S(2)}) %collective-permute-start) | collective-permute-done | bytes 262176 | tf_op jit(solution)/shard_map/ppermute | solution.py:99
  10.2 1.8 %collective-permute-start.4 = (bf16[256,2,256]{2,1,0:T(2,128)(2,1)S(1)}, bf16[256,2,256]{2,1,0:T(2,128)(2,1)S(1)}, u32[]{:S(2)}, u32[]{:S(2)}) collective-permute-start(bf16[256,2,256]{2,1,0:T(2,128)(2,1)S(1)} %collective-permute-done.refs_1_), channel_id=1, source_target_pairs={{0,8},{8,16},{16,24},{24,28},{28,20},{20,12},{12,4},{4,0},{1,9},{9... | collective-permute-start | bytes 786440 | tf_op jit(solution)/shard_map/ppermute | solution.py:99
  12.0 0.2 collective-permute-start.3
  12.2 1.7 %collective-permute-start.2 = (bf16[560,128]{1,0:T(8,128)(2,1)}, bf16[560,128]{1,0:T(8,128)(2,1)S(1)}, u32[]{:S(2)}, u32[]{:S(2)}) collective-permute-start(bf16[560,128]{1,0:T(8,128)(2,1)} %get-tuple-element.37), channel_id=1, source_target_pairs={{0,2},{1,3},{2,0},{3,1},{4,6},{5,7},{6,4},{7,5},{8,10},{9,11},{10,... | collective-permute-start | bytes 430088 | tf_op jit(solution)/shard_map/ppermute | solution.py:256
  13.9 2.5 %accumulate.3 = (f32[2,2048,256]{2,1,0:T(8,128)S(1)}, f32[8,128]{1,0:T(8,128)S(1)}) custom-call(bf16[8,256,2048]{2,1,0:T(8,128)(2,1)S(1)} %copy-done, bf16[256,2,256]{2,1,0:T(2,128)(2,1)S(1)} %copy-done.1, bf16[256,2,256]{2,1,0:T(2,128)(2,1)S(1)} %collective-permute-done.refs_1_, bf16[256,2,256]{2,1,0:T(2,128)(2,1)S(1)} %collective-permute-done.1.refs_2_), custom_call_target="tpu_custom_call" | custom-call | flops 1610612736 | bytes 3145728 | tf_op jit(solution)/shard_map/accumulate/pallas_call | solution.py:66
  16.4 1.3 %collective-permute-done.4.refs_0_ = bf16[256,2,256]{2,1,0:T(2,128)(2,1)S(1)} collective-permute-done((bf16[256,2,256]{2,1,0:T(2,128)(2,1)S(1)}, bf16[256,2,256]{2,1,0:T(2,128)(2,1)S(1)}, u32[]{:S(2)}, u32[]{:S(2)}) %collective-permute-start.4) | collective-permute-done | bytes 262176 | tf_op jit(solution)/shard_map/ppermute | solution.py:99
  17.7 1.5 %collective-permute-start.6 = (bf16[256,2,256]{2,1,0:T(2,128)(2,1)S(1)}, bf16[256,2,256]{2,1,0:T(2,128)(2,1)S(1)}, u32[]{:S(2)}, u32[]{:S(2)}) collective-permute-start(bf16[256,2,256]{2,1,0:T(2,128)(2,1)S(1)} %collective-permute-done.4.refs_0_), channel_id=1, source_target_pairs={{0,8},{8,16},{16,24},{24,28},{28,20},{20,12},{12,4},{4,0},{1,9},{9... | collective-permute-start | bytes 786440 | tf_op jit(solution)/shard_map/ppermute | solution.py:99
  19.1 0.5 %collective-permute-start.5 = (bf16[256,2,256]{2,1,0:T(2,128)(2,1)S(1)}, bf16[256,2,256]{2,1,0:T(2,128)(2,1)S(1)}, u32[]{:S(2)}, u32[]{:S(2)}) collective-permute-start(bf16[256,2,256]{2,1,0:T(2,128)(2,1)S(1)} %collective-permute-done.3.refs_1_), channel_id=1, source_target_pairs={{0,4},{8,0},{16,8},{24,16},{28,24},{20,28},{12,20},{4,12},{1,5},{9... | collective-permute-start | bytes 786440 | tf_op jit(solution)/shard_map/ppermute | solution.py:99
  19.7 0.1 collective-permute-start.7
  19.8 1.8 %accumulate.4 = (f32[2,2048,256]{2,1,0:T(8,128)S(1)}, f32[8,128]{1,0:T(8,128)S(1)}) custom-call(bf16[8,256,2048]{2,1,0:T(8,128)(2,1)S(1)} %copy-done, bf16[256,2,256]{2,1,0:T(2,128)(2,1)S(1)} %collective-permute-done.4.refs_0_, bf16[256,2,256]{2,1,0:T(2,128)(2,1)S(1)} %collective-permute-done.3.refs_1_, f32[8,128]{1,0:T(8,128)S(1)} %get-tuple-element.44.refs_2_, ...), custom_call_target="tpu_custom_call" | custom-call | flops 1073741824 | bytes 2097152 | tf_op jit(solution)/shard_map/accumulate/pallas_call | solution.py:66
  21.6 2.6 %collective-permute-done.6.refs_0_ = bf16[256,2,256]{2,1,0:T(2,128)(2,1)S(1)} collective-permute-done((bf16[256,2,256]{2,1,0:T(2,128)(2,1)S(1)}, bf16[256,2,256]{2,1,0:T(2,128)(2,1)S(1)}, u32[]{:S(2)}, u32[]{:S(2)}) %collective-permute-start.6) | collective-permute-done | bytes 262176 | tf_op jit(solution)/shard_map/ppermute | solution.py:99
  24.2 1.3 %collective-permute-done.5.refs_1_ = bf16[256,2,256]{2,1,0:T(2,128)(2,1)S(1)} collective-permute-done((bf16[256,2,256]{2,1,0:T(2,128)(2,1)S(1)}, bf16[256,2,256]{2,1,0:T(2,128)(2,1)S(1)}, u32[]{:S(2)}, u32[]{:S(2)}) %collective-permute-start.5) | collective-permute-done | bytes 262176 | tf_op jit(solution)/shard_map/ppermute | solution.py:99
  25.5 0.1 slice.11
  25.6 0.1 slice.10
  25.7 1.6 %collective-permute-start.8 = (bf16[128,2,256]{2,1,0:T(2,128)(2,1)S(1)}, bf16[128,2,256]{2,1,0:T(2,128)(2,1)S(1)}, u32[]{:S(2)}, u32[]{:S(2)}) collective-permute-start(bf16[128,2,256]{2,1,0:T(2,128)(2,1)S(1)} %slice.10), channel_id=1, source_target_pairs={{0,8},{8,16},{16,24},{24,28},{28,20},{20,12},{12,4},{4,0},{1,9},{9... | collective-permute-start | bytes 393224 | tf_op jit(solution)/shard_map/ppermute | solution.py:114
  27.3 0.4 collective-permute-start.9
  27.8 2.3 %accumulate.5 = (f32[2,2048,256]{2,1,0:T(8,128)S(1)}, f32[8,128]{1,0:T(8,128)}) custom-call(bf16[8,256,2048]{2,1,0:T(8,128)(2,1)S(1)} %copy-done, bf16[256,2,256]{2,1,0:T(2,128)(2,1)S(1)} %collective-permute-done.6.refs_0_, bf16[256,2,256]{2,1,0:T(2,128)(2,1)S(1)} %collective-permute-done.5.refs_1_, f32[8,128]{1,0:T(8,128)S(1)} %get-tuple-element.53.refs_2_, ...), custom_call_target="tpu_custom_call" | custom-call | flops 1073741824 | bytes 2097152 | tf_op jit(solution)/shard_map/accumulate/pallas_call | solution.py:66
  30.1 0.6 %collective-permute-done.8.refs_5_ = bf16[128,2,256]{2,1,0:T(2,128)(2,1)S(1)} collective-permute-done((bf16[128,2,256]{2,1,0:T(2,128)(2,1)S(1)}, bf16[128,2,256]{2,1,0:T(2,128)(2,1)S(1)}, u32[]{:S(2)}, u32[]{:S(2)}) %collective-permute-start.8) | collective-permute-done | bytes 131104 | tf_op jit(solution)/shard_map/ppermute | solution.py:114
  30.7 1.6 %collective-permute-done.9.refs_6_ = bf16[128,2,256]{2,1,0:T(2,128)(2,1)S(1)} collective-permute-done((bf16[128,2,256]{2,1,0:T(2,128)(2,1)S(1)}, bf16[128,2,256]{2,1,0:T(2,128)(2,1)S(1)}, u32[]{:S(2)}, u32[]{:S(2)}) %collective-permute-start.9) | collective-permute-done | bytes 131104 | tf_op jit(solution)/shard_map/ppermute | solution.py:114
  32.3 1.8 %measure.1 = f32[32,128]{1,0:T(8,128)S(1)} custom-call(bf16[8,256,2048]{2,1,0:T(8,128)(2,1)S(1)} %copy-done, f32[8,128]{1,0:T(8,128)S(1)} %copy-done.3, bf16[304,128]{1,0:T(8,128)(2,1)S(1)} %copy-done.2, bf16[560,128]{1,0:T(8,128)(2,1)S(1)} %collective-permute-done.2.refs_3_.refs_1_, bf16[608,128]{1,0:T(8,128)(2,1)S(1)} %collective-permute-done.7.refs_4_.refs_2_, ...), custom_call_target="tpu_custom_call" | custom-call | flops 536870912 | bytes 1048576 | tf_op jit(solution)/shard_map/measure/pallas_call | solution.py:363
  34.1 10.8 %all_to_all.11 = f32[32,1,128]{2,1,0:T(1,128)S(1)} all-to-all(f32[32,1,128]{2,1,0:T(1,128)S(1)} %bitcast.8), channel_id=1, replica_groups={{31,30,29,28,27,26,25,24,23,22,21,20,19,18,17,16,15,14,13,12,11,10,9,8,..., dimensions={0} | all-to-all | bytes 32768 | tf_op jit(solution)/shard_map/all_to_all | solution.py:449
  44.9 1.4 %finish.1 = (f32[1,4]{1,0:T(1,128)}, f32[1,4]{1,0:T(1,128)}, f32[128,128]{1,0:T(8,128)}) custom-call(f32[32,128]{1,0:T(8,128)S(1)} %bitcast.9, s32[4]{0:T(128)S(1)} %copy-done.4, bf16[304,128]{1,0:T(8,128)(2,1)S(1)} %copy-done.2, bf16[560,128]{1,0:T(8,128)(2,1)S(1)} %collective-permute-done.2.refs_3_.refs_1_, ...), custom_call_target="tpu_custom_call" | custom-call | flops 1000000 | bytes 600000 | tf_op jit(solution)/shard_map/finish/pallas_call | solution.py:418
  (19 shorter events, 0.1 us)
Async XLA Ops:
  0.6 9.5 %collective-permute-start = (bf16[256,2,256]{2,1,0:T(2,128)(2,1)}, bf16[256,2,256]{2,1,0:T(2,128)(2,1)S(1)}, u32[]{:S(2)}, u32[]{:S(2)}) collective-permute-start(bf16[256,2,256]{2,1,0:T(2,128)(2,1)} %refs_0_.2), channel_id=1, source_target_pairs={{0,8},{8,16},{16,24},{24,28},{28,20},{20,12},{12,4},{4,0},{1,9},{9... | collective-permute-start | bytes 786440 | tf_op jit(solution)/shard_map/ppermute | solution.py:99
  3.7 8.3 %collective-permute-start.1 = (bf16[256,2,256]{2,1,0:T(2,128)(2,1)}, bf16[256,2,256]{2,1,0:T(2,128)(2,1)S(1)}, u32[]{:S(2)}, u32[]{:S(2)}) collective-permute-start(bf16[256,2,256]{2,1,0:T(2,128)(2,1)} %refs_0_.2), channel_id=1, source_target_pairs={{0,4},{8,0},{16,8},{24,16},{28,24},{20,28},{12,20},{4,12},{1,5},{9... | collective-permute-start | bytes 786440 | tf_op jit(solution)/shard_map/ppermute | solution.py:99
  3.7 10.2 %copy-start = (bf16[8,256,2048]{2,1,0:T(8,128)(2,1)S(1)}, bf16[8,256,2048]{2,1,0:T(8,128)(2,1)}, u32[]{:S(2)}) copy-start(bf16[8,256,2048]{2,1,0:T(8,128)(2,1)} %refs_0_.3) | copy-start | bytes 25165828
  3.7 10.2 %copy-start.1 = (bf16[256,2,256]{2,1,0:T(2,128)(2,1)S(1)}, bf16[256,2,256]{2,1,0:T(2,128)(2,1)}, u32[]{:S(2)}) copy-start(bf16[256,2,256]{2,1,0:T(2,128)(2,1)} %refs_0_.2) | copy-start | bytes 786436
  10.2 7.5 %collective-permute-start.4 = (bf16[256,2,256]{2,1,0:T(2,128)(2,1)S(1)}, bf16[256,2,256]{2,1,0:T(2,128)(2,1)S(1)}, u32[]{:S(2)}, u32[]{:S(2)}) collective-permute-start(bf16[256,2,256]{2,1,0:T(2,128)(2,1)S(1)} %collective-permute-done.refs_1_), channel_id=1, source_target_pairs={{0,8},{8,16},{16,24},{24,28},{28,20},{20,12},{12,4},{4,0},{1,9},{9... | collective-permute-start | bytes 786440 | tf_op jit(solution)/shard_map/ppermute | solution.py:99
  12.0 7.7 %copy-start.5 = (bf16[304,128]{1,0:T(8,128)(2,1)S(1)}, bf16[304,128]{1,0:T(8,128)(2,1)}, u32[]{:S(2)}) copy-start(bf16[304,128]{1,0:T(8,128)(2,1)} %get-tuple-element.49) | copy-start | bytes 233476
  12.0 7.2 %collective-permute-start.3 = (bf16[256,2,256]{2,1,0:T(2,128)(2,1)S(1)}, bf16[256,2,256]{2,1,0:T(2,128)(2,1)S(1)}, u32[]{:S(2)}, u32[]{:S(2)}) collective-permute-start(bf16[256,2,256]{2,1,0:T(2,128)(2,1)S(1)} %collective-permute-done.1.refs_2_), channel_id=1, source_target_pairs={{0,4},{8,0},{16,8},{24,16},{28,24},{20,28},{12,20},{4,12},{1,5},{9... | collective-permute-start | bytes 786440 | tf_op jit(solution)/shard_map/ppermute | solution.py:99
  12.2 7.5 %collective-permute-start.2 = (bf16[560,128]{1,0:T(8,128)(2,1)}, bf16[560,128]{1,0:T(8,128)(2,1)S(1)}, u32[]{:S(2)}, u32[]{:S(2)}) collective-permute-start(bf16[560,128]{1,0:T(8,128)(2,1)} %get-tuple-element.37), channel_id=1, source_target_pairs={{0,2},{1,3},{2,0},{3,1},{4,6},{5,7},{6,4},{7,5},{8,10},{9,11},{10,... | collective-permute-start | bytes 430088 | tf_op jit(solution)/shard_map/ppermute | solution.py:256
  17.7 6.6 %collective-permute-start.6 = (bf16[256,2,256]{2,1,0:T(2,128)(2,1)S(1)}, bf16[256,2,256]{2,1,0:T(2,128)(2,1)S(1)}, u32[]{:S(2)}, u32[]{:S(2)}) collective-permute-start(bf16[256,2,256]{2,1,0:T(2,128)(2,1)S(1)} %collective-permute-done.4.refs_0_), channel_id=1, source_target_pairs={{0,8},{8,16},{16,24},{24,28},{28,20},{20,12},{12,4},{4,0},{1,9},{9... | collective-permute-start | bytes 786440 | tf_op jit(solution)/shard_map/ppermute | solution.py:99
  19.1 6.4 %collective-permute-start.5 = (bf16[256,2,256]{2,1,0:T(2,128)(2,1)S(1)}, bf16[256,2,256]{2,1,0:T(2,128)(2,1)S(1)}, u32[]{:S(2)}, u32[]{:S(2)}) collective-permute-start(bf16[256,2,256]{2,1,0:T(2,128)(2,1)S(1)} %collective-permute-done.3.refs_1_), channel_id=1, source_target_pairs={{0,4},{8,0},{16,8},{24,16},{28,24},{20,28},{12,20},{4,12},{1,5},{9... | collective-permute-start | bytes 786440 | tf_op jit(solution)/shard_map/ppermute | solution.py:99
  19.7 8.1 %collective-permute-start.7 = (bf16[608,128]{1,0:T(8,128)(2,1)S(1)}, bf16[608,128]{1,0:T(8,128)(2,1)S(1)}, u32[]{:S(2)}, u32[]{:S(2)}) collective-permute-start(bf16[608,128]{1,0:T(8,128)(2,1)S(1)} %pad_maximum_fusion), channel_id=1, source_target_pairs={{0,1},{1,0},{2,3},{3,2},{4,5},{5,4},{6,7},{7,6},{8,9},{9,8},{10,11... | collective-permute-start | bytes 466952 | tf_op jit(solution)/shard_map/ppermute | solution.py:267
  25.7 5.0 %collective-permute-start.8 = (bf16[128,2,256]{2,1,0:T(2,128)(2,1)S(1)}, bf16[128,2,256]{2,1,0:T(2,128)(2,1)S(1)}, u32[]{:S(2)}, u32[]{:S(2)}) collective-permute-start(bf16[128,2,256]{2,1,0:T(2,128)(2,1)S(1)} %slice.10), channel_id=1, source_target_pairs={{0,8},{8,16},{16,24},{24,28},{28,20},{20,12},{12,4},{4,0},{1,9},{9... | collective-permute-start | bytes 393224 | tf_op jit(solution)/shard_map/ppermute | solution.py:114
  27.3 5.0 %collective-permute-start.9 = (bf16[128,2,256]{2,1,0:T(2,128)(2,1)S(1)}, bf16[128,2,256]{2,1,0:T(2,128)(2,1)S(1)}, u32[]{:S(2)}, u32[]{:S(2)}) collective-permute-start(bf16[128,2,256]{2,1,0:T(2,128)(2,1)S(1)} %slice.11), channel_id=1, source_target_pairs={{0,4},{8,0},{16,8},{24,16},{28,24},{20,28},{12,20},{4,12},{1,5},{9... | collective-permute-start | bytes 393224 | tf_op jit(solution)/shard_map/ppermute | solution.py:114
  27.8 4.5 %copy-start.2 = (bf16[304,128]{1,0:T(8,128)(2,1)S(1)}, bf16[304,128]{1,0:T(8,128)(2,1)}, u32[]{:S(2)}) copy-start(bf16[304,128]{1,0:T(8,128)(2,1)} %get-tuple-element.36.refs_2_.refs_0_) | copy-start | bytes 233476
  27.8 4.5 %copy-start.3 = (f32[8,128]{1,0:T(8,128)S(1)}, f32[8,128]{1,0:T(8,128)}, u32[]{:S(2)}) copy-start(f32[8,128]{1,0:T(8,128)} %get-tuple-element.32.refs_1_) | copy-start | bytes 12292
  32.3 12.6 %copy-start.4 = (s32[4]{0:T(128)S(1)}, s32[4]{0:T(128)}, u32[]{:S(2)}) copy-start(s32[4]{0:T(128)} %counts_ref.1) | copy-start | bytes 52

commit v10 on v8

--- a/solution.py
+++ b/solution.py
@@ -47,7 +47,8 @@
 
 def accumulate(cholesky_rot, shifts, parts, total, mark):
     vectors, orbitals, _ = cholesky_rot.shape
-    rows, walkers, _ = parts[0].shape
+    walkers = parts[0].shape[1]
+    rows = sum(x.shape[0] for x in parts) // len(shifts)
     size = vectors * orbitals
     arrays = list(parts) + ([] if mark is None else [mark]) + ([] if total is None else [total])
 
@@ -87,35 +88,39 @@
 
 def ring(own, cholesky_rot, onebody, packed):
     size = lax.axis_size("chol")
+    half = own.shape[0] // 2
     order = ring_order(size)
 
     def send(x, places):
         return lax.ppermute(x, "chol", [(order[q], order[(q + places) % size]) for q in range(size)])
 
-    steps = size // 2 - 1
-    right, left = send(own, 1), send(own, -1)
-    opposite = send(own, size // 2)
+    steps = size // 2
+    right, back = send(own, 1), send(own, -1)
     right, onebody = tie(right, onebody)
-    left, *packed = tie(left, *packed)
-    shifts, parts = [0, -1, 1], [own, right, left]
-    total = mark = None
-    for step in range(2, steps + 1):
-        next_right, next_left = send(right, 1), send(left, -1)
+    upper, lower = send(right[:half], 1), send(right[half:], 1)
+    back, *packed = tie(back, *packed)
+    next_back = send(back, -1)
+    far = exchange_far(packed)
+    total, mark = accumulate(cholesky_rot, [0, -1, 1], [own, right, back], None, None)
+    back = next_back
+    shifts, parts = [], []
+    for step in range(2, steps):
+        upper, mark = tie(upper, mark)
+        next_upper = send(upper, 1)
+        lower, mark = tie(lower, mark)
+        next_lower = send(lower, 1)
+        shifts, parts = shifts + [-step], parts + [upper, lower]
+        if step < steps - 1:
+            back, mark = tie(back, mark)
+            next_back = send(back, -1)
+            shifts, parts = shifts + [step], parts + [back]
+            back = next_back
         if step == 2:
-            far = exchange_far(packed)
-        elif step == 3:
             near = exchange_near(packed, far)
-        if step == steps:
-            opposite, mark = tie(opposite, mark)
-            shifts, parts = shifts + [size // 2], parts + [opposite]
         total, mark = accumulate(cholesky_rot, shifts, parts, total, mark)
-        right, mark = tie(next_right, mark)
-        if step == 2:
-            left, mark, far = tie(next_left, mark, far)
-        else:
-            left, mark = tie(next_left, mark)
-        shifts, parts = [-step, step], [right, left]
-    return onebody, total, shifts, parts, [packed[0], far] + near
+        shifts, parts = [], []
+        upper, lower = next_upper, next_lower
+    return onebody, total, [-steps, steps - 1], [upper, lower, back], [packed[0], far] + near
 
 
 def table_height(vectors):
@@ -290,8 +295,7 @@
 
 def measure(cholesky_rot, total, shifts, last, packs, places, onebody, vectors, slots):
     _, walkers, orbitals = last[0].shape
-    rows = last[0].shape[0]
-    depth = rows * len(last)
+    rows = sum(x.shape[0] for x in last) // len(shifts)
     walk_size = len(places)
     targets = walk_size * lax.axis_size("chol")
     whole = total is None
@@ -374,8 +378,8 @@
         ],
         compiler_params=params(),
         cost_estimate=pl.CostEstimate(
-            flops=2 * vectors * orbitals * depth * walkers * orbitals,
-            bytes_accessed=2 * vectors * orbitals * depth,
+            flops=2 * vectors * orbitals * rows * len(shifts) * walkers * orbitals,
+            bytes_accessed=2 * vectors * orbitals * rows * len(shifts),
             transcendentals=0,
         ),
     )(cholesky_rot, onebody, *packs, *arrays)

time: 50.5 us -> 48.6 us (0.962)
  starting transfers between devices: 16.6 us -> 13.7 us
  waiting for transfers between devices: 5.75 us -> 8.57 us
  blocking collectives: 14.5 us -> 12.1 us
    ppermute x7 -> x10, waiting for transfers between devices: 4.41 us -> 8.56 us  [send(): lax.ppermute(x, 'chol', [(order[q], order[(q + places) % size]) for q in...]
    ppermute x7 -> x10, starting transfers between devices: 15 us -> 12.1 us  [send(): lax.ppermute(x, 'chol', [(order[q], order[(q + places) % size]) for q in...]
    all_to_all x1, blocking collectives: 14.5 us -> 12.1 us  [per_device(): lax.all_to_all(stats, ('chol', 'walk'), split_axis=0, concat_axis=0, tile...]
    ppermute x1, waiting for transfers between devices: 1.33 us -> 0.01 us  [exchange_far(): return lax.ppermute(packed[1], 'walk', [(q, q ^ 2) for q in range(size)])]
    pallas_call x2 -> x3, Pallas kernels: 5.48 us -> 5.91 us  [accumulate(): pl.pallas_call(kernel, name='accumulate', out_shape=[jax.ShapeDtypeStruct...]
  transfers between devices with their start and end apart: 9 -> 12, of which waited for: 5 -> 6; matrix products, arithmetic and copies ran while one was open for 0% -> 0% of each run, Pallas kernels for 17% -> 19%
where the time goes in v10:
time: 48.6 us; the launch traced here: 48.4 us
  starting transfers between devices  13.7 us (28%)
  Pallas kernels  13.1 us (27%)
  blocking collectives  12.1 us (25%)
  waiting for transfers between devices  8.57 us (18%)
  between operations  0.74 us (2%)
    all_to_all x1, blocking collectives, per_device(): lax.all_to_all(stats, ('chol', 'walk'), split_axis=0, concat_axis=0, tile...  12.1 us
    ppermute x10, starting transfers between devices, send(): lax.ppermute(x, 'chol', [(order[q], order[(q + places) % size]) for q in...  12.1 us
    ppermute x10, waiting for transfers between devices, send(): lax.ppermute(x, 'chol', [(order[q], order[(q + places) % size]) for q in...  8.56 us
    pallas_call x3, Pallas kernels, accumulate(): pl.pallas_call(kernel, name='accumulate', out_shape=[jax.ShapeDtypeStruct...  5.91 us
    pallas_call x1, Pallas kernels, pack(): pl.pallas_call(kernel, name='pack', out_shape=[jax.ShapeDtypeStruct((8, L...  3.32 us
    pallas_call x1, Pallas kernels, measure(): pl.pallas_call(kernel, name='measure', out_shape=jax.ShapeDtypeStruct((ta...  2.4 us
    ppermute x1, starting transfers between devices, exchange_far(): return lax.ppermute(packed[1], 'walk', [(q, q ^ 2) for q in range(size)])  1.6 us
    pallas_call x1, Pallas kernels, finish(): pl.pallas_call(kernel, name='finish', out_shape=[jax.ShapeDtypeStruct((1,...  1.43 us
  transfers between devices with their start and end apart: 12, of which 6 were waited for; matrix products, arithmetic and copies ran while one was open for 0% of the time, Pallas kernels for 19%

profile of v10, /device:TPU:0, one launch (start us, length us, event | category | flops | bytes accessed | tf_op | source)
XLA Modules:
  0.0 48.4 jit_solution(2841002754620624027)
XLA Ops:
  0.6 3.0 %collective-permute-start.1 = (bf16[256,2,256]{2,1,0:T(2,128)(2,1)}, bf16[256,2,256]{2,1,0:T(2,128)(2,1)S(1)}, u32[]{:S(2)}, u32[]{:S(2)}) collective-permute-start(bf16[256,2,256]{2,1,0:T(2,128)(2,1)} %refs_0_.2), channel_id=1, source_target_pairs={{0,4},{8,0},{16,8},{24,16},{28,24},{20,28},{12,20},{4,12},{1,5},{9... | collective-permute-start | bytes 786440 | tf_op jit(solution)/shard_map/ppermute | solution.py:95
  3.8 3.3 %pack.1 = (f32[8,128]{1,0:T(8,128)}, bf16[304,128]{1,0:T(8,128)(2,1)}, bf16[560,128]{1,0:T(8,128)(2,1)}, bf16[304,128]{1,0:T(8,128)(2,1)}) custom-call(bf16[256,2,256]{2,1,0:T(2,128)(2,1)} %refs_0_.2, bf16[256,256]{1,0:T(8,128)(2,1)} %body_any.1, f32[4,8]{1,0:T(4,128)} %bitcast.10, f32[2]{0:T(128)} %weights_any.1, s32[4]{0:T(128)} %sources_any.1, ...), custom_call_target="tpu_custom_call" | custom-call | flops 100000000 | bytes 1000000 | tf_op jit(solution)/shard_map/pack/pallas_call | solution.py:228
  7.1 3.1 %collective-permute-done.1.refs_2_ = bf16[256,2,256]{2,1,0:T(2,128)(2,1)S(1)} collective-permute-done((bf16[256,2,256]{2,1,0:T(2,128)(2,1)}, bf16[256,2,256]{2,1,0:T(2,128)(2,1)S(1)}, u32[]{:S(2)}, u32[]{:S(2)}) %collective-permute-start.1) | collective-permute-done | bytes 262176 | tf_op jit(solution)/shard_map/ppermute | solution.py:95
  10.2 1.4 %collective-permute-done.refs_1_ = bf16[256,2,256]{2,1,0:T(2,128)(2,1)S(1)} collective-permute-done((bf16[256,2,256]{2,1,0:T(2,128)(2,1)}, bf16[256,2,256]{2,1,0:T(2,128)(2,1)S(1)}, u32[]{:S(2)}, u32[]{:S(2)}) %collective-permute-start) | collective-permute-done | bytes 262176 | tf_op jit(solution)/shard_map/ppermute | solution.py:95
  11.6 0.2 fusion
  11.8 0.5 collective-permute-start.4
  12.3 1.7 %collective-permute-start.6 = (bf16[128,2,256]{2,1,0:T(2,128)(2,1)S(1)}, bf16[128,2,256]{2,1,0:T(2,128)(2,1)S(1)}, u32[]{:S(2)}, u32[]{:S(2)}) collective-permute-start(bf16[128,2,256]{2,1,0:T(2,128)(2,1)S(1)} %get-tuple-element.59), channel_id=1, source_target_pairs={{0,8},{8,16},{16,24},{24,28},{28,20},{20,12},{12,4},{4,0},{1,9},{9... | collective-permute-start | bytes 393224 | tf_op jit(solution)/shard_map/ppermute | solution.py:95
  14.0 0.3 collective-permute-start.7
  14.3 1.6 %collective-permute-start.2 = (bf16[560,128]{1,0:T(8,128)(2,1)}, bf16[560,128]{1,0:T(8,128)(2,1)S(1)}, u32[]{:S(2)}, u32[]{:S(2)}) collective-permute-start(bf16[560,128]{1,0:T(8,128)(2,1)} %get-tuple-element.37), channel_id=1, source_target_pairs={{0,2},{1,3},{2,0},{3,1},{4,6},{5,7},{6,4},{7,5},{8,10},{9,11},{10,... | collective-permute-start | bytes 430088 | tf_op jit(solution)/shard_map/ppermute | solution.py:262
  15.9 2.5 %accumulate.3 = (f32[2,2048,256]{2,1,0:T(8,128)S(1)}, f32[8,128]{1,0:T(8,128)S(1)}) custom-call(bf16[8,256,2048]{2,1,0:T(8,128)(2,1)S(1)} %copy-done, bf16[256,2,256]{2,1,0:T(2,128)(2,1)S(1)} %copy-done.1, bf16[256,2,256]{2,1,0:T(2,128)(2,1)S(1)} %collective-permute-done.refs_1_, bf16[256,2,256]{2,1,0:T(2,128)(2,1)S(1)} %collective-permute-done.1.refs_2_), custom_call_target="tpu_custom_call" | custom-call | flops 1610612736 | bytes 3145728 | tf_op jit(solution)/shard_map/accumulate/pallas_call | solution.py:67
  18.4 0.3 collective-permute-done.6.refs_1_
  18.7 1.3 %collective-permute-start.5 = (bf16[128,2,256]{2,1,0:T(2,128)(2,1)S(1)}, bf16[128,2,256]{2,1,0:T(2,128)(2,1)S(1)}, u32[]{:S(2)}, u32[]{:S(2)}) collective-permute-start(bf16[128,2,256]{2,1,0:T(2,128)(2,1)S(1)} %collective-permute-done.4.refs_0_), channel_id=1, source_target_pairs={{0,8},{8,16},{16,24},{24,28},{28,20},{20,12},{12,4},{4,0},{1,9},{9... | collective-permute-start | bytes 393224 | tf_op jit(solution)/shard_map/ppermute | solution.py:95
  20.0 1.6 %collective-permute-start.9 = (bf16[128,2,256]{2,1,0:T(2,128)(2,1)S(1)}, bf16[128,2,256]{2,1,0:T(2,128)(2,1)S(1)}, u32[]{:S(2)}, u32[]{:S(2)}) collective-permute-start(bf16[128,2,256]{2,1,0:T(2,128)(2,1)S(1)} %collective-permute-done.6.refs_1_), channel_id=1, source_target_pairs={{0,8},{8,16},{16,24},{24,28},{28,20},{20,12},{12,4},{4,0},{1,9},{9... | collective-permute-start | bytes 393224 | tf_op jit(solution)/shard_map/ppermute | solution.py:95
  21.7 0.5 %collective-permute-start.11 = (bf16[256,2,256]{2,1,0:T(2,128)(2,1)S(1)}, bf16[256,2,256]{2,1,0:T(2,128)(2,1)S(1)}, u32[]{:S(2)}, u32[]{:S(2)}) collective-permute-start(bf16[256,2,256]{2,1,0:T(2,128)(2,1)S(1)} %collective-permute-done.7.refs_2_), channel_id=1, source_target_pairs={{0,4},{8,0},{16,8},{24,16},{28,24},{20,28},{12,20},{4,12},{1,5},{9... | collective-permute-start | bytes 786440 | tf_op jit(solution)/shard_map/ppermute | solution.py:95
  22.2 1.8 %accumulate.4 = (f32[2,2048,256]{2,1,0:T(8,128)S(1)}, f32[8,128]{1,0:T(8,128)S(1)}) custom-call(bf16[8,256,2048]{2,1,0:T(8,128)(2,1)S(1)} %copy-done, bf16[128,2,256]{2,1,0:T(2,128)(2,1)S(1)} %collective-permute-done.4.refs_0_, bf16[128,2,256]{2,1,0:T(2,128)(2,1)S(1)} %collective-permute-done.6.refs_1_, ...), custom_call_target="tpu_custom_call" | custom-call | flops 1610612736 | bytes 3145728 | tf_op jit(solution)/shard_map/accumulate/pallas_call | solution.py:67
  24.0 1.1 %collective-permute-done.9.refs_1_ = bf16[128,2,256]{2,1,0:T(2,128)(2,1)S(1)} collective-permute-done((bf16[128,2,256]{2,1,0:T(2,128)(2,1)S(1)}, bf16[128,2,256]{2,1,0:T(2,128)(2,1)S(1)}, u32[]{:S(2)}, u32[]{:S(2)}) %collective-permute-start.9) | collective-permute-done | bytes 131104 | tf_op jit(solution)/shard_map/ppermute | solution.py:95
  25.1 1.5 %collective-permute-start.10 = (bf16[128,2,256]{2,1,0:T(2,128)(2,1)S(1)}, bf16[128,2,256]{2,1,0:T(2,128)(2,1)S(1)}, u32[]{:S(2)}, u32[]{:S(2)}) collective-permute-start(bf16[128,2,256]{2,1,0:T(2,128)(2,1)S(1)} %collective-permute-done.9.refs_1_), channel_id=1, source_target_pairs={{0,8},{8,16},{16,24},{24,28},{28,20},{20,12},{12,4},{4,0},{1,9},{9... | collective-permute-start | bytes 393224 | tf_op jit(solution)/shard_map/ppermute | solution.py:95
  26.6 1.6 %collective-permute-start.8 = (bf16[128,2,256]{2,1,0:T(2,128)(2,1)S(1)}, bf16[128,2,256]{2,1,0:T(2,128)(2,1)S(1)}, u32[]{:S(2)}, u32[]{:S(2)}) collective-permute-start(bf16[128,2,256]{2,1,0:T(2,128)(2,1)S(1)} %collective-permute-done.5.refs_0_), channel_id=1, source_target_pairs={{0,8},{8,16},{16,24},{24,28},{28,20},{20,12},{12,4},{4,0},{1,9},{9... | collective-permute-start | bytes 393224 | tf_op jit(solution)/shard_map/ppermute | solution.py:95
  28.2 1.7 %accumulate.5 = (f32[2,2048,256]{2,1,0:T(8,128)S(1)}, f32[8,128]{1,0:T(8,128)}) custom-call(bf16[8,256,2048]{2,1,0:T(8,128)(2,1)S(1)} %copy-done, bf16[128,2,256]{2,1,0:T(2,128)(2,1)S(1)} %collective-permute-done.5.refs_0_, bf16[128,2,256]{2,1,0:T(2,128)(2,1)S(1)} %collective-permute-done.9.refs_1_, f32[8,128]{1,0:T(8,128)S(1)} %get-tuple-element.53.refs_2_, ...), custom_call_target="tpu_custom_call" | custom-call | flops 1073741824 | bytes 2097152 | tf_op jit(solution)/shard_map/accumulate/pallas_call | solution.py:67
  29.8 1.2 %collective-permute-done.10.refs_6_ = bf16[128,2,256]{2,1,0:T(2,128)(2,1)S(1)} collective-permute-done((bf16[128,2,256]{2,1,0:T(2,128)(2,1)S(1)}, bf16[128,2,256]{2,1,0:T(2,128)(2,1)S(1)}, u32[]{:S(2)}, u32[]{:S(2)}) %collective-permute-start.10) | collective-permute-done | bytes 131104 | tf_op jit(solution)/shard_map/ppermute | solution.py:95
  31.1 1.4 %collective-permute-done.8.refs_5_ = bf16[128,2,256]{2,1,0:T(2,128)(2,1)S(1)} collective-permute-done((bf16[128,2,256]{2,1,0:T(2,128)(2,1)S(1)}, bf16[128,2,256]{2,1,0:T(2,128)(2,1)S(1)}, u32[]{:S(2)}, u32[]{:S(2)}) %collective-permute-start.8) | collective-permute-done | bytes 131104 | tf_op jit(solution)/shard_map/ppermute | solution.py:95
  32.5 2.4 %measure.1 = f32[32,128]{1,0:T(8,128)S(1)} custom-call(bf16[8,256,2048]{2,1,0:T(8,128)(2,1)S(1)} %copy-done, f32[8,128]{1,0:T(8,128)S(1)} %copy-done.3, bf16[304,128]{1,0:T(8,128)(2,1)S(1)} %copy-done.2, bf16[560,128]{1,0:T(8,128)(2,1)S(1)} %collective-permute-done.2.refs_3_.refs_1_, bf16[608,128]{1,0:T(8,128)(2,1)S(1)} %collective-permute-done.3.refs_4_.refs_2_, ...), custom_call_target="tpu_custom_call" | custom-call | flops 1073741824 | bytes 2097152 | tf_op jit(solution)/shard_map/measure/pallas_call | solution.py:370
  34.9 12.1 %all_to_all.11 = f32[32,1,128]{2,1,0:T(1,128)S(1)} all-to-all(f32[32,1,128]{2,1,0:T(1,128)S(1)} %bitcast.8), channel_id=1, replica_groups=mesh['chol'=8,'walk'=4] {'chol','walk'}, dimensions={0} | all-to-all | bytes 32768 | tf_op jit(solution)/shard_map/all_to_all | solution.py:455
  47.0 1.4 %finish.1 = (f32[1,4]{1,0:T(1,128)}, f32[1,4]{1,0:T(1,128)}, f32[128,128]{1,0:T(8,128)}) custom-call(f32[32,128]{1,0:T(8,128)S(1)} %bitcast.9, s32[4]{0:T(128)S(1)} %copy-done.4, bf16[304,128]{1,0:T(8,128)(2,1)S(1)} %copy-done.2, bf16[560,128]{1,0:T(8,128)(2,1)S(1)} %collective-permute-done.2.refs_3_.refs_1_, ...), custom_call_target="tpu_custom_call" | custom-call | flops 1000000 | bytes 600000 | tf_op jit(solution)/shard_map/finish/pallas_call | solution.py:425
  (22 shorter events, 0.3 us)
Async XLA Ops:
  0.6 9.6 %collective-permute-start.1 = (bf16[256,2,256]{2,1,0:T(2,128)(2,1)}, bf16[256,2,256]{2,1,0:T(2,128)(2,1)S(1)}, u32[]{:S(2)}, u32[]{:S(2)}) collective-permute-start(bf16[256,2,256]{2,1,0:T(2,128)(2,1)} %refs_0_.2), channel_id=1, source_target_pairs={{0,4},{8,0},{16,8},{24,16},{28,24},{20,28},{12,20},{4,12},{1,5},{9... | collective-permute-start | bytes 786440 | tf_op jit(solution)/shard_map/ppermute | solution.py:95
  3.7 8.0 %collective-permute-start = (bf16[256,2,256]{2,1,0:T(2,128)(2,1)}, bf16[256,2,256]{2,1,0:T(2,128)(2,1)S(1)}, u32[]{:S(2)}, u32[]{:S(2)}) collective-permute-start(bf16[256,2,256]{2,1,0:T(2,128)(2,1)} %refs_0_.2), channel_id=1, source_target_pairs={{0,8},{8,16},{16,24},{24,28},{28,20},{20,12},{12,4},{4,0},{1,9},{9... | collective-permute-start | bytes 786440 | tf_op jit(solution)/shard_map/ppermute | solution.py:95
  3.8 12.1 %copy-start = (bf16[8,256,2048]{2,1,0:T(8,128)(2,1)S(1)}, bf16[8,256,2048]{2,1,0:T(8,128)(2,1)}, u32[]{:S(2)}) copy-start(bf16[8,256,2048]{2,1,0:T(8,128)(2,1)} %refs_0_.3) | copy-start | bytes 25165828
  3.8 12.1 %copy-start.1 = (bf16[256,2,256]{2,1,0:T(2,128)(2,1)S(1)}, bf16[256,2,256]{2,1,0:T(2,128)(2,1)}, u32[]{:S(2)}) copy-start(bf16[256,2,256]{2,1,0:T(2,128)(2,1)} %refs_0_.2) | copy-start | bytes 786436
  11.8 6.6 %collective-permute-start.4 = (bf16[128,2,256]{2,1,0:T(2,128)(2,1)S(1)}, bf16[128,2,256]{2,1,0:T(2,128)(2,1)S(1)}, u32[]{:S(2)}, u32[]{:S(2)}) collective-permute-start(bf16[128,2,256]{2,1,0:T(2,128)(2,1)S(1)} %get-tuple-element.60), channel_id=1, source_target_pairs={{0,8},{8,16},{16,24},{24,28},{28,20},{20,12},{12,4},{4,0},{1,9},{9... | collective-permute-start | bytes 393224 | tf_op jit(solution)/shard_map/ppermute | solution.py:95
  12.3 9.3 %copy-start.5 = (bf16[304,128]{1,0:T(8,128)(2,1)S(1)}, bf16[304,128]{1,0:T(8,128)(2,1)}, u32[]{:S(2)}) copy-start(bf16[304,128]{1,0:T(8,128)(2,1)} %get-tuple-element.38) | copy-start | bytes 233476
  12.3 6.5 %collective-permute-start.6 = (bf16[128,2,256]{2,1,0:T(2,128)(2,1)S(1)}, bf16[128,2,256]{2,1,0:T(2,128)(2,1)S(1)}, u32[]{:S(2)}, u32[]{:S(2)}) collective-permute-start(bf16[128,2,256]{2,1,0:T(2,128)(2,1)S(1)} %get-tuple-element.59), channel_id=1, source_target_pairs={{0,8},{8,16},{16,24},{24,28},{28,20},{20,12},{12,4},{4,0},{1,9},{9... | collective-permute-start | bytes 393224 | tf_op jit(solution)/shard_map/ppermute | solution.py:95
  14.0 7.8 %collective-permute-start.7 = (bf16[256,2,256]{2,1,0:T(2,128)(2,1)S(1)}, bf16[256,2,256]{2,1,0:T(2,128)(2,1)S(1)}, u32[]{:S(2)}, u32[]{:S(2)}) collective-permute-start(bf16[256,2,256]{2,1,0:T(2,128)(2,1)S(1)} %collective-permute-done.1.refs_2_), channel_id=1, source_target_pairs={{0,4},{8,0},{16,8},{24,16},{28,24},{20,28},{12,20},{4,12},{1,5},{9... | collective-permute-start | bytes 786440 | tf_op jit(solution)/shard_map/ppermute | solution.py:95
  14.3 7.3 %collective-permute-start.2 = (bf16[560,128]{1,0:T(8,128)(2,1)}, bf16[560,128]{1,0:T(8,128)(2,1)S(1)}, u32[]{:S(2)}, u32[]{:S(2)}) collective-permute-start(bf16[560,128]{1,0:T(8,128)(2,1)} %get-tuple-element.37), channel_id=1, source_target_pairs={{0,2},{1,3},{2,0},{3,1},{4,6},{5,7},{6,4},{7,5},{8,10},{9,11},{10,... | collective-permute-start | bytes 430088 | tf_op jit(solution)/shard_map/ppermute | solution.py:262
  18.7 5.3 %collective-permute-start.5 = (bf16[128,2,256]{2,1,0:T(2,128)(2,1)S(1)}, bf16[128,2,256]{2,1,0:T(2,128)(2,1)S(1)}, u32[]{:S(2)}, u32[]{:S(2)}) collective-permute-start(bf16[128,2,256]{2,1,0:T(2,128)(2,1)S(1)} %collective-permute-done.4.refs_0_), channel_id=1, source_target_pairs={{0,8},{8,16},{16,24},{24,28},{28,20},{20,12},{12,4},{4,0},{1,9},{9... | collective-permute-start | bytes 393224 | tf_op jit(solution)/shard_map/ppermute | solution.py:95
  20.0 5.1 %collective-permute-start.9 = (bf16[128,2,256]{2,1,0:T(2,128)(2,1)S(1)}, bf16[128,2,256]{2,1,0:T(2,128)(2,1)S(1)}, u32[]{:S(2)}, u32[]{:S(2)}) collective-permute-start(bf16[128,2,256]{2,1,0:T(2,128)(2,1)S(1)} %collective-permute-done.6.refs_1_), channel_id=1, source_target_pairs={{0,8},{8,16},{16,24},{24,28},{28,20},{20,12},{12,4},{4,0},{1,9},{9... | collective-permute-start | bytes 393224 | tf_op jit(solution)/shard_map/ppermute | solution.py:95
  21.6 8.2 %collective-permute-start.3 = (bf16[608,128]{1,0:T(8,128)(2,1)S(1)}, bf16[608,128]{1,0:T(8,128)(2,1)S(1)}, u32[]{:S(2)}, u32[]{:S(2)}) collective-permute-start(bf16[608,128]{1,0:T(8,128)(2,1)S(1)} %pad_maximum_fusion), channel_id=1, source_target_pairs={{0,1},{1,0},{2,3},{3,2},{4,5},{5,4},{6,7},{7,6},{8,9},{9,8},{10,11... | collective-permute-start | bytes 466952 | tf_op jit(solution)/shard_map/ppermute | solution.py:273
  21.7 10.7 %collective-permute-start.11 = (bf16[256,2,256]{2,1,0:T(2,128)(2,1)S(1)}, bf16[256,2,256]{2,1,0:T(2,128)(2,1)S(1)}, u32[]{:S(2)}, u32[]{:S(2)}) collective-permute-start(bf16[256,2,256]{2,1,0:T(2,128)(2,1)S(1)} %collective-permute-done.7.refs_2_), channel_id=1, source_target_pairs={{0,4},{8,0},{16,8},{24,16},{28,24},{20,28},{12,20},{4,12},{1,5},{9... | collective-permute-start | bytes 786440 | tf_op jit(solution)/shard_map/ppermute | solution.py:95
  25.1 6.0 %collective-permute-start.10 = (bf16[128,2,256]{2,1,0:T(2,128)(2,1)S(1)}, bf16[128,2,256]{2,1,0:T(2,128)(2,1)S(1)}, u32[]{:S(2)}, u32[]{:S(2)}) collective-permute-start(bf16[128,2,256]{2,1,0:T(2,128)(2,1)S(1)} %collective-permute-done.9.refs_1_), channel_id=1, source_target_pairs={{0,8},{8,16},{16,24},{24,28},{28,20},{20,12},{12,4},{4,0},{1,9},{9... | collective-permute-start | bytes 393224 | tf_op jit(solution)/shard_map/ppermute | solution.py:95
  26.6 5.9 %collective-permute-start.8 = (bf16[128,2,256]{2,1,0:T(2,128)(2,1)S(1)}, bf16[128,2,256]{2,1,0:T(2,128)(2,1)S(1)}, u32[]{:S(2)}, u32[]{:S(2)}) collective-permute-start(bf16[128,2,256]{2,1,0:T(2,128)(2,1)S(1)} %collective-permute-done.5.refs_0_), channel_id=1, source_target_pairs={{0,8},{8,16},{16,24},{24,28},{28,20},{20,12},{12,4},{4,0},{1,9},{9... | collective-permute-start | bytes 393224 | tf_op jit(solution)/shard_map/ppermute | solution.py:95
  28.2 4.3 %copy-start.2 = (bf16[304,128]{1,0:T(8,128)(2,1)S(1)}, bf16[304,128]{1,0:T(8,128)(2,1)}, u32[]{:S(2)}) copy-start(bf16[304,128]{1,0:T(8,128)(2,1)} %get-tuple-element.36.refs_2_.refs_0_) | copy-start | bytes 233476
  28.2 4.3 %copy-start.3 = (f32[8,128]{1,0:T(8,128)S(1)}, f32[8,128]{1,0:T(8,128)}, u32[]{:S(2)}) copy-start(f32[8,128]{1,0:T(8,128)} %get-tuple-element.32.refs_1_) | copy-start | bytes 12292
  32.5 14.5 %copy-start.4 = (s32[4]{0:T(128)S(1)}, s32[4]{0:T(128)}, u32[]{:S(2)}) copy-start(s32[4]{0:T(128)} %counts_ref.1) | copy-start | bytes 52

commit v11 on v9

--- a/solution.py
+++ b/solution.py
@@ -85,7 +85,7 @@
     return lax.optimization_barrier(arrays)
 
 
-def ring(own, cholesky_rot, onebody, packed):
+def ring(own, cholesky_rot, onebody, packed, do_prepare):
     size = lax.axis_size("chol")
     rows = own.shape[0]
     order = ring_order(size)
@@ -113,8 +113,11 @@
         parts = parts + [right, left]
     last = [lax.ppermute(right[: rows // 2], "chol", ahead), lax.ppermute(left[rows // 2 :], "chol", back)]
     mark, *near = tie(mark, *near)
+    packs = [packed[0], far] + near
+    plan = do_prepare(packs)
+    mark, plan = tie(mark, plan)
     total, _ = accumulate(cholesky_rot, shifts, parts, total, mark)
-    return onebody, total, last, [packed[0], far] + near
+    return total, last, packs, plan
 
 
 def table_height(vectors):
@@ -287,35 +290,76 @@
     return total
 
 
-def measure(cholesky_rot, total, last, packs, places, onebody, vectors, slots):
+def plan_rows(vectors, walkers, walk_size):
+    shares = walkers * vectors
+    picks = shares + walkers * walk_size
+    single = picks + walkers
+    return 0, shares, picks, single, single + 1, single + 2, -(-(single + 3) // 8) * 8
+
+
+def prepare(packs, places, onebody, counts, vectors, slots, walkers):
+    walk_size = len(places)
+    at_drive, at_share, at_pick, at_single, at_live, at_mean, height = plan_rows(vectors, walkers, walk_size)
+
+    def kernel(counts_ref, onebody_ref, *refs):
+        pack_refs, plan_ref = refs[:-1], refs[-1]
+        walk = lax.axis_index("walk")
+        lane = lax.broadcasted_iota(jnp.int32, (1, LANES), 1)
+        all_slots = slots * walk_size
+        tables = [read_table(pack_refs[n], at, vectors) for n, _, at in places]
+        table = merge_tables(tables, walk, walk_size, slots, lane)
+        source = jnp.where(lane < all_slots, table[vectors : vectors + 1, :], -1.0)
+        total_weight = tables[0][vectors + 1 : vectors + 2, :]
+        for t in tables[1:]:
+            total_weight = total_weight + t[vectors + 1 : vectors + 2, :]
+        live_count = jnp.zeros((1, LANES), jnp.int32)
+        for q in range(walk_size):
+            live_count = jnp.where(lane // slots == q, counts_ref[q], live_count)
+        live = (lane < all_slots) & (lane % slots < live_count)
+        plan_ref[...] = jnp.zeros_like(plan_ref)
+        single = jnp.zeros((1, LANES), jnp.float32)
+        for b in range(walkers):
+            pick = jnp.where(source == (walk * walkers + b).astype(jnp.float32), 1.0, 0.0)
+            plan_ref[at_pick + b : at_pick + b + 1, :] = pick
+            plan_ref[at_drive + b * vectors : at_drive + (b + 1) * vectors, :] = -root_step * pick * table[:vectors, :]
+            single += pick * jnp.sum(onebody_ref[b : b + 1, :], axis=1, keepdims=True)
+        plan_ref[at_single : at_single + 1, :] = single
+        for d in range(walk_size):
+            group = walk_partner(walk, d, walk_size, True)
+            for b in range(walkers):
+                row = at_share + d * walkers + b
+                plan_ref[row : row + 1, :] = jnp.where(
+                    source == (group * walkers + b).astype(jnp.float32), 1.0, 0.0
+                )
+        plan_ref[at_live : at_live + 1, :] = jnp.where(live, 1.0, 0.0)
+        plan_ref[at_mean : at_mean + 1, :] = total_weight / (walkers * walk_size)
+
+    return pl.pallas_call(
+        kernel,
+        name="prepare",
+        out_shape=jax.ShapeDtypeStruct((height, LANES), jnp.float32),
+        in_specs=[smem()] + [vmem()] * (1 + len(packs)),
+        out_specs=vmem(),
+        compiler_params=params(),
+        cost_estimate=pl.CostEstimate(flops=10**8, bytes_accessed=10**6, transcendentals=0),
+    )(counts, onebody, *packs)
+
+
+def measure(cholesky_rot, total, last, plan, vectors, walk_size):
     _, walkers, orbitals = last[0].shape
     depth = sum(x.shape[0] for x in last)
-    walk_size = len(places)
     targets = walk_size * lax.axis_size("chol")
     whole = total is None
     quads = orbitals // LANES
+    at_drive, _, at_pick, at_single, _, _, _ = plan_rows(vectors, walkers, walk_size)
 
     def fold(x):
         return jnp.sum(x.reshape(-1, 8, LANES), axis=0)
 
     def kernel(*refs):
-        chol_ref, onebody_ref = refs[:2]
-        pack_refs = refs[2 : 2 + len(packs)]
-        last_refs = refs[2 + len(packs) : 2 + len(packs) + len(last)]
+        chol_ref, plan_ref = refs[:2]
+        last_refs = refs[2 : 2 + len(last)]
         out_ref, tensor_scr = refs[-2:]
-        walk = lax.axis_index("walk")
-        lane = lax.broadcasted_iota(jnp.int32, (1, LANES), 1)
-        table = merge_tables(
-            [read_table(pack_refs[n], at, vectors) for n, _, at in places], walk, walk_size, slots, lane
-        )
-        picks = [
-            jnp.where(
-                (lane < slots * walk_size) & (table[vectors : vectors + 1, :] == (walk * walkers + b).astype(jnp.float32)),
-                1.0,
-                0.0,
-            )
-            for b in range(walkers)
-        ]
         rhs = [jnp.concatenate([x[:, b, :] for x in last_refs], axis=0) for b in range(walkers)]
         eye = lax.broadcasted_iota(jnp.int32, (LANES, LANES), 0) == lax.broadcasted_iota(
             jnp.int32, (LANES, LANES), 1
@@ -327,7 +371,7 @@
         lhs = chol_ref[:, :, pl.ds(start, depth)].reshape(vectors * orbitals, depth)
         for b in range(walkers):
             value = jnp.dot(lhs, rhs[b], preferred_element_type=jnp.float32)
-            tensor_scr[b] = value if whole else refs[2 + len(packs) + len(last)][b] + value
+            tensor_scr[b] = value if whole else refs[2 + len(last)][b] + value
         for g in range(vectors):
             top = g * orbitals
             for b in range(walkers):
@@ -348,23 +392,24 @@
                 trace = jnp.sum(fold(jnp.where(eye, diagonal, 0.0)), axis=0, keepdims=True)
                 trace = jnp.sum(trace, axis=1, keepdims=True)
                 squares[b] = squares[b] + trace * trace
-                drive = drive - root_step * picks[b] * table[g : g + 1, :] * trace
-        raw = jnp.zeros((1, LANES), jnp.float32)
+                row = at_drive + b * vectors + g
+                drive = drive + plan_ref[row : row + 1, :] * trace
+        raw = plan_ref[at_single : at_single + 1, :]
         square = jnp.zeros((1, LANES), jnp.float32)
         for b in range(walkers):
             swapped = jnp.sum(jnp.sum(exchange[b], axis=0, keepdims=True), axis=1, keepdims=True)
-            single = jnp.sum(onebody_ref[b : b + 1, :], axis=1, keepdims=True)
-            raw += picks[b] * (single + 0.5 * squares[b] - 0.5 * swapped)
-            square += picks[b] * squares[b]
+            pick = plan_ref[at_pick + b : at_pick + b + 1, :]
+            raw += pick * (0.5 * squares[b] - 0.5 * swapped)
+            square += pick * squares[b]
         power = drive - 0.5 * time_step * square - time_step * raw
-        out_ref[...] = jnp.broadcast_to(raw + pltpu.roll(power, slots * walk_size, 1), (targets, LANES))
+        out_ref[...] = jnp.broadcast_to(raw + pltpu.roll(power, LANES // 2, 1), (targets, LANES))
 
     arrays = list(last) + ([] if whole else [total])
     return pl.pallas_call(
         kernel,
         name="measure",
         out_shape=jax.ShapeDtypeStruct((targets, LANES), jnp.float32),
-        in_specs=[vmem()] * (2 + len(packs) + len(arrays)),
+        in_specs=[vmem()] * (2 + len(arrays)),
         out_specs=vmem(),
         scratch_shapes=[
             pltpu.VMEM((walkers, vectors * orbitals, orbitals), jnp.float32),
@@ -375,40 +420,31 @@
             bytes_accessed=2 * vectors * orbitals * depth,
             transcendentals=0,
         ),
-    )(cholesky_rot, onebody, *packs, *arrays)
-
-
-def finish(stats, packs, places, counts, vectors, slots, walkers):
+    )(cholesky_rot, plan, *arrays)
+
+
+def finish(stats, plan, packs, places, vectors, slots, walkers):
     walk_size = len(places)
     rows = (packs[0].shape[0] - 3 * table_height(vectors)) // walkers
-
-    def kernel(stats_ref, counts_ref, *refs):
+    _, at_share, at_pick, _, at_live, at_mean, _ = plan_rows(vectors, walkers, walk_size)
+
+    def kernel(stats_ref, plan_ref, *refs):
         pack_refs = refs[: len(packs)]
         energies_ref, weights_ref, density_ref = refs[len(packs) :]
         walk = lax.axis_index("walk")
-        lane = lax.broadcasted_iota(jnp.int32, (1, LANES), 1)
-        all_slots = slots * walk_size
-        tables = [read_table(pack_refs[n], at, vectors) for n, _, at in places]
-        source = merge_tables([t[vectors : vectors + 1, :] for t in tables], walk, walk_size, slots, lane)
-        total_weight = tables[0][vectors + 1 : vectors + 2, :]
-        for t in tables[1:]:
-            total_weight = total_weight + t[vectors + 1 : vectors + 2, :]
-        mean_weight = total_weight / (walkers * walk_size)
         total = jnp.sum(stats_ref[...], axis=0, keepdims=True)
-        power = pltpu.roll(total, LANES - all_slots, 1)
-        live_count = jnp.zeros((1, LANES), jnp.int32)
-        for q in range(walk_size):
-            live_count = jnp.where(lane // slots == q, counts_ref[q], live_count)
-        live = (lane < all_slots) & (lane % slots < live_count)
+        power = pltpu.roll(total, LANES // 2, 1)
+        live = plan_ref[at_live : at_live + 1, :] > 0.0
         energies = jnp.where(live, total, 0.0)
-        new_weights = jnp.where(live, mean_weight * jnp.exp(jnp.where(live, power, 0.0)), 0.0)
+        new_weights = jnp.where(
+            live, plan_ref[at_mean : at_mean + 1, :] * jnp.exp(jnp.where(live, power, 0.0)), 0.0
+        )
         norm = jnp.sum(new_weights, axis=1, keepdims=True)
+        shares = jnp.sum(plan_ref[at_share:at_pick, :] * new_weights, axis=1, keepdims=True) / norm
         density = jnp.zeros((rows, LANES), jnp.float32)
         for d, (n, top, _) in enumerate(places):
-            group = walk_partner(walk, d, walk_size, True)
             for b in range(walkers):
-                walker = (group * walkers + b).astype(jnp.float32)
-                share = jnp.sum(jnp.where(source == walker, new_weights, 0.0), axis=1, keepdims=True) / norm
+                share = shares[d * walkers + b : d * walkers + b + 1, :]
                 density += share * pack_refs[n][top + b * rows : top + (b + 1) * rows, :].astype(jnp.float32)
         density_ref[...] = density
         first = lax.rem(LANES - walk * slots, LANES)
@@ -423,11 +459,11 @@
             jax.ShapeDtypeStruct((1, slots), jnp.float32),
             jax.ShapeDtypeStruct((rows, LANES), jnp.float32),
         ],
-        in_specs=[vmem(), smem()] + [vmem()] * len(packs),
+        in_specs=[vmem()] * (2 + len(packs)),
         out_specs=[vmem()] * 3,
         compiler_params=params(),
         cost_estimate=pl.CostEstimate(flops=10**6, bytes_accessed=6 * 10**5, transcendentals=128),
-    )(stats, counts, *packs)
+    )(stats, plan, *packs)
 
 
 def per_device(green_rows, cholesky_rot, one_body, fields, weights, sources, counts, owners):
@@ -436,20 +472,22 @@
     vectors, slots = fields.shape
     walkers = green_rows.shape[1]
     onebody, *packed = pack(green_rows, one_body, fields, weights, sources, owners, cholesky_rot)
+    table = 3 * table_height(vectors)
+    places = walk_places(packed[0].shape[0] - table, table, walk_size)
+
+    def do_prepare(packs):
+        return prepare(packs, places, onebody, counts, vectors, slots, walkers)
+
     if chol_size > RING_LIMIT or chol_size % 2 or chol_size < 8:
         far = exchange_far(packed)
         packs = [packed[0], far] + exchange_near(packed, far)
+        plan = do_prepare(packs)
         total, last = None, [lax.all_gather(green_rows, "chol", axis=0, tiled=True)]
     else:
-        onebody, total, last, packs = ring(green_rows, cholesky_rot, onebody, packed)
-    table = 3 * table_height(vectors)
-    places = walk_places(packs[0].shape[0] - table, table, walk_size)
-    stats = measure(cholesky_rot, total, last, packs, places, onebody, vectors, slots)
-    turned = [list(range(stats.shape[0]))[::-1]]
-    stats = lax.all_to_all(
-        stats, ("chol", "walk"), split_axis=0, concat_axis=0, axis_index_groups=turned, tiled=True
-    )
-    energies, new_weights, density = finish(stats, packs, places, counts, vectors, slots, walkers)
+        total, last, packs, plan = ring(green_rows, cholesky_rot, onebody, packed, do_prepare)
+    stats = measure(cholesky_rot, total, last, plan, vectors, walk_size)
+    stats = lax.all_to_all(stats, ("chol", "walk"), split_axis=0, concat_axis=0, tiled=True)
+    energies, new_weights, density = finish(stats, plan, packs, places, vectors, slots, walkers)
     return energies.reshape(slots), new_weights.reshape(slots), density.reshape(1, density.size)
 
 

time: 46.5 us -> 45.9 us (0.987)
  waiting for transfers between devices: 10.5 us -> 9.77 us
    ppermute x1, waiting for transfers between devices: 0.63 us -> 0.01 us  [ring(): lax.ppermute(right[:rows // 2], 'chol', ahead)]
    pallas_call x0 -> x1, Pallas kernels: none -> 0.62 us  [prepare(): pl.pallas_call(kernel, name='prepare', out_shape=jax.ShapeDtypeStruct((he...]
    pallas_call x1, Pallas kernels: 1.43 us -> 0.87 us  [finish(): pl.pallas_call(kernel, name='finish', out_shape=[jax.ShapeDtypeStruct((1,...]
  transfers between devices with their start and end apart: 10 -> 10, of which waited for: 6 -> 5; matrix products, arithmetic and copies ran while one was open for 0% -> 0% of each run, Pallas kernels for 21% -> 23%
where the time goes in v11:
time: 45.9 us; the launch traced here: 45.8 us
  Pallas kernels  13.2 us (29%)
  starting transfers between devices  11 us (24%)
  blocking collectives  10.8 us (24%)
  waiting for transfers between devices  9.77 us (21%)
  between operations  0.74 us (2%)
    all_to_all x1, blocking collectives, per_device(): lax.all_to_all(stats, ('chol', 'walk'), split_axis=0, concat_axis=0, tile...  10.8 us
    ppermute x3, waiting for transfers between devices, ring(): lax.ppermute(right, 'chol', ahead)  6.96 us
    pallas_call x3, Pallas kernels, accumulate(): pl.pallas_call(kernel, name='accumulate', out_shape=[jax.ShapeDtypeStruct...  6.63 us
    ppermute x3, starting transfers between devices, ring(): lax.ppermute(right, 'chol', ahead)  6.35 us
    pallas_call x1, Pallas kernels, pack(): pl.pallas_call(kernel, name='pack', out_shape=[jax.ShapeDtypeStruct((8, L...  3.32 us
    pallas_call x1, Pallas kernels, measure(): pl.pallas_call(kernel, name='measure', out_shape=jax.ShapeDtypeStruct((ta...  1.8 us
    ppermute x1, starting transfers between devices, exchange_far(): return lax.ppermute(packed[1], 'walk', [(q, q ^ 2) for q in range(size)])  1.71 us
    ppermute x1, starting transfers between devices, ring(): lax.ppermute(right[:rows // 2], 'chol', ahead)  1.63 us
  transfers between devices with their start and end apart: 10, of which 5 were waited for; matrix products, arithmetic and copies ran while one was open for 0% of the time, Pallas kernels for 23%

profile of v11, /device:TPU:0, one launch (start us, length us, event | category | flops | bytes accessed | tf_op | source)
XLA Modules:
  0.0 45.8 jit_solution(10618032562687305335)
XLA Ops:
  0.6 3.1 %collective-permute-start.2 = (bf16[256,2,256]{2,1,0:T(2,128)(2,1)}, bf16[256,2,256]{2,1,0:T(2,128)(2,1)S(1)}, u32[]{:S(2)}, u32[]{:S(2)}) collective-permute-start(bf16[256,2,256]{2,1,0:T(2,128)(2,1)} %refs_0_.2), channel_id=1, source_target_pairs={{0,8},{8,16},{16,24},{24,28},{28,20},{20,12},{12,4},{4,0},{1,9},{9... | collective-permute-start | bytes 786440 | tf_op jit(solution)/shard_map/ppermute | solution.py:99
  3.7 3.3 %pack.1 = (f32[8,128]{1,0:T(8,128)}, bf16[304,128]{1,0:T(8,128)(2,1)}, bf16[560,128]{1,0:T(8,128)(2,1)}, bf16[304,128]{1,0:T(8,128)(2,1)}) custom-call(bf16[256,2,256]{2,1,0:T(2,128)(2,1)} %refs_0_.2, bf16[256,256]{1,0:T(8,128)(2,1)} %body_any.1, f32[4,8]{1,0:T(4,128)} %bitcast.10, f32[2]{0:T(128)} %weights_any.1, s32[4]{0:T(128)} %sources_any.1, ...), custom_call_target="tpu_custom_call" | custom-call | flops 100000000 | bytes 1000000 | tf_op jit(solution)/shard_map/pack/pallas_call | solution.py:225
  7.0 3.1 %collective-permute-done.2.refs_1_ = bf16[256,2,256]{2,1,0:T(2,128)(2,1)S(1)} collective-permute-done((bf16[256,2,256]{2,1,0:T(2,128)(2,1)}, bf16[256,2,256]{2,1,0:T(2,128)(2,1)S(1)}, u32[]{:S(2)}, u32[]{:S(2)}) %collective-permute-start.2) | collective-permute-done | bytes 262176 | tf_op jit(solution)/shard_map/ppermute | solution.py:99
  10.2 1.8 %collective-permute-start.3 = (bf16[256,2,256]{2,1,0:T(2,128)(2,1)S(1)}, bf16[256,2,256]{2,1,0:T(2,128)(2,1)S(1)}, u32[]{:S(2)}, u32[]{:S(2)}) collective-permute-start(bf16[256,2,256]{2,1,0:T(2,128)(2,1)S(1)} %collective-permute-done.2.refs_1_), channel_id=1, source_target_pairs={{0,8},{8,16},{16,24},{24,28},{28,20},{20,12},{12,4},{4,0},{1,9},{9... | collective-permute-start | bytes 786440 | tf_op jit(solution)/shard_map/ppermute | solution.py:99
  12.0 0.2 collective-permute-start.1
  12.2 1.7 %collective-permute-start.6 = (bf16[560,128]{1,0:T(8,128)(2,1)}, bf16[560,128]{1,0:T(8,128)(2,1)S(1)}, u32[]{:S(2)}, u32[]{:S(2)}) collective-permute-start(bf16[560,128]{1,0:T(8,128)(2,1)} %get-tuple-element.48), channel_id=1, source_target_pairs={{0,2},{1,3},{2,0},{3,1},{4,6},{5,7},{6,4},{7,5},{8,10},{9,11},{10,... | collective-permute-start | bytes 430088 | tf_op jit(solution)/shard_map/ppermute | solution.py:259
  13.9 2.5 %accumulate.3 = (f32[2,2048,256]{2,1,0:T(8,128)S(1)}, f32[8,128]{1,0:T(8,128)S(1)}) custom-call(bf16[8,256,2048]{2,1,0:T(8,128)(2,1)S(1)} %copy-done, bf16[256,2,256]{2,1,0:T(2,128)(2,1)S(1)} %copy-done.1, bf16[256,2,256]{2,1,0:T(2,128)(2,1)S(1)} %collective-permute-done.2.refs_1_, bf16[256,2,256]{2,1,0:T(2,128)(2,1)S(1)} %collective-permute-done.refs_2_), custom_call_target="tpu_custom_call" | custom-call | flops 1610612736 | bytes 3145728 | tf_op jit(solution)/shard_map/accumulate/pallas_call | solution.py:66
  16.4 1.3 %collective-permute-done.3.refs_0_ = bf16[256,2,256]{2,1,0:T(2,128)(2,1)S(1)} collective-permute-done((bf16[256,2,256]{2,1,0:T(2,128)(2,1)S(1)}, bf16[256,2,256]{2,1,0:T(2,128)(2,1)S(1)}, u32[]{:S(2)}, u32[]{:S(2)}) %collective-permute-start.3) | collective-permute-done | bytes 262176 | tf_op jit(solution)/shard_map/ppermute | solution.py:99
  17.7 1.5 %collective-permute-start.5 = (bf16[256,2,256]{2,1,0:T(2,128)(2,1)S(1)}, bf16[256,2,256]{2,1,0:T(2,128)(2,1)S(1)}, u32[]{:S(2)}, u32[]{:S(2)}) collective-permute-start(bf16[256,2,256]{2,1,0:T(2,128)(2,1)S(1)} %collective-permute-done.3.refs_0_), channel_id=1, source_target_pairs={{0,8},{8,16},{16,24},{24,28},{28,20},{20,12},{12,4},{4,0},{1,9},{9... | collective-permute-start | bytes 786440 | tf_op jit(solution)/shard_map/ppermute | solution.py:99
  19.1 0.5 %collective-permute-start.4 = (bf16[256,2,256]{2,1,0:T(2,128)(2,1)S(1)}, bf16[256,2,256]{2,1,0:T(2,128)(2,1)S(1)}, u32[]{:S(2)}, u32[]{:S(2)}) collective-permute-start(bf16[256,2,256]{2,1,0:T(2,128)(2,1)S(1)} %collective-permute-done.1.refs_1_), channel_id=1, source_target_pairs={{0,4},{8,0},{16,8},{24,16},{28,24},{20,28},{12,20},{4,12},{1,5},{9... | collective-permute-start | bytes 786440 | tf_op jit(solution)/shard_map/ppermute | solution.py:99
  19.7 0.1 collective-permute-start.7
  19.8 1.8 %accumulate.4 = (f32[2,2048,256]{2,1,0:T(8,128)S(1)}, f32[8,128]{1,0:T(8,128)S(1)}) custom-call(bf16[8,256,2048]{2,1,0:T(8,128)(2,1)S(1)} %copy-done, bf16[256,2,256]{2,1,0:T(2,128)(2,1)S(1)} %collective-permute-done.3.refs_0_, bf16[256,2,256]{2,1,0:T(2,128)(2,1)S(1)} %collective-permute-done.1.refs_1_, f32[8,128]{1,0:T(8,128)S(1)} %get-tuple-element.42.refs_2_, ...), custom_call_target="tpu_custom_call" | custom-call | flops 1073741824 | bytes 2097152 | tf_op jit(solution)/shard_map/accumulate/pallas_call | solution.py:66
  21.6 2.6 %collective-permute-done.5.refs_0_ = bf16[256,2,256]{2,1,0:T(2,128)(2,1)S(1)} collective-permute-done((bf16[256,2,256]{2,1,0:T(2,128)(2,1)S(1)}, bf16[256,2,256]{2,1,0:T(2,128)(2,1)S(1)}, u32[]{:S(2)}, u32[]{:S(2)}) %collective-permute-start.5) | collective-permute-done | bytes 262176 | tf_op jit(solution)/shard_map/ppermute | solution.py:99
  24.2 1.3 %collective-permute-done.4.refs_1_ = bf16[256,2,256]{2,1,0:T(2,128)(2,1)S(1)} collective-permute-done((bf16[256,2,256]{2,1,0:T(2,128)(2,1)S(1)}, bf16[256,2,256]{2,1,0:T(2,128)(2,1)S(1)}, u32[]{:S(2)}, u32[]{:S(2)}) %collective-permute-start.4) | collective-permute-done | bytes 262176 | tf_op jit(solution)/shard_map/ppermute | solution.py:99
  25.5 0.1 slice.11
  25.6 0.1 slice.10
  25.7 1.6 %collective-permute-start.8 = (bf16[128,2,256]{2,1,0:T(2,128)(2,1)S(1)}, bf16[128,2,256]{2,1,0:T(2,128)(2,1)S(1)}, u32[]{:S(2)}, u32[]{:S(2)}) collective-permute-start(bf16[128,2,256]{2,1,0:T(2,128)(2,1)S(1)} %slice.10), channel_id=1, source_target_pairs={{0,8},{8,16},{16,24},{24,28},{28,20},{20,12},{12,4},{4,0},{1,9},{9... | collective-permute-start | bytes 393224 | tf_op jit(solution)/shard_map/ppermute | solution.py:114
  27.3 0.4 collective-permute-start.9
  27.8 0.6 %prepare.1.refs_1_.plan_ref = f32[32,128]{1,0:T(8,128)S(1)} custom-call(s32[4]{0:T(128)S(1)} %copy-done.4, f32[8,128]{1,0:T(8,128)S(1)} %copy-done.3, bf16[304,128]{1,0:T(8,128)(2,1)S(1)} %copy-done.2, bf16[560,128]{1,0:T(8,128)(2,1)S(1)} %collective-permute-done.6.refs_1_, bf16[608,128]{1,0:T(8,128)(2,1)S(1)} %collective-permute-done.7.refs_2_), custom_call_target="tpu_custom_call" | custom-call | flops 100000000 | bytes 1000000 | tf_op jit(solution)/shard_map/prepare/pallas_call | solution.py:337
  28.4 2.4 %accumulate.5 = (f32[2,2048,256]{2,1,0:T(8,128)S(1)}, f32[8,128]{1,0:T(8,128)}) custom-call(bf16[8,256,2048]{2,1,0:T(8,128)(2,1)S(1)} %copy-done, bf16[256,2,256]{2,1,0:T(2,128)(2,1)S(1)} %collective-permute-done.5.refs_0_, bf16[256,2,256]{2,1,0:T(2,128)(2,1)S(1)} %collective-permute-done.4.refs_1_, f32[8,128]{1,0:T(8,128)S(1)} %get-tuple-element.55.refs_2_, ...), custom_call_target="tpu_custom_call" | custom-call | flops 1073741824 | bytes 2097152 | tf_op jit(solution)/shard_map/accumulate/pallas_call | solution.py:66
  30.8 1.5 %collective-permute-done.9.refs_3_ = bf16[128,2,256]{2,1,0:T(2,128)(2,1)S(1)} collective-permute-done((bf16[128,2,256]{2,1,0:T(2,128)(2,1)S(1)}, bf16[128,2,256]{2,1,0:T(2,128)(2,1)S(1)}, u32[]{:S(2)}, u32[]{:S(2)}) %collective-permute-start.9) | collective-permute-done | bytes 131104 | tf_op jit(solution)/shard_map/ppermute | solution.py:114
  32.3 1.8 %measure.1 = f32[32,128]{1,0:T(8,128)S(1)} custom-call(bf16[8,256,2048]{2,1,0:T(8,128)(2,1)S(1)} %copy-done, f32[32,128]{1,0:T(8,128)S(1)} %prepare.1.refs_1_.plan_ref, bf16[128,2,256]{2,1,0:T(2,128)(2,1)S(1)} %collective-permute-done.8.refs_2_, bf16[128,2,256]{2,1,0:T(2,128)(2,1)S(1)} %collective-permute-done.9.refs_3_, ...), custom_call_target="tpu_custom_call" | custom-call | flops 536870912 | bytes 1048576 | tf_op jit(solution)/shard_map/measure/pallas_call | solution.py:408
  34.1 10.8 %all_to_all.11 = f32[32,1,128]{2,1,0:T(1,128)S(1)} all-to-all(f32[32,1,128]{2,1,0:T(1,128)S(1)} %bitcast.8), channel_id=1, replica_groups=mesh['chol'=8,'walk'=4] {'chol','walk'}, dimensions={0} | all-to-all | bytes 32768 | tf_op jit(solution)/shard_map/all_to_all | solution.py:489
  44.9 0.9 %finish.1 = (f32[1,4]{1,0:T(1,128)}, f32[1,4]{1,0:T(1,128)}, f32[128,128]{1,0:T(8,128)}) custom-call(f32[32,128]{1,0:T(8,128)S(1)} %bitcast.9, f32[32,128]{1,0:T(8,128)S(1)} %prepare.1.refs_1_.plan_ref, bf16[304,128]{1,0:T(8,128)(2,1)S(1)} %copy-done.2, bf16[560,128]{1,0:T(8,128)(2,1)S(1)} %collective-permute-done.6.refs_1_, ...), custom_call_target="tpu_custom_call" | custom-call | flops 1000000 | bytes 600000 | tf_op jit(solution)/shard_map/finish/pallas_call | solution.py:454
  (20 shorter events, 0.1 us)
Async XLA Ops:
  0.6 9.5 %collective-permute-start.2 = (bf16[256,2,256]{2,1,0:T(2,128)(2,1)}, bf16[256,2,256]{2,1,0:T(2,128)(2,1)S(1)}, u32[]{:S(2)}, u32[]{:S(2)}) collective-permute-start(bf16[256,2,256]{2,1,0:T(2,128)(2,1)} %refs_0_.2), channel_id=1, source_target_pairs={{0,8},{8,16},{16,24},{24,28},{28,20},{20,12},{12,4},{4,0},{1,9},{9... | collective-permute-start | bytes 786440 | tf_op jit(solution)/shard_map/ppermute | solution.py:99
  3.7 8.3 %collective-permute-start = (bf16[256,2,256]{2,1,0:T(2,128)(2,1)}, bf16[256,2,256]{2,1,0:T(2,128)(2,1)S(1)}, u32[]{:S(2)}, u32[]{:S(2)}) collective-permute-start(bf16[256,2,256]{2,1,0:T(2,128)(2,1)} %refs_0_.2), channel_id=1, source_target_pairs={{0,4},{8,0},{16,8},{24,16},{28,24},{20,28},{12,20},{4,12},{1,5},{9... | collective-permute-start | bytes 786440 | tf_op jit(solution)/shard_map/ppermute | solution.py:99
  3.7 10.2 %copy-start = (bf16[8,256,2048]{2,1,0:T(8,128)(2,1)S(1)}, bf16[8,256,2048]{2,1,0:T(8,128)(2,1)}, u32[]{:S(2)}) copy-start(bf16[8,256,2048]{2,1,0:T(8,128)(2,1)} %refs_0_.3) | copy-start | bytes 25165828
  3.7 10.2 %copy-start.1 = (bf16[256,2,256]{2,1,0:T(2,128)(2,1)S(1)}, bf16[256,2,256]{2,1,0:T(2,128)(2,1)}, u32[]{:S(2)}) copy-start(bf16[256,2,256]{2,1,0:T(2,128)(2,1)} %refs_0_.2) | copy-start | bytes 786436
  10.2 7.5 %collective-permute-start.3 = (bf16[256,2,256]{2,1,0:T(2,128)(2,1)S(1)}, bf16[256,2,256]{2,1,0:T(2,128)(2,1)S(1)}, u32[]{:S(2)}, u32[]{:S(2)}) collective-permute-start(bf16[256,2,256]{2,1,0:T(2,128)(2,1)S(1)} %collective-permute-done.2.refs_1_), channel_id=1, source_target_pairs={{0,8},{8,16},{16,24},{24,28},{28,20},{20,12},{12,4},{4,0},{1,9},{9... | collective-permute-start | bytes 786440 | tf_op jit(solution)/shard_map/ppermute | solution.py:99
  12.0 7.7 %copy-start.5 = (bf16[304,128]{1,0:T(8,128)(2,1)S(1)}, bf16[304,128]{1,0:T(8,128)(2,1)}, u32[]{:S(2)}) copy-start(bf16[304,128]{1,0:T(8,128)(2,1)} %get-tuple-element.47) | copy-start | bytes 233476
  12.0 7.2 %collective-permute-start.1 = (bf16[256,2,256]{2,1,0:T(2,128)(2,1)S(1)}, bf16[256,2,256]{2,1,0:T(2,128)(2,1)S(1)}, u32[]{:S(2)}, u32[]{:S(2)}) collective-permute-start(bf16[256,2,256]{2,1,0:T(2,128)(2,1)S(1)} %collective-permute-done.refs_2_), channel_id=1, source_target_pairs={{0,4},{8,0},{16,8},{24,16},{28,24},{20,28},{12,20},{4,12},{1,5},{9... | collective-permute-start | bytes 786440 | tf_op jit(solution)/shard_map/ppermute | solution.py:99
  12.2 7.5 %collective-permute-start.6 = (bf16[560,128]{1,0:T(8,128)(2,1)}, bf16[560,128]{1,0:T(8,128)(2,1)S(1)}, u32[]{:S(2)}, u32[]{:S(2)}) collective-permute-start(bf16[560,128]{1,0:T(8,128)(2,1)} %get-tuple-element.48), channel_id=1, source_target_pairs={{0,2},{1,3},{2,0},{3,1},{4,6},{5,7},{6,4},{7,5},{8,10},{9,11},{10,... | collective-permute-start | bytes 430088 | tf_op jit(solution)/shard_map/ppermute | solution.py:259
  17.7 6.6 %collective-permute-start.5 = (bf16[256,2,256]{2,1,0:T(2,128)(2,1)S(1)}, bf16[256,2,256]{2,1,0:T(2,128)(2,1)S(1)}, u32[]{:S(2)}, u32[]{:S(2)}) collective-permute-start(bf16[256,2,256]{2,1,0:T(2,128)(2,1)S(1)} %collective-permute-done.3.refs_0_), channel_id=1, source_target_pairs={{0,8},{8,16},{16,24},{24,28},{28,20},{20,12},{12,4},{4,0},{1,9},{9... | collective-permute-start | bytes 786440 | tf_op jit(solution)/shard_map/ppermute | solution.py:99
  19.1 6.4 %collective-permute-start.4 = (bf16[256,2,256]{2,1,0:T(2,128)(2,1)S(1)}, bf16[256,2,256]{2,1,0:T(2,128)(2,1)S(1)}, u32[]{:S(2)}, u32[]{:S(2)}) collective-permute-start(bf16[256,2,256]{2,1,0:T(2,128)(2,1)S(1)} %collective-permute-done.1.refs_1_), channel_id=1, source_target_pairs={{0,4},{8,0},{16,8},{24,16},{28,24},{20,28},{12,20},{4,12},{1,5},{9... | collective-permute-start | bytes 786440 | tf_op jit(solution)/shard_map/ppermute | solution.py:99
  19.7 8.1 %collective-permute-start.7 = (bf16[608,128]{1,0:T(8,128)(2,1)S(1)}, bf16[608,128]{1,0:T(8,128)(2,1)S(1)}, u32[]{:S(2)}, u32[]{:S(2)}) collective-permute-start(bf16[608,128]{1,0:T(8,128)(2,1)S(1)} %pad_maximum_fusion), channel_id=1, source_target_pairs={{0,1},{1,0},{2,3},{3,2},{4,5},{5,4},{6,7},{7,6},{8,9},{9,8},{10,11... | collective-permute-start | bytes 466952 | tf_op jit(solution)/shard_map/ppermute | solution.py:270
  19.8 8.0 %copy-start.2 = (bf16[304,128]{1,0:T(8,128)(2,1)S(1)}, bf16[304,128]{1,0:T(8,128)(2,1)}, u32[]{:S(2)}) copy-start(bf16[304,128]{1,0:T(8,128)(2,1)} %get-tuple-element.50.refs_0_) | copy-start | bytes 233476
  19.8 8.0 %copy-start.3 = (f32[8,128]{1,0:T(8,128)S(1)}, f32[8,128]{1,0:T(8,128)}, u32[]{:S(2)}) copy-start(f32[8,128]{1,0:T(8,128)} %get-tuple-element.36.onebody_ref) | copy-start | bytes 12292
  19.8 8.0 %copy-start.4 = (s32[4]{0:T(128)S(1)}, s32[4]{0:T(128)}, u32[]{:S(2)}) copy-start(s32[4]{0:T(128)} %counts_ref.1) | copy-start | bytes 52
  25.7 5.1 %collective-permute-start.8 = (bf16[128,2,256]{2,1,0:T(2,128)(2,1)S(1)}, bf16[128,2,256]{2,1,0:T(2,128)(2,1)S(1)}, u32[]{:S(2)}, u32[]{:S(2)}) collective-permute-start(bf16[128,2,256]{2,1,0:T(2,128)(2,1)S(1)} %slice.10), channel_id=1, source_target_pairs={{0,8},{8,16},{16,24},{24,28},{28,20},{20,12},{12,4},{4,0},{1,9},{9... | collective-permute-start | bytes 393224 | tf_op jit(solution)/shard_map/ppermute | solution.py:114
  27.3 5.0 %collective-permute-start.9 = (bf16[128,2,256]{2,1,0:T(2,128)(2,1)S(1)}, bf16[128,2,256]{2,1,0:T(2,128)(2,1)S(1)}, u32[]{:S(2)}, u32[]{:S(2)}) collective-permute-start(bf16[128,2,256]{2,1,0:T(2,128)(2,1)S(1)} %slice.11), channel_id=1, source_target_pairs={{0,4},{8,0},{16,8},{24,16},{28,24},{20,28},{12,20},{4,12},{1,5},{9... | collective-permute-start | bytes 393224 | tf_op jit(solution)/shard_map/ppermute | solution.py:114

commit v12 on v11

--- a/solution.py
+++ b/solution.py
@@ -47,7 +47,8 @@
 
 def accumulate(cholesky_rot, shifts, parts, total, mark):
     vectors, orbitals, _ = cholesky_rot.shape
-    rows, walkers, _ = parts[0].shape
+    walkers = parts[0].shape[1]
+    rows = sum(x.shape[0] for x in parts) // len(shifts)
     size = vectors * orbitals
     arrays = list(parts) + ([] if mark is None else [mark]) + ([] if total is None else [total])
 
@@ -74,8 +75,8 @@
         out_specs=[vmem()] * 2,
         compiler_params=params(ACCUMULATE_LIMIT),
         cost_estimate=pl.CostEstimate(
-            flops=2 * len(parts) * size * rows * walkers * orbitals,
-            bytes_accessed=2 * len(parts) * size * rows,
+            flops=2 * len(shifts) * size * rows * walkers * orbitals,
+            bytes_accessed=2 * len(shifts) * size * rows,
             transcendentals=0,
         ),
     )(cholesky_rot, *arrays)
@@ -92,31 +93,39 @@
     ahead = [(order[q], order[(q + 1) % size]) for q in range(size)]
     back = [(order[q], order[(q - 1) % size]) for q in range(size)]
     steps = size // 2
+    half = rows // 2
     right = left = own
     shifts, parts = [0], [own]
     total = mark = None
-    for step in range(1, steps):
+    for step in range(1, steps - 1):
         next_right, next_left = lax.ppermute(right, "chol", ahead), lax.ppermute(left, "chol", back)
         if step == 1:
             right, onebody = tie(next_right, onebody)
-            left, *packed = tie(next_left, *packed)
+            far = exchange_far(packed)
+            left = next_left
         else:
-            if step == 2:
-                far = exchange_far(packed)
-            elif step == 3:
-                near = exchange_near(packed, far)
             total, mark = accumulate(cholesky_rot, shifts, parts, total, mark)
             shifts, parts = [], []
+            if step == 2:
+                far, mark = tie(far, mark)
+                near = exchange_near(packed, far)
             right, mark = tie(next_right, mark)
             left, mark = tie(next_left, mark)
         shifts += [-step, step]
         parts = parts + [right, left]
-    last = [lax.ppermute(right[: rows // 2], "chol", ahead), lax.ppermute(left[rows // 2 :], "chol", back)]
+    upper = lax.ppermute(right[:half], "chol", ahead)
+    lower = lax.ppermute(left[half:], "chol", back)
+    rest = [lax.ppermute(right[half:], "chol", ahead), lax.ppermute(left[:half], "chol", back)]
+    total, mark = accumulate(cholesky_rot, shifts, parts, total, mark)
+    upper, mark = tie(upper, mark)
+    lower, mark = tie(lower, mark)
+    last = [lax.ppermute(upper, "chol", ahead), lax.ppermute(lower, "chol", back)]
     mark, *near = tie(mark, *near)
     packs = [packed[0], far] + near
     plan = do_prepare(packs)
-    mark, plan = tie(mark, plan)
-    total, _ = accumulate(cholesky_rot, shifts, parts, total, mark)
+    mark, plan, *rest = tie(mark, plan, *rest)
+    parts = [upper, rest[0], rest[1], lower]
+    total, _ = accumulate(cholesky_rot, [1 - steps, steps - 1], parts, total, mark)
     return total, last, packs, plan
 
 

time: 45.9 us -> 47 us (1.024)
  waiting for transfers between devices: 9.77 us -> 7.21 us
  starting transfers between devices: 11 us -> 13.4 us
  blocking collectives: 10.8 us -> 11.8 us
    ppermute x2 -> x6, starting transfers between devices: 2.08 us -> 6.18 us  [the longest x1 1.63 us: ring(): upper = lax.ppermute(right[:half], 'chol', ahead)]
    ppermute x3 -> x2, waiting for transfers between devices: 6.96 us -> 3.96 us  [ring(): lax.ppermute(right, 'chol', ahead)]
    ppermute x3 -> x2, starting transfers between devices: 6.35 us -> 4.87 us  [ring(): lax.ppermute(right, 'chol', ahead)]
    all_to_all x1, blocking collectives: 10.8 us -> 11.8 us  [per_device(): lax.all_to_all(stats, ('chol', 'walk'), split_axis=0, concat_axis=0, tile...]
    ppermute x3 -> x2, starting transfers between devices: 0.78 us -> 0.24 us  [ring(): lax.ppermute(left, 'chol', back)]
    ppermute x2 -> x6, waiting for transfers between devices: 1.51 us -> 2.04 us  [the longest x1 1.74 us: ring(): lower = lax.ppermute(left[half:], 'chol', back)]
    ppermute x3 -> x2, waiting for transfers between devices: 1.29 us -> 1.21 us  [ring(): lax.ppermute(left, 'chol', back)]
  transfers between devices with their start and end apart: 10 -> 12, of which waited for: 5 -> 5; matrix products, arithmetic and copies ran while one was open for 0% -> 1% of each run, Pallas kernels for 23% -> 23%
where the time goes in v12:
time: 47 us; the launch traced here: 46.8 us
  starting transfers between devices  13.4 us (29%)
  Pallas kernels  13.3 us (28%)
  blocking collectives  11.8 us (25%)
  waiting for transfers between devices  7.21 us (15%)
  between operations  0.74 us (2%)
    all_to_all x1, blocking collectives, per_device(): lax.all_to_all(stats, ('chol', 'walk'), split_axis=0, concat_axis=0, tile...  11.8 us
    pallas_call x3, Pallas kernels, accumulate(): pl.pallas_call(kernel, name='accumulate', out_shape=[jax.ShapeDtypeStruct...  6.68 us
    ppermute x2, starting transfers between devices, ring(): lax.ppermute(right, 'chol', ahead)  4.87 us
    ppermute x2, waiting for transfers between devices, ring(): lax.ppermute(right, 'chol', ahead)  3.96 us
    pallas_call x1, Pallas kernels, pack(): pl.pallas_call(kernel, name='pack', out_shape=[jax.ShapeDtypeStruct((8, L...  3.32 us
    ppermute x1, starting transfers between devices, exchange_far(): return lax.ppermute(packed[1], 'walk', [(q, q ^ 2) for q in range(size)])  2 us
    pallas_call x1, Pallas kernels, measure(): pl.pallas_call(kernel, name='measure', out_shape=jax.ShapeDtypeStruct((ta...  1.8 us
    ppermute x1, waiting for transfers between devices, ring(): lower = lax.ppermute(left[half:], 'chol', back)  1.74 us
  transfers between devices with their start and end apart: 12, of which 5 were waited for; matrix products, arithmetic and copies ran while one was open for 1% of the time, Pallas kernels for 23%

profile of v12, /device:TPU:0, one launch (start us, length us, event | category | flops | bytes accessed | tf_op | source)
XLA Modules:
  0.0 46.8 jit_solution(8313196954760838586)
XLA Ops:
  0.6 3.1 %collective-permute-start.2 = (bf16[256,2,256]{2,1,0:T(2,128)(2,1)}, bf16[256,2,256]{2,1,0:T(2,128)(2,1)S(1)}, u32[]{:S(2)}, u32[]{:S(2)}) collective-permute-start(bf16[256,2,256]{2,1,0:T(2,128)(2,1)} %refs_0_.2), channel_id=1, source_target_pairs={{0,8},{8,16},{16,24},{24,28},{28,20},{20,12},{12,4},{4,0},{1,9},{9... | collective-permute-start | bytes 786440 | tf_op jit(solution)/shard_map/ppermute | solution.py:101
  3.7 3.3 %pack.1 = (f32[8,128]{1,0:T(8,128)}, bf16[304,128]{1,0:T(8,128)(2,1)}, bf16[560,128]{1,0:T(8,128)(2,1)}, bf16[304,128]{1,0:T(8,128)(2,1)}) custom-call(bf16[256,2,256]{2,1,0:T(2,128)(2,1)} %refs_0_.2, bf16[256,256]{1,0:T(8,128)(2,1)} %body_any.1, f32[4,8]{1,0:T(4,128)} %bitcast.10, f32[2]{0:T(128)} %weights_any.1, s32[4]{0:T(128)} %sources_any.1, ...), custom_call_target="tpu_custom_call" | custom-call | flops 100000000 | bytes 1000000 | tf_op jit(solution)/shard_map/pack/pallas_call | solution.py:234
  7.0 2.0 %collective-permute-start.4 = (bf16[560,128]{1,0:T(8,128)(2,1)}, bf16[560,128]{1,0:T(8,128)(2,1)S(1)}, u32[]{:S(2)}, u32[]{:S(2)}) collective-permute-start(bf16[560,128]{1,0:T(8,128)(2,1)} %get-tuple-element.34), channel_id=1, source_target_pairs={{0,2},{1,3},{2,0},{3,1},{4,6},{5,7},{6,4},{7,5},{8,10},{9,11},{10,... | collective-permute-start | bytes 430088 | tf_op jit(solution)/shard_map/ppermute | solution.py:268
  9.0 1.1 %collective-permute-done.2.refs_1_ = bf16[256,2,256]{2,1,0:T(2,128)(2,1)S(1)} collective-permute-done((bf16[256,2,256]{2,1,0:T(2,128)(2,1)}, bf16[256,2,256]{2,1,0:T(2,128)(2,1)S(1)}, u32[]{:S(2)}, u32[]{:S(2)}) %collective-permute-start.2) | collective-permute-done | bytes 262176 | tf_op jit(solution)/shard_map/ppermute | solution.py:101
  10.2 1.8 %collective-permute-start.3 = (bf16[256,2,256]{2,1,0:T(2,128)(2,1)S(1)}, bf16[256,2,256]{2,1,0:T(2,128)(2,1)S(1)}, u32[]{:S(2)}, u32[]{:S(2)}) collective-permute-start(bf16[256,2,256]{2,1,0:T(2,128)(2,1)S(1)} %collective-permute-done.2.refs_1_), channel_id=1, source_target_pairs={{0,8},{8,16},{16,24},{24,28},{28,20},{20,12},{12,4},{4,0},{1,9},{9... | collective-permute-start | bytes 786440 | tf_op jit(solution)/shard_map/ppermute | solution.py:101
  12.0 0.2 collective-permute-start.1
  12.2 2.5 %accumulate.3 = (f32[2,2048,256]{2,1,0:T(8,128)S(1)}, f32[8,128]{1,0:T(8,128)S(1)}) custom-call(bf16[8,256,2048]{2,1,0:T(8,128)(2,1)S(1)} %copy-done, bf16[256,2,256]{2,1,0:T(2,128)(2,1)S(1)} %copy-done.1, bf16[256,2,256]{2,1,0:T(2,128)(2,1)S(1)} %collective-permute-done.2.refs_1_, bf16[256,2,256]{2,1,0:T(2,128)(2,1)S(1)} %collective-permute-done.refs_2_), custom_call_target="tpu_custom_call" | custom-call | flops 1610612736 | bytes 3145728 | tf_op jit(solution)/shard_map/accumulate/pallas_call | solution.py:67
  14.8 2.8 %collective-permute-done.3.refs_0_ = bf16[256,2,256]{2,1,0:T(2,128)(2,1)S(1)} collective-permute-done((bf16[256,2,256]{2,1,0:T(2,128)(2,1)S(1)}, bf16[256,2,256]{2,1,0:T(2,128)(2,1)S(1)}, u32[]{:S(2)}, u32[]{:S(2)}) %collective-permute-start.3) | collective-permute-done | bytes 262176 | tf_op jit(solution)/shard_map/ppermute | solution.py:101
  17.7 1.2 %collective-permute-done.1.refs_1_ = bf16[256,2,256]{2,1,0:T(2,128)(2,1)S(1)} collective-permute-done((bf16[256,2,256]{2,1,0:T(2,128)(2,1)S(1)}, bf16[256,2,256]{2,1,0:T(2,128)(2,1)S(1)}, u32[]{:S(2)}, u32[]{:S(2)}) %collective-permute-start.1) | collective-permute-done | bytes 262176 | tf_op jit(solution)/shard_map/ppermute | solution.py:101
  18.9 0.2 fusion.1
  19.1 1.6 %collective-permute-start.6 = (bf16[128,2,256]{2,1,0:T(2,128)(2,1)S(1)}, bf16[128,2,256]{2,1,0:T(2,128)(2,1)S(1)}, u32[]{:S(2)}, u32[]{:S(2)}) collective-permute-start(bf16[128,2,256]{2,1,0:T(2,128)(2,1)S(1)} %get-tuple-element.64), channel_id=1, source_target_pairs={{0,8},{8,16},{16,24},{24,28},{28,20},{20,12},{12,4},{4,0},{1,9},{9... | collective-permute-start | bytes 393224 | tf_op jit(solution)/shard_map/ppermute | solution.py:116
  20.9 0.5 %collective-permute-start.5 = (bf16[128,2,256]{2,1,0:T(2,128)(2,1)S(1)}, bf16[128,2,256]{2,1,0:T(2,128)(2,1)S(1)}, u32[]{:S(2)}, u32[]{:S(2)}) collective-permute-start(bf16[128,2,256]{2,1,0:T(2,128)(2,1)S(1)} %get-tuple-element.62), channel_id=1, source_target_pairs={{0,4},{8,0},{16,8},{24,16},{28,24},{20,28},{12,20},{4,12},{1,5},{9... | collective-permute-start | bytes 393224 | tf_op jit(solution)/shard_map/ppermute | solution.py:117
  21.4 0.5 %collective-permute-start.9 = (bf16[128,2,256]{2,1,0:T(2,128)(2,1)S(1)}, bf16[128,2,256]{2,1,0:T(2,128)(2,1)S(1)}, u32[]{:S(2)}, u32[]{:S(2)}) collective-permute-start(bf16[128,2,256]{2,1,0:T(2,128)(2,1)S(1)} %get-tuple-element.61), channel_id=1, source_target_pairs={{0,4},{8,0},{16,8},{24,16},{28,24},{20,28},{12,20},{4,12},{1,5},{9... | collective-permute-start | bytes 393224 | tf_op jit(solution)/shard_map/ppermute | solution.py:118
  21.9 1.5 %collective-permute-start.8 = (bf16[128,2,256]{2,1,0:T(2,128)(2,1)S(1)}, bf16[128,2,256]{2,1,0:T(2,128)(2,1)S(1)}, u32[]{:S(2)}, u32[]{:S(2)}) collective-permute-start(bf16[128,2,256]{2,1,0:T(2,128)(2,1)S(1)} %get-tuple-element.63), channel_id=1, source_target_pairs={{0,8},{8,16},{16,24},{24,28},{28,20},{20,12},{12,4},{4,0},{1,9},{9... | collective-permute-start | bytes 393224 | tf_op jit(solution)/shard_map/ppermute | solution.py:118
  23.4 1.8 %accumulate.4 = (f32[2,2048,256]{2,1,0:T(8,128)S(1)}, f32[8,128]{1,0:T(8,128)S(1)}) custom-call(bf16[8,256,2048]{2,1,0:T(8,128)(2,1)S(1)} %copy-done, bf16[256,2,256]{2,1,0:T(2,128)(2,1)S(1)} %collective-permute-done.3.refs_0_, bf16[256,2,256]{2,1,0:T(2,128)(2,1)S(1)} %collective-permute-done.1.refs_1_, f32[8,128]{1,0:T(8,128)S(1)} %get-tuple-element.40.refs_2_, ...), custom_call_target="tpu_custom_call" | custom-call | flops 1073741824 | bytes 2097152 | tf_op jit(solution)/shard_map/accumulate/pallas_call | solution.py:67
  25.2 1.7 %collective-permute-done.5.refs_3_ = bf16[128,2,256]{2,1,0:T(2,128)(2,1)S(1)} collective-permute-done((bf16[128,2,256]{2,1,0:T(2,128)(2,1)S(1)}, bf16[128,2,256]{2,1,0:T(2,128)(2,1)S(1)}, u32[]{:S(2)}, u32[]{:S(2)}) %collective-permute-start.5) | collective-permute-done | bytes 131104 | tf_op jit(solution)/shard_map/ppermute | solution.py:117
  27.0 0.4 collective-permute-start.11
  27.4 1.6 %collective-permute-start.10 = (bf16[128,2,256]{2,1,0:T(2,128)(2,1)S(1)}, bf16[128,2,256]{2,1,0:T(2,128)(2,1)S(1)}, u32[]{:S(2)}, u32[]{:S(2)}) collective-permute-start(bf16[128,2,256]{2,1,0:T(2,128)(2,1)S(1)} %collective-permute-done.6.refs_0_), channel_id=1, source_target_pairs={{0,8},{8,16},{16,24},{24,28},{28,20},{20,12},{12,4},{4,0},{1,9},{9... | collective-permute-start | bytes 393224 | tf_op jit(solution)/shard_map/ppermute | solution.py:122
  29.0 0.6 %prepare.1.refs_1_.plan_ref = f32[32,128]{1,0:T(8,128)S(1)} custom-call(s32[4]{0:T(128)S(1)} %copy-done.4, f32[8,128]{1,0:T(8,128)S(1)} %copy-done.3, bf16[304,128]{1,0:T(8,128)(2,1)S(1)} %copy-done.2, bf16[560,128]{1,0:T(8,128)(2,1)S(1)} %collective-permute-done.4.refs_1_, bf16[608,128]{1,0:T(8,128)(2,1)S(1)} %collective-permute-done.7.refs_2_), custom_call_target="tpu_custom_call" | custom-call | flops 100000000 | bytes 1000000 | tf_op jit(solution)/shard_map/prepare/pallas_call | solution.py:346
  29.6 2.4 %accumulate.5 = (f32[2,2048,256]{2,1,0:T(8,128)S(1)}, f32[8,128]{1,0:T(8,128)}) custom-call(bf16[8,256,2048]{2,1,0:T(8,128)(2,1)S(1)} %copy-done, bf16[128,2,256]{2,1,0:T(2,128)(2,1)S(1)} %collective-permute-done.6.refs_0_, bf16[128,2,256]{2,1,0:T(2,128)(2,1)S(1)} %collective-permute-done.8.refs_1_, bf16[128,2,256]{2,1,0:T(2,128)(2,1)S(1)} %collective-permute-done.9.refs_2_, ...), custom_call_target="tpu_custom_call" | custom-call | flops 1073741824 | bytes 2097152 | tf_op jit(solution)/shard_map/accumulate/pallas_call | solution.py:67
  32.0 0.3 collective-permute-done.10.refs_2_
  32.3 1.8 %measure.1 = f32[32,128]{1,0:T(8,128)S(1)} custom-call(bf16[8,256,2048]{2,1,0:T(8,128)(2,1)S(1)} %copy-done, f32[32,128]{1,0:T(8,128)S(1)} %prepare.1.refs_1_.plan_ref, bf16[128,2,256]{2,1,0:T(2,128)(2,1)S(1)} %collective-permute-done.10.refs_2_, bf16[128,2,256]{2,1,0:T(2,128)(2,1)S(1)} %collective-permute-done.11.refs_3_, ...), custom_call_target="tpu_custom_call" | custom-call | flops 536870912 | bytes 1048576 | tf_op jit(solution)/shard_map/measure/pallas_call | solution.py:417
  34.1 11.8 %all_to_all.11 = f32[32,1,128]{2,1,0:T(1,128)S(1)} all-to-all(f32[32,1,128]{2,1,0:T(1,128)S(1)} %bitcast.8), channel_id=1, replica_groups=mesh['chol'=8,'walk'=4] {'chol','walk'}, dimensions={0} | all-to-all | bytes 32768 | tf_op jit(solution)/shard_map/all_to_all | solution.py:498
  46.0 0.9 %finish.1 = (f32[1,4]{1,0:T(1,128)}, f32[1,4]{1,0:T(1,128)}, f32[128,128]{1,0:T(8,128)}) custom-call(f32[32,128]{1,0:T(8,128)S(1)} %bitcast.9, f32[32,128]{1,0:T(8,128)S(1)} %prepare.1.refs_1_.plan_ref, bf16[304,128]{1,0:T(8,128)(2,1)S(1)} %copy-done.2, bf16[560,128]{1,0:T(8,128)(2,1)S(1)} %collective-permute-done.4.refs_1_, ...), custom_call_target="tpu_custom_call" | custom-call | flops 1000000 | bytes 600000 | tf_op jit(solution)/shard_map/finish/pallas_call | solution.py:463
  (24 shorter events, 0.3 us)
Async XLA Ops:
  0.6 9.5 %collective-permute-start.2 = (bf16[256,2,256]{2,1,0:T(2,128)(2,1)}, bf16[256,2,256]{2,1,0:T(2,128)(2,1)S(1)}, u32[]{:S(2)}, u32[]{:S(2)}) collective-permute-start(bf16[256,2,256]{2,1,0:T(2,128)(2,1)} %refs_0_.2), channel_id=1, source_target_pairs={{0,8},{8,16},{16,24},{24,28},{28,20},{20,12},{12,4},{4,0},{1,9},{9... | collective-permute-start | bytes 786440 | tf_op jit(solution)/shard_map/ppermute | solution.py:101
  3.7 8.3 %collective-permute-start = (bf16[256,2,256]{2,1,0:T(2,128)(2,1)}, bf16[256,2,256]{2,1,0:T(2,128)(2,1)S(1)}, u32[]{:S(2)}, u32[]{:S(2)}) collective-permute-start(bf16[256,2,256]{2,1,0:T(2,128)(2,1)} %refs_0_.2), channel_id=1, source_target_pairs={{0,4},{8,0},{16,8},{24,16},{28,24},{20,28},{12,20},{4,12},{1,5},{9... | collective-permute-start | bytes 786440 | tf_op jit(solution)/shard_map/ppermute | solution.py:101
  3.7 8.5 %copy-start = (bf16[8,256,2048]{2,1,0:T(8,128)(2,1)S(1)}, bf16[8,256,2048]{2,1,0:T(8,128)(2,1)}, u32[]{:S(2)}) copy-start(bf16[8,256,2048]{2,1,0:T(8,128)(2,1)} %refs_0_.3) | copy-start | bytes 25165828
  3.7 8.5 %copy-start.1 = (bf16[256,2,256]{2,1,0:T(2,128)(2,1)S(1)}, bf16[256,2,256]{2,1,0:T(2,128)(2,1)}, u32[]{:S(2)}) copy-start(bf16[256,2,256]{2,1,0:T(2,128)(2,1)} %refs_0_.2) | copy-start | bytes 786436
  7.0 7.6 %collective-permute-start.4 = (bf16[560,128]{1,0:T(8,128)(2,1)}, bf16[560,128]{1,0:T(8,128)(2,1)S(1)}, u32[]{:S(2)}, u32[]{:S(2)}) collective-permute-start(bf16[560,128]{1,0:T(8,128)(2,1)} %get-tuple-element.34), channel_id=1, source_target_pairs={{0,2},{1,3},{2,0},{3,1},{4,6},{5,7},{6,4},{7,5},{8,10},{9,11},{10,... | collective-permute-start | bytes 430088 | tf_op jit(solution)/shard_map/ppermute | solution.py:268
  10.2 4.5 %copy-start.5 = (bf16[304,128]{1,0:T(8,128)(2,1)S(1)}, bf16[304,128]{1,0:T(8,128)(2,1)}, u32[]{:S(2)}) copy-start(bf16[304,128]{1,0:T(8,128)(2,1)} %get-tuple-element.45) | copy-start | bytes 233476
  10.2 7.5 %collective-permute-start.3 = (bf16[256,2,256]{2,1,0:T(2,128)(2,1)S(1)}, bf16[256,2,256]{2,1,0:T(2,128)(2,1)S(1)}, u32[]{:S(2)}, u32[]{:S(2)}) collective-permute-start(bf16[256,2,256]{2,1,0:T(2,128)(2,1)S(1)} %collective-permute-done.2.refs_1_), channel_id=1, source_target_pairs={{0,8},{8,16},{16,24},{24,28},{28,20},{20,12},{12,4},{4,0},{1,9},{9... | collective-permute-start | bytes 786440 | tf_op jit(solution)/shard_map/ppermute | solution.py:101
  12.0 6.9 %collective-permute-start.1 = (bf16[256,2,256]{2,1,0:T(2,128)(2,1)S(1)}, bf16[256,2,256]{2,1,0:T(2,128)(2,1)S(1)}, u32[]{:S(2)}, u32[]{:S(2)}) collective-permute-start(bf16[256,2,256]{2,1,0:T(2,128)(2,1)S(1)} %collective-permute-done.refs_2_), channel_id=1, source_target_pairs={{0,4},{8,0},{16,8},{24,16},{28,24},{20,28},{12,20},{4,12},{1,5},{9... | collective-permute-start | bytes 786440 | tf_op jit(solution)/shard_map/ppermute | solution.py:101
  14.7 14.2 %collective-permute-start.7 = (bf16[608,128]{1,0:T(8,128)(2,1)S(1)}, bf16[608,128]{1,0:T(8,128)(2,1)S(1)}, u32[]{:S(2)}, u32[]{:S(2)}) collective-permute-start(bf16[608,128]{1,0:T(8,128)(2,1)S(1)} %pad_maximum_fusion), channel_id=1, source_target_pairs={{0,1},{1,0},{2,3},{3,2},{4,5},{5,4},{6,7},{7,6},{8,9},{9,8},{10,11... | collective-permute-start | bytes 466952 | tf_op jit(solution)/shard_map/ppermute | solution.py:279
  19.1 6.2 %collective-permute-start.6 = (bf16[128,2,256]{2,1,0:T(2,128)(2,1)S(1)}, bf16[128,2,256]{2,1,0:T(2,128)(2,1)S(1)}, u32[]{:S(2)}, u32[]{:S(2)}) collective-permute-start(bf16[128,2,256]{2,1,0:T(2,128)(2,1)S(1)} %get-tuple-element.64), channel_id=1, source_target_pairs={{0,8},{8,16},{16,24},{24,28},{28,20},{20,12},{12,4},{4,0},{1,9},{9... | collective-permute-start | bytes 393224 | tf_op jit(solution)/shard_map/ppermute | solution.py:116
  20.9 6.1 %collective-permute-start.5 = (bf16[128,2,256]{2,1,0:T(2,128)(2,1)S(1)}, bf16[128,2,256]{2,1,0:T(2,128)(2,1)S(1)}, u32[]{:S(2)}, u32[]{:S(2)}) collective-permute-start(bf16[128,2,256]{2,1,0:T(2,128)(2,1)S(1)} %get-tuple-element.62), channel_id=1, source_target_pairs={{0,4},{8,0},{16,8},{24,16},{28,24},{20,28},{12,20},{4,12},{1,5},{9... | collective-permute-start | bytes 393224 | tf_op jit(solution)/shard_map/ppermute | solution.py:117
  21.4 8.3 %collective-permute-start.9 = (bf16[128,2,256]{2,1,0:T(2,128)(2,1)S(1)}, bf16[128,2,256]{2,1,0:T(2,128)(2,1)S(1)}, u32[]{:S(2)}, u32[]{:S(2)}) collective-permute-start(bf16[128,2,256]{2,1,0:T(2,128)(2,1)S(1)} %get-tuple-element.61), channel_id=1, source_target_pairs={{0,4},{8,0},{16,8},{24,16},{28,24},{20,28},{12,20},{4,12},{1,5},{9... | collective-permute-start | bytes 393224 | tf_op jit(solution)/shard_map/ppermute | solution.py:118
  21.9 7.7 %collective-permute-start.8 = (bf16[128,2,256]{2,1,0:T(2,128)(2,1)S(1)}, bf16[128,2,256]{2,1,0:T(2,128)(2,1)S(1)}, u32[]{:S(2)}, u32[]{:S(2)}) collective-permute-start(bf16[128,2,256]{2,1,0:T(2,128)(2,1)S(1)} %get-tuple-element.63), channel_id=1, source_target_pairs={{0,8},{8,16},{16,24},{24,28},{28,20},{20,12},{12,4},{4,0},{1,9},{9... | collective-permute-start | bytes 393224 | tf_op jit(solution)/shard_map/ppermute | solution.py:118
  23.4 5.6 %copy-start.2 = (bf16[304,128]{1,0:T(8,128)(2,1)S(1)}, bf16[304,128]{1,0:T(8,128)(2,1)}, u32[]{:S(2)}) copy-start(bf16[304,128]{1,0:T(8,128)(2,1)} %get-tuple-element.48.refs_0_) | copy-start | bytes 233476
  23.4 5.6 %copy-start.3 = (f32[8,128]{1,0:T(8,128)S(1)}, f32[8,128]{1,0:T(8,128)}, u32[]{:S(2)}) copy-start(f32[8,128]{1,0:T(8,128)} %get-tuple-element.32.onebody_ref) | copy-start | bytes 12292
  23.4 5.6 %copy-start.4 = (s32[4]{0:T(128)S(1)}, s32[4]{0:T(128)}, u32[]{:S(2)}) copy-start(s32[4]{0:T(128)} %counts_ref.1) | copy-start | bytes 52
  27.0 5.1 %collective-permute-start.11 = (bf16[128,2,256]{2,1,0:T(2,128)(2,1)S(1)}, bf16[128,2,256]{2,1,0:T(2,128)(2,1)S(1)}, u32[]{:S(2)}, u32[]{:S(2)}) collective-permute-start(bf16[128,2,256]{2,1,0:T(2,128)(2,1)S(1)} %collective-permute-done.5.refs_3_), channel_id=1, source_target_pairs={{0,4},{8,0},{16,8},{24,16},{28,24},{20,28},{12,20},{4,12},{1,5},{9... | collective-permute-start | bytes 393224 | tf_op jit(solution)/shard_map/ppermute | solution.py:122
  27.4 5.0 %collective-permute-start.10 = (bf16[128,2,256]{2,1,0:T(2,128)(2,1)S(1)}, bf16[128,2,256]{2,1,0:T(2,128)(2,1)S(1)}, u32[]{:S(2)}, u32[]{:S(2)}) collective-permute-start(bf16[128,2,256]{2,1,0:T(2,128)(2,1)S(1)} %collective-permute-done.6.refs_0_), channel_id=1, source_target_pairs={{0,8},{8,16},{16,24},{24,28},{28,20},{20,12},{12,4},{4,0},{1,9},{9... | collective-permute-start | bytes 393224 | tf_op jit(solution)/shard_map/ppermute | solution.py:122

commit v13 on v11

--- a/solution.py
+++ b/solution.py
@@ -368,25 +368,27 @@
         squares = [jnp.zeros((1, 1), jnp.float32) for _ in range(walkers)]
         drive = jnp.zeros((1, LANES), jnp.float32)
         start = 0 if whole else column_start(lax.axis_size("chol") // 2, depth)
-        lhs = chol_ref[:, :, pl.ds(start, depth)].reshape(vectors * orbitals, depth)
-        for b in range(walkers):
-            value = jnp.dot(lhs, rhs[b], preferred_element_type=jnp.float32)
-            tensor_scr[b] = value if whole else refs[2 + len(last)][b] + value
         for g in range(vectors):
+            lhs = chol_ref[g, :, pl.ds(start, depth)]
             top = g * orbitals
+            for b in range(walkers):
+                value = jnp.dot(lhs, rhs[b], preferred_element_type=jnp.float32)
+                if not whole:
+                    value = value + refs[2 + len(last)][b, top : top + orbitals, :]
+                tensor_scr[g % 2, b] = value
             for b in range(walkers):
                 diagonal = jnp.zeros((LANES, LANES), jnp.float32)
                 for q in range(quads):
                     for p in range(q + 1):
                         one = tensor_scr[
-                            b, top + q * LANES : top + (q + 1) * LANES, p * LANES : (p + 1) * LANES
+                            g % 2, b, q * LANES : (q + 1) * LANES, p * LANES : (p + 1) * LANES
                         ]
                         if p == q:
                             exchange[b] = exchange[b] + fold(one * one.T)
                             diagonal = diagonal + one
                         else:
                             two = tensor_scr[
-                                b, top + p * LANES : top + (p + 1) * LANES, q * LANES : (q + 1) * LANES
+                                g % 2, b, p * LANES : (p + 1) * LANES, q * LANES : (q + 1) * LANES
                             ]
                             exchange[b] = exchange[b] + 2.0 * fold(two * one.T)
                 trace = jnp.sum(fold(jnp.where(eye, diagonal, 0.0)), axis=0, keepdims=True)
@@ -412,7 +414,7 @@
         in_specs=[vmem()] * (2 + len(arrays)),
         out_specs=vmem(),
         scratch_shapes=[
-            pltpu.VMEM((walkers, vectors * orbitals, orbitals), jnp.float32),
+            pltpu.VMEM((2, walkers, orbitals, orbitals), jnp.float32),
         ],
         compiler_params=params(),
         cost_estimate=pl.CostEstimate(
@@ -486,7 +488,7 @@
     else:
         total, last, packs, plan = ring(green_rows, cholesky_rot, onebody, packed, do_prepare)
     stats = measure(cholesky_rot, total, last, plan, vectors, walk_size)
-    stats = lax.all_to_all(stats, ("chol", "walk"), split_axis=0, concat_axis=0, tiled=True)
+    stats = lax.all_to_all(stats, ("walk", "chol"), split_axis=0, concat_axis=0, tiled=True)
     energies, new_weights, density = finish(stats, plan, packs, places, vectors, slots, walkers)
     return energies.reshape(slots), new_weights.reshape(slots), density.reshape(1, density.size)
 

time: 45.9 us -> 46 us (level)
  no operation moved by 1% of the time
where the time goes in v13:
time: 46 us; the launch traced here: 45.8 us
  Pallas kernels  13.3 us (29%)
  starting transfers between devices  11 us (24%)
  blocking collectives  10.7 us (23%)
  waiting for transfers between devices  9.77 us (21%)
  between operations  0.74 us (2%)
    all_to_all x1, blocking collectives, per_device(): lax.all_to_all(stats, ('walk', 'chol'), split_axis=0, concat_axis=0, tile...  10.7 us
    ppermute x3, waiting for transfers between devices, ring(): lax.ppermute(right, 'chol', ahead)  6.96 us
    pallas_call x3, Pallas kernels, accumulate(): pl.pallas_call(kernel, name='accumulate', out_shape=[jax.ShapeDtypeStruct...  6.63 us
    ppermute x3, starting transfers between devices, ring(): lax.ppermute(right, 'chol', ahead)  6.35 us
    pallas_call x1, Pallas kernels, pack(): pl.pallas_call(kernel, name='pack', out_shape=[jax.ShapeDtypeStruct((8, L...  3.32 us
    pallas_call x1, Pallas kernels, measure(): pl.pallas_call(kernel, name='measure', out_shape=jax.ShapeDtypeStruct((ta...  1.87 us
    ppermute x1, starting transfers between devices, exchange_far(): return lax.ppermute(packed[1], 'walk', [(q, q ^ 2) for q in range(size)])  1.71 us
    ppermute x1, starting transfers between devices, ring(): lax.ppermute(right[:rows // 2], 'chol', ahead)  1.63 us
  transfers between devices with their start and end apart: 10, of which 5 were waited for; matrix products, arithmetic and copies ran while one was open for 0% of the time, Pallas kernels for 23%

profile of v13, /device:TPU:0, one launch (start us, length us, event | category | flops | bytes accessed | tf_op | source)
XLA Modules:
  0.0 45.8 jit_solution(3048882738102450734)
XLA Ops:
  0.6 3.1 %collective-permute-start.2 = (bf16[256,2,256]{2,1,0:T(2,128)(2,1)}, bf16[256,2,256]{2,1,0:T(2,128)(2,1)S(1)}, u32[]{:S(2)}, u32[]{:S(2)}) collective-permute-start(bf16[256,2,256]{2,1,0:T(2,128)(2,1)} %refs_0_.2), channel_id=1, source_target_pairs={{0,8},{8,16},{16,24},{24,28},{28,20},{20,12},{12,4},{4,0},{1,9},{9... | collective-permute-start | bytes 786440 | tf_op jit(solution)/shard_map/ppermute | solution.py:99
  3.7 3.3 %pack.1 = (f32[8,128]{1,0:T(8,128)}, bf16[304,128]{1,0:T(8,128)(2,1)}, bf16[560,128]{1,0:T(8,128)(2,1)}, bf16[304,128]{1,0:T(8,128)(2,1)}) custom-call(bf16[256,2,256]{2,1,0:T(2,128)(2,1)} %refs_0_.2, bf16[256,256]{1,0:T(8,128)(2,1)} %body_any.1, f32[4,8]{1,0:T(4,128)} %bitcast.10, f32[2]{0:T(128)} %weights_any.1, s32[4]{0:T(128)} %sources_any.1, ...), custom_call_target="tpu_custom_call" | custom-call | flops 100000000 | bytes 1000000 | tf_op jit(solution)/shard_map/pack/pallas_call | solution.py:225
  7.0 3.1 %collective-permute-done.2.refs_1_ = bf16[256,2,256]{2,1,0:T(2,128)(2,1)S(1)} collective-permute-done((bf16[256,2,256]{2,1,0:T(2,128)(2,1)}, bf16[256,2,256]{2,1,0:T(2,128)(2,1)S(1)}, u32[]{:S(2)}, u32[]{:S(2)}) %collective-permute-start.2) | collective-permute-done | bytes 262176 | tf_op jit(solution)/shard_map/ppermute | solution.py:99
  10.2 1.8 %collective-permute-start.3 = (bf16[256,2,256]{2,1,0:T(2,128)(2,1)S(1)}, bf16[256,2,256]{2,1,0:T(2,128)(2,1)S(1)}, u32[]{:S(2)}, u32[]{:S(2)}) collective-permute-start(bf16[256,2,256]{2,1,0:T(2,128)(2,1)S(1)} %collective-permute-done.2.refs_1_), channel_id=1, source_target_pairs={{0,8},{8,16},{16,24},{24,28},{28,20},{20,12},{12,4},{4,0},{1,9},{9... | collective-permute-start | bytes 786440 | tf_op jit(solution)/shard_map/ppermute | solution.py:99
  12.0 0.2 collective-permute-start.1
  12.2 1.7 %collective-permute-start.6 = (bf16[560,128]{1,0:T(8,128)(2,1)}, bf16[560,128]{1,0:T(8,128)(2,1)S(1)}, u32[]{:S(2)}, u32[]{:S(2)}) collective-permute-start(bf16[560,128]{1,0:T(8,128)(2,1)} %get-tuple-element.48), channel_id=1, source_target_pairs={{0,2},{1,3},{2,0},{3,1},{4,6},{5,7},{6,4},{7,5},{8,10},{9,11},{10,... | collective-permute-start | bytes 430088 | tf_op jit(solution)/shard_map/ppermute | solution.py:259
  13.9 2.5 %accumulate.3 = (f32[2,2048,256]{2,1,0:T(8,128)S(1)}, f32[8,128]{1,0:T(8,128)S(1)}) custom-call(bf16[8,256,2048]{2,1,0:T(8,128)(2,1)S(1)} %copy-done, bf16[256,2,256]{2,1,0:T(2,128)(2,1)S(1)} %copy-done.1, bf16[256,2,256]{2,1,0:T(2,128)(2,1)S(1)} %collective-permute-done.2.refs_1_, bf16[256,2,256]{2,1,0:T(2,128)(2,1)S(1)} %collective-permute-done.refs_2_), custom_call_target="tpu_custom_call" | custom-call | flops 1610612736 | bytes 3145728 | tf_op jit(solution)/shard_map/accumulate/pallas_call | solution.py:66
  16.4 1.3 %collective-permute-done.3.refs_0_ = bf16[256,2,256]{2,1,0:T(2,128)(2,1)S(1)} collective-permute-done((bf16[256,2,256]{2,1,0:T(2,128)(2,1)S(1)}, bf16[256,2,256]{2,1,0:T(2,128)(2,1)S(1)}, u32[]{:S(2)}, u32[]{:S(2)}) %collective-permute-start.3) | collective-permute-done | bytes 262176 | tf_op jit(solution)/shard_map/ppermute | solution.py:99
  17.7 1.5 %collective-permute-start.5 = (bf16[256,2,256]{2,1,0:T(2,128)(2,1)S(1)}, bf16[256,2,256]{2,1,0:T(2,128)(2,1)S(1)}, u32[]{:S(2)}, u32[]{:S(2)}) collective-permute-start(bf16[256,2,256]{2,1,0:T(2,128)(2,1)S(1)} %collective-permute-done.3.refs_0_), channel_id=1, source_target_pairs={{0,8},{8,16},{16,24},{24,28},{28,20},{20,12},{12,4},{4,0},{1,9},{9... | collective-permute-start | bytes 786440 | tf_op jit(solution)/shard_map/ppermute | solution.py:99
  19.1 0.5 %collective-permute-start.4 = (bf16[256,2,256]{2,1,0:T(2,128)(2,1)S(1)}, bf16[256,2,256]{2,1,0:T(2,128)(2,1)S(1)}, u32[]{:S(2)}, u32[]{:S(2)}) collective-permute-start(bf16[256,2,256]{2,1,0:T(2,128)(2,1)S(1)} %collective-permute-done.1.refs_1_), channel_id=1, source_target_pairs={{0,4},{8,0},{16,8},{24,16},{28,24},{20,28},{12,20},{4,12},{1,5},{9... | collective-permute-start | bytes 786440 | tf_op jit(solution)/shard_map/ppermute | solution.py:99
  19.7 0.1 collective-permute-start.7
  19.8 1.8 %accumulate.4 = (f32[2,2048,256]{2,1,0:T(8,128)S(1)}, f32[8,128]{1,0:T(8,128)S(1)}) custom-call(bf16[8,256,2048]{2,1,0:T(8,128)(2,1)S(1)} %copy-done, bf16[256,2,256]{2,1,0:T(2,128)(2,1)S(1)} %collective-permute-done.3.refs_0_, bf16[256,2,256]{2,1,0:T(2,128)(2,1)S(1)} %collective-permute-done.1.refs_1_, f32[8,128]{1,0:T(8,128)S(1)} %get-tuple-element.42.refs_2_, ...), custom_call_target="tpu_custom_call" | custom-call | flops 1073741824 | bytes 2097152 | tf_op jit(solution)/shard_map/accumulate/pallas_call | solution.py:66
  21.6 2.6 %collective-permute-done.5.refs_0_ = bf16[256,2,256]{2,1,0:T(2,128)(2,1)S(1)} collective-permute-done((bf16[256,2,256]{2,1,0:T(2,128)(2,1)S(1)}, bf16[256,2,256]{2,1,0:T(2,128)(2,1)S(1)}, u32[]{:S(2)}, u32[]{:S(2)}) %collective-permute-start.5) | collective-permute-done | bytes 262176 | tf_op jit(solution)/shard_map/ppermute | solution.py:99
  24.2 1.3 %collective-permute-done.4.refs_1_ = bf16[256,2,256]{2,1,0:T(2,128)(2,1)S(1)} collective-permute-done((bf16[256,2,256]{2,1,0:T(2,128)(2,1)S(1)}, bf16[256,2,256]{2,1,0:T(2,128)(2,1)S(1)}, u32[]{:S(2)}, u32[]{:S(2)}) %collective-permute-start.4) | collective-permute-done | bytes 262176 | tf_op jit(solution)/shard_map/ppermute | solution.py:99
  25.5 0.1 slice.11
  25.6 0.1 slice.10
  25.7 1.6 %collective-permute-start.8 = (bf16[128,2,256]{2,1,0:T(2,128)(2,1)S(1)}, bf16[128,2,256]{2,1,0:T(2,128)(2,1)S(1)}, u32[]{:S(2)}, u32[]{:S(2)}) collective-permute-start(bf16[128,2,256]{2,1,0:T(2,128)(2,1)S(1)} %slice.10), channel_id=1, source_target_pairs={{0,8},{8,16},{16,24},{24,28},{28,20},{20,12},{12,4},{4,0},{1,9},{9... | collective-permute-start | bytes 393224 | tf_op jit(solution)/shard_map/ppermute | solution.py:114
  27.3 0.4 collective-permute-start.9
  27.8 0.6 %prepare.1.refs_1_.plan_ref = f32[32,128]{1,0:T(8,128)S(1)} custom-call(s32[4]{0:T(128)S(1)} %copy-done.4, f32[8,128]{1,0:T(8,128)S(1)} %copy-done.3, bf16[304,128]{1,0:T(8,128)(2,1)S(1)} %copy-done.2, bf16[560,128]{1,0:T(8,128)(2,1)S(1)} %collective-permute-done.6.refs_1_, bf16[608,128]{1,0:T(8,128)(2,1)S(1)} %collective-permute-done.7.refs_2_), custom_call_target="tpu_custom_call" | custom-call | flops 100000000 | bytes 1000000 | tf_op jit(solution)/shard_map/prepare/pallas_call | solution.py:337
  28.4 2.4 %accumulate.5 = (f32[2,2048,256]{2,1,0:T(8,128)S(1)}, f32[8,128]{1,0:T(8,128)}) custom-call(bf16[8,256,2048]{2,1,0:T(8,128)(2,1)S(1)} %copy-done, bf16[256,2,256]{2,1,0:T(2,128)(2,1)S(1)} %collective-permute-done.5.refs_0_, bf16[256,2,256]{2,1,0:T(2,128)(2,1)S(1)} %collective-permute-done.4.refs_1_, f32[8,128]{1,0:T(8,128)S(1)} %get-tuple-element.55.refs_2_, ...), custom_call_target="tpu_custom_call" | custom-call | flops 1073741824 | bytes 2097152 | tf_op jit(solution)/shard_map/accumulate/pallas_call | solution.py:66
  30.8 1.5 %collective-permute-done.9.refs_3_ = bf16[128,2,256]{2,1,0:T(2,128)(2,1)S(1)} collective-permute-done((bf16[128,2,256]{2,1,0:T(2,128)(2,1)S(1)}, bf16[128,2,256]{2,1,0:T(2,128)(2,1)S(1)}, u32[]{:S(2)}, u32[]{:S(2)}) %collective-permute-start.9) | collective-permute-done | bytes 131104 | tf_op jit(solution)/shard_map/ppermute | solution.py:114
  32.3 1.9 %measure.1 = f32[32,128]{1,0:T(8,128)S(1)} custom-call(bf16[8,256,2048]{2,1,0:T(8,128)(2,1)S(1)} %copy-done, f32[32,128]{1,0:T(8,128)S(1)} %prepare.1.refs_1_.plan_ref, bf16[128,2,256]{2,1,0:T(2,128)(2,1)S(1)} %collective-permute-done.8.refs_2_, bf16[128,2,256]{2,1,0:T(2,128)(2,1)S(1)} %collective-permute-done.9.refs_3_, ...), custom_call_target="tpu_custom_call" | custom-call | flops 536870912 | bytes 1048576 | tf_op jit(solution)/shard_map/measure/pallas_call | solution.py:410
  34.2 10.7 %all_to_all.11 = f32[32,1,128]{2,1,0:T(1,128)S(1)} all-to-all(f32[32,1,128]{2,1,0:T(1,128)S(1)} %bitcast.8), channel_id=1, replica_groups=mesh['chol'=8,'walk'=4] {'walk','chol'}, dimensions={0} | all-to-all | bytes 32768 | tf_op jit(solution)/shard_map/all_to_all | solution.py:491
  44.9 0.9 %finish.1 = (f32[1,4]{1,0:T(1,128)}, f32[1,4]{1,0:T(1,128)}, f32[128,128]{1,0:T(8,128)}) custom-call(f32[32,128]{1,0:T(8,128)S(1)} %bitcast.9, f32[32,128]{1,0:T(8,128)S(1)} %prepare.1.refs_1_.plan_ref, bf16[304,128]{1,0:T(8,128)(2,1)S(1)} %copy-done.2, bf16[560,128]{1,0:T(8,128)(2,1)S(1)} %collective-permute-done.6.refs_1_, ...), custom_call_target="tpu_custom_call" | custom-call | flops 1000000 | bytes 600000 | tf_op jit(solution)/shard_map/finish/pallas_call | solution.py:456
  (20 shorter events, 0.1 us)
Async XLA Ops:
  0.6 9.5 %collective-permute-start.2 = (bf16[256,2,256]{2,1,0:T(2,128)(2,1)}, bf16[256,2,256]{2,1,0:T(2,128)(2,1)S(1)}, u32[]{:S(2)}, u32[]{:S(2)}) collective-permute-start(bf16[256,2,256]{2,1,0:T(2,128)(2,1)} %refs_0_.2), channel_id=1, source_target_pairs={{0,8},{8,16},{16,24},{24,28},{28,20},{20,12},{12,4},{4,0},{1,9},{9... | collective-permute-start | bytes 786440 | tf_op jit(solution)/shard_map/ppermute | solution.py:99
  3.7 8.3 %collective-permute-start = (bf16[256,2,256]{2,1,0:T(2,128)(2,1)}, bf16[256,2,256]{2,1,0:T(2,128)(2,1)S(1)}, u32[]{:S(2)}, u32[]{:S(2)}) collective-permute-start(bf16[256,2,256]{2,1,0:T(2,128)(2,1)} %refs_0_.2), channel_id=1, source_target_pairs={{0,4},{8,0},{16,8},{24,16},{28,24},{20,28},{12,20},{4,12},{1,5},{9... | collective-permute-start | bytes 786440 | tf_op jit(solution)/shard_map/ppermute | solution.py:99
  3.7 10.2 %copy-start = (bf16[8,256,2048]{2,1,0:T(8,128)(2,1)S(1)}, bf16[8,256,2048]{2,1,0:T(8,128)(2,1)}, u32[]{:S(2)}) copy-start(bf16[8,256,2048]{2,1,0:T(8,128)(2,1)} %refs_0_.3) | copy-start | bytes 25165828
  3.7 10.2 %copy-start.1 = (bf16[256,2,256]{2,1,0:T(2,128)(2,1)S(1)}, bf16[256,2,256]{2,1,0:T(2,128)(2,1)}, u32[]{:S(2)}) copy-start(bf16[256,2,256]{2,1,0:T(2,128)(2,1)} %refs_0_.2) | copy-start | bytes 786436
  10.2 7.5 %collective-permute-start.3 = (bf16[256,2,256]{2,1,0:T(2,128)(2,1)S(1)}, bf16[256,2,256]{2,1,0:T(2,128)(2,1)S(1)}, u32[]{:S(2)}, u32[]{:S(2)}) collective-permute-start(bf16[256,2,256]{2,1,0:T(2,128)(2,1)S(1)} %collective-permute-done.2.refs_1_), channel_id=1, source_target_pairs={{0,8},{8,16},{16,24},{24,28},{28,20},{20,12},{12,4},{4,0},{1,9},{9... | collective-permute-start | bytes 786440 | tf_op jit(solution)/shard_map/ppermute | solution.py:99
  12.0 7.7 %copy-start.5 = (bf16[304,128]{1,0:T(8,128)(2,1)S(1)}, bf16[304,128]{1,0:T(8,128)(2,1)}, u32[]{:S(2)}) copy-start(bf16[304,128]{1,0:T(8,128)(2,1)} %get-tuple-element.47) | copy-start | bytes 233476
  12.0 7.2 %collective-permute-start.1 = (bf16[256,2,256]{2,1,0:T(2,128)(2,1)S(1)}, bf16[256,2,256]{2,1,0:T(2,128)(2,1)S(1)}, u32[]{:S(2)}, u32[]{:S(2)}) collective-permute-start(bf16[256,2,256]{2,1,0:T(2,128)(2,1)S(1)} %collective-permute-done.refs_2_), channel_id=1, source_target_pairs={{0,4},{8,0},{16,8},{24,16},{28,24},{20,28},{12,20},{4,12},{1,5},{9... | collective-permute-start | bytes 786440 | tf_op jit(solution)/shard_map/ppermute | solution.py:99
  12.2 7.5 %collective-permute-start.6 = (bf16[560,128]{1,0:T(8,128)(2,1)}, bf16[560,128]{1,0:T(8,128)(2,1)S(1)}, u32[]{:S(2)}, u32[]{:S(2)}) collective-permute-start(bf16[560,128]{1,0:T(8,128)(2,1)} %get-tuple-element.48), channel_id=1, source_target_pairs={{0,2},{1,3},{2,0},{3,1},{4,6},{5,7},{6,4},{7,5},{8,10},{9,11},{10,... | collective-permute-start | bytes 430088 | tf_op jit(solution)/shard_map/ppermute | solution.py:259
  17.7 6.6 %collective-permute-start.5 = (bf16[256,2,256]{2,1,0:T(2,128)(2,1)S(1)}, bf16[256,2,256]{2,1,0:T(2,128)(2,1)S(1)}, u32[]{:S(2)}, u32[]{:S(2)}) collective-permute-start(bf16[256,2,256]{2,1,0:T(2,128)(2,1)S(1)} %collective-permute-done.3.refs_0_), channel_id=1, source_target_pairs={{0,8},{8,16},{16,24},{24,28},{28,20},{20,12},{12,4},{4,0},{1,9},{9... | collective-permute-start | bytes 786440 | tf_op jit(solution)/shard_map/ppermute | solution.py:99
  19.1 6.4 %collective-permute-start.4 = (bf16[256,2,256]{2,1,0:T(2,128)(2,1)S(1)}, bf16[256,2,256]{2,1,0:T(2,128)(2,1)S(1)}, u32[]{:S(2)}, u32[]{:S(2)}) collective-permute-start(bf16[256,2,256]{2,1,0:T(2,128)(2,1)S(1)} %collective-permute-done.1.refs_1_), channel_id=1, source_target_pairs={{0,4},{8,0},{16,8},{24,16},{28,24},{20,28},{12,20},{4,12},{1,5},{9... | collective-permute-start | bytes 786440 | tf_op jit(solution)/shard_map/ppermute | solution.py:99
  19.7 8.1 %collective-permute-start.7 = (bf16[608,128]{1,0:T(8,128)(2,1)S(1)}, bf16[608,128]{1,0:T(8,128)(2,1)S(1)}, u32[]{:S(2)}, u32[]{:S(2)}) collective-permute-start(bf16[608,128]{1,0:T(8,128)(2,1)S(1)} %pad_maximum_fusion), channel_id=1, source_target_pairs={{0,1},{1,0},{2,3},{3,2},{4,5},{5,4},{6,7},{7,6},{8,9},{9,8},{10,11... | collective-permute-start | bytes 466952 | tf_op jit(solution)/shard_map/ppermute | solution.py:270
  19.8 8.0 %copy-start.2 = (bf16[304,128]{1,0:T(8,128)(2,1)S(1)}, bf16[304,128]{1,0:T(8,128)(2,1)}, u32[]{:S(2)}) copy-start(bf16[304,128]{1,0:T(8,128)(2,1)} %get-tuple-element.50.refs_0_) | copy-start | bytes 233476
  19.8 8.0 %copy-start.3 = (f32[8,128]{1,0:T(8,128)S(1)}, f32[8,128]{1,0:T(8,128)}, u32[]{:S(2)}) copy-start(f32[8,128]{1,0:T(8,128)} %get-tuple-element.36.onebody_ref) | copy-start | bytes 12292
  19.8 8.0 %copy-start.4 = (s32[4]{0:T(128)S(1)}, s32[4]{0:T(128)}, u32[]{:S(2)}) copy-start(s32[4]{0:T(128)} %counts_ref.1) | copy-start | bytes 52
  25.7 5.1 %collective-permute-start.8 = (bf16[128,2,256]{2,1,0:T(2,128)(2,1)S(1)}, bf16[128,2,256]{2,1,0:T(2,128)(2,1)S(1)}, u32[]{:S(2)}, u32[]{:S(2)}) collective-permute-start(bf16[128,2,256]{2,1,0:T(2,128)(2,1)S(1)} %slice.10), channel_id=1, source_target_pairs={{0,8},{8,16},{16,24},{24,28},{28,20},{20,12},{12,4},{4,0},{1,9},{9... | collective-permute-start | bytes 393224 | tf_op jit(solution)/shard_map/ppermute | solution.py:114
  27.3 5.0 %collective-permute-start.9 = (bf16[128,2,256]{2,1,0:T(2,128)(2,1)S(1)}, bf16[128,2,256]{2,1,0:T(2,128)(2,1)S(1)}, u32[]{:S(2)}, u32[]{:S(2)}) collective-permute-start(bf16[128,2,256]{2,1,0:T(2,128)(2,1)S(1)} %slice.11), channel_id=1, source_target_pairs={{0,4},{8,0},{16,8},{24,16},{28,24},{20,28},{12,20},{4,12},{1,5},{9... | collective-permute-start | bytes 393224 | tf_op jit(solution)/shard_map/ppermute | solution.py:114

commit v14 on v11

--- a/solution.py
+++ b/solution.py
@@ -96,10 +96,10 @@
     shifts, parts = [0], [own]
     total = mark = None
     for step in range(1, steps):
-        next_right, next_left = lax.ppermute(right, "chol", ahead), lax.ppermute(left, "chol", back)
+        next_left, next_right = lax.ppermute(left, "chol", back), lax.ppermute(right, "chol", ahead)
         if step == 1:
-            right, onebody = tie(next_right, onebody)
-            left, *packed = tie(next_left, *packed)
+            left, onebody = tie(next_left, onebody)
+            right, *packed = tie(next_right, *packed)
         else:
             if step == 2:
                 far = exchange_far(packed)
@@ -107,11 +107,12 @@
                 near = exchange_near(packed, far)
             total, mark = accumulate(cholesky_rot, shifts, parts, total, mark)
             shifts, parts = [], []
+            left, mark = tie(next_left, mark)
             right, mark = tie(next_right, mark)
-            left, mark = tie(next_left, mark)
         shifts += [-step, step]
         parts = parts + [right, left]
-    last = [lax.ppermute(right[: rows // 2], "chol", ahead), lax.ppermute(left[rows // 2 :], "chol", back)]
+    lower = lax.ppermute(left[rows // 2 :], "chol", back)
+    last = [lax.ppermute(right[: rows // 2], "chol", ahead), lower]
     mark, *near = tie(mark, *near)
     packs = [packed[0], far] + near
     plan = do_prepare(packs)

time: 45.9 us -> 47 us (1.024)
  blocking collectives: 10.8 us -> 12.8 us
  waiting for transfers between devices: 9.77 us -> 8.8 us
    ppermute x3, waiting for transfers between devices: 1.29 us -> 7.03 us  [ring(): lax.ppermute(left, 'chol', back)]
    ppermute x3, waiting for transfers between devices: 6.96 us -> 1.36 us  [ring(): lax.ppermute(right, 'chol', ahead)]
    ppermute x3, starting transfers between devices: 0.78 us -> 6.07 us  [ring(): lax.ppermute(left, 'chol', back)]
    ppermute x3, starting transfers between devices: 6.35 us -> 1.12 us  [ring(): lax.ppermute(right, 'chol', ahead)]
    all_to_all x1, blocking collectives: 10.8 us -> 12.8 us  [per_device(): lax.all_to_all(stats, ('chol', 'walk'), split_axis=0, concat_axis=0, tile...]
    ppermute x2, waiting for transfers between devices: 1.51 us -> 0.41 us  [the longest x1 0.41 us: ring(): lower = lax.ppermute(left[rows // 2:], 'chol', back)]
where the time goes in v14:
time: 47 us; the launch traced here: 46.8 us
  Pallas kernels  13.2 us (28%)
  blocking collectives  12.8 us (27%)
  starting transfers between devices  11 us (23%)
  waiting for transfers between devices  8.8 us (19%)
  between operations  0.74 us (2%)
    all_to_all x1, blocking collectives, per_device(): lax.all_to_all(stats, ('chol', 'walk'), split_axis=0, concat_axis=0, tile...  12.8 us
    ppermute x3, waiting for transfers between devices, ring(): lax.ppermute(left, 'chol', back)  7.03 us
    pallas_call x3, Pallas kernels, accumulate(): pl.pallas_call(kernel, name='accumulate', out_shape=[jax.ShapeDtypeStruct...  6.62 us
    ppermute x3, starting transfers between devices, ring(): lax.ppermute(left, 'chol', back)  6.07 us
    pallas_call x1, Pallas kernels, pack(): pl.pallas_call(kernel, name='pack', out_shape=[jax.ShapeDtypeStruct((8, L...  3.32 us
    pallas_call x1, Pallas kernels, measure(): pl.pallas_call(kernel, name='measure', out_shape=jax.ShapeDtypeStruct((ta...  1.8 us
    ppermute x1, starting transfers between devices, exchange_far(): return lax.ppermute(packed[1], 'walk', [(q, q ^ 2) for q in range(size)])  1.66 us
    ppermute x1, starting transfers between devices, ring(): lower = lax.ppermute(left[rows // 2:], 'chol', back)  1.55 us
  transfers between devices with their start and end apart: 10, of which 5 were waited for; matrix products, arithmetic and copies ran while one was open for 0% of the time, Pallas kernels for 23%

profile of v14, /device:TPU:0, one launch (start us, length us, event | category | flops | bytes accessed | tf_op | source)
XLA Modules:
  0.0 46.8 jit_solution(12321661282656891416)
XLA Ops:
  0.6 3.0 %collective-permute-start.2 = (bf16[256,2,256]{2,1,0:T(2,128)(2,1)}, bf16[256,2,256]{2,1,0:T(2,128)(2,1)S(1)}, u32[]{:S(2)}, u32[]{:S(2)}) collective-permute-start(bf16[256,2,256]{2,1,0:T(2,128)(2,1)} %refs_0_.2), channel_id=1, source_target_pairs={{0,4},{8,0},{16,8},{24,16},{28,24},{20,28},{12,20},{4,12},{1,5},{9... | collective-permute-start | bytes 786440 | tf_op jit(solution)/shard_map/ppermute | solution.py:99
  3.7 0.1 collective-permute-start
  3.8 3.3 %pack.1 = (f32[8,128]{1,0:T(8,128)}, bf16[304,128]{1,0:T(8,128)(2,1)}, bf16[560,128]{1,0:T(8,128)(2,1)}, bf16[304,128]{1,0:T(8,128)(2,1)}) custom-call(bf16[256,2,256]{2,1,0:T(2,128)(2,1)} %refs_0_.2, bf16[256,256]{1,0:T(8,128)(2,1)} %body_any.1, f32[4,8]{1,0:T(4,128)} %bitcast.10, f32[2]{0:T(128)} %weights_any.1, s32[4]{0:T(128)} %sources_any.1, ...), custom_call_target="tpu_custom_call" | custom-call | flops 100000000 | bytes 1000000 | tf_op jit(solution)/shard_map/pack/pallas_call | solution.py:226
  7.1 3.1 %collective-permute-done.2.refs_2_ = bf16[256,2,256]{2,1,0:T(2,128)(2,1)S(1)} collective-permute-done((bf16[256,2,256]{2,1,0:T(2,128)(2,1)}, bf16[256,2,256]{2,1,0:T(2,128)(2,1)S(1)}, u32[]{:S(2)}, u32[]{:S(2)}) %collective-permute-start.2) | collective-permute-done | bytes 262176 | tf_op jit(solution)/shard_map/ppermute | solution.py:99
  10.2 1.7 %collective-permute-start.3 = (bf16[256,2,256]{2,1,0:T(2,128)(2,1)S(1)}, bf16[256,2,256]{2,1,0:T(2,128)(2,1)S(1)}, u32[]{:S(2)}, u32[]{:S(2)}) collective-permute-start(bf16[256,2,256]{2,1,0:T(2,128)(2,1)S(1)} %collective-permute-done.2.refs_2_), channel_id=1, source_target_pairs={{0,4},{8,0},{16,8},{24,16},{28,24},{20,28},{12,20},{4,12},{1,5},{9... | collective-permute-start | bytes 786440 | tf_op jit(solution)/shard_map/ppermute | solution.py:99
  11.9 0.3 collective-permute-start.1
  12.3 1.7 %collective-permute-start.6 = (bf16[560,128]{1,0:T(8,128)(2,1)}, bf16[560,128]{1,0:T(8,128)(2,1)S(1)}, u32[]{:S(2)}, u32[]{:S(2)}) collective-permute-start(bf16[560,128]{1,0:T(8,128)(2,1)} %get-tuple-element.48), channel_id=1, source_target_pairs={{0,2},{1,3},{2,0},{3,1},{4,6},{5,7},{6,4},{7,5},{8,10},{9,11},{10,... | collective-permute-start | bytes 430088 | tf_op jit(solution)/shard_map/ppermute | solution.py:260
  13.9 2.5 %accumulate.3 = (f32[2,2048,256]{2,1,0:T(8,128)S(1)}, f32[8,128]{1,0:T(8,128)S(1)}) custom-call(bf16[8,256,2048]{2,1,0:T(8,128)(2,1)S(1)} %copy-done, bf16[256,2,256]{2,1,0:T(2,128)(2,1)S(1)} %copy-done.1, bf16[256,2,256]{2,1,0:T(2,128)(2,1)S(1)} %collective-permute-done.refs_1_, bf16[256,2,256]{2,1,0:T(2,128)(2,1)S(1)} %collective-permute-done.2.refs_2_), custom_call_target="tpu_custom_call" | custom-call | flops 1610612736 | bytes 3145728 | tf_op jit(solution)/shard_map/accumulate/pallas_call | solution.py:66
  16.4 1.3 %collective-permute-done.3.refs_1_ = bf16[256,2,256]{2,1,0:T(2,128)(2,1)S(1)} collective-permute-done((bf16[256,2,256]{2,1,0:T(2,128)(2,1)S(1)}, bf16[256,2,256]{2,1,0:T(2,128)(2,1)S(1)}, u32[]{:S(2)}, u32[]{:S(2)}) %collective-permute-start.3) | collective-permute-done | bytes 262176 | tf_op jit(solution)/shard_map/ppermute | solution.py:99
  17.7 1.4 %collective-permute-start.5 = (bf16[256,2,256]{2,1,0:T(2,128)(2,1)S(1)}, bf16[256,2,256]{2,1,0:T(2,128)(2,1)S(1)}, u32[]{:S(2)}, u32[]{:S(2)}) collective-permute-start(bf16[256,2,256]{2,1,0:T(2,128)(2,1)S(1)} %collective-permute-done.3.refs_1_), channel_id=1, source_target_pairs={{0,4},{8,0},{16,8},{24,16},{28,24},{20,28},{12,20},{4,12},{1,5},{9... | collective-permute-start | bytes 786440 | tf_op jit(solution)/shard_map/ppermute | solution.py:99
  19.1 0.7 %collective-permute-start.4 = (bf16[256,2,256]{2,1,0:T(2,128)(2,1)S(1)}, bf16[256,2,256]{2,1,0:T(2,128)(2,1)S(1)}, u32[]{:S(2)}, u32[]{:S(2)}) collective-permute-start(bf16[256,2,256]{2,1,0:T(2,128)(2,1)S(1)} %collective-permute-done.1.refs_0_), channel_id=1, source_target_pairs={{0,8},{8,16},{16,24},{24,28},{28,20},{20,12},{12,4},{4,0},{1,9},{9... | collective-permute-start | bytes 786440 | tf_op jit(solution)/shard_map/ppermute | solution.py:99
  19.9 1.8 %accumulate.4 = (f32[2,2048,256]{2,1,0:T(8,128)S(1)}, f32[8,128]{1,0:T(8,128)S(1)}) custom-call(bf16[8,256,2048]{2,1,0:T(8,128)(2,1)S(1)} %copy-done, bf16[256,2,256]{2,1,0:T(2,128)(2,1)S(1)} %collective-permute-done.1.refs_0_, bf16[256,2,256]{2,1,0:T(2,128)(2,1)S(1)} %collective-permute-done.3.refs_1_, f32[8,128]{1,0:T(8,128)S(1)} %get-tuple-element.42.refs_2_, ...), custom_call_target="tpu_custom_call" | custom-call | flops 1073741824 | bytes 2097152 | tf_op jit(solution)/shard_map/accumulate/pallas_call | solution.py:66
  21.7 2.6 %collective-permute-done.5.refs_1_ = bf16[256,2,256]{2,1,0:T(2,128)(2,1)S(1)} collective-permute-done((bf16[256,2,256]{2,1,0:T(2,128)(2,1)S(1)}, bf16[256,2,256]{2,1,0:T(2,128)(2,1)S(1)}, u32[]{:S(2)}, u32[]{:S(2)}) %collective-permute-start.5) | collective-permute-done | bytes 262176 | tf_op jit(solution)/shard_map/ppermute | solution.py:99
  24.3 1.4 %collective-permute-done.4.refs_0_ = bf16[256,2,256]{2,1,0:T(2,128)(2,1)S(1)} collective-permute-done((bf16[256,2,256]{2,1,0:T(2,128)(2,1)S(1)}, bf16[256,2,256]{2,1,0:T(2,128)(2,1)S(1)}, u32[]{:S(2)}, u32[]{:S(2)}) %collective-permute-start.4) | collective-permute-done | bytes 262176 | tf_op jit(solution)/shard_map/ppermute | solution.py:99
  25.6 0.1 slice.11
  25.7 0.1 slice.10
  25.8 0.5 %collective-permute-start.8 = (bf16[128,2,256]{2,1,0:T(2,128)(2,1)S(1)}, bf16[128,2,256]{2,1,0:T(2,128)(2,1)S(1)}, u32[]{:S(2)}, u32[]{:S(2)}) collective-permute-start(bf16[128,2,256]{2,1,0:T(2,128)(2,1)S(1)} %slice.10), channel_id=1, source_target_pairs={{0,8},{8,16},{16,24},{24,28},{28,20},{20,12},{12,4},{4,0},{1,9},{9... | collective-permute-start | bytes 393224 | tf_op jit(solution)/shard_map/ppermute | solution.py:115
  26.4 1.5 %collective-permute-start.9 = (bf16[128,2,256]{2,1,0:T(2,128)(2,1)S(1)}, bf16[128,2,256]{2,1,0:T(2,128)(2,1)S(1)}, u32[]{:S(2)}, u32[]{:S(2)}) collective-permute-start(bf16[128,2,256]{2,1,0:T(2,128)(2,1)S(1)} %slice.11), channel_id=1, source_target_pairs={{0,4},{8,0},{16,8},{24,16},{28,24},{20,28},{12,20},{4,12},{1,5},{9... | collective-permute-start | bytes 393224 | tf_op jit(solution)/shard_map/ppermute | solution.py:114
  27.9 0.6 %prepare.1.refs_1_.plan_ref = f32[32,128]{1,0:T(8,128)S(1)} custom-call(s32[4]{0:T(128)S(1)} %copy-done.4, f32[8,128]{1,0:T(8,128)S(1)} %copy-done.3, bf16[304,128]{1,0:T(8,128)(2,1)S(1)} %copy-done.2, bf16[560,128]{1,0:T(8,128)(2,1)S(1)} %collective-permute-done.6.refs_1_, bf16[608,128]{1,0:T(8,128)(2,1)S(1)} %collective-permute-done.7.refs_2_), custom_call_target="tpu_custom_call" | custom-call | flops 100000000 | bytes 1000000 | tf_op jit(solution)/shard_map/prepare/pallas_call | solution.py:338
  28.6 2.4 %accumulate.5 = (f32[2,2048,256]{2,1,0:T(8,128)S(1)}, f32[8,128]{1,0:T(8,128)}) custom-call(bf16[8,256,2048]{2,1,0:T(8,128)(2,1)S(1)} %copy-done, bf16[256,2,256]{2,1,0:T(2,128)(2,1)S(1)} %collective-permute-done.4.refs_0_, bf16[256,2,256]{2,1,0:T(2,128)(2,1)S(1)} %collective-permute-done.5.refs_1_, f32[8,128]{1,0:T(8,128)S(1)} %get-tuple-element.55.refs_2_, ...), custom_call_target="tpu_custom_call" | custom-call | flops 1073741824 | bytes 2097152 | tf_op jit(solution)/shard_map/accumulate/pallas_call | solution.py:66
  30.9 0.4 collective-permute-done.9.refs_3_
  31.3 1.8 %measure.1 = f32[32,128]{1,0:T(8,128)S(1)} custom-call(bf16[8,256,2048]{2,1,0:T(8,128)(2,1)S(1)} %copy-done, f32[32,128]{1,0:T(8,128)S(1)} %prepare.1.refs_1_.plan_ref, bf16[128,2,256]{2,1,0:T(2,128)(2,1)S(1)} %collective-permute-done.8.refs_2_, bf16[128,2,256]{2,1,0:T(2,128)(2,1)S(1)} %collective-permute-done.9.refs_3_, ...), custom_call_target="tpu_custom_call" | custom-call | flops 536870912 | bytes 1048576 | tf_op jit(solution)/shard_map/measure/pallas_call | solution.py:409
  33.1 12.8 %all_to_all.11 = f32[32,1,128]{2,1,0:T(1,128)S(1)} all-to-all(f32[32,1,128]{2,1,0:T(1,128)S(1)} %bitcast.8), channel_id=1, replica_groups=mesh['chol'=8,'walk'=4] {'chol','walk'}, dimensions={0} | all-to-all | bytes 32768 | tf_op jit(solution)/shard_map/all_to_all | solution.py:490
  45.9 0.9 %finish.1 = (f32[1,4]{1,0:T(1,128)}, f32[1,4]{1,0:T(1,128)}, f32[128,128]{1,0:T(8,128)}) custom-call(f32[32,128]{1,0:T(8,128)S(1)} %bitcast.9, f32[32,128]{1,0:T(8,128)S(1)} %prepare.1.refs_1_.plan_ref, bf16[304,128]{1,0:T(8,128)(2,1)S(1)} %copy-done.2, bf16[560,128]{1,0:T(8,128)(2,1)S(1)} %collective-permute-done.6.refs_1_, ...), custom_call_target="tpu_custom_call" | custom-call | flops 1000000 | bytes 600000 | tf_op jit(solution)/shard_map/finish/pallas_call | solution.py:455
  (20 shorter events, 0.1 us)
Async XLA Ops:
  0.6 9.6 %collective-permute-start.2 = (bf16[256,2,256]{2,1,0:T(2,128)(2,1)}, bf16[256,2,256]{2,1,0:T(2,128)(2,1)S(1)}, u32[]{:S(2)}, u32[]{:S(2)}) collective-permute-start(bf16[256,2,256]{2,1,0:T(2,128)(2,1)} %refs_0_.2), channel_id=1, source_target_pairs={{0,4},{8,0},{16,8},{24,16},{28,24},{20,28},{12,20},{4,12},{1,5},{9... | collective-permute-start | bytes 786440 | tf_op jit(solution)/shard_map/ppermute | solution.py:99
  3.7 8.3 %collective-permute-start = (bf16[256,2,256]{2,1,0:T(2,128)(2,1)}, bf16[256,2,256]{2,1,0:T(2,128)(2,1)S(1)}, u32[]{:S(2)}, u32[]{:S(2)}) collective-permute-start(bf16[256,2,256]{2,1,0:T(2,128)(2,1)} %refs_0_.2), channel_id=1, source_target_pairs={{0,8},{8,16},{16,24},{24,28},{28,20},{20,12},{12,4},{4,0},{1,9},{9... | collective-permute-start | bytes 786440 | tf_op jit(solution)/shard_map/ppermute | solution.py:99
  3.8 10.1 %copy-start = (bf16[8,256,2048]{2,1,0:T(8,128)(2,1)S(1)}, bf16[8,256,2048]{2,1,0:T(8,128)(2,1)}, u32[]{:S(2)}) copy-start(bf16[8,256,2048]{2,1,0:T(8,128)(2,1)} %refs_0_.3) | copy-start | bytes 25165828
  3.8 10.1 %copy-start.1 = (bf16[256,2,256]{2,1,0:T(2,128)(2,1)S(1)}, bf16[256,2,256]{2,1,0:T(2,128)(2,1)}, u32[]{:S(2)}) copy-start(bf16[256,2,256]{2,1,0:T(2,128)(2,1)} %refs_0_.2) | copy-start | bytes 786436
  10.2 7.5 %collective-permute-start.3 = (bf16[256,2,256]{2,1,0:T(2,128)(2,1)S(1)}, bf16[256,2,256]{2,1,0:T(2,128)(2,1)S(1)}, u32[]{:S(2)}, u32[]{:S(2)}) collective-permute-start(bf16[256,2,256]{2,1,0:T(2,128)(2,1)S(1)} %collective-permute-done.2.refs_2_), channel_id=1, source_target_pairs={{0,4},{8,0},{16,8},{24,16},{28,24},{20,28},{12,20},{4,12},{1,5},{9... | collective-permute-start | bytes 786440 | tf_op jit(solution)/shard_map/ppermute | solution.py:99
  11.9 7.9 %copy-start.5 = (bf16[304,128]{1,0:T(8,128)(2,1)S(1)}, bf16[304,128]{1,0:T(8,128)(2,1)}, u32[]{:S(2)}) copy-start(bf16[304,128]{1,0:T(8,128)(2,1)} %get-tuple-element.47) | copy-start | bytes 233476
  11.9 7.2 %collective-permute-start.1 = (bf16[256,2,256]{2,1,0:T(2,128)(2,1)S(1)}, bf16[256,2,256]{2,1,0:T(2,128)(2,1)S(1)}, u32[]{:S(2)}, u32[]{:S(2)}) collective-permute-start(bf16[256,2,256]{2,1,0:T(2,128)(2,1)S(1)} %collective-permute-done.refs_1_), channel_id=1, source_target_pairs={{0,8},{8,16},{16,24},{24,28},{28,20},{20,12},{12,4},{4,0},{1,9},{9... | collective-permute-start | bytes 786440 | tf_op jit(solution)/shard_map/ppermute | solution.py:99
  12.3 7.5 %collective-permute-start.6 = (bf16[560,128]{1,0:T(8,128)(2,1)}, bf16[560,128]{1,0:T(8,128)(2,1)S(1)}, u32[]{:S(2)}, u32[]{:S(2)}) collective-permute-start(bf16[560,128]{1,0:T(8,128)(2,1)} %get-tuple-element.48), channel_id=1, source_target_pairs={{0,2},{1,3},{2,0},{3,1},{4,6},{5,7},{6,4},{7,5},{8,10},{9,11},{10,... | collective-permute-start | bytes 430088 | tf_op jit(solution)/shard_map/ppermute | solution.py:260
  17.7 6.6 %collective-permute-start.5 = (bf16[256,2,256]{2,1,0:T(2,128)(2,1)S(1)}, bf16[256,2,256]{2,1,0:T(2,128)(2,1)S(1)}, u32[]{:S(2)}, u32[]{:S(2)}) collective-permute-start(bf16[256,2,256]{2,1,0:T(2,128)(2,1)S(1)} %collective-permute-done.3.refs_1_), channel_id=1, source_target_pairs={{0,4},{8,0},{16,8},{24,16},{28,24},{20,28},{12,20},{4,12},{1,5},{9... | collective-permute-start | bytes 786440 | tf_op jit(solution)/shard_map/ppermute | solution.py:99
  19.1 6.6 %collective-permute-start.4 = (bf16[256,2,256]{2,1,0:T(2,128)(2,1)S(1)}, bf16[256,2,256]{2,1,0:T(2,128)(2,1)S(1)}, u32[]{:S(2)}, u32[]{:S(2)}) collective-permute-start(bf16[256,2,256]{2,1,0:T(2,128)(2,1)S(1)} %collective-permute-done.1.refs_0_), channel_id=1, source_target_pairs={{0,8},{8,16},{16,24},{24,28},{28,20},{20,12},{12,4},{4,0},{1,9},{9... | collective-permute-start | bytes 786440 | tf_op jit(solution)/shard_map/ppermute | solution.py:99
  19.8 8.1 %collective-permute-start.7 = (bf16[608,128]{1,0:T(8,128)(2,1)S(1)}, bf16[608,128]{1,0:T(8,128)(2,1)S(1)}, u32[]{:S(2)}, u32[]{:S(2)}) collective-permute-start(bf16[608,128]{1,0:T(8,128)(2,1)S(1)} %pad_maximum_fusion), channel_id=1, source_target_pairs={{0,1},{1,0},{2,3},{3,2},{4,5},{5,4},{6,7},{7,6},{8,9},{9,8},{10,11... | collective-permute-start | bytes 466952 | tf_op jit(solution)/shard_map/ppermute | solution.py:271
  19.9 8.1 %copy-start.2 = (bf16[304,128]{1,0:T(8,128)(2,1)S(1)}, bf16[304,128]{1,0:T(8,128)(2,1)}, u32[]{:S(2)}) copy-start(bf16[304,128]{1,0:T(8,128)(2,1)} %get-tuple-element.50.refs_0_) | copy-start | bytes 233476
  19.9 8.0 %copy-start.3 = (f32[8,128]{1,0:T(8,128)S(1)}, f32[8,128]{1,0:T(8,128)}, u32[]{:S(2)}) copy-start(f32[8,128]{1,0:T(8,128)} %get-tuple-element.36.onebody_ref) | copy-start | bytes 12292
  19.9 8.0 %copy-start.4 = (s32[4]{0:T(128)S(1)}, s32[4]{0:T(128)}, u32[]{:S(2)}) copy-start(s32[4]{0:T(128)} %counts_ref.1) | copy-start | bytes 52
  25.8 5.1 %collective-permute-start.8 = (bf16[128,2,256]{2,1,0:T(2,128)(2,1)S(1)}, bf16[128,2,256]{2,1,0:T(2,128)(2,1)S(1)}, u32[]{:S(2)}, u32[]{:S(2)}) collective-permute-start(bf16[128,2,256]{2,1,0:T(2,128)(2,1)S(1)} %slice.10), channel_id=1, source_target_pairs={{0,8},{8,16},{16,24},{24,28},{28,20},{20,12},{12,4},{4,0},{1,9},{9... | collective-permute-start | bytes 393224 | tf_op jit(solution)/shard_map/ppermute | solution.py:115
  26.4 5.0 %collective-permute-start.9 = (bf16[128,2,256]{2,1,0:T(2,128)(2,1)S(1)}, bf16[128,2,256]{2,1,0:T(2,128)(2,1)S(1)}, u32[]{:S(2)}, u32[]{:S(2)}) collective-permute-start(bf16[128,2,256]{2,1,0:T(2,128)(2,1)S(1)} %slice.11), channel_id=1, source_target_pairs={{0,4},{8,0},{16,8},{24,16},{28,24},{20,28},{12,20},{4,12},{1,5},{9... | collective-permute-start | bytes 393224 | tf_op jit(solution)/shard_map/ppermute | solution.py:114

commit v15 on v13

--- a/solution.py
+++ b/solution.py
@@ -364,38 +364,51 @@
         eye = lax.broadcasted_iota(jnp.int32, (LANES, LANES), 0) == lax.broadcasted_iota(
             jnp.int32, (LANES, LANES), 1
         )
-        exchange = [jnp.zeros((8, LANES), jnp.float32) for _ in range(walkers)]
-        squares = [jnp.zeros((1, 1), jnp.float32) for _ in range(walkers)]
-        drive = jnp.zeros((1, LANES), jnp.float32)
         start = 0 if whole else column_start(lax.axis_size("chol") // 2, depth)
-        for g in range(vectors):
+
+        def one_vector(g, slot, exchange, squares, drive):
+            top = pl.multiple_of(g * orbitals, orbitals)
             lhs = chol_ref[g, :, pl.ds(start, depth)]
-            top = g * orbitals
             for b in range(walkers):
                 value = jnp.dot(lhs, rhs[b], preferred_element_type=jnp.float32)
                 if not whole:
-                    value = value + refs[2 + len(last)][b, top : top + orbitals, :]
-                tensor_scr[g % 2, b] = value
+                    value = value + refs[2 + len(last)][b, pl.ds(top, orbitals), :]
+                tensor_scr[slot, b] = value
             for b in range(walkers):
                 diagonal = jnp.zeros((LANES, LANES), jnp.float32)
                 for q in range(quads):
                     for p in range(q + 1):
-                        one = tensor_scr[
-                            g % 2, b, q * LANES : (q + 1) * LANES, p * LANES : (p + 1) * LANES
-                        ]
+                        one = tensor_scr[slot, b, q * LANES : (q + 1) * LANES, p * LANES : (p + 1) * LANES]
                         if p == q:
                             exchange[b] = exchange[b] + fold(one * one.T)
                             diagonal = diagonal + one
                         else:
-                            two = tensor_scr[
-                                g % 2, b, p * LANES : (p + 1) * LANES, q * LANES : (q + 1) * LANES
-                            ]
+                            two = tensor_scr[slot, b, p * LANES : (p + 1) * LANES, q * LANES : (q + 1) * LANES]
                             exchange[b] = exchange[b] + 2.0 * fold(two * one.T)
                 trace = jnp.sum(fold(jnp.where(eye, diagonal, 0.0)), axis=0, keepdims=True)
                 trace = jnp.sum(trace, axis=1, keepdims=True)
                 squares[b] = squares[b] + trace * trace
-                row = at_drive + b * vectors + g
-                drive = drive + plan_ref[row : row + 1, :] * trace
+                drive = drive + plan_ref[pl.ds(at_drive + b * vectors + g, 1), :] * trace
+            return exchange, squares, drive
+
+        together = 2 if vectors % 2 == 0 else 1
+
+        def step(n, carry):
+            exchange, squares, drive = list(carry[0]), list(carry[1]), carry[2]
+            for slot in range(together):
+                exchange, squares, drive = one_vector(n * together + slot, slot, exchange, squares, drive)
+            return tuple(exchange), tuple(squares), drive
+
+        exchange, squares, drive = lax.fori_loop(
+            0,
+            vectors // together,
+            step,
+            (
+                tuple(jnp.zeros((8, LANES), jnp.float32) for _ in range(walkers)),
+                tuple(jnp.zeros((1, 1), jnp.float32) for _ in range(walkers)),
+                jnp.zeros((1, LANES), jnp.float32),
+            ),
+        )
         raw = plan_ref[at_single : at_single + 1, :]
         square = jnp.zeros((1, LANES), jnp.float32)
         for b in range(walkers):
@@ -488,7 +501,7 @@
     else:
         total, last, packs, plan = ring(green_rows, cholesky_rot, onebody, packed, do_prepare)
     stats = measure(cholesky_rot, total, last, plan, vectors, walk_size)
-    stats = lax.all_to_all(stats, ("walk", "chol"), split_axis=0, concat_axis=0, tiled=True)
+    stats = lax.all_to_all(stats, ("chol", "walk"), split_axis=0, concat_axis=0, tiled=True)
     energies, new_weights, density = finish(stats, plan, packs, places, vectors, slots, walkers)
     return energies.reshape(slots), new_weights.reshape(slots), density.reshape(1, density.size)
 

time: 46 us -> 47.2 us (1.026)
  Pallas kernels: 13.3 us -> 14.5 us
    pallas_call x1, Pallas kernels: 1.87 us -> 3.04 us  [measure(): pl.pallas_call(kernel, name='measure', out_shape=jax.ShapeDtypeStruct((ta...]
  transfers between devices with their start and end apart: 10 -> 10, of which waited for: 5 -> 5; matrix products, arithmetic and copies ran while one was open for 0% -> 0% of each run, Pallas kernels for 23% -> 22%
where the time goes in v15:
time: 47.2 us; the launch traced here: 47 us
  Pallas kernels  14.5 us (31%)
  starting transfers between devices  11 us (23%)
  blocking collectives  10.8 us (23%)
  waiting for transfers between devices  9.77 us (21%)
  between operations  0.74 us (2%)
    all_to_all x1, blocking collectives, per_device(): lax.all_to_all(stats, ('chol', 'walk'), split_axis=0, concat_axis=0, tile...  10.8 us
    ppermute x3, waiting for transfers between devices, ring(): lax.ppermute(right, 'chol', ahead)  6.96 us
    pallas_call x3, Pallas kernels, accumulate(): pl.pallas_call(kernel, name='accumulate', out_shape=[jax.ShapeDtypeStruct...  6.63 us
    ppermute x3, starting transfers between devices, ring(): lax.ppermute(right, 'chol', ahead)  6.35 us
    pallas_call x1, Pallas kernels, pack(): pl.pallas_call(kernel, name='pack', out_shape=[jax.ShapeDtypeStruct((8, L...  3.32 us
    pallas_call x1, Pallas kernels, measure(): pl.pallas_call(kernel, name='measure', out_shape=jax.ShapeDtypeStruct((ta...  3.04 us
    ppermute x1, starting transfers between devices, exchange_far(): return lax.ppermute(packed[1], 'walk', [(q, q ^ 2) for q in range(size)])  1.71 us
    ppermute x1, starting transfers between devices, ring(): lax.ppermute(right[:rows // 2], 'chol', ahead)  1.63 us
  transfers between devices with their start and end apart: 10, of which 5 were waited for; matrix products, arithmetic and copies ran while one was open for 0% of the time, Pallas kernels for 22%

profile of v15, /device:TPU:0, one launch (start us, length us, event | category | flops | bytes accessed | tf_op | source)
XLA Modules:
  0.0 47.0 jit_solution(5262447048689406806)
XLA Ops:
  0.6 3.1 %collective-permute-start.2 = (bf16[256,2,256]{2,1,0:T(2,128)(2,1)}, bf16[256,2,256]{2,1,0:T(2,128)(2,1)S(1)}, u32[]{:S(2)}, u32[]{:S(2)}) collective-permute-start(bf16[256,2,256]{2,1,0:T(2,128)(2,1)} %refs_0_.2), channel_id=1, source_target_pairs={{0,8},{8,16},{16,24},{24,28},{28,20},{20,12},{12,4},{4,0},{1,9},{9... | collective-permute-start | bytes 786440 | tf_op jit(solution)/shard_map/ppermute | solution.py:99
  3.7 3.3 %pack.1 = (f32[8,128]{1,0:T(8,128)}, bf16[304,128]{1,0:T(8,128)(2,1)}, bf16[560,128]{1,0:T(8,128)(2,1)}, bf16[304,128]{1,0:T(8,128)(2,1)}) custom-call(bf16[256,2,256]{2,1,0:T(2,128)(2,1)} %refs_0_.2, bf16[256,256]{1,0:T(8,128)(2,1)} %body_any.1, f32[4,8]{1,0:T(4,128)} %bitcast.10, f32[2]{0:T(128)} %weights_any.1, s32[4]{0:T(128)} %sources_any.1, ...), custom_call_target="tpu_custom_call" | custom-call | flops 100000000 | bytes 1000000 | tf_op jit(solution)/shard_map/pack/pallas_call | solution.py:225
  7.0 3.1 %collective-permute-done.2.refs_1_ = bf16[256,2,256]{2,1,0:T(2,128)(2,1)S(1)} collective-permute-done((bf16[256,2,256]{2,1,0:T(2,128)(2,1)}, bf16[256,2,256]{2,1,0:T(2,128)(2,1)S(1)}, u32[]{:S(2)}, u32[]{:S(2)}) %collective-permute-start.2) | collective-permute-done | bytes 262176 | tf_op jit(solution)/shard_map/ppermute | solution.py:99
  10.2 1.8 %collective-permute-start.3 = (bf16[256,2,256]{2,1,0:T(2,128)(2,1)S(1)}, bf16[256,2,256]{2,1,0:T(2,128)(2,1)S(1)}, u32[]{:S(2)}, u32[]{:S(2)}) collective-permute-start(bf16[256,2,256]{2,1,0:T(2,128)(2,1)S(1)} %collective-permute-done.2.refs_1_), channel_id=1, source_target_pairs={{0,8},{8,16},{16,24},{24,28},{28,20},{20,12},{12,4},{4,0},{1,9},{9... | collective-permute-start | bytes 786440 | tf_op jit(solution)/shard_map/ppermute | solution.py:99
  12.0 0.2 collective-permute-start.1
  12.2 1.7 %collective-permute-start.6 = (bf16[560,128]{1,0:T(8,128)(2,1)}, bf16[560,128]{1,0:T(8,128)(2,1)S(1)}, u32[]{:S(2)}, u32[]{:S(2)}) collective-permute-start(bf16[560,128]{1,0:T(8,128)(2,1)} %get-tuple-element.48), channel_id=1, source_target_pairs={{0,2},{1,3},{2,0},{3,1},{4,6},{5,7},{6,4},{7,5},{8,10},{9,11},{10,... | collective-permute-start | bytes 430088 | tf_op jit(solution)/shard_map/ppermute | solution.py:259
  13.9 2.5 %accumulate.3 = (f32[2,2048,256]{2,1,0:T(8,128)S(1)}, f32[8,128]{1,0:T(8,128)S(1)}) custom-call(bf16[8,256,2048]{2,1,0:T(8,128)(2,1)S(1)} %copy-done, bf16[256,2,256]{2,1,0:T(2,128)(2,1)S(1)} %copy-done.1, bf16[256,2,256]{2,1,0:T(2,128)(2,1)S(1)} %collective-permute-done.2.refs_1_, bf16[256,2,256]{2,1,0:T(2,128)(2,1)S(1)} %collective-permute-done.refs_2_), custom_call_target="tpu_custom_call" | custom-call | flops 1610612736 | bytes 3145728 | tf_op jit(solution)/shard_map/accumulate/pallas_call | solution.py:66
  16.4 1.3 %collective-permute-done.3.refs_0_ = bf16[256,2,256]{2,1,0:T(2,128)(2,1)S(1)} collective-permute-done((bf16[256,2,256]{2,1,0:T(2,128)(2,1)S(1)}, bf16[256,2,256]{2,1,0:T(2,128)(2,1)S(1)}, u32[]{:S(2)}, u32[]{:S(2)}) %collective-permute-start.3) | collective-permute-done | bytes 262176 | tf_op jit(solution)/shard_map/ppermute | solution.py:99
  17.7 1.5 %collective-permute-start.5 = (bf16[256,2,256]{2,1,0:T(2,128)(2,1)S(1)}, bf16[256,2,256]{2,1,0:T(2,128)(2,1)S(1)}, u32[]{:S(2)}, u32[]{:S(2)}) collective-permute-start(bf16[256,2,256]{2,1,0:T(2,128)(2,1)S(1)} %collective-permute-done.3.refs_0_), channel_id=1, source_target_pairs={{0,8},{8,16},{16,24},{24,28},{28,20},{20,12},{12,4},{4,0},{1,9},{9... | collective-permute-start | bytes 786440 | tf_op jit(solution)/shard_map/ppermute | solution.py:99
  19.1 0.5 %collective-permute-start.4 = (bf16[256,2,256]{2,1,0:T(2,128)(2,1)S(1)}, bf16[256,2,256]{2,1,0:T(2,128)(2,1)S(1)}, u32[]{:S(2)}, u32[]{:S(2)}) collective-permute-start(bf16[256,2,256]{2,1,0:T(2,128)(2,1)S(1)} %collective-permute-done.1.refs_1_), channel_id=1, source_target_pairs={{0,4},{8,0},{16,8},{24,16},{28,24},{20,28},{12,20},{4,12},{1,5},{9... | collective-permute-start | bytes 786440 | tf_op jit(solution)/shard_map/ppermute | solution.py:99
  19.7 0.1 collective-permute-start.7
  19.8 1.8 %accumulate.4 = (f32[2,2048,256]{2,1,0:T(8,128)S(1)}, f32[8,128]{1,0:T(8,128)S(1)}) custom-call(bf16[8,256,2048]{2,1,0:T(8,128)(2,1)S(1)} %copy-done, bf16[256,2,256]{2,1,0:T(2,128)(2,1)S(1)} %collective-permute-done.3.refs_0_, bf16[256,2,256]{2,1,0:T(2,128)(2,1)S(1)} %collective-permute-done.1.refs_1_, f32[8,128]{1,0:T(8,128)S(1)} %get-tuple-element.42.refs_2_, ...), custom_call_target="tpu_custom_call" | custom-call | flops 1073741824 | bytes 2097152 | tf_op jit(solution)/shard_map/accumulate/pallas_call | solution.py:66
  21.6 2.6 %collective-permute-done.5.refs_0_ = bf16[256,2,256]{2,1,0:T(2,128)(2,1)S(1)} collective-permute-done((bf16[256,2,256]{2,1,0:T(2,128)(2,1)S(1)}, bf16[256,2,256]{2,1,0:T(2,128)(2,1)S(1)}, u32[]{:S(2)}, u32[]{:S(2)}) %collective-permute-start.5) | collective-permute-done | bytes 262176 | tf_op jit(solution)/shard_map/ppermute | solution.py:99
  24.2 1.3 %collective-permute-done.4.refs_1_ = bf16[256,2,256]{2,1,0:T(2,128)(2,1)S(1)} collective-permute-done((bf16[256,2,256]{2,1,0:T(2,128)(2,1)S(1)}, bf16[256,2,256]{2,1,0:T(2,128)(2,1)S(1)}, u32[]{:S(2)}, u32[]{:S(2)}) %collective-permute-start.4) | collective-permute-done | bytes 262176 | tf_op jit(solution)/shard_map/ppermute | solution.py:99
  25.5 0.1 slice.11
  25.6 0.1 slice.10
  25.7 1.6 %collective-permute-start.8 = (bf16[128,2,256]{2,1,0:T(2,128)(2,1)S(1)}, bf16[128,2,256]{2,1,0:T(2,128)(2,1)S(1)}, u32[]{:S(2)}, u32[]{:S(2)}) collective-permute-start(bf16[128,2,256]{2,1,0:T(2,128)(2,1)S(1)} %slice.10), channel_id=1, source_target_pairs={{0,8},{8,16},{16,24},{24,28},{28,20},{20,12},{12,4},{4,0},{1,9},{9... | collective-permute-start | bytes 393224 | tf_op jit(solution)/shard_map/ppermute | solution.py:114
  27.3 0.4 collective-permute-start.9
  27.8 0.6 %prepare.1.refs_1_.plan_ref = f32[32,128]{1,0:T(8,128)S(1)} custom-call(s32[4]{0:T(128)S(1)} %copy-done.4, f32[8,128]{1,0:T(8,128)S(1)} %copy-done.3, bf16[304,128]{1,0:T(8,128)(2,1)S(1)} %copy-done.2, bf16[560,128]{1,0:T(8,128)(2,1)S(1)} %collective-permute-done.6.refs_1_, bf16[608,128]{1,0:T(8,128)(2,1)S(1)} %collective-permute-done.7.refs_2_), custom_call_target="tpu_custom_call" | custom-call | flops 100000000 | bytes 1000000 | tf_op jit(solution)/shard_map/prepare/pallas_call | solution.py:337
  28.4 2.4 %accumulate.5 = (f32[2,2048,256]{2,1,0:T(8,128)S(1)}, f32[8,128]{1,0:T(8,128)}) custom-call(bf16[8,256,2048]{2,1,0:T(8,128)(2,1)S(1)} %copy-done, bf16[256,2,256]{2,1,0:T(2,128)(2,1)S(1)} %collective-permute-done.5.refs_0_, bf16[256,2,256]{2,1,0:T(2,128)(2,1)S(1)} %collective-permute-done.4.refs_1_, f32[8,128]{1,0:T(8,128)S(1)} %get-tuple-element.55.refs_2_, ...), custom_call_target="tpu_custom_call" | custom-call | flops 1073741824 | bytes 2097152 | tf_op jit(solution)/shard_map/accumulate/pallas_call | solution.py:66
  30.8 1.5 %collective-permute-done.9.refs_3_ = bf16[128,2,256]{2,1,0:T(2,128)(2,1)S(1)} collective-permute-done((bf16[128,2,256]{2,1,0:T(2,128)(2,1)S(1)}, bf16[128,2,256]{2,1,0:T(2,128)(2,1)S(1)}, u32[]{:S(2)}, u32[]{:S(2)}) %collective-permute-start.9) | collective-permute-done | bytes 131104 | tf_op jit(solution)/shard_map/ppermute | solution.py:114
  32.3 3.0 %measure.1 = f32[32,128]{1,0:T(8,128)S(1)} custom-call(bf16[8,256,2048]{2,1,0:T(8,128)(2,1)S(1)} %copy-done, f32[32,128]{1,0:T(8,128)S(1)} %prepare.1.refs_1_.plan_ref, bf16[128,2,256]{2,1,0:T(2,128)(2,1)S(1)} %collective-permute-done.8.refs_2_, bf16[128,2,256]{2,1,0:T(2,128)(2,1)S(1)} %collective-permute-done.9.refs_3_, ...), custom_call_target="tpu_custom_call" | custom-call | flops 536870912 | bytes 1048576 | tf_op jit(solution)/shard_map/measure/pallas_call | solution.py:423
  35.3 10.8 %all_to_all.11 = f32[32,1,128]{2,1,0:T(1,128)S(1)} all-to-all(f32[32,1,128]{2,1,0:T(1,128)S(1)} %bitcast.8), channel_id=1, replica_groups=mesh['chol'=8,'walk'=4] {'chol','walk'}, dimensions={0} | all-to-all | bytes 32768 | tf_op jit(solution)/shard_map/all_to_all | solution.py:504
  46.1 0.9 %finish.1 = (f32[1,4]{1,0:T(1,128)}, f32[1,4]{1,0:T(1,128)}, f32[128,128]{1,0:T(8,128)}) custom-call(f32[32,128]{1,0:T(8,128)S(1)} %bitcast.9, f32[32,128]{1,0:T(8,128)S(1)} %prepare.1.refs_1_.plan_ref, bf16[304,128]{1,0:T(8,128)(2,1)S(1)} %copy-done.2, bf16[560,128]{1,0:T(8,128)(2,1)S(1)} %collective-permute-done.6.refs_1_, ...), custom_call_target="tpu_custom_call" | custom-call | flops 1000000 | bytes 600000 | tf_op jit(solution)/shard_map/finish/pallas_call | solution.py:469
  (20 shorter events, 0.1 us)
Async XLA Ops:
  0.6 9.5 %collective-permute-start.2 = (bf16[256,2,256]{2,1,0:T(2,128)(2,1)}, bf16[256,2,256]{2,1,0:T(2,128)(2,1)S(1)}, u32[]{:S(2)}, u32[]{:S(2)}) collective-permute-start(bf16[256,2,256]{2,1,0:T(2,128)(2,1)} %refs_0_.2), channel_id=1, source_target_pairs={{0,8},{8,16},{16,24},{24,28},{28,20},{20,12},{12,4},{4,0},{1,9},{9... | collective-permute-start | bytes 786440 | tf_op jit(solution)/shard_map/ppermute | solution.py:99
  3.7 8.3 %collective-permute-start = (bf16[256,2,256]{2,1,0:T(2,128)(2,1)}, bf16[256,2,256]{2,1,0:T(2,128)(2,1)S(1)}, u32[]{:S(2)}, u32[]{:S(2)}) collective-permute-start(bf16[256,2,256]{2,1,0:T(2,128)(2,1)} %refs_0_.2), channel_id=1, source_target_pairs={{0,4},{8,0},{16,8},{24,16},{28,24},{20,28},{12,20},{4,12},{1,5},{9... | collective-permute-start | bytes 786440 | tf_op jit(solution)/shard_map/ppermute | solution.py:99
  3.7 10.2 %copy-start = (bf16[8,256,2048]{2,1,0:T(8,128)(2,1)S(1)}, bf16[8,256,2048]{2,1,0:T(8,128)(2,1)}, u32[]{:S(2)}) copy-start(bf16[8,256,2048]{2,1,0:T(8,128)(2,1)} %refs_0_.3) | copy-start | bytes 25165828
  3.7 10.2 %copy-start.1 = (bf16[256,2,256]{2,1,0:T(2,128)(2,1)S(1)}, bf16[256,2,256]{2,1,0:T(2,128)(2,1)}, u32[]{:S(2)}) copy-start(bf16[256,2,256]{2,1,0:T(2,128)(2,1)} %refs_0_.2) | copy-start | bytes 786436
  10.2 7.5 %collective-permute-start.3 = (bf16[256,2,256]{2,1,0:T(2,128)(2,1)S(1)}, bf16[256,2,256]{2,1,0:T(2,128)(2,1)S(1)}, u32[]{:S(2)}, u32[]{:S(2)}) collective-permute-start(bf16[256,2,256]{2,1,0:T(2,128)(2,1)S(1)} %collective-permute-done.2.refs_1_), channel_id=1, source_target_pairs={{0,8},{8,16},{16,24},{24,28},{28,20},{20,12},{12,4},{4,0},{1,9},{9... | collective-permute-start | bytes 786440 | tf_op jit(solution)/shard_map/ppermute | solution.py:99
  12.0 7.7 %copy-start.5 = (bf16[304,128]{1,0:T(8,128)(2,1)S(1)}, bf16[304,128]{1,0:T(8,128)(2,1)}, u32[]{:S(2)}) copy-start(bf16[304,128]{1,0:T(8,128)(2,1)} %get-tuple-element.47) | copy-start | bytes 233476
  12.0 7.2 %collective-permute-start.1 = (bf16[256,2,256]{2,1,0:T(2,128)(2,1)S(1)}, bf16[256,2,256]{2,1,0:T(2,128)(2,1)S(1)}, u32[]{:S(2)}, u32[]{:S(2)}) collective-permute-start(bf16[256,2,256]{2,1,0:T(2,128)(2,1)S(1)} %collective-permute-done.refs_2_), channel_id=1, source_target_pairs={{0,4},{8,0},{16,8},{24,16},{28,24},{20,28},{12,20},{4,12},{1,5},{9... | collective-permute-start | bytes 786440 | tf_op jit(solution)/shard_map/ppermute | solution.py:99
  12.2 7.5 %collective-permute-start.6 = (bf16[560,128]{1,0:T(8,128)(2,1)}, bf16[560,128]{1,0:T(8,128)(2,1)S(1)}, u32[]{:S(2)}, u32[]{:S(2)}) collective-permute-start(bf16[560,128]{1,0:T(8,128)(2,1)} %get-tuple-element.48), channel_id=1, source_target_pairs={{0,2},{1,3},{2,0},{3,1},{4,6},{5,7},{6,4},{7,5},{8,10},{9,11},{10,... | collective-permute-start | bytes 430088 | tf_op jit(solution)/shard_map/ppermute | solution.py:259
  17.7 6.6 %collective-permute-start.5 = (bf16[256,2,256]{2,1,0:T(2,128)(2,1)S(1)}, bf16[256,2,256]{2,1,0:T(2,128)(2,1)S(1)}, u32[]{:S(2)}, u32[]{:S(2)}) collective-permute-start(bf16[256,2,256]{2,1,0:T(2,128)(2,1)S(1)} %collective-permute-done.3.refs_0_), channel_id=1, source_target_pairs={{0,8},{8,16},{16,24},{24,28},{28,20},{20,12},{12,4},{4,0},{1,9},{9... | collective-permute-start | bytes 786440 | tf_op jit(solution)/shard_map/ppermute | solution.py:99
  19.1 6.4 %collective-permute-start.4 = (bf16[256,2,256]{2,1,0:T(2,128)(2,1)S(1)}, bf16[256,2,256]{2,1,0:T(2,128)(2,1)S(1)}, u32[]{:S(2)}, u32[]{:S(2)}) collective-permute-start(bf16[256,2,256]{2,1,0:T(2,128)(2,1)S(1)} %collective-permute-done.1.refs_1_), channel_id=1, source_target_pairs={{0,4},{8,0},{16,8},{24,16},{28,24},{20,28},{12,20},{4,12},{1,5},{9... | collective-permute-start | bytes 786440 | tf_op jit(solution)/shard_map/ppermute | solution.py:99
  19.7 8.1 %collective-permute-start.7 = (bf16[608,128]{1,0:T(8,128)(2,1)S(1)}, bf16[608,128]{1,0:T(8,128)(2,1)S(1)}, u32[]{:S(2)}, u32[]{:S(2)}) collective-permute-start(bf16[608,128]{1,0:T(8,128)(2,1)S(1)} %pad_maximum_fusion), channel_id=1, source_target_pairs={{0,1},{1,0},{2,3},{3,2},{4,5},{5,4},{6,7},{7,6},{8,9},{9,8},{10,11... | collective-permute-start | bytes 466952 | tf_op jit(solution)/shard_map/ppermute | solution.py:270
  19.8 8.0 %copy-start.2 = (bf16[304,128]{1,0:T(8,128)(2,1)S(1)}, bf16[304,128]{1,0:T(8,128)(2,1)}, u32[]{:S(2)}) copy-start(bf16[304,128]{1,0:T(8,128)(2,1)} %get-tuple-element.50.refs_0_) | copy-start | bytes 233476
  19.8 8.0 %copy-start.3 = (f32[8,128]{1,0:T(8,128)S(1)}, f32[8,128]{1,0:T(8,128)}, u32[]{:S(2)}) copy-start(f32[8,128]{1,0:T(8,128)} %get-tuple-element.36.onebody_ref) | copy-start | bytes 12292
  19.8 8.0 %copy-start.4 = (s32[4]{0:T(128)S(1)}, s32[4]{0:T(128)}, u32[]{:S(2)}) copy-start(s32[4]{0:T(128)} %counts_ref.1) | copy-start | bytes 52
  25.7 5.1 %collective-permute-start.8 = (bf16[128,2,256]{2,1,0:T(2,128)(2,1)S(1)}, bf16[128,2,256]{2,1,0:T(2,128)(2,1)S(1)}, u32[]{:S(2)}, u32[]{:S(2)}) collective-permute-start(bf16[128,2,256]{2,1,0:T(2,128)(2,1)S(1)} %slice.10), channel_id=1, source_target_pairs={{0,8},{8,16},{16,24},{24,28},{28,20},{20,12},{12,4},{4,0},{1,9},{9... | collective-permute-start | bytes 393224 | tf_op jit(solution)/shard_map/ppermute | solution.py:114
  27.3 5.0 %collective-permute-start.9 = (bf16[128,2,256]{2,1,0:T(2,128)(2,1)S(1)}, bf16[128,2,256]{2,1,0:T(2,128)(2,1)S(1)}, u32[]{:S(2)}, u32[]{:S(2)}) collective-permute-start(bf16[128,2,256]{2,1,0:T(2,128)(2,1)S(1)} %slice.11), channel_id=1, source_target_pairs={{0,4},{8,0},{16,8},{24,16},{28,24},{20,28},{12,20},{4,12},{1,5},{9... | collective-permute-start | bytes 393224 | tf_op jit(solution)/shard_map/ppermute | solution.py:114

commit v16 on v13

--- a/solution.py
+++ b/solution.py
@@ -359,8 +359,12 @@
     def kernel(*refs):
         chol_ref, plan_ref = refs[:2]
         last_refs = refs[2 : 2 + len(last)]
-        out_ref, tensor_scr = refs[-2:]
-        rhs = [jnp.concatenate([x[:, b, :] for x in last_refs], axis=0) for b in range(walkers)]
+        out_ref, rhs_scr, tensor_scr = refs[-3:]
+        at = 0
+        for x in last_refs:
+            for b in range(walkers):
+                rhs_scr[at : at + x.shape[0], b * orbitals : (b + 1) * orbitals] = x[:, b, :]
+            at += x.shape[0]
         eye = lax.broadcasted_iota(jnp.int32, (LANES, LANES), 0) == lax.broadcasted_iota(
             jnp.int32, (LANES, LANES), 1
         )
@@ -369,13 +373,14 @@
         drive = jnp.zeros((1, LANES), jnp.float32)
         start = 0 if whole else column_start(lax.axis_size("chol") // 2, depth)
         for g in range(vectors):
-            lhs = chol_ref[g, :, pl.ds(start, depth)]
-            top = g * orbitals
+            value = jnp.dot(
+                chol_ref[g, :, pl.ds(start, depth)], rhs_scr[...], preferred_element_type=jnp.float32
+            )
             for b in range(walkers):
-                value = jnp.dot(lhs, rhs[b], preferred_element_type=jnp.float32)
+                part = value[:, b * orbitals : (b + 1) * orbitals]
                 if not whole:
-                    value = value + refs[2 + len(last)][b, top : top + orbitals, :]
-                tensor_scr[g % 2, b] = value
+                    part = part + refs[2 + len(last)][b, g * orbitals : (g + 1) * orbitals, :]
+                tensor_scr[g % 2, b] = part
             for b in range(walkers):
                 diagonal = jnp.zeros((LANES, LANES), jnp.float32)
                 for q in range(quads):
@@ -414,6 +419,7 @@
         in_specs=[vmem()] * (2 + len(arrays)),
         out_specs=vmem(),
         scratch_shapes=[
+            pltpu.VMEM((depth, walkers * orbitals), jnp.bfloat16),
             pltpu.VMEM((2, walkers, orbitals, orbitals), jnp.float32),
         ],
         compiler_params=params(),
@@ -488,7 +494,7 @@
     else:
         total, last, packs, plan = ring(green_rows, cholesky_rot, onebody, packed, do_prepare)
     stats = measure(cholesky_rot, total, last, plan, vectors, walk_size)
-    stats = lax.all_to_all(stats, ("walk", "chol"), split_axis=0, concat_axis=0, tiled=True)
+    stats = lax.all_to_all(stats, ("chol", "walk"), split_axis=0, concat_axis=0, tiled=True)
     energies, new_weights, density = finish(stats, plan, packs, places, vectors, slots, walkers)
     return energies.reshape(slots), new_weights.reshape(slots), density.reshape(1, density.size)
 

time: 46 us -> 45.9 us (level)
  no operation moved by 1% of the time
where the time goes in v16:
time: 45.9 us; the launch traced here: 45.8 us
  Pallas kernels  13.2 us (29%)
  starting transfers between devices  11 us (24%)
  blocking collectives  10.8 us (24%)
  waiting for transfers between devices  9.77 us (21%)
  between operations  0.74 us (2%)
    all_to_all x1, blocking collectives, per_device(): lax.all_to_all(stats, ('chol', 'walk'), split_axis=0, concat_axis=0, tile...  10.8 us
    ppermute x3, waiting for transfers between devices, ring(): lax.ppermute(right, 'chol', ahead)  6.96 us
    pallas_call x3, Pallas kernels, accumulate(): pl.pallas_call(kernel, name='accumulate', out_shape=[jax.ShapeDtypeStruct...  6.63 us
    ppermute x3, starting transfers between devices, ring(): lax.ppermute(right, 'chol', ahead)  6.35 us
    pallas_call x1, Pallas kernels, pack(): pl.pallas_call(kernel, name='pack', out_shape=[jax.ShapeDtypeStruct((8, L...  3.32 us
    pallas_call x1, Pallas kernels, measure(): pl.pallas_call(kernel, name='measure', out_shape=jax.ShapeDtypeStruct((ta...  1.81 us
    ppermute x1, starting transfers between devices, exchange_far(): return lax.ppermute(packed[1], 'walk', [(q, q ^ 2) for q in range(size)])  1.71 us
    ppermute x1, starting transfers between devices, ring(): lax.ppermute(right[:rows // 2], 'chol', ahead)  1.63 us
  transfers between devices with their start and end apart: 10, of which 5 were waited for; matrix products, arithmetic and copies ran while one was open for 0% of the time, Pallas kernels for 23%

profile of v16, /device:TPU:0, one launch (start us, length us, event | category | flops | bytes accessed | tf_op | source)
XLA Modules:
  0.0 45.8 jit_solution(4038506574173024210)
XLA Ops:
  0.6 3.1 %collective-permute-start.2 = (bf16[256,2,256]{2,1,0:T(2,128)(2,1)}, bf16[256,2,256]{2,1,0:T(2,128)(2,1)S(1)}, u32[]{:S(2)}, u32[]{:S(2)}) collective-permute-start(bf16[256,2,256]{2,1,0:T(2,128)(2,1)} %refs_0_.2), channel_id=1, source_target_pairs={{0,8},{8,16},{16,24},{24,28},{28,20},{20,12},{12,4},{4,0},{1,9},{9... | collective-permute-start | bytes 786440 | tf_op jit(solution)/shard_map/ppermute | solution.py:99
  3.7 3.3 %pack.1 = (f32[8,128]{1,0:T(8,128)}, bf16[304,128]{1,0:T(8,128)(2,1)}, bf16[560,128]{1,0:T(8,128)(2,1)}, bf16[304,128]{1,0:T(8,128)(2,1)}) custom-call(bf16[256,2,256]{2,1,0:T(2,128)(2,1)} %refs_0_.2, bf16[256,256]{1,0:T(8,128)(2,1)} %body_any.1, f32[4,8]{1,0:T(4,128)} %bitcast.10, f32[2]{0:T(128)} %weights_any.1, s32[4]{0:T(128)} %sources_any.1, ...), custom_call_target="tpu_custom_call" | custom-call | flops 100000000 | bytes 1000000 | tf_op jit(solution)/shard_map/pack/pallas_call | solution.py:225
  7.0 3.1 %collective-permute-done.2.refs_1_ = bf16[256,2,256]{2,1,0:T(2,128)(2,1)S(1)} collective-permute-done((bf16[256,2,256]{2,1,0:T(2,128)(2,1)}, bf16[256,2,256]{2,1,0:T(2,128)(2,1)S(1)}, u32[]{:S(2)}, u32[]{:S(2)}) %collective-permute-start.2) | collective-permute-done | bytes 262176 | tf_op jit(solution)/shard_map/ppermute | solution.py:99
  10.2 1.8 %collective-permute-start.3 = (bf16[256,2,256]{2,1,0:T(2,128)(2,1)S(1)}, bf16[256,2,256]{2,1,0:T(2,128)(2,1)S(1)}, u32[]{:S(2)}, u32[]{:S(2)}) collective-permute-start(bf16[256,2,256]{2,1,0:T(2,128)(2,1)S(1)} %collective-permute-done.2.refs_1_), channel_id=1, source_target_pairs={{0,8},{8,16},{16,24},{24,28},{28,20},{20,12},{12,4},{4,0},{1,9},{9... | collective-permute-start | bytes 786440 | tf_op jit(solution)/shard_map/ppermute | solution.py:99
  12.0 0.2 collective-permute-start.1
  12.2 1.7 %collective-permute-start.6 = (bf16[560,128]{1,0:T(8,128)(2,1)}, bf16[560,128]{1,0:T(8,128)(2,1)S(1)}, u32[]{:S(2)}, u32[]{:S(2)}) collective-permute-start(bf16[560,128]{1,0:T(8,128)(2,1)} %get-tuple-element.48), channel_id=1, source_target_pairs={{0,2},{1,3},{2,0},{3,1},{4,6},{5,7},{6,4},{7,5},{8,10},{9,11},{10,... | collective-permute-start | bytes 430088 | tf_op jit(solution)/shard_map/ppermute | solution.py:259
  13.9 2.5 %accumulate.3 = (f32[2,2048,256]{2,1,0:T(8,128)S(1)}, f32[8,128]{1,0:T(8,128)S(1)}) custom-call(bf16[8,256,2048]{2,1,0:T(8,128)(2,1)S(1)} %copy-done, bf16[256,2,256]{2,1,0:T(2,128)(2,1)S(1)} %copy-done.1, bf16[256,2,256]{2,1,0:T(2,128)(2,1)S(1)} %collective-permute-done.2.refs_1_, bf16[256,2,256]{2,1,0:T(2,128)(2,1)S(1)} %collective-permute-done.refs_2_), custom_call_target="tpu_custom_call" | custom-call | flops 1610612736 | bytes 3145728 | tf_op jit(solution)/shard_map/accumulate/pallas_call | solution.py:66
  16.4 1.3 %collective-permute-done.3.refs_0_ = bf16[256,2,256]{2,1,0:T(2,128)(2,1)S(1)} collective-permute-done((bf16[256,2,256]{2,1,0:T(2,128)(2,1)S(1)}, bf16[256,2,256]{2,1,0:T(2,128)(2,1)S(1)}, u32[]{:S(2)}, u32[]{:S(2)}) %collective-permute-start.3) | collective-permute-done | bytes 262176 | tf_op jit(solution)/shard_map/ppermute | solution.py:99
  17.7 1.5 %collective-permute-start.5 = (bf16[256,2,256]{2,1,0:T(2,128)(2,1)S(1)}, bf16[256,2,256]{2,1,0:T(2,128)(2,1)S(1)}, u32[]{:S(2)}, u32[]{:S(2)}) collective-permute-start(bf16[256,2,256]{2,1,0:T(2,128)(2,1)S(1)} %collective-permute-done.3.refs_0_), channel_id=1, source_target_pairs={{0,8},{8,16},{16,24},{24,28},{28,20},{20,12},{12,4},{4,0},{1,9},{9... | collective-permute-start | bytes 786440 | tf_op jit(solution)/shard_map/ppermute | solution.py:99
  19.1 0.5 %collective-permute-start.4 = (bf16[256,2,256]{2,1,0:T(2,128)(2,1)S(1)}, bf16[256,2,256]{2,1,0:T(2,128)(2,1)S(1)}, u32[]{:S(2)}, u32[]{:S(2)}) collective-permute-start(bf16[256,2,256]{2,1,0:T(2,128)(2,1)S(1)} %collective-permute-done.1.refs_1_), channel_id=1, source_target_pairs={{0,4},{8,0},{16,8},{24,16},{28,24},{20,28},{12,20},{4,12},{1,5},{9... | collective-permute-start | bytes 786440 | tf_op jit(solution)/shard_map/ppermute | solution.py:99
  19.7 0.1 collective-permute-start.7
  19.8 1.8 %accumulate.4 = (f32[2,2048,256]{2,1,0:T(8,128)S(1)}, f32[8,128]{1,0:T(8,128)S(1)}) custom-call(bf16[8,256,2048]{2,1,0:T(8,128)(2,1)S(1)} %copy-done, bf16[256,2,256]{2,1,0:T(2,128)(2,1)S(1)} %collective-permute-done.3.refs_0_, bf16[256,2,256]{2,1,0:T(2,128)(2,1)S(1)} %collective-permute-done.1.refs_1_, f32[8,128]{1,0:T(8,128)S(1)} %get-tuple-element.42.refs_2_, ...), custom_call_target="tpu_custom_call" | custom-call | flops 1073741824 | bytes 2097152 | tf_op jit(solution)/shard_map/accumulate/pallas_call | solution.py:66
  21.6 2.6 %collective-permute-done.5.refs_0_ = bf16[256,2,256]{2,1,0:T(2,128)(2,1)S(1)} collective-permute-done((bf16[256,2,256]{2,1,0:T(2,128)(2,1)S(1)}, bf16[256,2,256]{2,1,0:T(2,128)(2,1)S(1)}, u32[]{:S(2)}, u32[]{:S(2)}) %collective-permute-start.5) | collective-permute-done | bytes 262176 | tf_op jit(solution)/shard_map/ppermute | solution.py:99
  24.2 1.3 %collective-permute-done.4.refs_1_ = bf16[256,2,256]{2,1,0:T(2,128)(2,1)S(1)} collective-permute-done((bf16[256,2,256]{2,1,0:T(2,128)(2,1)S(1)}, bf16[256,2,256]{2,1,0:T(2,128)(2,1)S(1)}, u32[]{:S(2)}, u32[]{:S(2)}) %collective-permute-start.4) | collective-permute-done | bytes 262176 | tf_op jit(solution)/shard_map/ppermute | solution.py:99
  25.5 0.1 slice.11
  25.6 0.1 slice.10
  25.7 1.6 %collective-permute-start.8 = (bf16[128,2,256]{2,1,0:T(2,128)(2,1)S(1)}, bf16[128,2,256]{2,1,0:T(2,128)(2,1)S(1)}, u32[]{:S(2)}, u32[]{:S(2)}) collective-permute-start(bf16[128,2,256]{2,1,0:T(2,128)(2,1)S(1)} %slice.10), channel_id=1, source_target_pairs={{0,8},{8,16},{16,24},{24,28},{28,20},{20,12},{12,4},{4,0},{1,9},{9... | collective-permute-start | bytes 393224 | tf_op jit(solution)/shard_map/ppermute | solution.py:114
  27.3 0.4 collective-permute-start.9
  27.8 0.6 %prepare.1.refs_1_.plan_ref = f32[32,128]{1,0:T(8,128)S(1)} custom-call(s32[4]{0:T(128)S(1)} %copy-done.4, f32[8,128]{1,0:T(8,128)S(1)} %copy-done.3, bf16[304,128]{1,0:T(8,128)(2,1)S(1)} %copy-done.2, bf16[560,128]{1,0:T(8,128)(2,1)S(1)} %collective-permute-done.6.refs_1_, bf16[608,128]{1,0:T(8,128)(2,1)S(1)} %collective-permute-done.7.refs_2_), custom_call_target="tpu_custom_call" | custom-call | flops 100000000 | bytes 1000000 | tf_op jit(solution)/shard_map/prepare/pallas_call | solution.py:337
  28.4 2.4 %accumulate.5 = (f32[2,2048,256]{2,1,0:T(8,128)S(1)}, f32[8,128]{1,0:T(8,128)}) custom-call(bf16[8,256,2048]{2,1,0:T(8,128)(2,1)S(1)} %copy-done, bf16[256,2,256]{2,1,0:T(2,128)(2,1)S(1)} %collective-permute-done.5.refs_0_, bf16[256,2,256]{2,1,0:T(2,128)(2,1)S(1)} %collective-permute-done.4.refs_1_, f32[8,128]{1,0:T(8,128)S(1)} %get-tuple-element.55.refs_2_, ...), custom_call_target="tpu_custom_call" | custom-call | flops 1073741824 | bytes 2097152 | tf_op jit(solution)/shard_map/accumulate/pallas_call | solution.py:66
  30.8 1.5 %collective-permute-done.9.refs_3_ = bf16[128,2,256]{2,1,0:T(2,128)(2,1)S(1)} collective-permute-done((bf16[128,2,256]{2,1,0:T(2,128)(2,1)S(1)}, bf16[128,2,256]{2,1,0:T(2,128)(2,1)S(1)}, u32[]{:S(2)}, u32[]{:S(2)}) %collective-permute-start.9) | collective-permute-done | bytes 131104 | tf_op jit(solution)/shard_map/ppermute | solution.py:114
  32.3 1.8 %measure.1 = f32[32,128]{1,0:T(8,128)S(1)} custom-call(bf16[8,256,2048]{2,1,0:T(8,128)(2,1)S(1)} %copy-done, f32[32,128]{1,0:T(8,128)S(1)} %prepare.1.refs_1_.plan_ref, bf16[128,2,256]{2,1,0:T(2,128)(2,1)S(1)} %collective-permute-done.8.refs_2_, bf16[128,2,256]{2,1,0:T(2,128)(2,1)S(1)} %collective-permute-done.9.refs_3_, ...), custom_call_target="tpu_custom_call" | custom-call | flops 536870912 | bytes 1048576 | tf_op jit(solution)/shard_map/measure/pallas_call | solution.py:415
  34.1 10.8 %all_to_all.11 = f32[32,1,128]{2,1,0:T(1,128)S(1)} all-to-all(f32[32,1,128]{2,1,0:T(1,128)S(1)} %bitcast.8), channel_id=1, replica_groups=mesh['chol'=8,'walk'=4] {'chol','walk'}, dimensions={0} | all-to-all | bytes 32768 | tf_op jit(solution)/shard_map/all_to_all | solution.py:497
  44.9 0.9 %finish.1 = (f32[1,4]{1,0:T(1,128)}, f32[1,4]{1,0:T(1,128)}, f32[128,128]{1,0:T(8,128)}) custom-call(f32[32,128]{1,0:T(8,128)S(1)} %bitcast.9, f32[32,128]{1,0:T(8,128)S(1)} %prepare.1.refs_1_.plan_ref, bf16[304,128]{1,0:T(8,128)(2,1)S(1)} %copy-done.2, bf16[560,128]{1,0:T(8,128)(2,1)S(1)} %collective-permute-done.6.refs_1_, ...), custom_call_target="tpu_custom_call" | custom-call | flops 1000000 | bytes 600000 | tf_op jit(solution)/shard_map/finish/pallas_call | solution.py:462
  (20 shorter events, 0.1 us)
Async XLA Ops:
  0.6 9.5 %collective-permute-start.2 = (bf16[256,2,256]{2,1,0:T(2,128)(2,1)}, bf16[256,2,256]{2,1,0:T(2,128)(2,1)S(1)}, u32[]{:S(2)}, u32[]{:S(2)}) collective-permute-start(bf16[256,2,256]{2,1,0:T(2,128)(2,1)} %refs_0_.2), channel_id=1, source_target_pairs={{0,8},{8,16},{16,24},{24,28},{28,20},{20,12},{12,4},{4,0},{1,9},{9... | collective-permute-start | bytes 786440 | tf_op jit(solution)/shard_map/ppermute | solution.py:99
  3.7 8.3 %collective-permute-start = (bf16[256,2,256]{2,1,0:T(2,128)(2,1)}, bf16[256,2,256]{2,1,0:T(2,128)(2,1)S(1)}, u32[]{:S(2)}, u32[]{:S(2)}) collective-permute-start(bf16[256,2,256]{2,1,0:T(2,128)(2,1)} %refs_0_.2), channel_id=1, source_target_pairs={{0,4},{8,0},{16,8},{24,16},{28,24},{20,28},{12,20},{4,12},{1,5},{9... | collective-permute-start | bytes 786440 | tf_op jit(solution)/shard_map/ppermute | solution.py:99
  3.7 10.2 %copy-start = (bf16[8,256,2048]{2,1,0:T(8,128)(2,1)S(1)}, bf16[8,256,2048]{2,1,0:T(8,128)(2,1)}, u32[]{:S(2)}) copy-start(bf16[8,256,2048]{2,1,0:T(8,128)(2,1)} %refs_0_.3) | copy-start | bytes 25165828
  3.7 10.2 %copy-start.1 = (bf16[256,2,256]{2,1,0:T(2,128)(2,1)S(1)}, bf16[256,2,256]{2,1,0:T(2,128)(2,1)}, u32[]{:S(2)}) copy-start(bf16[256,2,256]{2,1,0:T(2,128)(2,1)} %refs_0_.2) | copy-start | bytes 786436
  10.2 7.5 %collective-permute-start.3 = (bf16[256,2,256]{2,1,0:T(2,128)(2,1)S(1)}, bf16[256,2,256]{2,1,0:T(2,128)(2,1)S(1)}, u32[]{:S(2)}, u32[]{:S(2)}) collective-permute-start(bf16[256,2,256]{2,1,0:T(2,128)(2,1)S(1)} %collective-permute-done.2.refs_1_), channel_id=1, source_target_pairs={{0,8},{8,16},{16,24},{24,28},{28,20},{20,12},{12,4},{4,0},{1,9},{9... | collective-permute-start | bytes 786440 | tf_op jit(solution)/shard_map/ppermute | solution.py:99
  12.0 7.7 %copy-start.5 = (bf16[304,128]{1,0:T(8,128)(2,1)S(1)}, bf16[304,128]{1,0:T(8,128)(2,1)}, u32[]{:S(2)}) copy-start(bf16[304,128]{1,0:T(8,128)(2,1)} %get-tuple-element.47) | copy-start | bytes 233476
  12.0 7.2 %collective-permute-start.1 = (bf16[256,2,256]{2,1,0:T(2,128)(2,1)S(1)}, bf16[256,2,256]{2,1,0:T(2,128)(2,1)S(1)}, u32[]{:S(2)}, u32[]{:S(2)}) collective-permute-start(bf16[256,2,256]{2,1,0:T(2,128)(2,1)S(1)} %collective-permute-done.refs_2_), channel_id=1, source_target_pairs={{0,4},{8,0},{16,8},{24,16},{28,24},{20,28},{12,20},{4,12},{1,5},{9... | collective-permute-start | bytes 786440 | tf_op jit(solution)/shard_map/ppermute | solution.py:99
  12.2 7.5 %collective-permute-start.6 = (bf16[560,128]{1,0:T(8,128)(2,1)}, bf16[560,128]{1,0:T(8,128)(2,1)S(1)}, u32[]{:S(2)}, u32[]{:S(2)}) collective-permute-start(bf16[560,128]{1,0:T(8,128)(2,1)} %get-tuple-element.48), channel_id=1, source_target_pairs={{0,2},{1,3},{2,0},{3,1},{4,6},{5,7},{6,4},{7,5},{8,10},{9,11},{10,... | collective-permute-start | bytes 430088 | tf_op jit(solution)/shard_map/ppermute | solution.py:259
  17.7 6.6 %collective-permute-start.5 = (bf16[256,2,256]{2,1,0:T(2,128)(2,1)S(1)}, bf16[256,2,256]{2,1,0:T(2,128)(2,1)S(1)}, u32[]{:S(2)}, u32[]{:S(2)}) collective-permute-start(bf16[256,2,256]{2,1,0:T(2,128)(2,1)S(1)} %collective-permute-done.3.refs_0_), channel_id=1, source_target_pairs={{0,8},{8,16},{16,24},{24,28},{28,20},{20,12},{12,4},{4,0},{1,9},{9... | collective-permute-start | bytes 786440 | tf_op jit(solution)/shard_map/ppermute | solution.py:99
  19.1 6.4 %collective-permute-start.4 = (bf16[256,2,256]{2,1,0:T(2,128)(2,1)S(1)}, bf16[256,2,256]{2,1,0:T(2,128)(2,1)S(1)}, u32[]{:S(2)}, u32[]{:S(2)}) collective-permute-start(bf16[256,2,256]{2,1,0:T(2,128)(2,1)S(1)} %collective-permute-done.1.refs_1_), channel_id=1, source_target_pairs={{0,4},{8,0},{16,8},{24,16},{28,24},{20,28},{12,20},{4,12},{1,5},{9... | collective-permute-start | bytes 786440 | tf_op jit(solution)/shard_map/ppermute | solution.py:99
  19.7 8.1 %collective-permute-start.7 = (bf16[608,128]{1,0:T(8,128)(2,1)S(1)}, bf16[608,128]{1,0:T(8,128)(2,1)S(1)}, u32[]{:S(2)}, u32[]{:S(2)}) collective-permute-start(bf16[608,128]{1,0:T(8,128)(2,1)S(1)} %pad_maximum_fusion), channel_id=1, source_target_pairs={{0,1},{1,0},{2,3},{3,2},{4,5},{5,4},{6,7},{7,6},{8,9},{9,8},{10,11... | collective-permute-start | bytes 466952 | tf_op jit(solution)/shard_map/ppermute | solution.py:270
  19.8 8.0 %copy-start.2 = (bf16[304,128]{1,0:T(8,128)(2,1)S(1)}, bf16[304,128]{1,0:T(8,128)(2,1)}, u32[]{:S(2)}) copy-start(bf16[304,128]{1,0:T(8,128)(2,1)} %get-tuple-element.50.refs_0_) | copy-start | bytes 233476
  19.8 8.0 %copy-start.3 = (f32[8,128]{1,0:T(8,128)S(1)}, f32[8,128]{1,0:T(8,128)}, u32[]{:S(2)}) copy-start(f32[8,128]{1,0:T(8,128)} %get-tuple-element.36.onebody_ref) | copy-start | bytes 12292
  19.8 8.0 %copy-start.4 = (s32[4]{0:T(128)S(1)}, s32[4]{0:T(128)}, u32[]{:S(2)}) copy-start(s32[4]{0:T(128)} %counts_ref.1) | copy-start | bytes 52
  25.7 5.1 %collective-permute-start.8 = (bf16[128,2,256]{2,1,0:T(2,128)(2,1)S(1)}, bf16[128,2,256]{2,1,0:T(2,128)(2,1)S(1)}, u32[]{:S(2)}, u32[]{:S(2)}) collective-permute-start(bf16[128,2,256]{2,1,0:T(2,128)(2,1)S(1)} %slice.10), channel_id=1, source_target_pairs={{0,8},{8,16},{16,24},{24,28},{28,20},{20,12},{12,4},{4,0},{1,9},{9... | collective-permute-start | bytes 393224 | tf_op jit(solution)/shard_map/ppermute | solution.py:114
  27.3 5.0 %collective-permute-start.9 = (bf16[128,2,256]{2,1,0:T(2,128)(2,1)S(1)}, bf16[128,2,256]{2,1,0:T(2,128)(2,1)S(1)}, u32[]{:S(2)}, u32[]{:S(2)}) collective-permute-start(bf16[128,2,256]{2,1,0:T(2,128)(2,1)S(1)} %slice.11), channel_id=1, source_target_pairs={{0,4},{8,0},{16,8},{24,16},{28,24},{20,28},{12,20},{4,12},{1,5},{9... | collective-permute-start | bytes 393224 | tf_op jit(solution)/shard_map/ppermute | solution.py:114

commit v17 on v11

--- a/solution.py
+++ b/solution.py
@@ -38,6 +38,26 @@
     return jnp.where(place < size // 2, 2 * place, 2 * (size - 1 - place) + 1)
 
 
+def split_walkers(green_rows):
+    rows, walkers, orbitals = green_rows.shape
+    steps = 4 if rows % 64 == 0 else 1
+
+    def kernel(green_ref, out_ref):
+        for b in range(walkers):
+            out_ref[:, b * orbitals : (b + 1) * orbitals] = green_ref[:, b, :]
+
+    return pl.pallas_call(
+        kernel,
+        name="split_walkers",
+        grid=(steps,),
+        out_shape=jax.ShapeDtypeStruct((rows, walkers * orbitals), green_rows.dtype),
+        in_specs=[pl.BlockSpec((rows // steps, walkers, orbitals), lambda n: (n, 0, 0))],
+        out_specs=pl.BlockSpec((rows // steps, walkers * orbitals), lambda n: (n, 0)),
+        compiler_params=params(),
+        cost_estimate=pl.CostEstimate(flops=0, bytes_accessed=4 * rows * walkers * orbitals, transcendentals=0),
+    )(green_rows)
+
+
 def column_start(shift, rows):
     size = lax.axis_size("chol")
     place = ring_place(lax.axis_index("chol"), size)
@@ -47,7 +67,8 @@
 
 def accumulate(cholesky_rot, shifts, parts, total, mark):
     vectors, orbitals, _ = cholesky_rot.shape
-    rows, walkers, _ = parts[0].shape
+    rows, columns = parts[0].shape
+    walkers = columns // orbitals
     size = vectors * orbitals
     arrays = list(parts) + ([] if mark is None else [mark]) + ([] if total is None else [total])
 
@@ -59,7 +80,7 @@
             [chol_ref[:, :, pl.ds(column_start(shift, rows), rows)].reshape(size, rows) for shift in shifts], axis=1
         )
         for b in range(walkers):
-            rhs = jnp.concatenate([x[:, b, :] for x in shards], axis=0)
+            rhs = jnp.concatenate([x[:, b * orbitals : (b + 1) * orbitals] for x in shards], axis=0)
             value = jnp.dot(lhs, rhs, preferred_element_type=jnp.float32)
             total_ref[b] = value if total is None else refs[len(arrays) - 1][b] + value
 
@@ -125,7 +146,8 @@
 
 
 def pack(own, one_body, fields, weights, sources, owners, cholesky_rot):
-    rows, walkers, orbitals = own.shape
+    rows, orbitals = one_body.shape
+    walkers = own.shape[1] // orbitals
     walk_size = lax.axis_size("walk")
     width = orbitals // walk_size
     pair = LANES // width
@@ -157,7 +179,7 @@
             copy.start()
         for copy in small:
             copy.wait()
-        green = [own_ref[:, b, :] for b in range(walkers)]
+        green = [own_ref[:, b * orbitals : (b + 1) * orbitals] for b in range(walkers)]
         walk = lax.axis_index("walk")
         lane = lax.broadcasted_iota(jnp.int32, (1, LANES), 1)
         body = body_ref[...].astype(jnp.float32)
@@ -345,8 +367,9 @@
     )(counts, onebody, *packs)
 
 
-def measure(cholesky_rot, total, last, plan, vectors, walk_size):
-    _, walkers, orbitals = last[0].shape
+def measure(cholesky_rot, total, last, plan, walk_size):
+    vectors, orbitals, _ = cholesky_rot.shape
+    walkers = last[0].shape[1] // orbitals
     depth = sum(x.shape[0] for x in last)
     targets = walk_size * lax.axis_size("chol")
     whole = total is None
@@ -360,7 +383,10 @@
         chol_ref, plan_ref = refs[:2]
         last_refs = refs[2 : 2 + len(last)]
         out_ref, tensor_scr = refs[-2:]
-        rhs = [jnp.concatenate([x[:, b, :] for x in last_refs], axis=0) for b in range(walkers)]
+        rhs = [
+            jnp.concatenate([x[:, b * orbitals : (b + 1) * orbitals] for x in last_refs], axis=0)
+            for b in range(walkers)
+        ]
         eye = lax.broadcasted_iota(jnp.int32, (LANES, LANES), 0) == lax.broadcasted_iota(
             jnp.int32, (LANES, LANES), 1
         )
@@ -471,7 +497,8 @@
     walk_size = lax.axis_size("walk")
     vectors, slots = fields.shape
     walkers = green_rows.shape[1]
-    onebody, *packed = pack(green_rows, one_body, fields, weights, sources, owners, cholesky_rot)
+    own = split_walkers(green_rows)
+    onebody, *packed = pack(own, one_body, fields, weights, sources, owners, cholesky_rot)
     table = 3 * table_height(vectors)
     places = walk_places(packed[0].shape[0] - table, table, walk_size)
 
@@ -482,10 +509,10 @@
         far = exchange_far(packed)
         packs = [packed[0], far] + exchange_near(packed, far)
         plan = do_prepare(packs)
-        total, last = None, [lax.all_gather(green_rows, "chol", axis=0, tiled=True)]
+        total, last = None, [lax.all_gather(own, "chol", axis=0, tiled=True)]
     else:
-        total, last, packs, plan = ring(green_rows, cholesky_rot, onebody, packed, do_prepare)
-    stats = measure(cholesky_rot, total, last, plan, vectors, walk_size)
+        total, last, packs, plan = ring(own, cholesky_rot, onebody, packed, do_prepare)
+    stats = measure(cholesky_rot, total, last, plan, walk_size)
     stats = lax.all_to_all(stats, ("chol", "walk"), split_axis=0, concat_axis=0, tiled=True)
     energies, new_weights, density = finish(stats, plan, packs, places, vectors, slots, walkers)
     return energies.reshape(slots), new_weights.reshape(slots), density.reshape(1, density.size)

time: 45.9 us -> 46.7 us (1.017)
  Pallas kernels: 13.2 us -> 10.8 us
  local copies, waits for them, and re-layouts: 0.22 us -> 1.95 us
  waiting for transfers between devices: 9.77 us -> 11.2 us
    unnamed x12 -> x16, local copies, waits for them, and re-layouts: 0.03 us -> 1.92 us
    pallas_call x3, Pallas kernels: 6.63 us -> 4.9 us  [accumulate(): pl.pallas_call(kernel, name='accumulate', out_shape=[jax.ShapeDtypeStruct...]
    ppermute x3, waiting for transfers between devices: 6.96 us -> 7.86 us  [ring(): lax.ppermute(right, 'chol', ahead)]
    pallas_call x1, Pallas kernels: 3.32 us -> 2.49 us  [pack(): pl.pallas_call(kernel, name='pack', out_shape=[jax.ShapeDtypeStruct((8, L...]
    pallas_call x0 -> x1, Pallas kernels: none -> 0.62 us  [split_walkers(): pl.pallas_call(kernel, name='split_walkers', grid=(steps,), out_shape=jax...]
  transfers between devices with their start and end apart: 10 -> 10, of which waited for: 5 -> 6; matrix products, arithmetic and copies ran while one was open for 0% -> 0% of each run, Pallas kernels for 23% -> 17%
where the time goes in v17:
time: 46.7 us; the launch traced here: 46.5 us
  waiting for transfers between devices  11.2 us (24%)
  starting transfers between devices  11 us (24%)
  Pallas kernels  10.8 us (23%)
  blocking collectives  10.8 us (23%)
  local copies, waits for them, and re-layouts  1.95 us (4%)
  between operations  0.76 us (2%)
    all_to_all x1, blocking collectives, per_device(): lax.all_to_all(stats, ('chol', 'walk'), split_axis=0, concat_axis=0, tile...  10.8 us
    ppermute x3, waiting for transfers between devices, ring(): lax.ppermute(right, 'chol', ahead)  7.86 us
    ppermute x3, starting transfers between devices, ring(): lax.ppermute(right, 'chol', ahead)  6.35 us
    pallas_call x3, Pallas kernels, accumulate(): pl.pallas_call(kernel, name='accumulate', out_shape=[jax.ShapeDtypeStruct...  4.9 us
    pallas_call x1, Pallas kernels, pack(): pl.pallas_call(kernel, name='pack', out_shape=[jax.ShapeDtypeStruct((8, L...  2.49 us
    unnamed x16, local copies, waits for them, and re-layouts  1.92 us
    ppermute x1, starting transfers between devices, exchange_far(): return lax.ppermute(packed[1], 'walk', [(q, q ^ 2) for q in range(size)])  1.71 us
    ppermute x1, starting transfers between devices, ring(): lax.ppermute(right[:rows // 2], 'chol', ahead)  1.63 us
  transfers between devices with their start and end apart: 10, of which 6 were waited for; matrix products, arithmetic and copies ran while one was open for 0% of the time, Pallas kernels for 17%

profile of v17, /device:TPU:0, one launch (start us, length us, event | category | flops | bytes accessed | tf_op | source)
XLA Modules:
  0.0 46.5 jit_solution(13668201105099833271)
XLA Ops:
  0.6 0.9 %copy-done.4 = bf16[256,2,256]{2,1,0:T(2,128)(2,1)S(1)} copy-done((bf16[256,2,256]{2,1,0:T(2,128)(2,1)S(1)}, bf16[256,2,256]{2,1,0:T(2,128)(2,1)}, u32[]{:S(2)}) %copy-start.4) | copy-done | bytes 262168
  1.6 0.6 %split_walkers.1.own_any.refs_0_ = bf16[256,512]{1,0:T(8,128)(2,1)S(1)} custom-call(bf16[256,2,256]{2,1,0:T(2,128)(2,1)S(1)} %copy-done.4), custom_call_target="tpu_custom_call" | custom-call | bytes 524288 | tf_op jit(solution)/shard_map/split_walkers/pallas_call | solution.py:49
  2.2 3.1 %collective-permute-start.2 = (bf16[256,512]{1,0:T(8,128)(2,1)S(1)}, bf16[256,512]{1,0:T(8,128)(2,1)S(1)}, u32[]{:S(2)}, u32[]{:S(2)}) collective-permute-start(bf16[256,512]{1,0:T(8,128)(2,1)S(1)} %split_walkers.1.own_any.refs_0_), channel_id=1, source_target_pairs={{0,8},{8,16},{16,24},{24,28},{28,20},{20,12},{12,4},{4,0},{1,9},{9... | collective-permute-start | bytes 786440 | tf_op jit(solution)/shard_map/ppermute | solution.py:120
  5.3 2.5 %pack.1 = (f32[8,128]{1,0:T(8,128)}, bf16[304,128]{1,0:T(8,128)(2,1)}, bf16[560,128]{1,0:T(8,128)(2,1)}, bf16[304,128]{1,0:T(8,128)(2,1)}) custom-call(bf16[256,512]{1,0:T(8,128)(2,1)} %copy-done.1, bf16[256,256]{1,0:T(8,128)(2,1)} %body_any.1, f32[4,8]{1,0:T(4,128)} %bitcast.10, f32[2]{0:T(128)} %weights_any.1, s32[4]{0:T(128)} %sources_any.1, ...), custom_call_target="tpu_custom_call" | custom-call | flops 100000000 | bytes 1000000 | tf_op jit(solution)/shard_map/pack/pallas_call | solution.py:247
  7.8 3.7 %collective-permute-done.2.refs_1_ = bf16[256,512]{1,0:T(8,128)(2,1)S(1)} collective-permute-done((bf16[256,512]{1,0:T(8,128)(2,1)S(1)}, bf16[256,512]{1,0:T(8,128)(2,1)S(1)}, u32[]{:S(2)}, u32[]{:S(2)}) %collective-permute-start.2) | collective-permute-done | bytes 262176 | tf_op jit(solution)/shard_map/ppermute | solution.py:120
  11.5 1.8 %collective-permute-start.3 = (bf16[256,512]{1,0:T(8,128)(2,1)S(1)}, bf16[256,512]{1,0:T(8,128)(2,1)S(1)}, u32[]{:S(2)}, u32[]{:S(2)}) collective-permute-start(bf16[256,512]{1,0:T(8,128)(2,1)S(1)} %collective-permute-done.2.refs_1_), channel_id=1, source_target_pairs={{0,8},{8,16},{16,24},{24,28},{28,20},{20,12},{12,4},{4,0},{1,9},{9... | collective-permute-start | bytes 786440 | tf_op jit(solution)/shard_map/ppermute | solution.py:120
  13.6 1.7 %collective-permute-start.6 = (bf16[560,128]{1,0:T(8,128)(2,1)}, bf16[560,128]{1,0:T(8,128)(2,1)S(1)}, u32[]{:S(2)}, u32[]{:S(2)}) collective-permute-start(bf16[560,128]{1,0:T(8,128)(2,1)} %get-tuple-element.48), channel_id=1, source_target_pairs={{0,2},{1,3},{2,0},{3,1},{4,6},{5,7},{6,4},{7,5},{8,10},{9,11},{10,... | collective-permute-start | bytes 430088 | tf_op jit(solution)/shard_map/ppermute | solution.py:281
  15.3 0.9 %copy-done.2 = bf16[256,512]{1,0:T(8,128)(2,1)S(1)} copy-done((bf16[256,512]{1,0:T(8,128)(2,1)S(1)}, bf16[256,512]{1,0:T(8,128)(2,1)}, u32[]{:S(2)}) %copy-start.2) | copy-done | bytes 262168
  16.2 1.8 %accumulate.3 = (f32[2,2048,256]{2,1,0:T(8,128)S(1)}, f32[8,128]{1,0:T(8,128)S(1)}) custom-call(bf16[8,256,2048]{2,1,0:T(8,128)(2,1)S(1)} %copy-done, bf16[256,512]{1,0:T(8,128)(2,1)S(1)} %copy-done.2, bf16[256,512]{1,0:T(8,128)(2,1)S(1)} %collective-permute-done.2.refs_1_, bf16[256,512]{1,0:T(8,128)(2,1)S(1)} %collective-permute-done.refs_2_), custom_call_target="tpu_custom_call" | custom-call | flops 1610612736 | bytes 3145728 | tf_op jit(solution)/shard_map/accumulate/pallas_call | solution.py:87
  18.0 1.0 %collective-permute-done.3.refs_0_ = bf16[256,512]{1,0:T(8,128)(2,1)S(1)} collective-permute-done((bf16[256,512]{1,0:T(8,128)(2,1)S(1)}, bf16[256,512]{1,0:T(8,128)(2,1)S(1)}, u32[]{:S(2)}, u32[]{:S(2)}) %collective-permute-start.3) | collective-permute-done | bytes 262176 | tf_op jit(solution)/shard_map/ppermute | solution.py:120
  19.0 1.5 %collective-permute-start.5 = (bf16[256,512]{1,0:T(8,128)(2,1)S(1)}, bf16[256,512]{1,0:T(8,128)(2,1)S(1)}, u32[]{:S(2)}, u32[]{:S(2)}) collective-permute-start(bf16[256,512]{1,0:T(8,128)(2,1)S(1)} %collective-permute-done.3.refs_0_), channel_id=1, source_target_pairs={{0,8},{8,16},{16,24},{24,28},{28,20},{20,12},{12,4},{4,0},{1,9},{9... | collective-permute-start | bytes 786440 | tf_op jit(solution)/shard_map/ppermute | solution.py:120
  20.5 0.5 %collective-permute-start.4 = (bf16[256,512]{1,0:T(8,128)(2,1)S(1)}, bf16[256,512]{1,0:T(8,128)(2,1)S(1)}, u32[]{:S(2)}, u32[]{:S(2)}) collective-permute-start(bf16[256,512]{1,0:T(8,128)(2,1)S(1)} %collective-permute-done.1.refs_1_), channel_id=1, source_target_pairs={{0,4},{8,0},{16,8},{24,16},{28,24},{20,28},{12,20},{4,12},{1,5},{9... | collective-permute-start | bytes 786440 | tf_op jit(solution)/shard_map/ppermute | solution.py:120
  21.2 1.3 %accumulate.4 = (f32[2,2048,256]{2,1,0:T(8,128)S(1)}, f32[8,128]{1,0:T(8,128)S(1)}) custom-call(bf16[8,256,2048]{2,1,0:T(8,128)(2,1)S(1)} %copy-done, bf16[256,512]{1,0:T(8,128)(2,1)S(1)} %collective-permute-done.3.refs_0_, bf16[256,512]{1,0:T(8,128)(2,1)S(1)} %collective-permute-done.1.refs_1_, f32[8,128]{1,0:T(8,128)S(1)} %get-tuple-element.42.refs_2_, ...), custom_call_target="tpu_custom_call" | custom-call | flops 1073741824 | bytes 2097152 | tf_op jit(solution)/shard_map/accumulate/pallas_call | solution.py:87
  22.5 3.1 %collective-permute-done.5.refs_0_ = bf16[256,512]{1,0:T(8,128)(2,1)S(1)} collective-permute-done((bf16[256,512]{1,0:T(8,128)(2,1)S(1)}, bf16[256,512]{1,0:T(8,128)(2,1)S(1)}, u32[]{:S(2)}, u32[]{:S(2)}) %collective-permute-start.5) | collective-permute-done | bytes 262176 | tf_op jit(solution)/shard_map/ppermute | solution.py:120
  25.6 1.3 %collective-permute-done.4.refs_1_ = bf16[256,512]{1,0:T(8,128)(2,1)S(1)} collective-permute-done((bf16[256,512]{1,0:T(8,128)(2,1)S(1)}, bf16[256,512]{1,0:T(8,128)(2,1)S(1)}, u32[]{:S(2)}, u32[]{:S(2)}) %collective-permute-start.4) | collective-permute-done | bytes 262176 | tf_op jit(solution)/shard_map/ppermute | solution.py:120
  26.9 1.6 %collective-permute-start.8 = (bf16[128,512]{1,0:T(8,128)(2,1)S(1)}, bf16[128,512]{1,0:T(8,128)(2,1)S(1)}, u32[]{:S(2)}, u32[]{:S(2)}) collective-permute-start(bf16[128,512]{1,0:T(8,128)(2,1)S(1)} %slice.10), channel_id=1, source_target_pairs={{0,8},{8,16},{16,24},{24,28},{28,20},{20,12},{12,4},{4,0},{1,9},{9... | collective-permute-start | bytes 393224 | tf_op jit(solution)/shard_map/ppermute | solution.py:135
  28.5 0.4 collective-permute-start.9
  29.0 0.6 %prepare.1.refs_1_.plan_ref = f32[32,128]{1,0:T(8,128)S(1)} custom-call(s32[4]{0:T(128)S(1)} %copy-done.6, f32[8,128]{1,0:T(8,128)S(1)} %copy-done.5, bf16[304,128]{1,0:T(8,128)(2,1)S(1)} %copy-done.3, bf16[560,128]{1,0:T(8,128)(2,1)S(1)} %collective-permute-done.6.refs_1_, bf16[608,128]{1,0:T(8,128)(2,1)S(1)} %collective-permute-done.7.refs_2_), custom_call_target="tpu_custom_call" | custom-call | flops 100000000 | bytes 1000000 | tf_op jit(solution)/shard_map/prepare/pallas_call | solution.py:359
  29.6 1.8 %accumulate.5 = (f32[2,2048,256]{2,1,0:T(8,128)S(1)}, f32[8,128]{1,0:T(8,128)}) custom-call(bf16[8,256,2048]{2,1,0:T(8,128)(2,1)S(1)} %copy-done, bf16[256,512]{1,0:T(8,128)(2,1)S(1)} %collective-permute-done.5.refs_0_, bf16[256,512]{1,0:T(8,128)(2,1)S(1)} %collective-permute-done.4.refs_1_, f32[8,128]{1,0:T(8,128)S(1)} %get-tuple-element.55.refs_2_, ...), custom_call_target="tpu_custom_call" | custom-call | flops 1073741824 | bytes 2097152 | tf_op jit(solution)/shard_map/accumulate/pallas_call | solution.py:87
  31.5 0.4 collective-permute-done.8.refs_2_
  31.9 1.6 %collective-permute-done.9.refs_3_ = bf16[128,512]{1,0:T(8,128)(2,1)S(1)} collective-permute-done((bf16[128,512]{1,0:T(8,128)(2,1)S(1)}, bf16[128,512]{1,0:T(8,128)(2,1)S(1)}, u32[]{:S(2)}, u32[]{:S(2)}) %collective-permute-start.9) | collective-permute-done | bytes 131104 | tf_op jit(solution)/shard_map/ppermute | solution.py:135
  33.5 1.3 %measure.1 = f32[32,128]{1,0:T(8,128)S(1)} custom-call(bf16[8,256,2048]{2,1,0:T(8,128)(2,1)S(1)} %copy-done, f32[32,128]{1,0:T(8,128)S(1)} %prepare.1.refs_1_.plan_ref, bf16[128,512]{1,0:T(8,128)(2,1)S(1)} %collective-permute-done.8.refs_2_, bf16[128,512]{1,0:T(8,128)(2,1)S(1)} %collective-permute-done.9.refs_3_, f32[2,2048,256]{2,1,0:T(8,128)S(1)} %get-tuple-element.57.refs_4_), custom_call_target="tpu_custom_call" | custom-call | flops 536870912 | bytes 1048576 | tf_op jit(solution)/shard_map/measure/pallas_call | solution.py:434
  34.9 10.8 %all_to_all.11 = f32[32,1,128]{2,1,0:T(1,128)S(1)} all-to-all(f32[32,1,128]{2,1,0:T(1,128)S(1)} %bitcast.8), channel_id=1, replica_groups=mesh['chol'=8,'walk'=4] {'chol','walk'}, dimensions={0} | all-to-all | bytes 32768 | tf_op jit(solution)/shard_map/all_to_all | solution.py:516
  45.6 0.9 %finish.1 = (f32[1,4]{1,0:T(1,128)}, f32[1,4]{1,0:T(1,128)}, f32[128,128]{1,0:T(8,128)}) custom-call(f32[32,128]{1,0:T(8,128)S(1)} %bitcast.9, f32[32,128]{1,0:T(8,128)S(1)} %prepare.1.refs_1_.plan_ref, bf16[304,128]{1,0:T(8,128)(2,1)S(1)} %copy-done.3, bf16[560,128]{1,0:T(8,128)(2,1)S(1)} %collective-permute-done.6.refs_1_, ...), custom_call_target="tpu_custom_call" | custom-call | flops 1000000 | bytes 600000 | tf_op jit(solution)/shard_map/finish/pallas_call | solution.py:480
  (25 shorter events, 0.4 us)
Async XLA Ops:
  0.6 1.0 %copy-start.4 = (bf16[256,2,256]{2,1,0:T(2,128)(2,1)S(1)}, bf16[256,2,256]{2,1,0:T(2,128)(2,1)}, u32[]{:S(2)}) copy-start(bf16[256,2,256]{2,1,0:T(2,128)(2,1)} %green_ref.1) | copy-start | bytes 786436
  2.2 3.1 %copy-start.1 = (bf16[256,512]{1,0:T(8,128)(2,1)}, bf16[256,512]{1,0:T(8,128)(2,1)S(1)}, u32[]{:S(2)}) copy-start(bf16[256,512]{1,0:T(8,128)(2,1)S(1)} %split_walkers.1.own_any.refs_0_) | copy-start | bytes 786436
  2.2 9.3 %collective-permute-start.2 = (bf16[256,512]{1,0:T(8,128)(2,1)S(1)}, bf16[256,512]{1,0:T(8,128)(2,1)S(1)}, u32[]{:S(2)}, u32[]{:S(2)}) collective-permute-start(bf16[256,512]{1,0:T(8,128)(2,1)S(1)} %split_walkers.1.own_any.refs_0_), channel_id=1, source_target_pairs={{0,8},{8,16},{16,24},{24,28},{28,20},{20,12},{12,4},{4,0},{1,9},{9... | collective-permute-start | bytes 786440 | tf_op jit(solution)/shard_map/ppermute | solution.py:120
  5.3 8.0 %collective-permute-start = (bf16[256,512]{1,0:T(8,128)(2,1)S(1)}, bf16[256,512]{1,0:T(8,128)(2,1)S(1)}, u32[]{:S(2)}, u32[]{:S(2)}) collective-permute-start(bf16[256,512]{1,0:T(8,128)(2,1)S(1)} %split_walkers.1.own_any.refs_0_), channel_id=1, source_target_pairs={{0,4},{8,0},{16,8},{24,16},{28,24},{20,28},{12,20},{4,12},{1,5},{9... | collective-permute-start | bytes 786440 | tf_op jit(solution)/shard_map/ppermute | solution.py:120
  5.3 10.0 %copy-start = (bf16[8,256,2048]{2,1,0:T(8,128)(2,1)S(1)}, bf16[8,256,2048]{2,1,0:T(8,128)(2,1)}, u32[]{:S(2)}) copy-start(bf16[8,256,2048]{2,1,0:T(8,128)(2,1)} %refs_0_.1) | copy-start | bytes 25165828
  11.5 7.5 %collective-permute-start.3 = (bf16[256,512]{1,0:T(8,128)(2,1)S(1)}, bf16[256,512]{1,0:T(8,128)(2,1)S(1)}, u32[]{:S(2)}, u32[]{:S(2)}) collective-permute-start(bf16[256,512]{1,0:T(8,128)(2,1)S(1)} %collective-permute-done.2.refs_1_), channel_id=1, source_target_pairs={{0,8},{8,16},{16,24},{24,28},{28,20},{20,12},{12,4},{4,0},{1,9},{9... | collective-permute-start | bytes 786440 | tf_op jit(solution)/shard_map/ppermute | solution.py:120
  13.3 7.2 %collective-permute-start.1 = (bf16[256,512]{1,0:T(8,128)(2,1)S(1)}, bf16[256,512]{1,0:T(8,128)(2,1)S(1)}, u32[]{:S(2)}, u32[]{:S(2)}) collective-permute-start(bf16[256,512]{1,0:T(8,128)(2,1)S(1)} %collective-permute-done.refs_2_), channel_id=1, source_target_pairs={{0,4},{8,0},{16,8},{24,16},{28,24},{20,28},{12,20},{4,12},{1,5},{9... | collective-permute-start | bytes 786440 | tf_op jit(solution)/shard_map/ppermute | solution.py:120
  13.6 7.5 %collective-permute-start.6 = (bf16[560,128]{1,0:T(8,128)(2,1)}, bf16[560,128]{1,0:T(8,128)(2,1)S(1)}, u32[]{:S(2)}, u32[]{:S(2)}) collective-permute-start(bf16[560,128]{1,0:T(8,128)(2,1)} %get-tuple-element.48), channel_id=1, source_target_pairs={{0,2},{1,3},{2,0},{3,1},{4,6},{5,7},{6,4},{7,5},{8,10},{9,11},{10,... | collective-permute-start | bytes 430088 | tf_op jit(solution)/shard_map/ppermute | solution.py:281
  15.3 1.0 %copy-start.2 = (bf16[256,512]{1,0:T(8,128)(2,1)S(1)}, bf16[256,512]{1,0:T(8,128)(2,1)}, u32[]{:S(2)}) copy-start(bf16[256,512]{1,0:T(8,128)(2,1)} %copy-done.1) | copy-start | bytes 786436
  16.2 4.8 %copy-start.7 = (bf16[304,128]{1,0:T(8,128)(2,1)S(1)}, bf16[304,128]{1,0:T(8,128)(2,1)}, u32[]{:S(2)}) copy-start(bf16[304,128]{1,0:T(8,128)(2,1)} %get-tuple-element.47) | copy-start | bytes 233476
  19.0 6.6 %collective-permute-start.5 = (bf16[256,512]{1,0:T(8,128)(2,1)S(1)}, bf16[256,512]{1,0:T(8,128)(2,1)S(1)}, u32[]{:S(2)}, u32[]{:S(2)}) collective-permute-start(bf16[256,512]{1,0:T(8,128)(2,1)S(1)} %collective-permute-done.3.refs_0_), channel_id=1, source_target_pairs={{0,8},{8,16},{16,24},{24,28},{28,20},{20,12},{12,4},{4,0},{1,9},{9... | collective-permute-start | bytes 786440 | tf_op jit(solution)/shard_map/ppermute | solution.py:120
  20.5 6.4 %collective-permute-start.4 = (bf16[256,512]{1,0:T(8,128)(2,1)S(1)}, bf16[256,512]{1,0:T(8,128)(2,1)S(1)}, u32[]{:S(2)}, u32[]{:S(2)}) collective-permute-start(bf16[256,512]{1,0:T(8,128)(2,1)S(1)} %collective-permute-done.1.refs_1_), channel_id=1, source_target_pairs={{0,4},{8,0},{16,8},{24,16},{28,24},{20,28},{12,20},{4,12},{1,5},{9... | collective-permute-start | bytes 786440 | tf_op jit(solution)/shard_map/ppermute | solution.py:120
  21.1 7.9 %collective-permute-start.7 = (bf16[608,128]{1,0:T(8,128)(2,1)S(1)}, bf16[608,128]{1,0:T(8,128)(2,1)S(1)}, u32[]{:S(2)}, u32[]{:S(2)}) collective-permute-start(bf16[608,128]{1,0:T(8,128)(2,1)S(1)} %pad_maximum_fusion), channel_id=1, source_target_pairs={{0,1},{1,0},{2,3},{3,2},{4,5},{5,4},{6,7},{7,6},{8,9},{9,8},{10,11... | collective-permute-start | bytes 466952 | tf_op jit(solution)/shard_map/ppermute | solution.py:292
  21.2 7.8 %copy-start.3 = (bf16[304,128]{1,0:T(8,128)(2,1)S(1)}, bf16[304,128]{1,0:T(8,128)(2,1)}, u32[]{:S(2)}) copy-start(bf16[304,128]{1,0:T(8,128)(2,1)} %get-tuple-element.50.refs_0_) | copy-start | bytes 233476
  21.2 7.8 %copy-start.5 = (f32[8,128]{1,0:T(8,128)S(1)}, f32[8,128]{1,0:T(8,128)}, u32[]{:S(2)}) copy-start(f32[8,128]{1,0:T(8,128)} %get-tuple-element.36.onebody_ref) | copy-start | bytes 12292
  21.2 7.8 %copy-start.6 = (s32[4]{0:T(128)S(1)}, s32[4]{0:T(128)}, u32[]{:S(2)}) copy-start(s32[4]{0:T(128)} %counts_ref.1) | copy-start | bytes 52
  26.9 5.0 %collective-permute-start.8 = (bf16[128,512]{1,0:T(8,128)(2,1)S(1)}, bf16[128,512]{1,0:T(8,128)(2,1)S(1)}, u32[]{:S(2)}, u32[]{:S(2)}) collective-permute-start(bf16[128,512]{1,0:T(8,128)(2,1)S(1)} %slice.10), channel_id=1, source_target_pairs={{0,8},{8,16},{16,24},{24,28},{28,20},{20,12},{12,4},{4,0},{1,9},{9... | collective-permute-start | bytes 393224 | tf_op jit(solution)/shard_map/ppermute | solution.py:135
  28.5 5.0 %collective-permute-start.9 = (bf16[128,512]{1,0:T(8,128)(2,1)S(1)}, bf16[128,512]{1,0:T(8,128)(2,1)S(1)}, u32[]{:S(2)}, u32[]{:S(2)}) collective-permute-start(bf16[128,512]{1,0:T(8,128)(2,1)S(1)} %slice.11), channel_id=1, source_target_pairs={{0,4},{8,0},{16,8},{24,16},{28,24},{20,28},{12,20},{4,12},{1,5},{9... | collective-permute-start | bytes 393224 | tf_op jit(solution)/shard_map/ppermute | solution.py:135

commit v18 on v11

--- a/solution.py
+++ b/solution.py
@@ -79,6 +79,27 @@
             transcendentals=0,
         ),
     )(cholesky_rot, *arrays)
+
+
+def cut(right, left):
+    rows, walkers, orbitals = right.shape
+    half = rows // 2
+
+    def kernel(right_ref, left_ref, upper_ref, lower_ref):
+        for b in range(walkers):
+            at = slice(b * orbitals, (b + 1) * orbitals)
+            upper_ref[:, at] = right_ref[:half, b, :]
+            lower_ref[:, at] = left_ref[half:, b, :]
+
+    return pl.pallas_call(
+        kernel,
+        name="cut",
+        out_shape=[jax.ShapeDtypeStruct((n, walkers * orbitals), right.dtype) for n in (half, rows - half)],
+        in_specs=[vmem()] * 2,
+        out_specs=[vmem()] * 2,
+        compiler_params=params(),
+        cost_estimate=pl.CostEstimate(flops=0, bytes_accessed=4 * right.size, transcendentals=0),
+    )(right, left)
 
 
 def tie(*arrays):
@@ -111,7 +132,8 @@
             left, mark = tie(next_left, mark)
         shifts += [-step, step]
         parts = parts + [right, left]
-    last = [lax.ppermute(right[: rows // 2], "chol", ahead), lax.ppermute(left[rows // 2 :], "chol", back)]
+    upper, lower = cut(right, left)
+    last = [lax.ppermute(upper, "chol", ahead), lax.ppermute(lower, "chol", back)]
     mark, *near = tie(mark, *near)
     packs = [packed[0], far] + near
     plan = do_prepare(packs)
@@ -346,7 +368,8 @@
 
 
 def measure(cholesky_rot, total, last, plan, vectors, walk_size):
-    _, walkers, orbitals = last[0].shape
+    _, orbitals, _ = cholesky_rot.shape
+    walkers = last[0].size // (last[0].shape[0] * orbitals)
     depth = sum(x.shape[0] for x in last)
     targets = walk_size * lax.axis_size("chol")
     whole = total is None
@@ -360,7 +383,11 @@
         chol_ref, plan_ref = refs[:2]
         last_refs = refs[2 : 2 + len(last)]
         out_ref, tensor_scr = refs[-2:]
-        rhs = [jnp.concatenate([x[:, b, :] for x in last_refs], axis=0) for b in range(walkers)]
+
+        def walker_rows(x, b):
+            return x[:, b, :] if len(x.shape) == 3 else x[:, b * orbitals : (b + 1) * orbitals]
+
+        rhs = [jnp.concatenate([walker_rows(x, b) for x in last_refs], axis=0) for b in range(walkers)]
         eye = lax.broadcasted_iota(jnp.int32, (LANES, LANES), 0) == lax.broadcasted_iota(
             jnp.int32, (LANES, LANES), 1
         )

time: 45.9 us -> 45.8 us (level)
    pallas_call x0 -> x1, Pallas kernels: none -> 0.55 us  [cut(): pl.pallas_call(kernel, name='cut', out_shape=[jax.ShapeDtypeStruct((n, wa...]
  transfers between devices with their start and end apart: 10 -> 10, of which waited for: 5 -> 5; matrix products, arithmetic and copies ran while one was open for 0% -> 0% of each run, Pallas kernels for 23% -> 24%
where the time goes in v18:
time: 45.8 us; the launch traced here: 45.7 us
  Pallas kernels  13.4 us (29%)
  starting transfers between devices  11 us (24%)
  blocking collectives  10.8 us (24%)
  waiting for transfers between devices  9.71 us (21%)
  between operations  0.73 us (2%)
    all_to_all x1, blocking collectives, per_device(): lax.all_to_all(stats, ('chol', 'walk'), split_axis=0, concat_axis=0, tile...  10.8 us
    ppermute x3, waiting for transfers between devices, ring(): lax.ppermute(right, 'chol', ahead)  6.96 us
    pallas_call x3, Pallas kernels, accumulate(): pl.pallas_call(kernel, name='accumulate', out_shape=[jax.ShapeDtypeStruct...  6.69 us
    ppermute x3, starting transfers between devices, ring(): lax.ppermute(right, 'chol', ahead)  6.35 us
    pallas_call x1, Pallas kernels, pack(): pl.pallas_call(kernel, name='pack', out_shape=[jax.ShapeDtypeStruct((8, L...  3.32 us
    ppermute x1, starting transfers between devices, exchange_far(): return lax.ppermute(packed[1], 'walk', [(q, q ^ 2) for q in range(size)])  1.71 us
    ppermute x1, starting transfers between devices, ring(): lax.ppermute(upper, 'chol', ahead)  1.63 us
    ppermute x1, waiting for transfers between devices, ring(): lax.ppermute(lower, 'chol', back)  1.45 us
  transfers between devices with their start and end apart: 10, of which 5 were waited for; matrix products, arithmetic and copies ran while one was open for 0% of the time, Pallas kernels for 24%

profile of v18, /device:TPU:0, one launch (start us, length us, event | category | flops | bytes accessed | tf_op | source)
XLA Modules:
  0.0 45.7 jit_solution(14731301112011361435)
XLA Ops:
  0.6 3.1 %collective-permute-start.2 = (bf16[256,2,256]{2,1,0:T(2,128)(2,1)}, bf16[256,2,256]{2,1,0:T(2,128)(2,1)S(1)}, u32[]{:S(2)}, u32[]{:S(2)}) collective-permute-start(bf16[256,2,256]{2,1,0:T(2,128)(2,1)} %refs_0_.2), channel_id=1, source_target_pairs={{0,8},{8,16},{16,24},{24,28},{28,20},{20,12},{12,4},{4,0},{1,9},{9... | collective-permute-start | bytes 786440 | tf_op jit(solution)/shard_map/ppermute | solution.py:120
  3.7 0.0 collective-permute-start
  3.7 3.3 %pack.1 = (f32[8,128]{1,0:T(8,128)}, bf16[304,128]{1,0:T(8,128)(2,1)}, bf16[560,128]{1,0:T(8,128)(2,1)}, bf16[304,128]{1,0:T(8,128)(2,1)}) custom-call(bf16[256,2,256]{2,1,0:T(2,128)(2,1)} %refs_0_.2, bf16[256,256]{1,0:T(8,128)(2,1)} %body_any.1, f32[4,8]{1,0:T(4,128)} %bitcast.10, f32[2]{0:T(128)} %weights_any.1, s32[4]{0:T(128)} %sources_any.1, ...), custom_call_target="tpu_custom_call" | custom-call | flops 100000000 | bytes 1000000 | tf_op jit(solution)/shard_map/pack/pallas_call | solution.py:247
  7.0 3.1 %collective-permute-done.2.refs_1_ = bf16[256,2,256]{2,1,0:T(2,128)(2,1)S(1)} collective-permute-done((bf16[256,2,256]{2,1,0:T(2,128)(2,1)}, bf16[256,2,256]{2,1,0:T(2,128)(2,1)S(1)}, u32[]{:S(2)}, u32[]{:S(2)}) %collective-permute-start.2) | collective-permute-done | bytes 262176 | tf_op jit(solution)/shard_map/ppermute | solution.py:120
  10.2 1.8 %collective-permute-start.3 = (bf16[256,2,256]{2,1,0:T(2,128)(2,1)S(1)}, bf16[256,2,256]{2,1,0:T(2,128)(2,1)S(1)}, u32[]{:S(2)}, u32[]{:S(2)}) collective-permute-start(bf16[256,2,256]{2,1,0:T(2,128)(2,1)S(1)} %collective-permute-done.2.refs_1_), channel_id=1, source_target_pairs={{0,8},{8,16},{16,24},{24,28},{28,20},{20,12},{12,4},{4,0},{1,9},{9... | collective-permute-start | bytes 786440 | tf_op jit(solution)/shard_map/ppermute | solution.py:120
  12.0 0.2 collective-permute-start.1
  12.2 1.7 %collective-permute-start.6 = (bf16[560,128]{1,0:T(8,128)(2,1)}, bf16[560,128]{1,0:T(8,128)(2,1)S(1)}, u32[]{:S(2)}, u32[]{:S(2)}) collective-permute-start(bf16[560,128]{1,0:T(8,128)(2,1)} %get-tuple-element.50), channel_id=1, source_target_pairs={{0,2},{1,3},{2,0},{3,1},{4,6},{5,7},{6,4},{7,5},{8,10},{9,11},{10,... | collective-permute-start | bytes 430088 | tf_op jit(solution)/shard_map/ppermute | solution.py:281
  13.9 2.5 %accumulate.3 = (f32[2,2048,256]{2,1,0:T(8,128)S(1)}, f32[8,128]{1,0:T(8,128)S(1)}) custom-call(bf16[8,256,2048]{2,1,0:T(8,128)(2,1)S(1)} %copy-done, bf16[256,2,256]{2,1,0:T(2,128)(2,1)S(1)} %copy-done.1, bf16[256,2,256]{2,1,0:T(2,128)(2,1)S(1)} %collective-permute-done.2.refs_1_, bf16[256,2,256]{2,1,0:T(2,128)(2,1)S(1)} %collective-permute-done.refs_2_), custom_call_target="tpu_custom_call" | custom-call | flops 1610612736 | bytes 3145728 | tf_op jit(solution)/shard_map/accumulate/pallas_call | solution.py:66
  16.4 1.3 %collective-permute-done.3.refs_0_ = bf16[256,2,256]{2,1,0:T(2,128)(2,1)S(1)} collective-permute-done((bf16[256,2,256]{2,1,0:T(2,128)(2,1)S(1)}, bf16[256,2,256]{2,1,0:T(2,128)(2,1)S(1)}, u32[]{:S(2)}, u32[]{:S(2)}) %collective-permute-start.3) | collective-permute-done | bytes 262176 | tf_op jit(solution)/shard_map/ppermute | solution.py:120
  17.7 1.5 %collective-permute-start.5 = (bf16[256,2,256]{2,1,0:T(2,128)(2,1)S(1)}, bf16[256,2,256]{2,1,0:T(2,128)(2,1)S(1)}, u32[]{:S(2)}, u32[]{:S(2)}) collective-permute-start(bf16[256,2,256]{2,1,0:T(2,128)(2,1)S(1)} %collective-permute-done.3.refs_0_), channel_id=1, source_target_pairs={{0,8},{8,16},{16,24},{24,28},{28,20},{20,12},{12,4},{4,0},{1,9},{9... | collective-permute-start | bytes 786440 | tf_op jit(solution)/shard_map/ppermute | solution.py:120
  19.1 0.5 %collective-permute-start.4 = (bf16[256,2,256]{2,1,0:T(2,128)(2,1)S(1)}, bf16[256,2,256]{2,1,0:T(2,128)(2,1)S(1)}, u32[]{:S(2)}, u32[]{:S(2)}) collective-permute-start(bf16[256,2,256]{2,1,0:T(2,128)(2,1)S(1)} %collective-permute-done.1.refs_1_), channel_id=1, source_target_pairs={{0,4},{8,0},{16,8},{24,16},{28,24},{20,28},{12,20},{4,12},{1,5},{9... | collective-permute-start | bytes 786440 | tf_op jit(solution)/shard_map/ppermute | solution.py:120
  19.7 0.1 collective-permute-start.7
  19.8 1.8 %accumulate.4 = (f32[2,2048,256]{2,1,0:T(8,128)S(1)}, f32[8,128]{1,0:T(8,128)S(1)}) custom-call(bf16[8,256,2048]{2,1,0:T(8,128)(2,1)S(1)} %copy-done, bf16[256,2,256]{2,1,0:T(2,128)(2,1)S(1)} %collective-permute-done.3.refs_0_, bf16[256,2,256]{2,1,0:T(2,128)(2,1)S(1)} %collective-permute-done.1.refs_1_, f32[8,128]{1,0:T(8,128)S(1)} %get-tuple-element.44.refs_2_, ...), custom_call_target="tpu_custom_call" | custom-call | flops 1073741824 | bytes 2097152 | tf_op jit(solution)/shard_map/accumulate/pallas_call | solution.py:66
  21.6 2.6 %collective-permute-done.5.right_ref.refs_0_ = bf16[256,2,256]{2,1,0:T(2,128)(2,1)S(1)} collective-permute-done((bf16[256,2,256]{2,1,0:T(2,128)(2,1)S(1)}, bf16[256,2,256]{2,1,0:T(2,128)(2,1)S(1)}, u32[]{:S(2)}, u32[]{:S(2)}) %collective-permute-start.5) | collective-permute-done | bytes 262176 | tf_op jit(solution)/shard_map/ppermute | solution.py:120
  24.2 1.3 %collective-permute-done.4.left_ref.refs_1_ = bf16[256,2,256]{2,1,0:T(2,128)(2,1)S(1)} collective-permute-done((bf16[256,2,256]{2,1,0:T(2,128)(2,1)S(1)}, bf16[256,2,256]{2,1,0:T(2,128)(2,1)S(1)}, u32[]{:S(2)}, u32[]{:S(2)}) %collective-permute-start.4) | collective-permute-done | bytes 262176 | tf_op jit(solution)/shard_map/ppermute | solution.py:120
  25.5 0.6 %cut.1 = (bf16[128,512]{1,0:T(8,128)(2,1)S(1)}, bf16[128,512]{1,0:T(8,128)(2,1)S(1)}) custom-call(bf16[256,2,256]{2,1,0:T(2,128)(2,1)S(1)} %collective-permute-done.5.right_ref.refs_0_, bf16[256,2,256]{2,1,0:T(2,128)(2,1)S(1)} %collective-permute-done.4.left_ref.refs_1_), custom_call_target="tpu_custom_call" | custom-call | bytes 524288 | tf_op jit(solution)/shard_map/cut/pallas_call | solution.py:94
  26.1 1.6 %collective-permute-start.8 = (bf16[128,512]{1,0:T(8,128)(2,1)S(1)}, bf16[128,512]{1,0:T(8,128)(2,1)S(1)}, u32[]{:S(2)}, u32[]{:S(2)}) collective-permute-start(bf16[128,512]{1,0:T(8,128)(2,1)S(1)} %get-tuple-element.57), channel_id=1, source_target_pairs={{0,8},{8,16},{16,24},{24,28},{28,20},{20,12},{12,4},{4,0},{1,9},{9... | collective-permute-start | bytes 393224 | tf_op jit(solution)/shard_map/ppermute | solution.py:136
  27.7 0.4 collective-permute-start.9
  28.2 0.6 %prepare.1.refs_1_.plan_ref = f32[32,128]{1,0:T(8,128)S(1)} custom-call(s32[4]{0:T(128)S(1)} %copy-done.4, f32[8,128]{1,0:T(8,128)S(1)} %copy-done.3, bf16[304,128]{1,0:T(8,128)(2,1)S(1)} %copy-done.2, bf16[560,128]{1,0:T(8,128)(2,1)S(1)} %collective-permute-done.6.refs_1_, bf16[608,128]{1,0:T(8,128)(2,1)S(1)} %collective-permute-done.7.refs_2_), custom_call_target="tpu_custom_call" | custom-call | flops 100000000 | bytes 1000000 | tf_op jit(solution)/shard_map/prepare/pallas_call | solution.py:359
  28.8 2.4 %accumulate.5 = (f32[2,2048,256]{2,1,0:T(8,128)S(1)}, f32[8,128]{1,0:T(8,128)}) custom-call(bf16[8,256,2048]{2,1,0:T(8,128)(2,1)S(1)} %copy-done, bf16[256,2,256]{2,1,0:T(2,128)(2,1)S(1)} %collective-permute-done.5.right_ref.refs_0_, bf16[256,2,256]{2,1,0:T(2,128)(2,1)S(1)} %collective-permute-done.4.left_ref.refs_1_, ...), custom_call_target="tpu_custom_call" | custom-call | flops 1073741824 | bytes 2097152 | tf_op jit(solution)/shard_map/accumulate/pallas_call | solution.py:66
  31.2 1.5 %collective-permute-done.9.refs_3_ = bf16[128,512]{1,0:T(8,128)(2,1)S(1)} collective-permute-done((bf16[128,512]{1,0:T(8,128)(2,1)S(1)}, bf16[128,512]{1,0:T(8,128)(2,1)S(1)}, u32[]{:S(2)}, u32[]{:S(2)}) %collective-permute-start.9) | collective-permute-done | bytes 131104 | tf_op jit(solution)/shard_map/ppermute | solution.py:136
  32.7 1.3 %measure.1 = f32[32,128]{1,0:T(8,128)S(1)} custom-call(bf16[8,256,2048]{2,1,0:T(8,128)(2,1)S(1)} %copy-done, f32[32,128]{1,0:T(8,128)S(1)} %prepare.1.refs_1_.plan_ref, bf16[128,512]{1,0:T(8,128)(2,1)S(1)} %collective-permute-done.8.refs_2_, bf16[128,512]{1,0:T(8,128)(2,1)S(1)} %collective-permute-done.9.refs_3_, f32[2,2048,256]{2,1,0:T(8,128)S(1)} %get-tuple-element.61.refs_4_), custom_call_target="tpu_custom_call" | custom-call | flops 536870912 | bytes 1048576 | tf_op jit(solution)/shard_map/measure/pallas_call | solution.py:435
  34.0 10.8 %all_to_all.11 = f32[32,1,128]{2,1,0:T(1,128)S(1)} all-to-all(f32[32,1,128]{2,1,0:T(1,128)S(1)} %bitcast.8), channel_id=1, replica_groups=mesh['chol'=8,'walk'=4] {'chol','walk'}, dimensions={0} | all-to-all | bytes 32768 | tf_op jit(solution)/shard_map/all_to_all | solution.py:516
  44.8 0.9 %finish.1 = (f32[1,4]{1,0:T(1,128)}, f32[1,4]{1,0:T(1,128)}, f32[128,128]{1,0:T(8,128)}) custom-call(f32[32,128]{1,0:T(8,128)S(1)} %bitcast.9, f32[32,128]{1,0:T(8,128)S(1)} %prepare.1.refs_1_.plan_ref, bf16[304,128]{1,0:T(8,128)(2,1)S(1)} %copy-done.2, bf16[560,128]{1,0:T(8,128)(2,1)S(1)} %collective-permute-done.6.refs_1_, ...), custom_call_target="tpu_custom_call" | custom-call | flops 1000000 | bytes 600000 | tf_op jit(solution)/shard_map/finish/pallas_call | solution.py:481
  (19 shorter events, 0.1 us)
Async XLA Ops:
  0.6 9.5 %collective-permute-start.2 = (bf16[256,2,256]{2,1,0:T(2,128)(2,1)}, bf16[256,2,256]{2,1,0:T(2,128)(2,1)S(1)}, u32[]{:S(2)}, u32[]{:S(2)}) collective-permute-start(bf16[256,2,256]{2,1,0:T(2,128)(2,1)} %refs_0_.2), channel_id=1, source_target_pairs={{0,8},{8,16},{16,24},{24,28},{28,20},{20,12},{12,4},{4,0},{1,9},{9... | collective-permute-start | bytes 786440 | tf_op jit(solution)/shard_map/ppermute | solution.py:120
  3.7 8.3 %collective-permute-start = (bf16[256,2,256]{2,1,0:T(2,128)(2,1)}, bf16[256,2,256]{2,1,0:T(2,128)(2,1)S(1)}, u32[]{:S(2)}, u32[]{:S(2)}) collective-permute-start(bf16[256,2,256]{2,1,0:T(2,128)(2,1)} %refs_0_.2), channel_id=1, source_target_pairs={{0,4},{8,0},{16,8},{24,16},{28,24},{20,28},{12,20},{4,12},{1,5},{9... | collective-permute-start | bytes 786440 | tf_op jit(solution)/shard_map/ppermute | solution.py:120
  3.7 10.2 %copy-start = (bf16[8,256,2048]{2,1,0:T(8,128)(2,1)S(1)}, bf16[8,256,2048]{2,1,0:T(8,128)(2,1)}, u32[]{:S(2)}) copy-start(bf16[8,256,2048]{2,1,0:T(8,128)(2,1)} %refs_0_.3) | copy-start | bytes 25165828
  3.7 10.2 %copy-start.1 = (bf16[256,2,256]{2,1,0:T(2,128)(2,1)S(1)}, bf16[256,2,256]{2,1,0:T(2,128)(2,1)}, u32[]{:S(2)}) copy-start(bf16[256,2,256]{2,1,0:T(2,128)(2,1)} %refs_0_.2) | copy-start | bytes 786436
  10.2 7.5 %collective-permute-start.3 = (bf16[256,2,256]{2,1,0:T(2,128)(2,1)S(1)}, bf16[256,2,256]{2,1,0:T(2,128)(2,1)S(1)}, u32[]{:S(2)}, u32[]{:S(2)}) collective-permute-start(bf16[256,2,256]{2,1,0:T(2,128)(2,1)S(1)} %collective-permute-done.2.refs_1_), channel_id=1, source_target_pairs={{0,8},{8,16},{16,24},{24,28},{28,20},{20,12},{12,4},{4,0},{1,9},{9... | collective-permute-start | bytes 786440 | tf_op jit(solution)/shard_map/ppermute | solution.py:120
  12.0 7.7 %copy-start.5 = (bf16[304,128]{1,0:T(8,128)(2,1)S(1)}, bf16[304,128]{1,0:T(8,128)(2,1)}, u32[]{:S(2)}) copy-start(bf16[304,128]{1,0:T(8,128)(2,1)} %get-tuple-element.49) | copy-start | bytes 233476
  12.0 7.2 %collective-permute-start.1 = (bf16[256,2,256]{2,1,0:T(2,128)(2,1)S(1)}, bf16[256,2,256]{2,1,0:T(2,128)(2,1)S(1)}, u32[]{:S(2)}, u32[]{:S(2)}) collective-permute-start(bf16[256,2,256]{2,1,0:T(2,128)(2,1)S(1)} %collective-permute-done.refs_2_), channel_id=1, source_target_pairs={{0,4},{8,0},{16,8},{24,16},{28,24},{20,28},{12,20},{4,12},{1,5},{9... | collective-permute-start | bytes 786440 | tf_op jit(solution)/shard_map/ppermute | solution.py:120
  12.2 7.5 %collective-permute-start.6 = (bf16[560,128]{1,0:T(8,128)(2,1)}, bf16[560,128]{1,0:T(8,128)(2,1)S(1)}, u32[]{:S(2)}, u32[]{:S(2)}) collective-permute-start(bf16[560,128]{1,0:T(8,128)(2,1)} %get-tuple-element.50), channel_id=1, source_target_pairs={{0,2},{1,3},{2,0},{3,1},{4,6},{5,7},{6,4},{7,5},{8,10},{9,11},{10,... | collective-permute-start | bytes 430088 | tf_op jit(solution)/shard_map/ppermute | solution.py:281
  17.7 6.6 %collective-permute-start.5 = (bf16[256,2,256]{2,1,0:T(2,128)(2,1)S(1)}, bf16[256,2,256]{2,1,0:T(2,128)(2,1)S(1)}, u32[]{:S(2)}, u32[]{:S(2)}) collective-permute-start(bf16[256,2,256]{2,1,0:T(2,128)(2,1)S(1)} %collective-permute-done.3.refs_0_), channel_id=1, source_target_pairs={{0,8},{8,16},{16,24},{24,28},{28,20},{20,12},{12,4},{4,0},{1,9},{9... | collective-permute-start | bytes 786440 | tf_op jit(solution)/shard_map/ppermute | solution.py:120
  19.1 6.4 %collective-permute-start.4 = (bf16[256,2,256]{2,1,0:T(2,128)(2,1)S(1)}, bf16[256,2,256]{2,1,0:T(2,128)(2,1)S(1)}, u32[]{:S(2)}, u32[]{:S(2)}) collective-permute-start(bf16[256,2,256]{2,1,0:T(2,128)(2,1)S(1)} %collective-permute-done.1.refs_1_), channel_id=1, source_target_pairs={{0,4},{8,0},{16,8},{24,16},{28,24},{20,28},{12,20},{4,12},{1,5},{9... | collective-permute-start | bytes 786440 | tf_op jit(solution)/shard_map/ppermute | solution.py:120
  19.7 8.4 %collective-permute-start.7 = (bf16[608,128]{1,0:T(8,128)(2,1)S(1)}, bf16[608,128]{1,0:T(8,128)(2,1)S(1)}, u32[]{:S(2)}, u32[]{:S(2)}) collective-permute-start(bf16[608,128]{1,0:T(8,128)(2,1)S(1)} %pad_maximum_fusion), channel_id=1, source_target_pairs={{0,1},{1,0},{2,3},{3,2},{4,5},{5,4},{6,7},{7,6},{8,9},{9,8},{10,11... | collective-permute-start | bytes 466952 | tf_op jit(solution)/shard_map/ppermute | solution.py:292
  19.8 8.3 %copy-start.2 = (bf16[304,128]{1,0:T(8,128)(2,1)S(1)}, bf16[304,128]{1,0:T(8,128)(2,1)}, u32[]{:S(2)}) copy-start(bf16[304,128]{1,0:T(8,128)(2,1)} %get-tuple-element.52.refs_0_) | copy-start | bytes 233476
  19.8 8.3 %copy-start.3 = (f32[8,128]{1,0:T(8,128)S(1)}, f32[8,128]{1,0:T(8,128)}, u32[]{:S(2)}) copy-start(f32[8,128]{1,0:T(8,128)} %get-tuple-element.38.onebody_ref) | copy-start | bytes 12292
  19.8 8.3 %copy-start.4 = (s32[4]{0:T(128)S(1)}, s32[4]{0:T(128)}, u32[]{:S(2)}) copy-start(s32[4]{0:T(128)} %counts_ref.1) | copy-start | bytes 52
  26.1 5.1 %collective-permute-start.8 = (bf16[128,512]{1,0:T(8,128)(2,1)S(1)}, bf16[128,512]{1,0:T(8,128)(2,1)S(1)}, u32[]{:S(2)}, u32[]{:S(2)}) collective-permute-start(bf16[128,512]{1,0:T(8,128)(2,1)S(1)} %get-tuple-element.57), channel_id=1, source_target_pairs={{0,8},{8,16},{16,24},{24,28},{28,20},{20,12},{12,4},{4,0},{1,9},{9... | collective-permute-start | bytes 393224 | tf_op jit(solution)/shard_map/ppermute | solution.py:136
  27.7 5.0 %collective-permute-start.9 = (bf16[128,512]{1,0:T(8,128)(2,1)S(1)}, bf16[128,512]{1,0:T(8,128)(2,1)S(1)}, u32[]{:S(2)}, u32[]{:S(2)}) collective-permute-start(bf16[128,512]{1,0:T(8,128)(2,1)S(1)} %get-tuple-element.58), channel_id=1, source_target_pairs={{0,4},{8,0},{16,8},{24,16},{28,24},{20,28},{12,20},{4,12},{1,5},{9... | collective-permute-start | bytes 393224 | tf_op jit(solution)/shard_map/ppermute | solution.py:136

commit v19 on v18

--- a/solution.py
+++ b/solution.py
@@ -128,8 +128,12 @@
                 near = exchange_near(packed, far)
             total, mark = accumulate(cholesky_rot, shifts, parts, total, mark)
             shifts, parts = [], []
-            right, mark = tie(next_right, mark)
-            left, mark = tie(next_left, mark)
+            if step == 2:
+                left, mark = tie(next_left, mark)
+                right, mark = tie(next_right, mark)
+            else:
+                right, mark = tie(next_right, mark)
+                left, mark = tie(next_left, mark)
         shifts += [-step, step]
         parts = parts + [right, left]
     upper, lower = cut(right, left)

time: 45.8 us -> 47 us (1.026)
  blocking collectives: 10.8 us -> 11.8 us
    ppermute x3, starting transfers between devices: 0.78 us -> 6.07 us  [ring(): lax.ppermute(left, 'chol', back)]
    ppermute x3, starting transfers between devices: 6.35 us -> 1.12 us  [ring(): lax.ppermute(right, 'chol', ahead)]
    ppermute x3, waiting for transfers between devices: 1.29 us -> 5.1 us  [ring(): lax.ppermute(left, 'chol', back)]
    ppermute x3, waiting for transfers between devices: 6.96 us -> 3.49 us  [ring(): lax.ppermute(right, 'chol', ahead)]
    all_to_all x1, blocking collectives: 10.8 us -> 11.8 us  [per_device(): lax.all_to_all(stats, ('chol', 'walk'), split_axis=0, concat_axis=0, tile...]
  transfers between devices with their start and end apart: 10 -> 10, of which waited for: 5 -> 6; matrix products, arithmetic and copies ran while one was open for 0% -> 0% of each run, Pallas kernels for 24% -> 24%
where the time goes in v19:
time: 47 us; the launch traced here: 46.8 us
  Pallas kernels  13.4 us (29%)
  blocking collectives  11.8 us (25%)
  starting transfers between devices  11 us (23%)
  waiting for transfers between devices  9.9 us (21%)
  between operations  0.73 us (2%)
    all_to_all x1, blocking collectives, per_device(): lax.all_to_all(stats, ('chol', 'walk'), split_axis=0, concat_axis=0, tile...  11.8 us
    pallas_call x3, Pallas kernels, accumulate(): pl.pallas_call(kernel, name='accumulate', out_shape=[jax.ShapeDtypeStruct...  6.67 us
    ppermute x3, starting transfers between devices, ring(): lax.ppermute(left, 'chol', back)  6.07 us
    ppermute x3, waiting for transfers between devices, ring(): lax.ppermute(left, 'chol', back)  5.1 us
    ppermute x3, waiting for transfers between devices, ring(): lax.ppermute(right, 'chol', ahead)  3.49 us
    pallas_call x1, Pallas kernels, pack(): pl.pallas_call(kernel, name='pack', out_shape=[jax.ShapeDtypeStruct((8, L...  3.32 us
    ppermute x1, starting transfers between devices, exchange_far(): return lax.ppermute(packed[1], 'walk', [(q, q ^ 2) for q in range(size)])  1.66 us
    ppermute x1, starting transfers between devices, ring(): lax.ppermute(upper, 'chol', ahead)  1.47 us
  transfers between devices with their start and end apart: 10, of which 6 were waited for; matrix products, arithmetic and copies ran while one was open for 0% of the time, Pallas kernels for 24%

profile of v19, /device:TPU:0, one launch (start us, length us, event | category | flops | bytes accessed | tf_op | source)
XLA Modules:
  0.0 46.8 jit_solution(5705255916917722988)
XLA Ops:
  0.6 3.0 %collective-permute-start = (bf16[256,2,256]{2,1,0:T(2,128)(2,1)}, bf16[256,2,256]{2,1,0:T(2,128)(2,1)S(1)}, u32[]{:S(2)}, u32[]{:S(2)}) collective-permute-start(bf16[256,2,256]{2,1,0:T(2,128)(2,1)} %refs_0_.2), channel_id=1, source_target_pairs={{0,4},{8,0},{16,8},{24,16},{28,24},{20,28},{12,20},{4,12},{1,5},{9... | collective-permute-start | bytes 786440 | tf_op jit(solution)/shard_map/ppermute | solution.py:120
  3.7 0.1 collective-permute-start.2
  3.8 3.3 %pack.1 = (f32[8,128]{1,0:T(8,128)}, bf16[304,128]{1,0:T(8,128)(2,1)}, bf16[560,128]{1,0:T(8,128)(2,1)}, bf16[304,128]{1,0:T(8,128)(2,1)}) custom-call(bf16[256,2,256]{2,1,0:T(2,128)(2,1)} %refs_0_.2, bf16[256,256]{1,0:T(8,128)(2,1)} %body_any.1, f32[4,8]{1,0:T(4,128)} %bitcast.10, f32[2]{0:T(128)} %weights_any.1, s32[4]{0:T(128)} %sources_any.1, ...), custom_call_target="tpu_custom_call" | custom-call | flops 100000000 | bytes 1000000 | tf_op jit(solution)/shard_map/pack/pallas_call | solution.py:251
  7.1 3.1 %collective-permute-done.refs_2_ = bf16[256,2,256]{2,1,0:T(2,128)(2,1)S(1)} collective-permute-done((bf16[256,2,256]{2,1,0:T(2,128)(2,1)}, bf16[256,2,256]{2,1,0:T(2,128)(2,1)S(1)}, u32[]{:S(2)}, u32[]{:S(2)}) %collective-permute-start) | collective-permute-done | bytes 262176 | tf_op jit(solution)/shard_map/ppermute | solution.py:120
  10.2 1.7 %collective-permute-start.1 = (bf16[256,2,256]{2,1,0:T(2,128)(2,1)S(1)}, bf16[256,2,256]{2,1,0:T(2,128)(2,1)S(1)}, u32[]{:S(2)}, u32[]{:S(2)}) collective-permute-start(bf16[256,2,256]{2,1,0:T(2,128)(2,1)S(1)} %collective-permute-done.refs_2_), channel_id=1, source_target_pairs={{0,4},{8,0},{16,8},{24,16},{28,24},{20,28},{12,20},{4,12},{1,5},{9... | collective-permute-start | bytes 786440 | tf_op jit(solution)/shard_map/ppermute | solution.py:120
  11.9 0.3 collective-permute-start.4
  12.3 1.7 %collective-permute-start.6 = (bf16[560,128]{1,0:T(8,128)(2,1)}, bf16[560,128]{1,0:T(8,128)(2,1)S(1)}, u32[]{:S(2)}, u32[]{:S(2)}) collective-permute-start(bf16[560,128]{1,0:T(8,128)(2,1)} %get-tuple-element.50), channel_id=1, source_target_pairs={{0,2},{1,3},{2,0},{3,1},{4,6},{5,7},{6,4},{7,5},{8,10},{9,11},{10,... | collective-permute-start | bytes 430088 | tf_op jit(solution)/shard_map/ppermute | solution.py:285
  13.9 2.5 %accumulate.3 = (f32[2,2048,256]{2,1,0:T(8,128)S(1)}, f32[8,128]{1,0:T(8,128)S(1)}) custom-call(bf16[8,256,2048]{2,1,0:T(8,128)(2,1)S(1)} %copy-done, bf16[256,2,256]{2,1,0:T(2,128)(2,1)S(1)} %copy-done.1, bf16[256,2,256]{2,1,0:T(2,128)(2,1)S(1)} %collective-permute-done.2.refs_1_, bf16[256,2,256]{2,1,0:T(2,128)(2,1)S(1)} %collective-permute-done.refs_2_), custom_call_target="tpu_custom_call" | custom-call | flops 1610612736 | bytes 3145728 | tf_op jit(solution)/shard_map/accumulate/pallas_call | solution.py:66
  16.4 1.3 %collective-permute-done.1.refs_1_ = bf16[256,2,256]{2,1,0:T(2,128)(2,1)S(1)} collective-permute-done((bf16[256,2,256]{2,1,0:T(2,128)(2,1)S(1)}, bf16[256,2,256]{2,1,0:T(2,128)(2,1)S(1)}, u32[]{:S(2)}, u32[]{:S(2)}) %collective-permute-start.1) | collective-permute-done | bytes 262176 | tf_op jit(solution)/shard_map/ppermute | solution.py:120
  17.7 1.1 %collective-permute-done.4.refs_0_ = bf16[256,2,256]{2,1,0:T(2,128)(2,1)S(1)} collective-permute-done((bf16[256,2,256]{2,1,0:T(2,128)(2,1)S(1)}, bf16[256,2,256]{2,1,0:T(2,128)(2,1)S(1)}, u32[]{:S(2)}, u32[]{:S(2)}) %collective-permute-start.4) | collective-permute-done | bytes 262176 | tf_op jit(solution)/shard_map/ppermute | solution.py:120
  18.8 0.7 %collective-permute-start.5 = (bf16[256,2,256]{2,1,0:T(2,128)(2,1)S(1)}, bf16[256,2,256]{2,1,0:T(2,128)(2,1)S(1)}, u32[]{:S(2)}, u32[]{:S(2)}) collective-permute-start(bf16[256,2,256]{2,1,0:T(2,128)(2,1)S(1)} %collective-permute-done.4.refs_0_), channel_id=1, source_target_pairs={{0,8},{8,16},{16,24},{24,28},{28,20},{20,12},{12,4},{4,0},{1,9},{9... | collective-permute-start | bytes 786440 | tf_op jit(solution)/shard_map/ppermute | solution.py:120
  19.5 1.4 %collective-permute-start.3 = (bf16[256,2,256]{2,1,0:T(2,128)(2,1)S(1)}, bf16[256,2,256]{2,1,0:T(2,128)(2,1)S(1)}, u32[]{:S(2)}, u32[]{:S(2)}) collective-permute-start(bf16[256,2,256]{2,1,0:T(2,128)(2,1)S(1)} %collective-permute-done.1.refs_1_), channel_id=1, source_target_pairs={{0,4},{8,0},{16,8},{24,16},{28,24},{20,28},{12,20},{4,12},{1,5},{9... | collective-permute-start | bytes 786440 | tf_op jit(solution)/shard_map/ppermute | solution.py:120
  21.0 1.8 %accumulate.4 = (f32[2,2048,256]{2,1,0:T(8,128)S(1)}, f32[8,128]{1,0:T(8,128)S(1)}) custom-call(bf16[8,256,2048]{2,1,0:T(8,128)(2,1)S(1)} %copy-done, bf16[256,2,256]{2,1,0:T(2,128)(2,1)S(1)} %collective-permute-done.4.refs_0_, bf16[256,2,256]{2,1,0:T(2,128)(2,1)S(1)} %collective-permute-done.1.refs_1_, f32[8,128]{1,0:T(8,128)S(1)} %get-tuple-element.44.refs_2_, ...), custom_call_target="tpu_custom_call" | custom-call | flops 1073741824 | bytes 2097152 | tf_op jit(solution)/shard_map/accumulate/pallas_call | solution.py:66
  22.8 2.4 %collective-permute-done.5.right_ref.refs_0_ = bf16[256,2,256]{2,1,0:T(2,128)(2,1)S(1)} collective-permute-done((bf16[256,2,256]{2,1,0:T(2,128)(2,1)S(1)}, bf16[256,2,256]{2,1,0:T(2,128)(2,1)S(1)}, u32[]{:S(2)}, u32[]{:S(2)}) %collective-permute-start.5) | collective-permute-done | bytes 262176 | tf_op jit(solution)/shard_map/ppermute | solution.py:120
  25.2 0.7 %collective-permute-done.3.left_ref.refs_1_ = bf16[256,2,256]{2,1,0:T(2,128)(2,1)S(1)} collective-permute-done((bf16[256,2,256]{2,1,0:T(2,128)(2,1)S(1)}, bf16[256,2,256]{2,1,0:T(2,128)(2,1)S(1)}, u32[]{:S(2)}, u32[]{:S(2)}) %collective-permute-start.3) | collective-permute-done | bytes 262176 | tf_op jit(solution)/shard_map/ppermute | solution.py:120
  25.8 0.6 %cut.1 = (bf16[128,512]{1,0:T(8,128)(2,1)S(1)}, bf16[128,512]{1,0:T(8,128)(2,1)S(1)}) custom-call(bf16[256,2,256]{2,1,0:T(2,128)(2,1)S(1)} %collective-permute-done.5.right_ref.refs_0_, bf16[256,2,256]{2,1,0:T(2,128)(2,1)S(1)} %collective-permute-done.3.left_ref.refs_1_), custom_call_target="tpu_custom_call" | custom-call | bytes 524288 | tf_op jit(solution)/shard_map/cut/pallas_call | solution.py:94
  26.4 1.5 %collective-permute-start.8 = (bf16[128,512]{1,0:T(8,128)(2,1)S(1)}, bf16[128,512]{1,0:T(8,128)(2,1)S(1)}, u32[]{:S(2)}, u32[]{:S(2)}) collective-permute-start(bf16[128,512]{1,0:T(8,128)(2,1)S(1)} %get-tuple-element.57), channel_id=1, source_target_pairs={{0,8},{8,16},{16,24},{24,28},{28,20},{20,12},{12,4},{4,0},{1,9},{9... | collective-permute-start | bytes 393224 | tf_op jit(solution)/shard_map/ppermute | solution.py:140
  27.9 0.6 %collective-permute-start.9 = (bf16[128,512]{1,0:T(8,128)(2,1)S(1)}, bf16[128,512]{1,0:T(8,128)(2,1)S(1)}, u32[]{:S(2)}, u32[]{:S(2)}) collective-permute-start(bf16[128,512]{1,0:T(8,128)(2,1)S(1)} %get-tuple-element.58), channel_id=1, source_target_pairs={{0,4},{8,0},{16,8},{24,16},{28,24},{20,28},{12,20},{4,12},{1,5},{9... | collective-permute-start | bytes 393224 | tf_op jit(solution)/shard_map/ppermute | solution.py:140
  28.5 0.6 %prepare.1.refs_1_.plan_ref = f32[32,128]{1,0:T(8,128)S(1)} custom-call(s32[4]{0:T(128)S(1)} %copy-done.4, f32[8,128]{1,0:T(8,128)S(1)} %copy-done.3, bf16[304,128]{1,0:T(8,128)(2,1)S(1)} %copy-done.2, bf16[560,128]{1,0:T(8,128)(2,1)S(1)} %collective-permute-done.6.refs_1_, bf16[608,128]{1,0:T(8,128)(2,1)S(1)} %collective-permute-done.7.refs_2_), custom_call_target="tpu_custom_call" | custom-call | flops 100000000 | bytes 1000000 | tf_op jit(solution)/shard_map/prepare/pallas_call | solution.py:363
  29.1 2.4 %accumulate.5 = (f32[2,2048,256]{2,1,0:T(8,128)S(1)}, f32[8,128]{1,0:T(8,128)}) custom-call(bf16[8,256,2048]{2,1,0:T(8,128)(2,1)S(1)} %copy-done, bf16[256,2,256]{2,1,0:T(2,128)(2,1)S(1)} %collective-permute-done.5.right_ref.refs_0_, bf16[256,2,256]{2,1,0:T(2,128)(2,1)S(1)} %collective-permute-done.3.left_ref.refs_1_, ...), custom_call_target="tpu_custom_call" | custom-call | flops 1073741824 | bytes 2097152 | tf_op jit(solution)/shard_map/accumulate/pallas_call | solution.py:66
  31.5 1.3 %collective-permute-done.9.refs_3_ = bf16[128,512]{1,0:T(8,128)(2,1)S(1)} collective-permute-done((bf16[128,512]{1,0:T(8,128)(2,1)S(1)}, bf16[128,512]{1,0:T(8,128)(2,1)S(1)}, u32[]{:S(2)}, u32[]{:S(2)}) %collective-permute-start.9) | collective-permute-done | bytes 131104 | tf_op jit(solution)/shard_map/ppermute | solution.py:140
  32.8 1.3 %measure.1 = f32[32,128]{1,0:T(8,128)S(1)} custom-call(bf16[8,256,2048]{2,1,0:T(8,128)(2,1)S(1)} %copy-done, f32[32,128]{1,0:T(8,128)S(1)} %prepare.1.refs_1_.plan_ref, bf16[128,512]{1,0:T(8,128)(2,1)S(1)} %collective-permute-done.8.refs_2_, bf16[128,512]{1,0:T(8,128)(2,1)S(1)} %collective-permute-done.9.refs_3_, f32[2,2048,256]{2,1,0:T(8,128)S(1)} %get-tuple-element.61.refs_4_), custom_call_target="tpu_custom_call" | custom-call | flops 536870912 | bytes 1048576 | tf_op jit(solution)/shard_map/measure/pallas_call | solution.py:439
  34.2 11.8 %all_to_all.11 = f32[32,1,128]{2,1,0:T(1,128)S(1)} all-to-all(f32[32,1,128]{2,1,0:T(1,128)S(1)} %bitcast.8), channel_id=1, replica_groups=mesh['chol'=8,'walk'=4] {'chol','walk'}, dimensions={0} | all-to-all | bytes 32768 | tf_op jit(solution)/shard_map/all_to_all | solution.py:520
  46.0 0.9 %finish.1 = (f32[1,4]{1,0:T(1,128)}, f32[1,4]{1,0:T(1,128)}, f32[128,128]{1,0:T(8,128)}) custom-call(f32[32,128]{1,0:T(8,128)S(1)} %bitcast.9, f32[32,128]{1,0:T(8,128)S(1)} %prepare.1.refs_1_.plan_ref, bf16[304,128]{1,0:T(8,128)(2,1)S(1)} %copy-done.2, bf16[560,128]{1,0:T(8,128)(2,1)S(1)} %collective-permute-done.6.refs_1_, ...), custom_call_target="tpu_custom_call" | custom-call | flops 1000000 | bytes 600000 | tf_op jit(solution)/shard_map/finish/pallas_call | solution.py:485
  (19 shorter events, 0.1 us)
Async XLA Ops:
  0.6 9.6 %collective-permute-start = (bf16[256,2,256]{2,1,0:T(2,128)(2,1)}, bf16[256,2,256]{2,1,0:T(2,128)(2,1)S(1)}, u32[]{:S(2)}, u32[]{:S(2)}) collective-permute-start(bf16[256,2,256]{2,1,0:T(2,128)(2,1)} %refs_0_.2), channel_id=1, source_target_pairs={{0,4},{8,0},{16,8},{24,16},{28,24},{20,28},{12,20},{4,12},{1,5},{9... | collective-permute-start | bytes 786440 | tf_op jit(solution)/shard_map/ppermute | solution.py:120
  3.7 8.3 %collective-permute-start.2 = (bf16[256,2,256]{2,1,0:T(2,128)(2,1)}, bf16[256,2,256]{2,1,0:T(2,128)(2,1)S(1)}, u32[]{:S(2)}, u32[]{:S(2)}) collective-permute-start(bf16[256,2,256]{2,1,0:T(2,128)(2,1)} %refs_0_.2), channel_id=1, source_target_pairs={{0,8},{8,16},{16,24},{24,28},{28,20},{20,12},{12,4},{4,0},{1,9},{9... | collective-permute-start | bytes 786440 | tf_op jit(solution)/shard_map/ppermute | solution.py:120
  3.8 10.1 %copy-start = (bf16[8,256,2048]{2,1,0:T(8,128)(2,1)S(1)}, bf16[8,256,2048]{2,1,0:T(8,128)(2,1)}, u32[]{:S(2)}) copy-start(bf16[8,256,2048]{2,1,0:T(8,128)(2,1)} %refs_0_.3) | copy-start | bytes 25165828
  3.8 10.1 %copy-start.1 = (bf16[256,2,256]{2,1,0:T(2,128)(2,1)S(1)}, bf16[256,2,256]{2,1,0:T(2,128)(2,1)}, u32[]{:S(2)}) copy-start(bf16[256,2,256]{2,1,0:T(2,128)(2,1)} %refs_0_.2) | copy-start | bytes 786436
  10.2 7.5 %collective-permute-start.1 = (bf16[256,2,256]{2,1,0:T(2,128)(2,1)S(1)}, bf16[256,2,256]{2,1,0:T(2,128)(2,1)S(1)}, u32[]{:S(2)}, u32[]{:S(2)}) collective-permute-start(bf16[256,2,256]{2,1,0:T(2,128)(2,1)S(1)} %collective-permute-done.refs_2_), channel_id=1, source_target_pairs={{0,4},{8,0},{16,8},{24,16},{28,24},{20,28},{12,20},{4,12},{1,5},{9... | collective-permute-start | bytes 786440 | tf_op jit(solution)/shard_map/ppermute | solution.py:120
  11.9 8.9 %copy-start.5 = (bf16[304,128]{1,0:T(8,128)(2,1)S(1)}, bf16[304,128]{1,0:T(8,128)(2,1)}, u32[]{:S(2)}) copy-start(bf16[304,128]{1,0:T(8,128)(2,1)} %get-tuple-element.49) | copy-start | bytes 233476
  11.9 6.9 %collective-permute-start.4 = (bf16[256,2,256]{2,1,0:T(2,128)(2,1)S(1)}, bf16[256,2,256]{2,1,0:T(2,128)(2,1)S(1)}, u32[]{:S(2)}, u32[]{:S(2)}) collective-permute-start(bf16[256,2,256]{2,1,0:T(2,128)(2,1)S(1)} %collective-permute-done.2.refs_1_), channel_id=1, source_target_pairs={{0,8},{8,16},{16,24},{24,28},{28,20},{20,12},{12,4},{4,0},{1,9},{9... | collective-permute-start | bytes 786440 | tf_op jit(solution)/shard_map/ppermute | solution.py:120
  12.3 8.6 %collective-permute-start.6 = (bf16[560,128]{1,0:T(8,128)(2,1)}, bf16[560,128]{1,0:T(8,128)(2,1)S(1)}, u32[]{:S(2)}, u32[]{:S(2)}) collective-permute-start(bf16[560,128]{1,0:T(8,128)(2,1)} %get-tuple-element.50), channel_id=1, source_target_pairs={{0,2},{1,3},{2,0},{3,1},{4,6},{5,7},{6,4},{7,5},{8,10},{9,11},{10,... | collective-permute-start | bytes 430088 | tf_op jit(solution)/shard_map/ppermute | solution.py:285
  18.8 6.4 %collective-permute-start.5 = (bf16[256,2,256]{2,1,0:T(2,128)(2,1)S(1)}, bf16[256,2,256]{2,1,0:T(2,128)(2,1)S(1)}, u32[]{:S(2)}, u32[]{:S(2)}) collective-permute-start(bf16[256,2,256]{2,1,0:T(2,128)(2,1)S(1)} %collective-permute-done.4.refs_0_), channel_id=1, source_target_pairs={{0,8},{8,16},{16,24},{24,28},{28,20},{20,12},{12,4},{4,0},{1,9},{9... | collective-permute-start | bytes 786440 | tf_op jit(solution)/shard_map/ppermute | solution.py:120
  19.5 6.4 %collective-permute-start.3 = (bf16[256,2,256]{2,1,0:T(2,128)(2,1)S(1)}, bf16[256,2,256]{2,1,0:T(2,128)(2,1)S(1)}, u32[]{:S(2)}, u32[]{:S(2)}) collective-permute-start(bf16[256,2,256]{2,1,0:T(2,128)(2,1)S(1)} %collective-permute-done.1.refs_1_), channel_id=1, source_target_pairs={{0,4},{8,0},{16,8},{24,16},{28,24},{20,28},{12,20},{4,12},{1,5},{9... | collective-permute-start | bytes 786440 | tf_op jit(solution)/shard_map/ppermute | solution.py:120
  20.9 7.6 %collective-permute-start.7 = (bf16[608,128]{1,0:T(8,128)(2,1)S(1)}, bf16[608,128]{1,0:T(8,128)(2,1)S(1)}, u32[]{:S(2)}, u32[]{:S(2)}) collective-permute-start(bf16[608,128]{1,0:T(8,128)(2,1)S(1)} %pad_maximum_fusion), channel_id=1, source_target_pairs={{0,1},{1,0},{2,3},{3,2},{4,5},{5,4},{6,7},{7,6},{8,9},{9,8},{10,11... | collective-permute-start | bytes 466952 | tf_op jit(solution)/shard_map/ppermute | solution.py:296
  21.0 7.5 %copy-start.2 = (bf16[304,128]{1,0:T(8,128)(2,1)S(1)}, bf16[304,128]{1,0:T(8,128)(2,1)}, u32[]{:S(2)}) copy-start(bf16[304,128]{1,0:T(8,128)(2,1)} %get-tuple-element.52.refs_0_) | copy-start | bytes 233476
  21.0 7.5 %copy-start.3 = (f32[8,128]{1,0:T(8,128)S(1)}, f32[8,128]{1,0:T(8,128)}, u32[]{:S(2)}) copy-start(f32[8,128]{1,0:T(8,128)} %get-tuple-element.38.onebody_ref) | copy-start | bytes 12292
  21.0 7.5 %copy-start.4 = (s32[4]{0:T(128)S(1)}, s32[4]{0:T(128)}, u32[]{:S(2)}) copy-start(s32[4]{0:T(128)} %counts_ref.1) | copy-start | bytes 52
  26.4 5.1 %collective-permute-start.8 = (bf16[128,512]{1,0:T(8,128)(2,1)S(1)}, bf16[128,512]{1,0:T(8,128)(2,1)S(1)}, u32[]{:S(2)}, u32[]{:S(2)}) collective-permute-start(bf16[128,512]{1,0:T(8,128)(2,1)S(1)} %get-tuple-element.57), channel_id=1, source_target_pairs={{0,8},{8,16},{16,24},{24,28},{28,20},{20,12},{12,4},{4,0},{1,9},{9... | collective-permute-start | bytes 393224 | tf_op jit(solution)/shard_map/ppermute | solution.py:140
  27.9 5.0 %collective-permute-start.9 = (bf16[128,512]{1,0:T(8,128)(2,1)S(1)}, bf16[128,512]{1,0:T(8,128)(2,1)S(1)}, u32[]{:S(2)}, u32[]{:S(2)}) collective-permute-start(bf16[128,512]{1,0:T(8,128)(2,1)S(1)} %get-tuple-element.58), channel_id=1, source_target_pairs={{0,4},{8,0},{16,8},{24,16},{28,24},{20,28},{12,20},{4,12},{1,5},{9... | collective-permute-start | bytes 393224 | tf_op jit(solution)/shard_map/ppermute | solution.py:140

commit v20 on v18

--- a/solution.py
+++ b/solution.py
@@ -392,6 +392,7 @@
             jnp.int32, (LANES, LANES), 1
         )
         exchange = [jnp.zeros((8, LANES), jnp.float32) for _ in range(walkers)]
+        crossed = [jnp.zeros((8, LANES), jnp.float32) for _ in range(walkers)]
         squares = [jnp.zeros((1, 1), jnp.float32) for _ in range(walkers)]
         drive = jnp.zeros((1, LANES), jnp.float32)
         start = 0 if whole else column_start(lax.axis_size("chol") // 2, depth)
@@ -415,7 +416,7 @@
                             two = tensor_scr[
                                 b, top + p * LANES : top + (p + 1) * LANES, q * LANES : (q + 1) * LANES
                             ]
-                            exchange[b] = exchange[b] + 2.0 * fold(two * one.T)
+                            crossed[b] = crossed[b] + fold(two * one.T)
                 trace = jnp.sum(fold(jnp.where(eye, diagonal, 0.0)), axis=0, keepdims=True)
                 trace = jnp.sum(trace, axis=1, keepdims=True)
                 squares[b] = squares[b] + trace * trace
@@ -424,7 +425,8 @@
         raw = plan_ref[at_single : at_single + 1, :]
         square = jnp.zeros((1, LANES), jnp.float32)
         for b in range(walkers):
-            swapped = jnp.sum(jnp.sum(exchange[b], axis=0, keepdims=True), axis=1, keepdims=True)
+            both = exchange[b] + 2.0 * crossed[b]
+            swapped = jnp.sum(jnp.sum(both, axis=0, keepdims=True), axis=1, keepdims=True)
             pick = plan_ref[at_pick + b : at_pick + b + 1, :]
             raw += pick * (0.5 * squares[b] - 0.5 * swapped)
             square += pick * squares[b]

time: 45.8 us -> 45.8 us (level)
  transfers between devices with their start and end apart: 10 -> 10, of which waited for: 5 -> 5; matrix products, arithmetic and copies ran while one was open for 0% -> 0% of each run, Pallas kernels for 24% -> 25%
where the time goes in v20:
time: 45.8 us; the launch traced here: 45.6 us
  Pallas kernels  13.4 us (29%)
  starting transfers between devices  11 us (24%)
  blocking collectives  10.8 us (24%)
  waiting for transfers between devices  9.71 us (21%)
  between operations  0.73 us (2%)
    all_to_all x1, blocking collectives, per_device(): lax.all_to_all(stats, ('chol', 'walk'), split_axis=0, concat_axis=0, tile...  10.8 us
    ppermute x3, waiting for transfers between devices, ring(): lax.ppermute(right, 'chol', ahead)  6.96 us
    pallas_call x3, Pallas kernels, accumulate(): pl.pallas_call(kernel, name='accumulate', out_shape=[jax.ShapeDtypeStruct...  6.69 us
    ppermute x3, starting transfers between devices, ring(): lax.ppermute(right, 'chol', ahead)  6.35 us
    pallas_call x1, Pallas kernels, pack(): pl.pallas_call(kernel, name='pack', out_shape=[jax.ShapeDtypeStruct((8, L...  3.32 us
    ppermute x1, starting transfers between devices, exchange_far(): return lax.ppermute(packed[1], 'walk', [(q, q ^ 2) for q in range(size)])  1.71 us
    ppermute x1, starting transfers between devices, ring(): lax.ppermute(upper, 'chol', ahead)  1.63 us
    ppermute x1, waiting for transfers between devices, ring(): lax.ppermute(lower, 'chol', back)  1.45 us
  transfers between devices with their start and end apart: 10, of which 5 were waited for; matrix products, arithmetic and copies ran while one was open for 0% of the time, Pallas kernels for 25%

profile of v20, /device:TPU:0, one launch (start us, length us, event | category | flops | bytes accessed | tf_op | source)
XLA Modules:
  0.0 45.6 jit_solution(16014342212702940080)
XLA Ops:
  0.6 3.1 %collective-permute-start.2 = (bf16[256,2,256]{2,1,0:T(2,128)(2,1)}, bf16[256,2,256]{2,1,0:T(2,128)(2,1)S(1)}, u32[]{:S(2)}, u32[]{:S(2)}) collective-permute-start(bf16[256,2,256]{2,1,0:T(2,128)(2,1)} %refs_0_.2), channel_id=1, source_target_pairs={{0,8},{8,16},{16,24},{24,28},{28,20},{20,12},{12,4},{4,0},{1,9},{9... | collective-permute-start | bytes 786440 | tf_op jit(solution)/shard_map/ppermute | solution.py:120
  3.7 0.0 collective-permute-start
  3.7 3.3 %pack.1 = (f32[8,128]{1,0:T(8,128)}, bf16[304,128]{1,0:T(8,128)(2,1)}, bf16[560,128]{1,0:T(8,128)(2,1)}, bf16[304,128]{1,0:T(8,128)(2,1)}) custom-call(bf16[256,2,256]{2,1,0:T(2,128)(2,1)} %refs_0_.2, bf16[256,256]{1,0:T(8,128)(2,1)} %body_any.1, f32[4,8]{1,0:T(4,128)} %bitcast.10, f32[2]{0:T(128)} %weights_any.1, s32[4]{0:T(128)} %sources_any.1, ...), custom_call_target="tpu_custom_call" | custom-call | flops 100000000 | bytes 1000000 | tf_op jit(solution)/shard_map/pack/pallas_call | solution.py:247
  7.0 3.1 %collective-permute-done.2.refs_1_ = bf16[256,2,256]{2,1,0:T(2,128)(2,1)S(1)} collective-permute-done((bf16[256,2,256]{2,1,0:T(2,128)(2,1)}, bf16[256,2,256]{2,1,0:T(2,128)(2,1)S(1)}, u32[]{:S(2)}, u32[]{:S(2)}) %collective-permute-start.2) | collective-permute-done | bytes 262176 | tf_op jit(solution)/shard_map/ppermute | solution.py:120
  10.2 1.8 %collective-permute-start.3 = (bf16[256,2,256]{2,1,0:T(2,128)(2,1)S(1)}, bf16[256,2,256]{2,1,0:T(2,128)(2,1)S(1)}, u32[]{:S(2)}, u32[]{:S(2)}) collective-permute-start(bf16[256,2,256]{2,1,0:T(2,128)(2,1)S(1)} %collective-permute-done.2.refs_1_), channel_id=1, source_target_pairs={{0,8},{8,16},{16,24},{24,28},{28,20},{20,12},{12,4},{4,0},{1,9},{9... | collective-permute-start | bytes 786440 | tf_op jit(solution)/shard_map/ppermute | solution.py:120
  12.0 0.2 collective-permute-start.1
  12.2 1.7 %collective-permute-start.6 = (bf16[560,128]{1,0:T(8,128)(2,1)}, bf16[560,128]{1,0:T(8,128)(2,1)S(1)}, u32[]{:S(2)}, u32[]{:S(2)}) collective-permute-start(bf16[560,128]{1,0:T(8,128)(2,1)} %get-tuple-element.50), channel_id=1, source_target_pairs={{0,2},{1,3},{2,0},{3,1},{4,6},{5,7},{6,4},{7,5},{8,10},{9,11},{10,... | collective-permute-start | bytes 430088 | tf_op jit(solution)/shard_map/ppermute | solution.py:281
  13.9 2.5 %accumulate.3 = (f32[2,2048,256]{2,1,0:T(8,128)S(1)}, f32[8,128]{1,0:T(8,128)S(1)}) custom-call(bf16[8,256,2048]{2,1,0:T(8,128)(2,1)S(1)} %copy-done, bf16[256,2,256]{2,1,0:T(2,128)(2,1)S(1)} %copy-done.1, bf16[256,2,256]{2,1,0:T(2,128)(2,1)S(1)} %collective-permute-done.2.refs_1_, bf16[256,2,256]{2,1,0:T(2,128)(2,1)S(1)} %collective-permute-done.refs_2_), custom_call_target="tpu_custom_call" | custom-call | flops 1610612736 | bytes 3145728 | tf_op jit(solution)/shard_map/accumulate/pallas_call | solution.py:66
  16.4 1.3 %collective-permute-done.3.refs_0_ = bf16[256,2,256]{2,1,0:T(2,128)(2,1)S(1)} collective-permute-done((bf16[256,2,256]{2,1,0:T(2,128)(2,1)S(1)}, bf16[256,2,256]{2,1,0:T(2,128)(2,1)S(1)}, u32[]{:S(2)}, u32[]{:S(2)}) %collective-permute-start.3) | collective-permute-done | bytes 262176 | tf_op jit(solution)/shard_map/ppermute | solution.py:120
  17.7 1.5 %collective-permute-start.5 = (bf16[256,2,256]{2,1,0:T(2,128)(2,1)S(1)}, bf16[256,2,256]{2,1,0:T(2,128)(2,1)S(1)}, u32[]{:S(2)}, u32[]{:S(2)}) collective-permute-start(bf16[256,2,256]{2,1,0:T(2,128)(2,1)S(1)} %collective-permute-done.3.refs_0_), channel_id=1, source_target_pairs={{0,8},{8,16},{16,24},{24,28},{28,20},{20,12},{12,4},{4,0},{1,9},{9... | collective-permute-start | bytes 786440 | tf_op jit(solution)/shard_map/ppermute | solution.py:120
  19.1 0.5 %collective-permute-start.4 = (bf16[256,2,256]{2,1,0:T(2,128)(2,1)S(1)}, bf16[256,2,256]{2,1,0:T(2,128)(2,1)S(1)}, u32[]{:S(2)}, u32[]{:S(2)}) collective-permute-start(bf16[256,2,256]{2,1,0:T(2,128)(2,1)S(1)} %collective-permute-done.1.refs_1_), channel_id=1, source_target_pairs={{0,4},{8,0},{16,8},{24,16},{28,24},{20,28},{12,20},{4,12},{1,5},{9... | collective-permute-start | bytes 786440 | tf_op jit(solution)/shard_map/ppermute | solution.py:120
  19.7 0.1 collective-permute-start.7
  19.8 1.8 %accumulate.4 = (f32[2,2048,256]{2,1,0:T(8,128)S(1)}, f32[8,128]{1,0:T(8,128)S(1)}) custom-call(bf16[8,256,2048]{2,1,0:T(8,128)(2,1)S(1)} %copy-done, bf16[256,2,256]{2,1,0:T(2,128)(2,1)S(1)} %collective-permute-done.3.refs_0_, bf16[256,2,256]{2,1,0:T(2,128)(2,1)S(1)} %collective-permute-done.1.refs_1_, f32[8,128]{1,0:T(8,128)S(1)} %get-tuple-element.44.refs_2_, ...), custom_call_target="tpu_custom_call" | custom-call | flops 1073741824 | bytes 2097152 | tf_op jit(solution)/shard_map/accumulate/pallas_call | solution.py:66
  21.6 2.6 %collective-permute-done.5.right_ref.refs_0_ = bf16[256,2,256]{2,1,0:T(2,128)(2,1)S(1)} collective-permute-done((bf16[256,2,256]{2,1,0:T(2,128)(2,1)S(1)}, bf16[256,2,256]{2,1,0:T(2,128)(2,1)S(1)}, u32[]{:S(2)}, u32[]{:S(2)}) %collective-permute-start.5) | collective-permute-done | bytes 262176 | tf_op jit(solution)/shard_map/ppermute | solution.py:120
  24.2 1.3 %collective-permute-done.4.left_ref.refs_1_ = bf16[256,2,256]{2,1,0:T(2,128)(2,1)S(1)} collective-permute-done((bf16[256,2,256]{2,1,0:T(2,128)(2,1)S(1)}, bf16[256,2,256]{2,1,0:T(2,128)(2,1)S(1)}, u32[]{:S(2)}, u32[]{:S(2)}) %collective-permute-start.4) | collective-permute-done | bytes 262176 | tf_op jit(solution)/shard_map/ppermute | solution.py:120
  25.5 0.6 %cut.1 = (bf16[128,512]{1,0:T(8,128)(2,1)S(1)}, bf16[128,512]{1,0:T(8,128)(2,1)S(1)}) custom-call(bf16[256,2,256]{2,1,0:T(2,128)(2,1)S(1)} %collective-permute-done.5.right_ref.refs_0_, bf16[256,2,256]{2,1,0:T(2,128)(2,1)S(1)} %collective-permute-done.4.left_ref.refs_1_), custom_call_target="tpu_custom_call" | custom-call | bytes 524288 | tf_op jit(solution)/shard_map/cut/pallas_call | solution.py:94
  26.1 1.6 %collective-permute-start.8 = (bf16[128,512]{1,0:T(8,128)(2,1)S(1)}, bf16[128,512]{1,0:T(8,128)(2,1)S(1)}, u32[]{:S(2)}, u32[]{:S(2)}) collective-permute-start(bf16[128,512]{1,0:T(8,128)(2,1)S(1)} %get-tuple-element.57), channel_id=1, source_target_pairs={{0,8},{8,16},{16,24},{24,28},{28,20},{20,12},{12,4},{4,0},{1,9},{9... | collective-permute-start | bytes 393224 | tf_op jit(solution)/shard_map/ppermute | solution.py:136
  27.7 0.4 collective-permute-start.9
  28.2 0.6 %prepare.1.refs_1_.plan_ref = f32[32,128]{1,0:T(8,128)S(1)} custom-call(s32[4]{0:T(128)S(1)} %copy-done.4, f32[8,128]{1,0:T(8,128)S(1)} %copy-done.3, bf16[304,128]{1,0:T(8,128)(2,1)S(1)} %copy-done.2, bf16[560,128]{1,0:T(8,128)(2,1)S(1)} %collective-permute-done.6.refs_1_, bf16[608,128]{1,0:T(8,128)(2,1)S(1)} %collective-permute-done.7.refs_2_), custom_call_target="tpu_custom_call" | custom-call | flops 100000000 | bytes 1000000 | tf_op jit(solution)/shard_map/prepare/pallas_call | solution.py:359
  28.8 2.4 %accumulate.5 = (f32[2,2048,256]{2,1,0:T(8,128)S(1)}, f32[8,128]{1,0:T(8,128)}) custom-call(bf16[8,256,2048]{2,1,0:T(8,128)(2,1)S(1)} %copy-done, bf16[256,2,256]{2,1,0:T(2,128)(2,1)S(1)} %collective-permute-done.5.right_ref.refs_0_, bf16[256,2,256]{2,1,0:T(2,128)(2,1)S(1)} %collective-permute-done.4.left_ref.refs_1_, ...), custom_call_target="tpu_custom_call" | custom-call | flops 1073741824 | bytes 2097152 | tf_op jit(solution)/shard_map/accumulate/pallas_call | solution.py:66
  31.2 1.5 %collective-permute-done.9.refs_3_ = bf16[128,512]{1,0:T(8,128)(2,1)S(1)} collective-permute-done((bf16[128,512]{1,0:T(8,128)(2,1)S(1)}, bf16[128,512]{1,0:T(8,128)(2,1)S(1)}, u32[]{:S(2)}, u32[]{:S(2)}) %collective-permute-start.9) | collective-permute-done | bytes 131104 | tf_op jit(solution)/shard_map/ppermute | solution.py:136
  32.7 1.3 %measure.1 = f32[32,128]{1,0:T(8,128)S(1)} custom-call(bf16[8,256,2048]{2,1,0:T(8,128)(2,1)S(1)} %copy-done, f32[32,128]{1,0:T(8,128)S(1)} %prepare.1.refs_1_.plan_ref, bf16[128,512]{1,0:T(8,128)(2,1)S(1)} %collective-permute-done.8.refs_2_, bf16[128,512]{1,0:T(8,128)(2,1)S(1)} %collective-permute-done.9.refs_3_, f32[2,2048,256]{2,1,0:T(8,128)S(1)} %get-tuple-element.61.refs_4_), custom_call_target="tpu_custom_call" | custom-call | flops 536870912 | bytes 1048576 | tf_op jit(solution)/shard_map/measure/pallas_call | solution.py:437
  34.0 10.8 %all_to_all.11 = f32[32,1,128]{2,1,0:T(1,128)S(1)} all-to-all(f32[32,1,128]{2,1,0:T(1,128)S(1)} %bitcast.8), channel_id=1, replica_groups=mesh['chol'=8,'walk'=4] {'chol','walk'}, dimensions={0} | all-to-all | bytes 32768 | tf_op jit(solution)/shard_map/all_to_all | solution.py:518
  44.8 0.9 %finish.1 = (f32[1,4]{1,0:T(1,128)}, f32[1,4]{1,0:T(1,128)}, f32[128,128]{1,0:T(8,128)}) custom-call(f32[32,128]{1,0:T(8,128)S(1)} %bitcast.9, f32[32,128]{1,0:T(8,128)S(1)} %prepare.1.refs_1_.plan_ref, bf16[304,128]{1,0:T(8,128)(2,1)S(1)} %copy-done.2, bf16[560,128]{1,0:T(8,128)(2,1)S(1)} %collective-permute-done.6.refs_1_, ...), custom_call_target="tpu_custom_call" | custom-call | flops 1000000 | bytes 600000 | tf_op jit(solution)/shard_map/finish/pallas_call | solution.py:483
  (19 shorter events, 0.1 us)
Async XLA Ops:
  0.6 9.5 %collective-permute-start.2 = (bf16[256,2,256]{2,1,0:T(2,128)(2,1)}, bf16[256,2,256]{2,1,0:T(2,128)(2,1)S(1)}, u32[]{:S(2)}, u32[]{:S(2)}) collective-permute-start(bf16[256,2,256]{2,1,0:T(2,128)(2,1)} %refs_0_.2), channel_id=1, source_target_pairs={{0,8},{8,16},{16,24},{24,28},{28,20},{20,12},{12,4},{4,0},{1,9},{9... | collective-permute-start | bytes 786440 | tf_op jit(solution)/shard_map/ppermute | solution.py:120
  3.7 8.3 %collective-permute-start = (bf16[256,2,256]{2,1,0:T(2,128)(2,1)}, bf16[256,2,256]{2,1,0:T(2,128)(2,1)S(1)}, u32[]{:S(2)}, u32[]{:S(2)}) collective-permute-start(bf16[256,2,256]{2,1,0:T(2,128)(2,1)} %refs_0_.2), channel_id=1, source_target_pairs={{0,4},{8,0},{16,8},{24,16},{28,24},{20,28},{12,20},{4,12},{1,5},{9... | collective-permute-start | bytes 786440 | tf_op jit(solution)/shard_map/ppermute | solution.py:120
  3.7 10.2 %copy-start = (bf16[8,256,2048]{2,1,0:T(8,128)(2,1)S(1)}, bf16[8,256,2048]{2,1,0:T(8,128)(2,1)}, u32[]{:S(2)}) copy-start(bf16[8,256,2048]{2,1,0:T(8,128)(2,1)} %refs_0_.3) | copy-start | bytes 25165828
  3.7 10.2 %copy-start.1 = (bf16[256,2,256]{2,1,0:T(2,128)(2,1)S(1)}, bf16[256,2,256]{2,1,0:T(2,128)(2,1)}, u32[]{:S(2)}) copy-start(bf16[256,2,256]{2,1,0:T(2,128)(2,1)} %refs_0_.2) | copy-start | bytes 786436
  10.2 7.5 %collective-permute-start.3 = (bf16[256,2,256]{2,1,0:T(2,128)(2,1)S(1)}, bf16[256,2,256]{2,1,0:T(2,128)(2,1)S(1)}, u32[]{:S(2)}, u32[]{:S(2)}) collective-permute-start(bf16[256,2,256]{2,1,0:T(2,128)(2,1)S(1)} %collective-permute-done.2.refs_1_), channel_id=1, source_target_pairs={{0,8},{8,16},{16,24},{24,28},{28,20},{20,12},{12,4},{4,0},{1,9},{9... | collective-permute-start | bytes 786440 | tf_op jit(solution)/shard_map/ppermute | solution.py:120
  12.0 7.7 %copy-start.5 = (bf16[304,128]{1,0:T(8,128)(2,1)S(1)}, bf16[304,128]{1,0:T(8,128)(2,1)}, u32[]{:S(2)}) copy-start(bf16[304,128]{1,0:T(8,128)(2,1)} %get-tuple-element.49) | copy-start | bytes 233476
  12.0 7.2 %collective-permute-start.1 = (bf16[256,2,256]{2,1,0:T(2,128)(2,1)S(1)}, bf16[256,2,256]{2,1,0:T(2,128)(2,1)S(1)}, u32[]{:S(2)}, u32[]{:S(2)}) collective-permute-start(bf16[256,2,256]{2,1,0:T(2,128)(2,1)S(1)} %collective-permute-done.refs_2_), channel_id=1, source_target_pairs={{0,4},{8,0},{16,8},{24,16},{28,24},{20,28},{12,20},{4,12},{1,5},{9... | collective-permute-start | bytes 786440 | tf_op jit(solution)/shard_map/ppermute | solution.py:120
  12.2 7.5 %collective-permute-start.6 = (bf16[560,128]{1,0:T(8,128)(2,1)}, bf16[560,128]{1,0:T(8,128)(2,1)S(1)}, u32[]{:S(2)}, u32[]{:S(2)}) collective-permute-start(bf16[560,128]{1,0:T(8,128)(2,1)} %get-tuple-element.50), channel_id=1, source_target_pairs={{0,2},{1,3},{2,0},{3,1},{4,6},{5,7},{6,4},{7,5},{8,10},{9,11},{10,... | collective-permute-start | bytes 430088 | tf_op jit(solution)/shard_map/ppermute | solution.py:281
  17.7 6.6 %collective-permute-start.5 = (bf16[256,2,256]{2,1,0:T(2,128)(2,1)S(1)}, bf16[256,2,256]{2,1,0:T(2,128)(2,1)S(1)}, u32[]{:S(2)}, u32[]{:S(2)}) collective-permute-start(bf16[256,2,256]{2,1,0:T(2,128)(2,1)S(1)} %collective-permute-done.3.refs_0_), channel_id=1, source_target_pairs={{0,8},{8,16},{16,24},{24,28},{28,20},{20,12},{12,4},{4,0},{1,9},{9... | collective-permute-start | bytes 786440 | tf_op jit(solution)/shard_map/ppermute | solution.py:120
  19.1 6.4 %collective-permute-start.4 = (bf16[256,2,256]{2,1,0:T(2,128)(2,1)S(1)}, bf16[256,2,256]{2,1,0:T(2,128)(2,1)S(1)}, u32[]{:S(2)}, u32[]{:S(2)}) collective-permute-start(bf16[256,2,256]{2,1,0:T(2,128)(2,1)S(1)} %collective-permute-done.1.refs_1_), channel_id=1, source_target_pairs={{0,4},{8,0},{16,8},{24,16},{28,24},{20,28},{12,20},{4,12},{1,5},{9... | collective-permute-start | bytes 786440 | tf_op jit(solution)/shard_map/ppermute | solution.py:120
  19.7 8.4 %collective-permute-start.7 = (bf16[608,128]{1,0:T(8,128)(2,1)S(1)}, bf16[608,128]{1,0:T(8,128)(2,1)S(1)}, u32[]{:S(2)}, u32[]{:S(2)}) collective-permute-start(bf16[608,128]{1,0:T(8,128)(2,1)S(1)} %pad_maximum_fusion), channel_id=1, source_target_pairs={{0,1},{1,0},{2,3},{3,2},{4,5},{5,4},{6,7},{7,6},{8,9},{9,8},{10,11... | collective-permute-start | bytes 466952 | tf_op jit(solution)/shard_map/ppermute | solution.py:292
  19.8 8.3 %copy-start.2 = (bf16[304,128]{1,0:T(8,128)(2,1)S(1)}, bf16[304,128]{1,0:T(8,128)(2,1)}, u32[]{:S(2)}) copy-start(bf16[304,128]{1,0:T(8,128)(2,1)} %get-tuple-element.52.refs_0_) | copy-start | bytes 233476
  19.8 8.3 %copy-start.3 = (f32[8,128]{1,0:T(8,128)S(1)}, f32[8,128]{1,0:T(8,128)}, u32[]{:S(2)}) copy-start(f32[8,128]{1,0:T(8,128)} %get-tuple-element.38.onebody_ref) | copy-start | bytes 12292
  19.8 8.3 %copy-start.4 = (s32[4]{0:T(128)S(1)}, s32[4]{0:T(128)}, u32[]{:S(2)}) copy-start(s32[4]{0:T(128)} %counts_ref.1) | copy-start | bytes 52
  26.1 5.1 %collective-permute-start.8 = (bf16[128,512]{1,0:T(8,128)(2,1)S(1)}, bf16[128,512]{1,0:T(8,128)(2,1)S(1)}, u32[]{:S(2)}, u32[]{:S(2)}) collective-permute-start(bf16[128,512]{1,0:T(8,128)(2,1)S(1)} %get-tuple-element.57), channel_id=1, source_target_pairs={{0,8},{8,16},{16,24},{24,28},{28,20},{20,12},{12,4},{4,0},{1,9},{9... | collective-permute-start | bytes 393224 | tf_op jit(solution)/shard_map/ppermute | solution.py:136
  27.7 5.0 %collective-permute-start.9 = (bf16[128,512]{1,0:T(8,128)(2,1)S(1)}, bf16[128,512]{1,0:T(8,128)(2,1)S(1)}, u32[]{:S(2)}, u32[]{:S(2)}) collective-permute-start(bf16[128,512]{1,0:T(8,128)(2,1)S(1)} %get-tuple-element.58), channel_id=1, source_target_pairs={{0,4},{8,0},{16,8},{24,16},{28,24},{20,28},{12,20},{4,12},{1,5},{9... | collective-permute-start | bytes 393224 | tf_op jit(solution)/shard_map/ppermute | solution.py:136
